TPU v7x, 128 devices: a whole 4x4x4 slice. The times are simulated.
128 devices in a mesh: pool: 16 (over y, x), tp: 8 (over z, core).
Axes of the slice: x: 4, y: 4, z: 4, core: 2. Of those that a mesh axis runs over, the one named last changes fastest.
Arguments:
- hidden: bfloat16 [8192, 8192], P('pool', 'tp'), may hold values from -6 to 6
- w_query: bfloat16 [8192, 4096], P(None, 'tp'), may hold values from -0.15625 to 0.15625
- w_keyval: bfloat16 [8192, 2048], P(None, 'tp'), may hold values from -0.0625 to 0.0625
- store: bfloat16 [1024, 8, 64, 2, 128], P('pool', 'tp'), may hold values from -270 to 270
- page_owner: int32 [16, 32], replicated, may hold values from 0 to 15, as said below
- page_slot: int32 [16, 32], replicated, may hold values from 0 to 63, as said below
- new_owner: int32 [16, 8], replicated, may hold values from 0 to 15, as said below
Outputs:
- attended: bfloat16 [8192, 4096], P('pool', 'tp')
- new_store: bfloat16 [512, 8, 64, 2, 128], P('pool', 'tp')
Inputs may be any that keep to these rules, and one draw needn't show every extreme that they name: `page_owner`: one request has at most 4 pages on one owner, and every request has exactly 4 pages on some owner. `page_slot`: pages on one owner have distinct slots. `new_owner`: at most 2 pages of one request go to one owner, and in every draw one owner receives exactly 2 pages from every request.
All inputs are finite; a program needn't handle non-finite values.
Results may differ from a plain program's by a relative error of at most 0.02.
Values may be sent and summed in bfloat16 or wider, within the bound.
No kernel may reach another device: no remote copies, remote signals or barrier semaphores. Data moves between devices by JAX's collectives and lax.ppermute only.
A program may use at most 192 MiB of HBM per device.

v0:
```python
import math

import jax
import jax.numpy as jnp
from jax import lax
from jax.sharding import PartitionSpec as P

D = 8192
HD = 128
PAGE = 64
PUSH_CAP = 2


neg_big = -1e30


def rope_tables(row_count, offset):
    half_dim = HD // 2
    frequency = 500000.0 ** (-(jnp.arange(half_dim, dtype=jnp.float32) * (2.0 / HD)))
    positions = (offset + jnp.arange(row_count, dtype=jnp.int32)).astype(jnp.float32)
    angles = positions[:, None] * frequency[None, :]
    return (jnp.cos(angles), jnp.sin(angles))


def rotate(values, cosine, sine_table):
    half_dim = HD // 2
    first_half = values[..., :half_dim]
    second_half = values[..., half_dim:]
    cosine = cosine[:, None, :]
    sine_table = sine_table[:, None, :]
    return jnp.concatenate(
        [
            first_half * cosine - second_half * sine_table,
            second_half * cosine + first_half * sine_table,
        ],
        axis=-1,
    )


def suffix_part(queries, fresh_kv, group_size, causal, inv_root):

    def suffix_one_head(head_index):
        query_head = lax.dynamic_index_in_dim(queries, head_index, 1, keepdims=False)
        fresh_head = lax.dynamic_index_in_dim(fresh_kv, head_index // group_size, 1, keepdims=False)
        scores = (
            jnp.einsum(
                "qd,kd->qk", query_head, fresh_head[:, 0], preferred_element_type=jnp.float32
            )
            * inv_root
        )
        scores = jnp.where(causal, scores, neg_big)
        row_max = jnp.max(scores, axis=1)
        weights = jnp.exp(scores - row_max[:, None])
        summed = jnp.einsum(
            "qk,kd->qd",
            weights.astype(jnp.bfloat16),
            fresh_head[:, 1],
            preferred_element_type=jnp.float32,
        )
        return (summed, row_max, jnp.sum(weights, axis=1))

    return lax.map(suffix_one_head, jnp.arange(queries.shape[1], dtype=jnp.int32))


def body(hidden, w_query, w_keyval, store, page_owner, page_slot, new_owner):
    row_count = hidden.shape[0]
    head_count = w_query.shape[1] // HD
    kv_heads = store.shape[1]
    group_size = head_count // kv_heads
    owner_count = lax.axis_size("pool")
    my_group = lax.axis_index("pool")
    page_count = page_owner.shape[1]
    capacity = store.shape[0] // owner_count
    inv_root = 1.0 / math.sqrt(HD)
    piece = lax.all_gather(hidden, "tp", axis=1, tiled=True)
    widened = piece.astype(jnp.float32)
    query_sum = jnp.dot(piece, w_query, preferred_element_type=jnp.float32)
    keyval_sum = jnp.dot(piece, w_keyval, preferred_element_type=jnp.float32)
    squares = jnp.sum(widened * widened, axis=1)
    inv_norm = lax.rsqrt(squares / D + 1e-05)[:, None]
    cosine, sine_table = rope_tables(row_count, page_count * PAGE)
    queries = rotate(
        (query_sum * inv_norm).reshape(row_count, head_count, HD), cosine, sine_table
    ).astype(jnp.bfloat16)
    keyval = (keyval_sum * inv_norm).reshape(row_count, kv_heads, 2, HD)
    fresh_kv = jnp.stack(
        [rotate(keyval[:, :, 0], cosine, sine_table), keyval[:, :, 1]], axis=2
    ).astype(jnp.bfloat16)
    causal = jnp.arange(row_count)[:, None] >= jnp.arange(row_count)[None, :]
    same_owner = page_owner[:, :, None] == page_owner[:, None, :]
    earlier = jnp.arange(page_count)[None, :] < jnp.arange(page_count)[:, None]
    ranks = jnp.sum(same_owner & earlier[None], axis=2)
    held_here = (page_owner == my_group)[:, :, None] & (
        ranks[:, :, None] == jnp.arange(capacity, dtype=jnp.int32)[None, None, :]
    )
    slot_for = jnp.sum(jnp.where(held_here, page_slot[:, :, None], 0), axis=1)
    filled = jnp.any(held_here, axis=1)
    packed = jnp.where(
        filled[:, :, None, None, None, None], store[slot_for], jnp.zeros((), jnp.bfloat16)
    )
    copies = jnp.broadcast_to(
        queries.reshape(1, row_count, head_count * HD), (owner_count, row_count, head_count * HD)
    )
    live_keys = jnp.broadcast_to(filled[:, :, None], (owner_count, capacity, PAGE)).reshape(
        owner_count, capacity * PAGE
    )
    arrived = lax.all_to_all(copies, "pool", split_axis=0, concat_axis=0, tiled=True)
    item_count = arrived.shape[1]
    asked_rows = arrived.reshape(owner_count, item_count, head_count, HD)

    def attend_one_head(head_index):
        asked_head = lax.dynamic_index_in_dim(asked_rows, head_index, 2, keepdims=False)
        held_head = lax.dynamic_index_in_dim(packed, head_index // group_size, 2, keepdims=False)
        key_rows = held_head[:, :, :, 0].reshape(owner_count, capacity * PAGE, HD)
        value_rows = held_head[:, :, :, 1].reshape(owner_count, capacity * PAGE, HD)
        scores = (
            jnp.einsum("snd,skd->snk", asked_head, key_rows, preferred_element_type=jnp.float32)
            * inv_root
        )
        scores = jnp.where(live_keys[:, None, :], scores, neg_big)
        row_max = jnp.max(scores, axis=2)
        weights = jnp.where(live_keys[:, None, :], jnp.exp(scores - row_max[:, :, None]), 0.0)
        summed = jnp.einsum(
            "snk,skd->snd",
            weights.astype(jnp.bfloat16),
            value_rows,
            preferred_element_type=jnp.float32,
        )
        return (summed, row_max, jnp.sum(weights, axis=2))

    summed, row_max, totals = lax.map(attend_one_head, jnp.arange(head_count, dtype=jnp.int32))
    summed = jnp.transpose(summed, (1, 2, 0, 3))
    row_max = jnp.transpose(row_max, (1, 2, 0))
    totals = jnp.transpose(totals, (1, 2, 0))
    parts_sum = lax.all_to_all(summed, "pool", split_axis=0, concat_axis=0, tiled=True)
    parts_max = lax.all_to_all(row_max, "pool", split_axis=0, concat_axis=0, tiled=True)
    parts_total = lax.all_to_all(totals, "pool", split_axis=0, concat_axis=0, tiled=True)
    own_sum, own_max, own_total = suffix_part(queries, fresh_kv, group_size, causal, inv_root)
    own_sum = jnp.transpose(own_sum, (1, 0, 2))
    own_max = jnp.transpose(own_max, (1, 0))
    own_total = jnp.transpose(own_total, (1, 0))
    row_best = jnp.maximum(jnp.max(parts_max, axis=0), own_max)
    factor = jnp.exp(parts_max - row_best[None])
    own_factor = jnp.exp(own_max - row_best)
    numerator = jnp.sum(parts_sum * factor[..., None], axis=0) + own_sum * own_factor[..., None]
    denominator = jnp.sum(parts_total * factor, axis=0) + own_total * own_factor
    result = numerator / denominator[..., None]
    attended = result.reshape(row_count, head_count * HD).astype(jnp.bfloat16)
    new_count = row_count // PAGE
    fresh_pages = jnp.transpose(fresh_kv.reshape(new_count, PAGE, kv_heads, 2, HD), (0, 2, 1, 3, 4))
    slot_total = PUSH_CAP * owner_count
    slot_range = jnp.arange(slot_total, dtype=jnp.int32)
    gathered = lax.all_gather(fresh_pages, "pool", axis=0, tiled=True)
    targets = new_owner.reshape(-1)
    to_owner = (targets[:, None] == jnp.arange(owner_count, dtype=jnp.int32)[None, :]).astype(
        jnp.int32
    )
    earlier_count = jnp.cumsum(to_owner, axis=0) - to_owner
    placed = jnp.sum(earlier_count * to_owner, axis=1)
    matched = (targets == my_group)[:, None] & (placed[:, None] == slot_range[None, :])
    picked = jnp.sum(
        jnp.where(matched, jnp.arange(targets.shape[0], dtype=jnp.int32)[:, None], 0), axis=0
    )
    used_slots = jnp.any(matched, axis=0)
    new_store = jnp.where(
        used_slots[:, None, None, None, None], gathered[picked], jnp.zeros((), jnp.bfloat16)
    )
    return (attended, new_store)


def solution(mesh):
    in_specs = (
        P("pool", "tp"),
        P(None, "tp"),
        P(None, "tp"),
        P("pool", "tp", None, None, None),
        P(),
        P(),
        P(),
    )
    out_specs = (P("pool", "tp"), P("pool", "tp", None, None, None))
    return jax.shard_map(body, mesh=mesh, in_specs=in_specs, out_specs=out_specs, check_vma=False)
```

profile of v0, /device:TPU:0, one launch (start us, length us, event | category | flops | bytes accessed | tf_op | source)
XLA Modules:
  0.0 573.3 jit_solution(6342999201093476247)
XLA Ops:
  7.2 0.7 all-gather.3.cloned.1.call-update
  8.5 53.6 %all-gather.3.cloned.1.call-done = bf16[512,8192]{1,0:T(8,128)(2,1)} async-done(((bf16[512,1024]{1,0:T(8,128)(2,1)}), bf16[512,8192]{1,0:T(8,128)(2,1)}) %all-gather.3.cloned.1.call-update) | async-done | bytes 8388624 | tf_op jit(solution)/shard_map/all_gather | solution.py:75
  62.1 5.1 multiply_reduce_fusion.1
  67.2 9.5 %convolution_multiply_fusion.1 = f32[512,512]{0,1:T(8,128)S(1)} fusion(bf16[512,8192]{1,0:T(8,128)(2,1)} %all-gather.3.cloned.1.call-done, bf16[8192,512]{1,0:T(8,128)(2,1)} %param.12, f32[512]{0:T(512)S(1)} %add_rsqrt_fusion), kind=kOutput, calls=%fused_computation.40 | convolution fusion | flops 4295229440 | bytes 17827840 | tf_op jit(solution)/shard_map/dot_general | solution.py:77
  76.9 4.0 broadcast_in_dim.146
  80.9 7.0 %all-to-all-start = ((bf16[16,512,512]{1,2,0:T(8,128)(2,1)}), bf16[16,512,512]{1,2,0:T(8,128)(2,1)}, u32[]{:S(2)}, u32[]{:S(2)}) async-start(bf16[16,512,512]{1,2,0:T(8,128)(2,1)} %broadcast_in_dim.146), calls=%async_computation | async-start | bytes 16777216 | tf_op jit(solution)/shard_map/all_to_all | solution.py:107
  89.1 6.8 %gather_fusion = bf16[64,64,2,128]{3,2,1,0:T(2,128)(2,1)} fusion(bf16[64,64,2,128]{3,2,1,0:T(2,128)(2,1)S(1)} %bitcast.133, s32[1024]{0:T(1024)S(1)} %pad_clamp_fusion.1), kind=kCustom, calls=%fused_computation | custom fusion | bytes 4194560 | tf_op jit(solution)/shard_map/gather | solution.py:99
  95.9 3.4 copy.58
  99.3 1.8 broadcast_select_fusion
  101.1 112.6 %all-to-all-done = bf16[16,512,512]{1,2,0:T(8,128)(2,1)} async-done(((bf16[16,512,512]{1,2,0:T(8,128)(2,1)}), bf16[16,512,512]{1,2,0:T(8,128)(2,1)}, u32[]{:S(2)}, u32[]{:S(2)}) %all-to-all-start) | async-done | bytes 8388640 | tf_op jit(solution)/shard_map/all_to_all | solution.py:107
  213.7 57.3 %while.30 = (s32[]{:T(128)}, f32[4,16,512,128]{3,2,0,1:T(8,128)}, f32[4,16,512]{2,0,1:T(4,128)S(1)}, f32[4,16,512]{2,0,1:T(4,128)S(1)}, s32[4]{0:T(128)S(1)}, /*...) while((s32[]{:T(128)}, f32[4,16,512,128]{3,2,0,1:T(8,128)}, ...), condition=%wide.region_7.8_spmd.clone, body=%wide.region_4.7_spmd.clone.sunk | while | flops 1100988416 | bytes 38167268 | solution.py:131
  213.7 0.6 dynamic_slice.40
  216.7 3.5 fusion.75
  220.2 5.0 bitcast_dynamic-update-slice_fusion.2
  225.2 2.4 fusion.76
  228.1 0.6 dynamic_slice.40
  231.0 3.5 fusion.75
  234.6 5.0 bitcast_dynamic-update-slice_fusion.2
  239.5 2.4 fusion.76
  242.4 0.6 dynamic_slice.40
  245.3 3.5 fusion.75
  248.9 5.0 bitcast_dynamic-update-slice_fusion.2
  253.8 2.4 fusion.76
  256.7 0.6 dynamic_slice.40
  259.6 3.5 fusion.75
  263.2 5.0 bitcast_dynamic-update-slice_fusion.2
  268.2 2.4 fusion.76
  271.0 12.2 %all_to_all.20 = f32[16,512,4]{1,2,0:T(4,128)S(1)} all-to-all(f32[16,512,4]{1,2,0:T(4,128)S(1)} %bitcast.153), channel_id=1, replica_groups=mesh['pool'=16,'tp'=8] {'pool'}, dimensions={0} | all-to-all | bytes 262144 | tf_op jit(solution)/shard_map/all_to_all | solution.py:136
  283.3 11.1 %all_to_all.21 = f32[16,512,4]{1,2,0:T(4,128)S(1)} all-to-all(f32[16,512,4]{1,2,0:T(4,128)S(1)} %bitcast.154), channel_id=1, replica_groups=mesh['pool'=16,'tp'=8] {'pool'}, dimensions={0} | all-to-all | bytes 262144 | tf_op jit(solution)/shard_map/all_to_all | solution.py:137
  294.3 5.2 all-to-all-start.1
  299.8 6.9 %convolution_multiply_fusion.2 = f32[512,256]{0,1:T(8,128)S(1)} fusion(bf16[512,8192]{1,0:T(8,128)(2,1)} %all-gather.3.cloned.1.call-done, bf16[8192,256]{1,0:T(8,128)(2,1)} %param.13, f32[512]{0:T(512)S(1)} %add_rsqrt_fusion), kind=kOutput, calls=%fused_computation.41 | convolution fusion | flops 2147614720 | bytes 13109248 | tf_op jit(solution)/shard_map/dot_general | solution.py:78
  307.0 1.2 fusion.40
  308.4 0.7 copy.69
  310.2 17.6 %while.31 = (s32[]{:T(128)}, f32[4,512,128]{2,1,0:T(8,128)}, f32[4,512]{1,0:T(4,128)S(1)}, f32[4,512]{1,0:T(4,128)S(1)}, s32[4]{0:T(128)S(1)}, /*index=5*/bf16[5...) while((s32[]{:T(128)}, f32[4,512,128]{2,1,0:T(8,128)}, ...), condition=%wide.region_12.13_spmd.clone, body=%wide.region_9.12_spmd.clone.sunk | while | flops 136313856 | bytes 3818143 | solution.py:62
  310.2 0.7 dynamic_slice.42
  313.5 1.1 fusion.79
  314.6 0.7 dynamic_slice.42
  317.9 1.0 fusion.79
  319.0 0.7 dynamic_slice.42
  322.3 1.0 fusion.79
  323.4 0.7 dynamic_slice.42
  326.7 1.1 fusion.79
  327.8 207.3 %all-gather.5.cloned.1.call-done = bf16[128,1,64,2,128]{4,2,3,1,0:T(8,128)(2,1)} async-done(((bf16[8,1,64,2,128]{4,2,3,1,0:T(8,128)(2,1)}), bf16[128,1,64,2,128]{4,2,3,1,0:T(8,128)(2,1)}) %all-gather.5.cloned.1.call-update) | async-done | bytes 4194320 | tf_op jit(solution)/shard_map/all_gather | solution.py:153
  535.1 2.9 gather_fusion.1
  538.2 2.1 copy.70
  540.4 16.7 %all-to-all-done.1 = f32[16,512,4,128]{3,1,2,0:T(8,128)} async-done(((f32[16,512,4,128]{3,1,2,0:T(8,128)}), f32[16,512,4,128]{3,1,2,0:T(8,128)}, u32[]{:S(2)}, u32[]{:S(2)}) %all-to-all-start.1) | async-done | bytes 16777248 | tf_op jit(solution)/shard_map/all_to_all | solution.py:135
  557.0 7.9 %multiply_reduce_fusion = f32[512,4,128]{2,0,1:T(8,128)S(1)} fusion(f32[16,512,4,128]{3,1,2,0:T(8,128)} %all-to-all-done.1, f32[16,512,4]{1,2,0:T(4,128)S(1)} %get-tuple-element.225), kind=kLoop, calls=%fused_computation.37 | loop fusion | flops 8126464 | bytes 17956864 | tf_op jit(solution)/shard_map/reduce_sum | solution.py:145
  565.0 1.4 copy_bitcast_fusion
  (106 shorter events, 9.3 us)
Async XLA Ops:
  7.2 81.9 %copy-start = (bf16[64,1,64,2,128]{4,3,2,1,0:T(2,128)(2,1)S(1)}, bf16[64,1,64,2,128]{4,3,2,1,0:T(2,128)(2,1)}, u32[]{:S(2)}) copy-start(bf16[64,1,64,2,128]{4,3,2,1,0:T(2,128)(2,1)} %param.14) | copy-start | bytes 6291460
  7.2 54.9 %all-gather.3.cloned.1.call-start = ((), (), s32[]{:S(2)}) async-start(), calls=%async_computation.4 | async-start | bytes 9437184 | tf_op jit(solution)/shard_map/all_gather | solution.py:75
  80.9 7.1 %copy-start.3 = (s32[16,32]{1,0:T(8,128)S(1)}, s32[16,32]{1,0:T(8,128)}, u32[]{:S(2)}) copy-start(s32[16,32]{1,0:T(8,128)} %param.15) | copy-start | bytes 6148
  80.9 7.8 %copy-start.4 = (s32[16,32]{1,0:T(8,128)S(1)}, s32[16,32]{1,0:T(8,128)}, u32[]{:S(2)}) copy-start(s32[16,32]{1,0:T(8,128)} %param.16) | copy-start | bytes 6148
  80.9 132.8 %all-to-all-start = ((bf16[16,512,512]{1,2,0:T(8,128)(2,1)}), bf16[16,512,512]{1,2,0:T(8,128)(2,1)}, u32[]{:S(2)}, u32[]{:S(2)}) async-start(bf16[16,512,512]{1,2,0:T(8,128)(2,1)} %broadcast_in_dim.146), calls=%async_computation | async-start | bytes 16777216 | tf_op jit(solution)/shard_map/all_to_all | solution.py:107
  294.3 262.7 %all-to-all-start.1 = ((f32[16,512,4,128]{3,1,2,0:T(8,128)}), f32[16,512,4,128]{3,1,2,0:T(8,128)}, u32[]{:S(2)}, u32[]{:S(2)}) async-start(f32[16,512,4,128]{3,1,2,0:T(8,128)} %bitcast.137), calls=%async_computation.1 | async-start | bytes 33554432 | tf_op jit(solution)/shard_map/all_to_all | solution.py:135
  299.5 9.7 %copy-start.5 = (s32[16,8]{0,1:T(8,128)S(1)}, s32[16,8]{0,1:T(8,128)}, u32[]{:S(2)}) copy-start(s32[16,8]{0,1:T(8,128)} %param.17) | copy-start | bytes 1540
  299.5 235.6 %all-gather.5.cloned.1.call-start = ((), (), s32[]{:S(2)}) async-start(), calls=%async_computation.5 | async-start | bytes 4456448 | tf_op jit(solution)/shard_map/all_gather | solution.py:153
  557.0 9.4 %copy-start.1 = (bf16[64,1,64,2,128]{4,3,2,1,0:T(2,128)(2,1)S(1)}, bf16[64,1,64,2,128]{4,3,2,1,0:T(2,128)(2,1)}, u32[]{:S(2)}) copy-start(bf16[64,1,64,2,128]{4,3,2,1,0:T(2,128)(2,1)} %param.14) | copy-start | bytes 6291460
  557.0 8.0 %copy-start.2 = (f32[4,512,128]{2,1,0:T(8,128)S(1)}, f32[4,512,128]{2,1,0:T(8,128)}, u32[]{:S(2)}) copy-start(f32[4,512,128]{2,1,0:T(8,128)} %get-tuple-element.93) | copy-start | bytes 3145732
Sparse Core Ops, SparseCore 0:
  9.7 52.3 all-gather.2
  309.3 225.7 all-gather.4
where the time goes:
time: 575 us; the launch traced here: 573 us
  waiting for transfers between devices  391 us (68%)
  matrix products  55.9 us (10%)
  other arithmetic  30.7 us (5%)
  local copies, waits for them, and re-layouts  29.2 us (5%)
  blocking collectives  23.3 us (4%)
  loops' own time  16.5 us (3%)
  between operations  14.4 us (3%)
  starting transfers between devices  12.5 us (2%)
    all_gather x1, waiting for transfers between devices, body(): gathered = lax.all_gather(fresh_pages, 'pool', axis=0, tiled=True)  207 us
    all_to_all x1, waiting for transfers between devices, body(): lax.all_to_all(copies, 'pool', split_axis=0, concat_axis=0, tiled=True)  113 us
    all_gather x1, waiting for transfers between devices, body(): piece = lax.all_gather(hidden, 'tp', axis=1, tiled=True)  53.6 us
    dot_general x4, matrix products, attend_one_head(): jnp.einsum('snk,skd->snd', weights.astype(jnp.bfloat16), value_rows, pref...  19.9 us
    all_to_all x1, waiting for transfers between devices, body(): lax.all_to_all(summed, 'pool', split_axis=0, concat_axis=0, tiled=True)  16.7 us
    dot_general x4, matrix products, attend_one_head(): jnp.einsum('snd,skd->snk', asked_head, key_rows, preferred_element_type=j...  14.2 us
    all_to_all x1, blocking collectives, body(): lax.all_to_all(row_max, 'pool', split_axis=0, concat_axis=0, tiled=True)  12.2 us
  transfers between devices with their start and end apart: 4, of which 4 were waited for; matrix products, arithmetic and copies ran while one was open for 7% of the time, Pallas kernels for 0%

commit v1 on v0

v1 whole, which is shorter than its diff:
```python
import functools
import math

import jax
import jax.numpy as jnp
from jax import lax
from jax.experimental import pallas as pl
from jax.experimental.pallas import tpu as pltpu
from jax.sharding import PartitionSpec as P

D = 8192
HD = 128
PAGE = 64
CAP = 4
PUSH_CAP = 2
HEADS = 4
FEAT = 1024
QW = 512
KVW = 256
POOL = 16
PAGES = 32
NEW_PAGES = 8
SLOTS = 32
CHUNKS = (48, 16)
MIB = 1024 * 1024
SCALE = math.log2(math.e) / math.sqrt(HD)
F32 = jnp.float32
BF16 = jnp.bfloat16
ANY = pl.BlockSpec(memory_space=pl.ANY)
VMEM = pl.BlockSpec(memory_space=pltpu.VMEM)
SMEM = pl.BlockSpec(memory_space=pltpu.SMEM)


def params(mib):
    return pltpu.CompilerParams(vmem_limit_bytes=mib * MIB)


def cost(flops, nbytes):
    return pl.CostEstimate(flops=flops, bytes_accessed=nbytes, transcendentals=0)


def shape(dims, dtype):
    return jax.ShapeDtypeStruct(dims, dtype)


def gather_kernel(owner_ref, slot_ref, store_ref, out_ref, sems, counts):
    me = lax.axis_index("pool")

    def copy(slot, index):
        return pltpu.make_async_copy(store_ref.at[slot], out_ref.at[index], sems.at[index])

    def start_request(request, _):
        def start_page(page, rank):
            mine = owner_ref[request, page] == me

            @pl.when(mine)
            def _():
                copy(slot_ref[request, page], request * CAP + rank).start()

            return rank + mine.astype(jnp.int32)

        counts[request] = lax.fori_loop(0, PAGES, start_page, jnp.int32(0), unroll=8)
        return 0

    def finish_request(request, _):
        def finish_page(rank, _):
            copy(0, request * CAP + rank).wait()
            return 0

        return lax.fori_loop(0, counts[request], finish_page, 0)

    lax.fori_loop(0, POOL, start_request, 0)
    lax.fori_loop(0, POOL, finish_request, 0)


def gather_pages(page_owner, page_slot, store):
    return pl.pallas_call(
        gather_kernel,
        out_shape=shape((POOL * CAP, 2 * PAGE, HD), BF16),
        in_specs=[SMEM, SMEM, ANY],
        out_specs=ANY,
        scratch_shapes=[
            pltpu.SemaphoreType.DMA((POOL * CAP,)),
            pltpu.SMEM((POOL,), jnp.int32),
        ],
        cost_estimate=cost(0, 4 * MIB),
        name="gather_pages",
    )(page_owner, page_slot, store)


def split_matrix():
    row = lax.broadcasted_iota(jnp.int32, (2 * PAGE, 2 * PAGE), 0)
    column = lax.broadcasted_iota(jnp.int32, (2 * PAGE, 2 * PAGE), 1)
    wanted = jnp.where(row < PAGE, 2 * row, 2 * (row - PAGE) + 1)
    return (column == wanted).astype(BF16)


def split_kernel(owner_ref, pages_ref, keys_ref, values_ref, counts):
    me = lax.axis_index("pool")
    picker = split_matrix()
    for owner in range(POOL):
        counts[owner] = 0
    values_ref[:, HD:] = jnp.ones((PAGES * PAGE, HD), BF16)
    for page in range(PAGES):
        owner = owner_ref[me, page]
        rank = counts[owner]
        counts[owner] = rank + 1
        both = jnp.dot(picker, pages_ref[owner * CAP + rank], preferred_element_type=F32)
        rows = pl.ds(page * PAGE, PAGE)
        keys_ref[rows, :] = both[:PAGE].astype(BF16)
        values_ref[rows, :HD] = both[PAGE:].astype(BF16)


def split_pages(page_owner, pages):
    return pl.pallas_call(
        split_kernel,
        out_shape=[
            shape((PAGES * PAGE, HD), BF16),
            shape((PAGES * PAGE, 2 * HD), BF16),
        ],
        in_specs=[SMEM, VMEM],
        out_specs=[VMEM, VMEM],
        scratch_shapes=[pltpu.SMEM((POOL,), jnp.int32)],
        compiler_params=params(16),
        cost_estimate=cost(2 * 2048 * 128 * 256, 4 * MIB),
        name="split_pages",
    )(page_owner, pages)


def block_index(z_step, other_core):
    index = lax.axis_index("tp")
    z = lax.rem(index // 2 + z_step, 4)
    core = lax.rem(index, 2)
    return 2 * z + (1 - core if other_core else core)


def squares_of(rows):
    wide = rows.astype(F32)
    total = None
    for lane in range(0, FEAT, HD):
        part = wide[:, lane : lane + HD]
        total = part * part if total is None else total + part * part
    return total


def weight_copies(wq_ref, wkv_ref, wq_buf, wkv_buf, sems, blocks):
    copies = []
    for i, (z_step, other) in enumerate(blocks):
        start = pl.multiple_of(block_index(z_step, other) * FEAT, FEAT)
        rows = pl.ds(start, FEAT)
        copies.append(
            (
                pltpu.make_async_copy(wq_ref.at[rows, :], wq_buf.at[i], sems.at[2 * i]),
                pltpu.make_async_copy(wkv_ref.at[rows, :], wkv_buf.at[i], sems.at[2 * i + 1]),
            )
        )
    return copies


EARLY = ((0, False), (0, True), (3, False), (3, True), (1, False), (1, True))
LATE = ((2, False), (2, True))


def early_kernel(*refs):
    count = len(EARLY)
    x_refs = refs[:count]
    wq_ref, wkv_ref, q_ref, kv_ref, sq_ref, x_buf, wq_buf, wkv_buf, x_sems, w_sems = refs[count:]
    x_copies = [
        pltpu.make_async_copy(x_refs[i], x_buf.at[i], x_sems.at[i]) for i in range(count)
    ]
    w_copies = weight_copies(wq_ref, wkv_ref, wq_buf, wkv_buf, w_sems, EARLY)
    for i in range(count):
        x_copies[i].start()
        w_copies[i][0].start()
        w_copies[i][1].start()
    for i in range(count):
        x_copies[i].wait()
        w_copies[i][0].wait()
        w_copies[i][1].wait()
        rows = x_buf[i]
        q_part = jnp.dot(rows, wq_buf[i], preferred_element_type=F32)
        kv_part = jnp.dot(rows, wkv_buf[i], preferred_element_type=F32)
        sq_part = squares_of(rows)
        if i == 0:
            q_ref[...] = q_part
            kv_ref[...] = kv_part
            sq_ref[...] = sq_part
        else:
            q_ref[...] += q_part
            kv_ref[...] += kv_part
            sq_ref[...] += sq_part


def project_early(blocks, w_query, w_keyval):
    rows = blocks[0].shape[0]
    count = len(EARLY)
    return pl.pallas_call(
        early_kernel,
        out_shape=[shape((rows, QW), F32), shape((rows, KVW), F32), shape((rows, HD), F32)],
        in_specs=[ANY] * (count + 2),
        out_specs=[VMEM] * 3,
        scratch_shapes=[
            pltpu.VMEM((count, rows, FEAT), BF16),
            pltpu.VMEM((count, FEAT, QW), BF16),
            pltpu.VMEM((count, FEAT, KVW), BF16),
            pltpu.SemaphoreType.DMA((count,)),
            pltpu.SemaphoreType.DMA((2 * count,)),
        ],
        compiler_params=params(32),
        cost_estimate=cost(
            2 * rows * count * FEAT * (QW + KVW), count * FEAT * (QW + KVW + rows) * 2
        ),
        name="project_early",
    )(*blocks, w_query, w_keyval)


def turn(values, cosine, sine):
    return values * cosine + pltpu.roll(values, HD // 2, 1) * sine


def late_kernel(
    length,
    owner_ref,
    top_ref,
    bottom_ref,
    top_other_ref,
    bottom_other_ref,
    q_in,
    kv_in,
    sq_in,
    cos_ref,
    sin_ref,
    wq_ref,
    wkv_ref,
    q_ref,
    kv_ref,
    send_ref,
    x_buf,
    wq_buf,
    wkv_buf,
    x_sems,
    w_sems,
    counts,
):
    half = top_ref.shape[0]
    sources = ((top_ref, bottom_ref), (top_other_ref, bottom_other_ref))
    x_copies = [
        pltpu.make_async_copy(
            sources[i][j], x_buf.at[i, pl.ds(j * half, half), :], x_sems.at[2 * i + j]
        )
        for i in range(2)
        for j in range(2)
    ]
    w_copies = weight_copies(wq_ref, wkv_ref, wq_buf, wkv_buf, w_sems, LATE)
    for i in range(2):
        for copy in (x_copies[2 * i], x_copies[2 * i + 1], *w_copies[i]):
            copy.start()
    q_sum = q_in[...]
    kv_sum = kv_in[...]
    squares = sq_in[...]
    for i in range(2):
        for copy in (x_copies[2 * i], x_copies[2 * i + 1], *w_copies[i]):
            copy.wait()
        rows = x_buf[i]
        q_sum += jnp.dot(rows, wq_buf[i], preferred_element_type=F32)
        kv_sum += jnp.dot(rows, wkv_buf[i], preferred_element_type=F32)
        squares += squares_of(rows)
    inv_norm = lax.rsqrt(jnp.sum(squares, axis=1, keepdims=True) / D + 1e-05)
    cosine = cos_ref[...]
    sine = sin_ref[...]
    for head in range(HEADS):
        lanes = slice(head * HD, (head + 1) * HD)
        q_ref[:, lanes] = turn(q_sum[:, lanes] * inv_norm, cosine, sine).astype(BF16)
    keys = turn(kv_sum[:, :HD] * inv_norm, cosine, sine).astype(BF16)
    values = (kv_sum[:, HD:] * inv_norm).astype(BF16)
    kv_ref[:, :HD] = keys
    kv_ref[:, HD:] = values
    row = lax.broadcasted_iota(jnp.int32, (2 * length, 2 * length), 0)
    column = lax.broadcasted_iota(jnp.int32, (2 * length, 2 * length), 1)
    picker = (column == (row >> 1) + (row & 1) * length).astype(BF16)
    me = lax.axis_index("pool")
    for owner in range(POOL):
        counts[owner] = 0
    for page in range(NEW_PAGES):
        owner = owner_ref[me, page]
        rank = counts[owner]
        counts[owner] = rank + 1
        rows = slice(page * length, (page + 1) * length)
        both = jnp.concatenate([keys[rows], values[rows]], axis=0)
        mixed = jnp.dot(picker, both, preferred_element_type=F32).astype(BF16)
        send_ref[owner * PUSH_CAP + rank] = mixed


def project_late(length, new_owner, halves, sums, cosine, sine, w_query, w_keyval):
    rows = sums[0].shape[0]
    return pl.pallas_call(
        functools.partial(late_kernel, length),
        out_shape=[
            shape((rows, QW), BF16),
            shape((rows, KVW), BF16),
            shape((POOL * PUSH_CAP, 2 * length, HD), BF16),
        ],
        in_specs=[SMEM] + [ANY] * 4 + [VMEM] * 5 + [ANY] * 2,
        out_specs=[VMEM] * 3,
        scratch_shapes=[
            pltpu.VMEM((2, rows, FEAT), BF16),
            pltpu.VMEM((2, FEAT, QW), BF16),
            pltpu.VMEM((2, FEAT, KVW), BF16),
            pltpu.SemaphoreType.DMA((4,)),
            pltpu.SemaphoreType.DMA((4,)),
            pltpu.SMEM((POOL,), jnp.int32),
        ],
        compiler_params=params(24),
        cost_estimate=cost(2 * rows * 2 * FEAT * (QW + KVW), 2 * FEAT * (QW + KVW + rows) * 2),
        name="project_late",
    )(new_owner, *halves, *sums, cosine, sine, w_query, w_keyval)


def dot_nt(a, b):
    return lax.dot_general(a, b, (((1,), (1,)), ((), ())), preferred_element_type=F32)


def prefix_kernel(q_ref, keys_ref, values_ref, sum_ref, top_ref, total_ref):
    block = 128

    def one(index, _):
        rows = pl.ds(pl.multiple_of(index * block, block), block)
        for head in range(HEADS):
            lanes = slice(head * HD, (head + 1) * HD)
            scores = dot_nt(q_ref[rows, lanes], keys_ref[...])
            top = jnp.max(scores, axis=1, keepdims=True)
            weights = jnp.exp2((scores - top) * SCALE).astype(BF16)
            both = jnp.dot(weights, values_ref[...], preferred_element_type=F32)
            sum_ref[rows, lanes] = both[:, :HD]
            total_ref[rows, lanes] = both[:, HD:]
            top_ref[rows, lanes] = jnp.broadcast_to(top, (block, HD))
        return 0

    lax.fori_loop(0, q_ref.shape[0] // block, one, 0)


def attend_prefix(queries, keys, values):
    rows = queries.shape[0]
    return pl.pallas_call(
        prefix_kernel,
        out_shape=[shape((rows, QW), F32)] * 3,
        in_specs=[VMEM] * 3,
        out_specs=[VMEM] * 3,
        compiler_params=params(32),
        cost_estimate=cost(2 * rows * 4 * 2048 * 512, 4 * MIB),
        name="attend_prefix",
    )(queries, keys, values)


def positions(length, offset, dims, axis):
    index = lax.broadcasted_iota(jnp.int32, dims, axis)
    return lax.div(index, jnp.int32(length)) * PAGE + offset + lax.rem(index, jnp.int32(length))


def suffix_kernel(*refs):
    count = len(CHUNKS)
    q_refs = refs[:count]
    kv_refs = refs[count : 2 * count]
    partial_refs = [refs[2 * count + 3 * i : 2 * count + 3 * i + 3] for i in range(count)]
    out_ref, keys_buf, values_buf = refs[5 * count :]
    row_total = NEW_PAGES * PAGE
    base = 0
    key_positions = []
    offset = 0
    for i, length in enumerate(CHUNKS):
        rows = NEW_PAGES * length
        keys_buf[base : base + rows, :] = kv_refs[i][:, :HD]
        values_buf[base : base + rows, :HD] = kv_refs[i][:, HD:]
        key_positions.append(positions(length, offset, (1, rows), 1))
        base += rows
        offset += length
    values_buf[:, HD:] = jnp.ones((row_total, HD), BF16)
    key_position = jnp.concatenate(key_positions, axis=1)
    offset = 0
    for i, length in enumerate(CHUNKS):
        rows = NEW_PAGES * length
        allowed = positions(length, offset, (rows, 1), 0) >= key_position
        sum_ref, top_ref, total_ref = partial_refs[i]
        for head in range(HEADS):
            lanes = slice(head * HD, (head + 1) * HD)
            scores = dot_nt(q_refs[i][:, lanes], keys_buf[...])
            scores = jnp.where(allowed, scores, -1e30)
            before = top_ref[:, lanes]
            top = jnp.maximum(jnp.max(scores, axis=1, keepdims=True), before)
            weights = jnp.exp2((scores - top[:, :1]) * SCALE).astype(BF16)
            both = jnp.dot(weights, values_buf[...], preferred_element_type=F32)
            factor = jnp.exp2((before - top) * SCALE)
            result = (both[:, :HD] + sum_ref[:, lanes] * factor) / (
                both[:, HD:] + total_ref[:, lanes] * factor
            )
            out_ref[:, offset : offset + length, lanes] = result.astype(BF16).reshape(
                NEW_PAGES, length, HD
            )
        offset += length


def attend_suffix(queries, keyvals, partials):
    count = len(CHUNKS)
    rows = NEW_PAGES * PAGE
    return pl.pallas_call(
        suffix_kernel,
        out_shape=shape((NEW_PAGES, PAGE, QW), BF16),
        in_specs=[VMEM] * (5 * count),
        out_specs=VMEM,
        scratch_shapes=[pltpu.VMEM((rows, HD), BF16), pltpu.VMEM((rows, 2 * HD), BF16)],
        compiler_params=params(32),
        cost_estimate=cost(2 * rows * 4 * 512 * 512, 8 * MIB),
        name="attend_suffix",
    )(*queries, *keyvals, *[p for partial in partials for p in partial])


def place_kernel(offset, first, owner_ref, received_ref, *refs):
    out_ref, zeros, sems = refs[-3:]
    me = lax.axis_index("pool")
    height = received_ref.shape[1]
    zeros[...] = jnp.zeros_like(zeros)

    def target(slot):
        return out_ref.at[slot, pl.ds(2 * offset, height), :]

    def request_loop(request, slot):
        def page_loop(page, state):
            slot, rank = state
            mine = owner_ref[request, page] == me

            @pl.when(mine)
            def _():
                source = received_ref.at[request * PUSH_CAP + rank]
                pltpu.make_async_copy(source, target(slot), sems.at[slot]).start()

            step = mine.astype(jnp.int32)
            return slot + step, rank + step

        slot, _ = lax.fori_loop(0, NEW_PAGES, page_loop, (slot, jnp.int32(0)), unroll=True)
        return slot

    used = lax.fori_loop(0, POOL, request_loop, jnp.int32(0))

    def clear(slot, _):
        pltpu.make_async_copy(zeros, target(slot), sems.at[slot]).start()
        return 0

    lax.fori_loop(used, SLOTS, clear, 0)

    def finish(slot, _):
        pltpu.make_async_copy(zeros, target(slot), sems.at[slot]).wait()
        return 0

    lax.fori_loop(0, SLOTS, finish, 0)


def place_pages(offset, new_owner, received, placed):
    first = placed is None
    height = received.shape[1]
    return pl.pallas_call(
        functools.partial(place_kernel, offset, first),
        out_shape=shape((SLOTS, 2 * PAGE, HD), BF16),
        in_specs=[SMEM, ANY] + ([] if first else [ANY]),
        out_specs=ANY,
        scratch_shapes=[pltpu.VMEM((height, HD), BF16), pltpu.SemaphoreType.DMA((SLOTS,))],
        input_output_aliases={} if first else {2: 0},
        cost_estimate=cost(0, 2 * SLOTS * height * HD * 2),
        name="place_pages",
    )(new_owner, received, *([] if first else [placed]))


def shift(values, step):
    pairs = [(i, ((i // 2 + step) % 4) * 2 + i % 2) for i in range(8)]
    return lax.ppermute(values, "tp", pairs)


def swap(values):
    return lax.ppermute(values, "tp", [(i, i ^ 1) for i in range(8)])


def rope_tables(row_count, offset):
    half_dim = HD // 2
    frequency = 500000.0 ** (-(jnp.arange(half_dim, dtype=F32) * (2.0 / HD)))
    place = (offset + jnp.arange(row_count, dtype=jnp.int32)).astype(F32)
    angles = place[:, None] * frequency[None, :]
    cosine, sine = jnp.cos(angles), jnp.sin(angles)
    return jnp.concatenate([cosine, cosine], 1), jnp.concatenate([-sine, sine], 1)


def take(values, offset, length):
    parts = values.reshape(NEW_PAGES, PAGE, values.shape[1])[:, offset : offset + length]
    return parts.reshape(NEW_PAGES * length, values.shape[1])


def body(hidden, w_query, w_keyval, store, page_owner, page_slot, new_owner):
    offsets = [sum(CHUNKS[:i]) for i in range(len(CHUNKS))]
    chunks = [take(hidden, o, n) for o, n in zip(offsets, CHUNKS)]
    ahead = [shift(x, 1) for x in chunks]
    behind = [shift(x, -1) for x in chunks]
    packed = gather_pages(page_owner, page_slot, store.reshape(64, 2 * PAGE, HD))
    pages = lax.all_to_all(packed, "pool", split_axis=0, concat_axis=0, tiled=True)
    cosine, sine = rope_tables(NEW_PAGES * PAGE, PAGES * PAGE)
    keys, values = split_pages(page_owner, pages)
    queries, keyvals, partials = [], [], []
    placed = None
    for i, (offset, length) in enumerate(zip(offsets, CHUNKS)):
        half = NEW_PAGES * length // 2
        top = shift(ahead[i][:half], 1)
        bottom = shift(behind[i][half:], -1)
        blocks = (
            chunks[i],
            swap(chunks[i]),
            ahead[i],
            swap(ahead[i]),
            behind[i],
            swap(behind[i]),
        )
        sums = project_early(blocks, w_query, w_keyval)
        q, kv, send = project_late(
            length,
            new_owner,
            (top, bottom, swap(top), swap(bottom)),
            sums,
            take(cosine, offset, length),
            take(sine, offset, length),
            w_query,
            w_keyval,
        )
        received = lax.all_to_all(send, "pool", split_axis=0, concat_axis=0, tiled=True)
        placed = place_pages(offset, new_owner, received, placed)
        queries.append(q)
        keyvals.append(kv)
        partials.append(attend_prefix(q, keys, values))
    attended = attend_suffix(queries, keyvals, partials).reshape(NEW_PAGES * PAGE, QW)
    return attended, placed.reshape(SLOTS, 1, PAGE, 2, HD)


def solution(mesh):
    in_specs = (
        P("pool", "tp"),
        P(None, "tp"),
        P(None, "tp"),
        P("pool", "tp", None, None, None),
        P(),
        P(),
        P(),
    )
    out_specs = (P("pool", "tp"), P("pool", "tp", None, None, None))
    return jax.shard_map(body, mesh=mesh, in_specs=in_specs, out_specs=out_specs, check_vma=False)
```

time: 575 us -> 193 us (0.34)
  the two profiles are of different devices: /device:TPU:0 before, /device:TPU:22 now
where the time goes in v1:
time: 193 us; the launch traced here: 192 us
  Pallas kernels  99 us (51%)
  starting transfers between devices  47.1 us (24%)
  local copies, waits for them, and re-layouts  23.6 us (12%)
  waiting for transfers between devices  16.6 us (9%)
  other arithmetic  4.14 us (2%)
    pallas_call x2, Pallas kernels, place_pages(): pl.pallas_call(functools.partial(place_kernel, offset, first), out_shape=...  36.2 us
    pallas_call x1, Pallas kernels, gather_pages(): pl.pallas_call(gather_kernel, out_shape=shape((POOL * CAP, 2 * PAGE, HD),...  33.6 us
    unnamed x33, local copies, waits for them, and re-layouts  19.3 us
    ppermute x8, waiting for transfers between devices, shift(): return lax.ppermute(values, 'tp', pairs)  16.6 us
    all_to_all x1, starting transfers between devices, body(): lax.all_to_all(packed, 'pool', split_axis=0, concat_axis=0, tiled=True)  16.1 us
    ppermute x8, starting transfers between devices, shift(): return lax.ppermute(values, 'tp', pairs)  14.6 us
    all_to_all x2, starting transfers between devices, body(): lax.all_to_all(send, 'pool', split_axis=0, concat_axis=0, tiled=True)  14.5 us
    pallas_call x2, Pallas kernels, project_early(): pl.pallas_call(early_kernel, out_shape=[shape((rows, QW), F32), shape((ro...  9.78 us
  transfers between devices with their start and end apart: 21, of which 4 were waited for; matrix products, arithmetic and copies ran while one was open for 4% of the time, Pallas kernels for 46%

profile of v1, /device:TPU:22, one launch (start us, length us, event | category | flops | bytes accessed | tf_op | source)
XLA Modules:
  0.0 191.5 jit_solution(1997912569527206307)
XLA Ops:
  0.6 1.2 slice.40
  1.8 2.0 %collective-permute-start = (bf16[384,1024]{1,0:T(8,128)(2,1)S(1)}, bf16[384,1024]{1,0:T(8,128)(2,1)}, u32[]{:S(2)}, u32[]{:S(2)}) collective-permute-start(bf16[384,1024]{1,0:T(8,128)(2,1)S(1)} %bitcast.12), channel_id=1, source_target_pairs={{0,2},{1,3},{2,4},{3,5},{4,6},{5,7},{6,0},{7,1},{8,10},{9,11},{10,... | collective-permute-start | bytes 2359304 | tf_op jit(solution)/shard_map/ppermute | solution.py:474
  3.8 2.2 %collective-permute-start.2 = (bf16[384,1024]{1,0:T(8,128)(2,1)S(1)}, bf16[384,1024]{1,0:T(8,128)(2,1)}, u32[]{:S(2)}, u32[]{:S(2)}) collective-permute-start(bf16[384,1024]{1,0:T(8,128)(2,1)S(1)} %bitcast.13), channel_id=1, source_target_pairs={{0,6},{1,7},{2,0},{3,1},{4,2},{5,3},{6,4},{7,5},{8,14},{9,15},{10,... | collective-permute-start | bytes 2359304 | tf_op jit(solution)/shard_map/ppermute | solution.py:474
  6.0 33.6 %gather_pages.1 = bf16[64,128,128]{2,1,0:T(8,128)(2,1)} custom-call(s32[16,32]{1,0:T(8,128)} %owner_ref.7, s32[16,32]{1,0:T(8,128)} %slot_ref.1, bf16[64,128,128]{2,1,0:T(8,128)(2,1)} %bitcast.25), custom_call_target="tpu_custom_call" | custom-call | bytes 4194304 | tf_op jit(solution)/shard_map/gather_pages/pallas_call | solution.py:77
  39.6 16.1 %all-to-all-start = ((bf16[64,128,128]{2,1,0:T(8,128)(2,1)}), bf16[64,128,128]{2,1,0:T(8,128)(2,1)S(1)}, u32[]{:S(2)}, u32[]{:S(2)}) async-start(bf16[64,128,128]{2,1,0:T(8,128)(2,1)} %gather_pages.1), calls=%async_computation | async-start | bytes 4194304 | tf_op jit(solution)/shard_map/all_to_all | solution.py:501
  55.7 0.1 collective-permute-start.6
  55.8 0.5 collective-permute-start.7
  56.3 0.1 collective-permute-start.8
  56.4 1.0 slice.41
  57.5 1.0 slice.42
  58.5 3.3 %collective-permute-start.3 = (bf16[192,1024]{1,0:T(8,128)(2,1)S(1)}, bf16[192,1024]{1,0:T(8,128)(2,1)}, u32[]{:S(2)}, u32[]{:S(2)}) collective-permute-start(bf16[192,1024]{1,0:T(8,128)(2,1)S(1)} %slice.42), channel_id=1, source_target_pairs={{0,6},{1,7},{2,0},{3,1},{4,2},{5,3},{6,4},{7,5},{8,14},{9,15},{10,... | collective-permute-start | bytes 1179656 | tf_op jit(solution)/shard_map/ppermute | solution.py:474
  61.8 1.8 multiply_sine_fusion
  63.7 6.6 %collective-permute-done.1.top_ref = bf16[192,1024]{1,0:T(8,128)(2,1)} collective-permute-done((bf16[192,1024]{1,0:T(8,128)(2,1)S(1)}, bf16[192,1024]{1,0:T(8,128)(2,1)}, u32[]{:S(2)}, u32[]{:S(2)}) %collective-permute-start.1) | collective-permute-done | bytes 393248 | tf_op jit(solution)/shard_map/ppermute | solution.py:474
  70.3 0.2 collective-permute-done.3.bottom_ref
  70.5 0.3 collective-permute-start.5
  70.8 1.3 fusion
  72.2 3.4 %copy-done = bf16[8192,512]{1,0:T(8,128)(2,1)S(1)} copy-done((bf16[8192,512]{1,0:T(8,128)(2,1)S(1)}, bf16[8192,512]{1,0:T(8,128)(2,1)}, u32[]{:S(2)}) %copy-start) | copy-done | bytes 8388632
  75.6 2.2 %copy-done.4 = bf16[8192,256]{1,0:T(8,128)(2,1)S(1)} copy-done((bf16[8192,256]{1,0:T(8,128)(2,1)S(1)}, bf16[8192,256]{1,0:T(8,128)(2,1)}, u32[]{:S(2)}) %copy-start.4) | copy-done | bytes 4194328
  77.8 6.6 %project_early.2 = (f32[384,512]{1,0:T(8,128)S(1)}, f32[384,256]{1,0:T(8,128)S(1)}, f32[384,128]{1,0:T(8,128)S(1)}) custom-call(bf16[384,1024]{1,0:T(8,128)(2,1)S(1)} %bitcast.15, bf16[384,1024]{1,0:T(8,128)(2,1)} %collective-permute-done.6.refs_1_, bf16[384,1024]{1,0:T(8,128)(2,1)} %collective-permute-done.refs_2_, ...), custom_call_target="tpu_custom_call" | custom-call | flops 3623878656 | bytes 14155776 | tf_op jit(solution)/shard_map/project_early/pallas_call | solution.py:197
  84.4 4.8 %project_late.2 = (bf16[384,512]{1,0:T(8,128)(2,1)S(1)}, bf16[384,256]{1,0:T(8,128)(2,1)S(1)}, bf16[32,96,128]{2,1,0:T(8,128)(2,1)}) custom-call(s32[16,8]{1,0:T(8,128)S(1)} %copy.10.owner_ref, bf16[192,1024]{1,0:T(8,128)(2,1)} %collective-permute-done.1.top_ref, bf16[192,1024]{1,0:T(8,128)(2,1)} %collective-permute-done.3.bottom_ref, ...), custom_call_target="tpu_custom_call" | custom-call | flops 1207959552 | bytes 4718592 | tf_op jit(solution)/shard_map/project_late/pallas_call | solution.py:296
  89.2 7.2 %all-to-all-start.2 = ((bf16[32,96,128]{2,1,0:T(8,128)(2,1)}), bf16[32,96,128]{2,1,0:T(8,128)(2,1)}, u32[]{:S(2)}, u32[]{:S(2)}) async-start(bf16[32,96,128]{2,1,0:T(8,128)(2,1)} %get-tuple-element.41), calls=%async_computation.2 | async-start | bytes 1572864 | tf_op jit(solution)/shard_map/all_to_all | solution.py:529
  96.4 1.0 slice.47
  97.4 0.9 collective-permute-start.9
  98.3 2.8 %collective-permute-start.11 = (bf16[128,1024]{1,0:T(8,128)(2,1)S(1)}, bf16[128,1024]{1,0:T(8,128)(2,1)S(1)}, u32[]{:S(2)}, u32[]{:S(2)}) collective-permute-start(bf16[128,1024]{1,0:T(8,128)(2,1)S(1)} %bitcast.17), channel_id=1, source_target_pairs={{0,6},{1,7},{2,0},{3,1},{4,2},{5,3},{6,4},{7,5},{8,14},{9,15},{10,... | collective-permute-start | bytes 786440 | tf_op jit(solution)/shard_map/ppermute | solution.py:474
  101.1 6.3 %collective-permute-done.9.refs_2_ = bf16[128,1024]{1,0:T(8,128)(2,1)S(1)} collective-permute-done((bf16[128,1024]{1,0:T(8,128)(2,1)S(1)}, bf16[128,1024]{1,0:T(8,128)(2,1)S(1)}, u32[]{:S(2)}, u32[]{:S(2)}) %collective-permute-start.9) | collective-permute-done | bytes 262176 | tf_op jit(solution)/shard_map/ppermute | solution.py:474
  107.4 0.5 collective-permute-start.17
  107.9 0.7 collective-permute-start.10
  108.7 2.7 %collective-permute-start.12 = (bf16[64,1024]{1,0:T(8,128)(2,1)S(1)}, bf16[64,1024]{1,0:T(8,128)(2,1)S(1)}, u32[]{:S(2)}, u32[]{:S(2)}) collective-permute-start(bf16[64,1024]{1,0:T(8,128)(2,1)S(1)} %slice.49), channel_id=1, source_target_pairs={{0,6},{1,7},{2,0},{3,1},{4,2},{5,3},{6,4},{7,5},{8,14},{9,15},{10,... | collective-permute-start | bytes 393224 | tf_op jit(solution)/shard_map/ppermute | solution.py:474
  111.3 3.4 %collective-permute-done.10.top_ref = bf16[64,1024]{1,0:T(8,128)(2,1)S(1)} collective-permute-done((bf16[64,1024]{1,0:T(8,128)(2,1)S(1)}, bf16[64,1024]{1,0:T(8,128)(2,1)S(1)}, u32[]{:S(2)}, u32[]{:S(2)}) %collective-permute-start.10) | collective-permute-done | bytes 131104 | tf_op jit(solution)/shard_map/ppermute | solution.py:474
  114.7 0.5 collective-permute-start.14
  115.2 1.0 pad_maximum_fusion
  116.3 3.4 %copy-done.2 = bf16[8192,512]{1,0:T(8,128)(2,1)S(1)} copy-done((bf16[8192,512]{1,0:T(8,128)(2,1)S(1)}, bf16[8192,512]{1,0:T(8,128)(2,1)}, u32[]{:S(2)}) %copy-start.2) | copy-done | bytes 8388632
  119.7 2.2 %copy-done.5 = bf16[8192,256]{1,0:T(8,128)(2,1)S(1)} copy-done((bf16[8192,256]{1,0:T(8,128)(2,1)S(1)}, bf16[8192,256]{1,0:T(8,128)(2,1)}, u32[]{:S(2)}) %copy-start.5) | copy-done | bytes 4194328
  121.8 3.2 %project_early.3 = (f32[128,512]{1,0:T(8,128)S(1)}, f32[128,256]{1,0:T(8,128)S(1)}, f32[128,128]{1,0:T(8,128)S(1)}) custom-call(bf16[128,1024]{1,0:T(8,128)(2,1)S(1)} %bitcast.19, bf16[128,1024]{1,0:T(8,128)(2,1)S(1)} %collective-permute-done.15.refs_1_, bf16[128,1024]{1,0:T(8,128)(2,1)S(1)} %collective-permute-done.9.refs_2_, ...), custom_call_target="tpu_custom_call" | custom-call | flops 1207959552 | bytes 11010048 | tf_op jit(solution)/shard_map/project_early/pallas_call | solution.py:197
  125.1 3.4 %copy-done.3 = bf16[8192,512]{1,0:T(8,128)(2,1)S(1)} copy-done((bf16[8192,512]{1,0:T(8,128)(2,1)S(1)}, bf16[8192,512]{1,0:T(8,128)(2,1)}, u32[]{:S(2)}) %copy-start.3) | copy-done | bytes 8388632
  128.4 3.3 %project_late.3 = (bf16[128,512]{1,0:T(8,128)(2,1)S(1)}, bf16[128,256]{1,0:T(8,128)(2,1)S(1)}, bf16[32,32,128]{2,1,0:T(8,128)(2,1)}) custom-call(s32[16,8]{1,0:T(8,128)S(1)} %copy.10.owner_ref, bf16[64,1024]{1,0:T(8,128)(2,1)S(1)} %collective-permute-done.10.top_ref, bf16[64,1024]{1,0:T(8,128)(2,1)S(1)} %collective-permute-done.12.bottom_ref, ...), custom_call_target="tpu_custom_call" | custom-call | flops 402653184 | bytes 3670016 | tf_op jit(solution)/shard_map/project_late/pallas_call | solution.py:296
  131.8 1.1 split_pages.1
  132.9 1.0 copy-done.8
  133.9 0.8 copy-done.11
  134.7 7.2 %all-to-all-start.1 = ((bf16[32,32,128]{2,1,0:T(8,128)(2,1)}), bf16[32,32,128]{2,1,0:T(8,128)(2,1)S(1)}, u32[]{:S(2)}, u32[]{:S(2)}) async-start(bf16[32,32,128]{2,1,0:T(8,128)(2,1)} %get-tuple-element.40), calls=%async_computation.1 | async-start | bytes 524288 | tf_op jit(solution)/shard_map/all_to_all | solution.py:529
  141.9 1.2 copy-done.9
  143.2 1.0 copy-done.12
  144.2 5.4 %attend_prefix.2 = (f32[384,512]{1,0:T(8,128)S(1)}, f32[384,512]{1,0:T(8,128)S(1)}, f32[384,512]{1,0:T(8,128)S(1)}) custom-call(bf16[384,512]{1,0:T(8,128)(2,1)S(1)} %get-tuple-element.25.q_ref.refs_0_, bf16[2048,128]{1,0:T(8,128)(2,1)S(1)} %copy-done.12, bf16[2048,256]{1,0:T(8,128)(2,1)S(1)} %copy-done.9), custom_call_target="tpu_custom_call" | custom-call | flops 3221225472 | bytes 4194304 | tf_op jit(solution)/shard_map/attend_prefix/pallas_call | solution.py:344
  149.6 1.8 attend_prefix.3
  151.4 3.1 %attend_suffix.1 = bf16[8,64,512]{2,1,0:T(8,128)(2,1)} custom-call(bf16[384,512]{1,0:T(8,128)(2,1)S(1)} %get-tuple-element.25.q_ref.refs_0_, bf16[128,512]{1,0:T(8,128)(2,1)S(1)} %get-tuple-element.29.q_ref.refs_1_, bf16[384,256]{1,0:T(8,128)(2,1)S(1)} %get-tuple-element.30.refs_2_, bf16[128,256]{1,0:T(8,128)(2,1)S(1)} %get-tuple-element.31.refs_3_, ...), custom_call_target="tpu_custom_call" | custom-call | flops 1073741824 | bytes 8388608 | tf_op jit(solution)/shard_map/attend_suffix/pallas_call | solution.py:405
  154.5 26.0 %place_pages.2.refs_0_ = bf16[32,128,128]{2,1,0:T(8,128)(2,1)} custom-call(s32[16,8]{1,0:T(8,128)} %copy-done.6, bf16[32,96,128]{2,1,0:T(8,128)(2,1)} %all-to-all-done.2.received_ref), custom_call_target="tpu_custom_call" | custom-call | bytes 1572864 | tf_op jit(solution)/shard_map/place_pages/pallas_call | solution.py:460
  180.5 0.7 copy-done.14
  181.2 10.2 %place_pages.3 = bf16[32,128,128]{2,1,0:T(8,128)(2,1)} custom-call(s32[16,8]{1,0:T(8,128)} %copy-done.6, bf16[32,32,128]{2,1,0:T(8,128)(2,1)} %copy-done.14, bf16[32,128,128]{2,1,0:T(8,128)(2,1)} %place_pages.2.refs_0_), custom_call_target="tpu_custom_call", output_to_operand_aliasing={{}: (2, {})} | custom-call | bytes 524288 | tf_op jit(solution)/shard_map/place_pages/pallas_call | solution.py:460
  (49 shorter events, 0.3 us)
Async XLA Ops:
  1.8 54.0 %collective-permute-start = (bf16[384,1024]{1,0:T(8,128)(2,1)S(1)}, bf16[384,1024]{1,0:T(8,128)(2,1)}, u32[]{:S(2)}, u32[]{:S(2)}) collective-permute-start(bf16[384,1024]{1,0:T(8,128)(2,1)S(1)} %bitcast.12), channel_id=1, source_target_pairs={{0,2},{1,3},{2,4},{3,5},{4,6},{5,7},{6,0},{7,1},{8,10},{9,11},{10,... | collective-permute-start | bytes 2359304 | tf_op jit(solution)/shard_map/ppermute | solution.py:474
  3.8 52.5 %collective-permute-start.2 = (bf16[384,1024]{1,0:T(8,128)(2,1)S(1)}, bf16[384,1024]{1,0:T(8,128)(2,1)}, u32[]{:S(2)}, u32[]{:S(2)}) collective-permute-start(bf16[384,1024]{1,0:T(8,128)(2,1)S(1)} %bitcast.13), channel_id=1, source_target_pairs={{0,6},{1,7},{2,0},{3,1},{4,2},{5,3},{6,4},{7,5},{8,14},{9,15},{10,... | collective-permute-start | bytes 2359304 | tf_op jit(solution)/shard_map/ppermute | solution.py:474
  39.6 49.6 %all-to-all-start = ((bf16[64,128,128]{2,1,0:T(8,128)(2,1)}), bf16[64,128,128]{2,1,0:T(8,128)(2,1)S(1)}, u32[]{:S(2)}, u32[]{:S(2)}) async-start(bf16[64,128,128]{2,1,0:T(8,128)(2,1)} %gather_pages.1), calls=%async_computation | async-start | bytes 4194304 | tf_op jit(solution)/shard_map/all_to_all | solution.py:501
  55.7 16.4 %copy-start.15 = (s32[16,8]{0,1:T(8,128)S(1)}, s32[16,8]{0,1:T(8,128)}, u32[]{:S(2)}) copy-start(s32[16,8]{0,1:T(8,128)} %param.13) | copy-start | bytes 1540
  55.7 16.5 %collective-permute-start.6 = (bf16[384,1024]{1,0:T(8,128)(2,1)S(1)}, bf16[384,1024]{1,0:T(8,128)(2,1)}, u32[]{:S(2)}, u32[]{:S(2)}) collective-permute-start(bf16[384,1024]{1,0:T(8,128)(2,1)S(1)} %bitcast.14), channel_id=1, source_target_pairs={{0,1},{1,0},{2,3},{3,2},{4,5},{5,4},{6,7},{7,6},{8,9},{9,8},{10,11... | collective-permute-start | bytes 2359304 | tf_op jit(solution)/shard_map/ppermute | solution.py:478
  55.8 16.4 %collective-permute-start.7 = (bf16[384,1024]{1,0:T(8,128)(2,1)}, bf16[384,1024]{1,0:T(8,128)(2,1)}, u32[]{:S(2)}, u32[]{:S(2)}) collective-permute-start(bf16[384,1024]{1,0:T(8,128)(2,1)} %collective-permute-done.refs_2_), channel_id=1, source_target_pairs={{0,1},{1,0},{2,3},{3,2},{4,5},{5,4},{6,7},{7,6},{8,9},{9,8},{10,11... | collective-permute-start | bytes 2359304 | tf_op jit(solution)/shard_map/ppermute | solution.py:478
  56.3 15.9 %collective-permute-start.8 = (bf16[384,1024]{1,0:T(8,128)(2,1)}, bf16[384,1024]{1,0:T(8,128)(2,1)}, u32[]{:S(2)}, u32[]{:S(2)}) collective-permute-start(bf16[384,1024]{1,0:T(8,128)(2,1)} %collective-permute-done.2.refs_4_), channel_id=1, source_target_pairs={{0,1},{1,0},{2,3},{3,2},{4,5},{5,4},{6,7},{7,6},{8,9},{9,8},{10,11... | collective-permute-start | bytes 2359304 | tf_op jit(solution)/shard_map/ppermute | solution.py:478
  57.4 12.8 %collective-permute-start.1 = (bf16[192,1024]{1,0:T(8,128)(2,1)S(1)}, bf16[192,1024]{1,0:T(8,128)(2,1)}, u32[]{:S(2)}, u32[]{:S(2)}) collective-permute-start(bf16[192,1024]{1,0:T(8,128)(2,1)S(1)} %slice.41), channel_id=1, source_target_pairs={{0,2},{1,3},{2,4},{3,5},{4,6},{5,7},{6,0},{7,1},{8,10},{9,11},{10,... | collective-permute-start | bytes 1179656 | tf_op jit(solution)/shard_map/ppermute | solution.py:474
  58.5 12.0 %collective-permute-start.3 = (bf16[192,1024]{1,0:T(8,128)(2,1)S(1)}, bf16[192,1024]{1,0:T(8,128)(2,1)}, u32[]{:S(2)}, u32[]{:S(2)}) collective-permute-start(bf16[192,1024]{1,0:T(8,128)(2,1)S(1)} %slice.42), channel_id=1, source_target_pairs={{0,6},{1,7},{2,0},{3,1},{4,2},{5,3},{6,4},{7,5},{8,14},{9,15},{10,... | collective-permute-start | bytes 1179656 | tf_op jit(solution)/shard_map/ppermute | solution.py:474
  70.3 14.1 %collective-permute-start.4 = (bf16[192,1024]{1,0:T(8,128)(2,1)}, bf16[192,1024]{1,0:T(8,128)(2,1)}, u32[]{:S(2)}, u32[]{:S(2)}) collective-permute-start(bf16[192,1024]{1,0:T(8,128)(2,1)} %collective-permute-done.1.top_ref), channel_id=1, source_target_pairs={{0,1},{1,0},{2,3},{3,2},{4,5},{5,4},{6,7},{7,6},{8,9},{9,8},{10,11... | collective-permute-start | bytes 1179656 | tf_op jit(solution)/shard_map/ppermute | solution.py:478
  70.5 13.9 %collective-permute-start.5 = (bf16[192,1024]{1,0:T(8,128)(2,1)}, bf16[192,1024]{1,0:T(8,128)(2,1)}, u32[]{:S(2)}, u32[]{:S(2)}) collective-permute-start(bf16[192,1024]{1,0:T(8,128)(2,1)} %collective-permute-done.3.bottom_ref), channel_id=1, source_target_pairs={{0,1},{1,0},{2,3},{3,2},{4,5},{5,4},{6,7},{7,6},{8,9},{9,8},{10,11... | collective-permute-start | bytes 1179656 | tf_op jit(solution)/shard_map/ppermute | solution.py:478
  72.2 52.9 %copy-start.6 = (s32[16,8]{1,0:T(8,128)}, s32[16,8]{1,0:T(8,128)S(1)}, u32[]{:S(2)}) copy-start(s32[16,8]{1,0:T(8,128)S(1)} %copy.10.owner_ref) | copy-start | bytes 1540
  72.2 3.4 %copy-start = (bf16[8192,512]{1,0:T(8,128)(2,1)S(1)}, bf16[8192,512]{1,0:T(8,128)(2,1)}, u32[]{:S(2)}) copy-start(bf16[8192,512]{1,0:T(8,128)(2,1)} %wq_ref.3) | copy-start | bytes 25165828
  75.6 2.2 %copy-start.4 = (bf16[8192,256]{1,0:T(8,128)(2,1)S(1)}, bf16[8192,256]{1,0:T(8,128)(2,1)}, u32[]{:S(2)}) copy-start(bf16[8192,256]{1,0:T(8,128)(2,1)} %wkv_ref.3) | copy-start | bytes 12582916
  77.8 6.6 %copy-start.1 = (bf16[8192,512]{1,0:T(8,128)(2,1)S(1)}, bf16[8192,512]{1,0:T(8,128)(2,1)}, u32[]{:S(2)}) copy-start(bf16[8192,512]{1,0:T(8,128)(2,1)} %wq_ref.3) | copy-start | bytes 25165828
  89.2 45.5 %all-to-all-start.2 = ((bf16[32,96,128]{2,1,0:T(8,128)(2,1)}), bf16[32,96,128]{2,1,0:T(8,128)(2,1)}, u32[]{:S(2)}, u32[]{:S(2)}) async-start(bf16[32,96,128]{2,1,0:T(8,128)(2,1)} %get-tuple-element.41), calls=%async_computation.2 | async-start | bytes 1572864 | tf_op jit(solution)/shard_map/all_to_all | solution.py:529
  97.4 10.0 %collective-permute-start.9 = (bf16[128,1024]{1,0:T(8,128)(2,1)S(1)}, bf16[128,1024]{1,0:T(8,128)(2,1)S(1)}, u32[]{:S(2)}, u32[]{:S(2)}) collective-permute-start(bf16[128,1024]{1,0:T(8,128)(2,1)S(1)} %bitcast.16), channel_id=1, source_target_pairs={{0,2},{1,3},{2,4},{3,5},{4,6},{5,7},{6,0},{7,1},{8,10},{9,11},{10,... | collective-permute-start | bytes 786440 | tf_op jit(solution)/shard_map/ppermute | solution.py:474
  98.3 9.1 %collective-permute-start.11 = (bf16[128,1024]{1,0:T(8,128)(2,1)S(1)}, bf16[128,1024]{1,0:T(8,128)(2,1)S(1)}, u32[]{:S(2)}, u32[]{:S(2)}) collective-permute-start(bf16[128,1024]{1,0:T(8,128)(2,1)S(1)} %bitcast.17), channel_id=1, source_target_pairs={{0,6},{1,7},{2,0},{3,1},{4,2},{5,3},{6,4},{7,5},{8,14},{9,15},{10,... | collective-permute-start | bytes 786440 | tf_op jit(solution)/shard_map/ppermute | solution.py:474
  101.1 15.2 %collective-permute-start.15 = (bf16[128,1024]{1,0:T(8,128)(2,1)S(1)}, bf16[128,1024]{1,0:T(8,128)(2,1)S(1)}, u32[]{:S(2)}, u32[]{:S(2)}) collective-permute-start(bf16[128,1024]{1,0:T(8,128)(2,1)S(1)} %bitcast.18), channel_id=1, source_target_pairs={{0,1},{1,0},{2,3},{3,2},{4,5},{5,4},{6,7},{7,6},{8,9},{9,8},{10,11... | collective-permute-start | bytes 786440 | tf_op jit(solution)/shard_map/ppermute | solution.py:478
  107.4 8.8 %collective-permute-start.16 = (bf16[128,1024]{1,0:T(8,128)(2,1)S(1)}, bf16[128,1024]{1,0:T(8,128)(2,1)S(1)}, u32[]{:S(2)}, u32[]{:S(2)}) collective-permute-start(bf16[128,1024]{1,0:T(8,128)(2,1)S(1)} %collective-permute-done.9.refs_2_), channel_id=1, source_target_pairs={{0,1},{1,0},{2,3},{3,2},{4,5},{5,4},{6,7},{7,6},{8,9},{9,8},{10,11... | collective-permute-start | bytes 786440 | tf_op jit(solution)/shard_map/ppermute | solution.py:478
  107.4 8.8 %collective-permute-start.17 = (bf16[128,1024]{1,0:T(8,128)(2,1)S(1)}, bf16[128,1024]{1,0:T(8,128)(2,1)S(1)}, u32[]{:S(2)}, u32[]{:S(2)}) collective-permute-start(bf16[128,1024]{1,0:T(8,128)(2,1)S(1)} %collective-permute-done.11.refs_4_), channel_id=1, source_target_pairs={{0,1},{1,0},{2,3},{3,2},{4,5},{5,4},{6,7},{7,6},{8,9},{9,8},{10,11... | collective-permute-start | bytes 786440 | tf_op jit(solution)/shard_map/ppermute | solution.py:478
  107.9 6.8 %collective-permute-start.10 = (bf16[64,1024]{1,0:T(8,128)(2,1)S(1)}, bf16[64,1024]{1,0:T(8,128)(2,1)S(1)}, u32[]{:S(2)}, u32[]{:S(2)}) collective-permute-start(bf16[64,1024]{1,0:T(8,128)(2,1)S(1)} %slice.48), channel_id=1, source_target_pairs={{0,2},{1,3},{2,4},{3,5},{4,6},{5,7},{6,0},{7,1},{8,10},{9,11},{10,... | collective-permute-start | bytes 393224 | tf_op jit(solution)/shard_map/ppermute | solution.py:474
  108.7 6.1 %collective-permute-start.12 = (bf16[64,1024]{1,0:T(8,128)(2,1)S(1)}, bf16[64,1024]{1,0:T(8,128)(2,1)S(1)}, u32[]{:S(2)}, u32[]{:S(2)}) collective-permute-start(bf16[64,1024]{1,0:T(8,128)(2,1)S(1)} %slice.49), channel_id=1, source_target_pairs={{0,6},{1,7},{2,0},{3,1},{4,2},{5,3},{6,4},{7,5},{8,14},{9,15},{10,... | collective-permute-start | bytes 393224 | tf_op jit(solution)/shard_map/ppermute | solution.py:474
  114.7 10.3 %collective-permute-start.13 = (bf16[64,1024]{1,0:T(8,128)(2,1)S(1)}, bf16[64,1024]{1,0:T(8,128)(2,1)S(1)}, u32[]{:S(2)}, u32[]{:S(2)}) collective-permute-start(bf16[64,1024]{1,0:T(8,128)(2,1)S(1)} %collective-permute-done.10.top_ref), channel_id=1, source_target_pairs={{0,1},{1,0},{2,3},{3,2},{4,5},{5,4},{6,7},{7,6},{8,9},{9,8},{10,11... | collective-permute-start | bytes 393224 | tf_op jit(solution)/shard_map/ppermute | solution.py:478
  114.7 10.3 %collective-permute-start.14 = (bf16[64,1024]{1,0:T(8,128)(2,1)S(1)}, bf16[64,1024]{1,0:T(8,128)(2,1)S(1)}, u32[]{:S(2)}, u32[]{:S(2)}) collective-permute-start(bf16[64,1024]{1,0:T(8,128)(2,1)S(1)} %collective-permute-done.12.bottom_ref), channel_id=1, source_target_pairs={{0,1},{1,0},{2,3},{3,2},{4,5},{5,4},{6,7},{7,6},{8,9},{9,8},{10,11... | collective-permute-start | bytes 393224 | tf_op jit(solution)/shard_map/ppermute | solution.py:478
  116.3 3.4 %copy-start.2 = (bf16[8192,512]{1,0:T(8,128)(2,1)S(1)}, bf16[8192,512]{1,0:T(8,128)(2,1)}, u32[]{:S(2)}) copy-start(bf16[8192,512]{1,0:T(8,128)(2,1)} %wq_ref.3) | copy-start | bytes 25165828
  119.7 2.2 %copy-start.5 = (bf16[8192,256]{1,0:T(8,128)(2,1)S(1)}, bf16[8192,256]{1,0:T(8,128)(2,1)}, u32[]{:S(2)}) copy-start(bf16[8192,256]{1,0:T(8,128)(2,1)} %wkv_ref.3) | copy-start | bytes 12582916
  125.1 3.4 %copy-start.3 = (bf16[8192,512]{1,0:T(8,128)(2,1)S(1)}, bf16[8192,512]{1,0:T(8,128)(2,1)}, u32[]{:S(2)}) copy-start(bf16[8192,512]{1,0:T(8,128)(2,1)} %wq_ref.3) | copy-start | bytes 25165828
  128.4 3.3 %copy-start.7 = (s32[16,32]{1,0:T(8,128)S(1)}, s32[16,32]{1,0:T(8,128)}, u32[]{:S(2)}) copy-start(s32[16,32]{1,0:T(8,128)} %owner_ref.7) | copy-start | bytes 6148
  132.9 1.0 copy-start.8
  133.9 0.8 copy-start.11
  134.7 45.8 %all-to-all-start.1 = ((bf16[32,32,128]{2,1,0:T(8,128)(2,1)}), bf16[32,32,128]{2,1,0:T(8,128)(2,1)S(1)}, u32[]{:S(2)}, u32[]{:S(2)}) async-start(bf16[32,32,128]{2,1,0:T(8,128)(2,1)} %get-tuple-element.40), calls=%async_computation.1 | async-start | bytes 524288 | tf_op jit(solution)/shard_map/all_to_all | solution.py:529
  141.9 1.2 copy-start.9
  143.2 1.0 copy-start.12
  144.2 5.4 %copy-start.10 = (bf16[2048,256]{1,0:T(8,128)(2,1)S(1)}, bf16[2048,256]{1,0:T(8,128)(2,1)}, u32[]{:S(2)}) copy-start(bf16[2048,256]{1,0:T(8,128)(2,1)} %copy-done.8) | copy-start | bytes 3145732
  144.2 5.4 %copy-start.13 = (bf16[2048,128]{1,0:T(8,128)(2,1)S(1)}, bf16[2048,128]{1,0:T(8,128)(2,1)}, u32[]{:S(2)}) copy-start(bf16[2048,128]{1,0:T(8,128)(2,1)} %copy-done.11) | copy-start | bytes 1572868
  180.5 0.7 copy-start.14

commit v2 on v0

v2 whole, which is shorter than its diff:
```python
import functools
import math

import jax
import jax.numpy as jnp
from jax import lax
from jax.experimental import pallas as pl
from jax.experimental.pallas import tpu as pltpu
from jax.sharding import PartitionSpec as P

D = 8192
HD = 128
PAGE = 64
CAP = 4
PUSH_CAP = 2
HEADS = 4
FEAT = 1024
QW = 512
KVW = 256
POOL = 16
PAGES = 32
NEW_PAGES = 8
SLOTS = 32
ROWS = 512
TAKE, PUSH, PLACE = 16, 17, 18
MIB = 1024 * 1024
SCALE = math.log2(math.e) / math.sqrt(HD)
F32 = jnp.float32
BF16 = jnp.bfloat16
HBM = pl.BlockSpec(memory_space=pltpu.HBM)
VMEM = pl.BlockSpec(memory_space=pltpu.VMEM)
SMEM = pl.BlockSpec(memory_space=pltpu.SMEM)


def params(mib):
    return pltpu.CompilerParams(vmem_limit_bytes=mib * MIB)


def cost(flops, nbytes):
    return pl.CostEstimate(flops=flops, bytes_accessed=nbytes, transcendentals=0)


def shape(dims, dtype):
    return jax.ShapeDtypeStruct(dims, dtype)


def ranks_of(owners, lanes):
    ranks = jnp.zeros_like(owners)
    for j in range(owners.shape[1]):
        ranks += ((owners == owners[:, j : j + 1]) & (lanes > j)).astype(jnp.int32)
    return ranks


def table_kernel(page_owner_ref, page_slot_ref, new_owner_ref, out_ref):
    me = lax.axis_index("pool")
    out_ref[...] = jnp.zeros_like(out_ref)
    owners, slots = page_owner_ref[...], page_slot_ref[...]
    lanes = lax.broadcasted_iota(jnp.int32, owners.shape, 1)
    rows = lax.broadcasted_iota(jnp.int32, owners.shape, 0)
    ranks = ranks_of(owners, lanes)
    for k in range(CAP):
        chosen = jnp.where((owners == me) & (ranks == k), slots, 0)
        out_ref[:POOL, k : k + 1] = jnp.sum(chosen, axis=1, keepdims=True)
    mine = jnp.where(rows == me, owners * CAP + ranks, 0)
    out_ref[TAKE : TAKE + 1, :PAGES] = jnp.sum(mine, axis=0, keepdims=True)
    targets = new_owner_ref[...]
    target_lanes = lax.broadcasted_iota(jnp.int32, targets.shape, 1)
    target_rows = lax.broadcasted_iota(jnp.int32, targets.shape, 0)
    ranks = ranks_of(targets, target_lanes)
    mine = jnp.where(target_rows == me, targets * PUSH_CAP + ranks, 0)
    out_ref[PUSH : PUSH + 1, :NEW_PAGES] = jnp.sum(mine, axis=0, keepdims=True)
    kept = (targets == me).astype(jnp.int32)
    slot = jnp.zeros_like(targets)
    for j in range(NEW_PAGES):
        slot += jnp.where(target_lanes > j, kept[:, j : j + 1], 0)
    in_row = jnp.sum(kept, axis=1, keepdims=True)
    for r in range(POOL):
        slot += jnp.where(target_rows > r, in_row[r : r + 1, :], 0)
    source = jnp.zeros((POOL, SLOTS), jnp.int32)
    slot_lanes = lax.broadcasted_iota(jnp.int32, source.shape, 1)
    slot_rows = lax.broadcasted_iota(jnp.int32, source.shape, 0)
    for j in range(NEW_PAGES):
        hit = (kept[:, j : j + 1] > 0) & (slot[:, j : j + 1] == slot_lanes)
        source += jnp.where(hit, slot_rows * PUSH_CAP + ranks[:, j : j + 1] + 1, 0)
    out_ref[PLACE : PLACE + 1, :SLOTS] = jnp.sum(source, axis=0, keepdims=True)


def make_table(page_owner, page_slot, new_owner):
    return pl.pallas_call(
        table_kernel,
        out_shape=shape((24, HD), jnp.int32),
        in_specs=[VMEM] * 3,
        out_specs=VMEM,
        compiler_params=params(4),
        cost_estimate=cost(0, 16384),
        name="make_table",
    )(page_owner, page_slot, new_owner)


def gather_kernel(table_ref, store_ref, out_ref):
    def one(index, _):
        out_ref[index] = store_ref[table_ref[index >> 2, index & 3]]
        return 0

    lax.fori_loop(0, POOL * CAP, one, 0, unroll=8)


def gather_pages(table, store):
    return pl.pallas_call(
        gather_kernel,
        out_shape=shape((POOL * CAP, 2 * PAGE, HD), BF16),
        in_specs=[SMEM, VMEM],
        out_specs=VMEM,
        compiler_params=params(8),
        cost_estimate=cost(0, 4 * MIB),
        name="gather_pages",
    )(table, store)


def split_kernel(table_ref, pages_ref, keys_ref, values_ref):
    row = lax.broadcasted_iota(jnp.int32, (2 * PAGE, 2 * PAGE), 0)
    column = lax.broadcasted_iota(jnp.int32, (2 * PAGE, 2 * PAGE), 1)
    wanted = jnp.where(row < PAGE, 2 * row, 2 * (row - PAGE) + 1)
    picker = (column == wanted).astype(BF16)
    values_ref[:, HD:] = jnp.ones((PAGES * PAGE, HD), BF16)
    for page in range(PAGES):
        both = jnp.dot(picker, pages_ref[table_ref[TAKE, page]], preferred_element_type=F32)
        rows = pl.ds(page * PAGE, PAGE)
        keys_ref[rows, :] = both[:PAGE].astype(BF16)
        values_ref[rows, :HD] = both[PAGE:].astype(BF16)


def split_pages(table, pages):
    return pl.pallas_call(
        split_kernel,
        out_shape=[
            shape((PAGES * PAGE, HD), BF16),
            shape((PAGES * PAGE, 2 * HD), BF16),
        ],
        in_specs=[SMEM, VMEM],
        out_specs=[VMEM, VMEM],
        compiler_params=params(8),
        cost_estimate=cost(2 * 2048 * 128 * 256, 4 * MIB),
        name="split_pages",
    )(table, pages)


def block_index(z_step, other_core):
    index = lax.axis_index("tp")
    z = lax.rem(index // 2 + z_step, 4)
    core = lax.rem(index, 2)
    return 2 * z + (1 - core if other_core else core)


def squares_of(rows):
    wide = rows.astype(F32)
    total = None
    for lane in range(0, FEAT, HD):
        part = wide[:, lane : lane + HD]
        total = part * part if total is None else total + part * part
    return total


def weight_copies(refs, buffers, sems, blocks):
    copies = []
    for i, (z_step, other) in enumerate(blocks):
        rows = pl.ds(pl.multiple_of(block_index(z_step, other) * FEAT, FEAT), FEAT)
        copies.append(
            [
                pltpu.make_async_copy(ref.at[rows, :], buffer.at[i], sems.at[len(refs) * i + j])
                for j, (ref, buffer) in enumerate(zip(refs, buffers))
            ]
        )
    for group in copies:
        for copy in group:
            copy.start()
    return copies


EARLY = ((0, False), (0, True), (3, False), (3, True), (1, False), (1, True))
LATE = ((2, False), (2, True))


def early_kernel(*refs):
    count = len(EARLY)
    x_refs = refs[:count]
    wq_ref, wkv_ref, q_ref, kv_ref, sq_ref, wq_buf, wkv_buf, sems = refs[count:]
    copies = weight_copies((wq_ref, wkv_ref), (wq_buf, wkv_buf), sems, EARLY)
    for i in range(count):
        copies[i][0].wait()
        copies[i][1].wait()
        rows = x_refs[i][...]
        q_part = jnp.dot(rows, wq_buf[i], preferred_element_type=F32)
        kv_part = jnp.dot(rows, wkv_buf[i], preferred_element_type=F32)
        sq_part = squares_of(rows)
        if i == 0:
            q_ref[...] = q_part
            kv_ref[...] = kv_part
            sq_ref[...] = sq_part
        else:
            q_ref[...] += q_part
            kv_ref[...] += kv_part
            sq_ref[...] += sq_part


def project_early(blocks, w_query, w_keyval):
    rows = blocks[0].shape[0]
    count = len(EARLY)
    return pl.pallas_call(
        early_kernel,
        out_shape=[shape((rows, QW), F32), shape((rows, KVW), F32), shape((rows, HD), F32)],
        in_specs=[VMEM] * count + [HBM] * 2,
        out_specs=[VMEM] * 3,
        scratch_shapes=[
            pltpu.VMEM((count, FEAT, QW), BF16),
            pltpu.VMEM((count, FEAT, KVW), BF16),
            pltpu.SemaphoreType.DMA((2 * count,)),
        ],
        compiler_params=params(16),
        cost_estimate=cost(
            2 * rows * count * FEAT * (QW + KVW), count * FEAT * (QW + KVW + rows) * 2
        ),
        name="project_early",
    )(*blocks, w_query, w_keyval)


def turn(values, cosine, sine):
    return values * cosine + pltpu.roll(values, HD // 2, 1) * sine


def late_dot(x_refs, buffers, index):
    parts = [
        jnp.dot(ref[...], buffers[index], preferred_element_type=F32)
        for ref in x_refs[2 * index : 2 * index + 2]
    ]
    return jnp.concatenate(parts, axis=0)


def keyval_kernel(table_ref, *refs):
    x_refs = refs[:4]
    kv_in, sq_in, cos_ref, sin_ref, wkv_ref = refs[4:9]
    keys_ref, values_ref, inv_ref, send_ref, wkv_buf, sems = refs[9:]
    copies = weight_copies((wkv_ref,), (wkv_buf,), sems, LATE)
    squares = sq_in[...]
    for i in range(2):
        halves = [squares_of(ref[...]) for ref in x_refs[2 * i : 2 * i + 2]]
        squares += jnp.concatenate(halves, axis=0)
    mean = jnp.sum(squares, axis=1, keepdims=True) / D
    inv_norm = jnp.broadcast_to(lax.rsqrt(mean + 1e-05), (ROWS, HD))
    inv_ref[...] = inv_norm
    kv_sum = kv_in[...]
    for i in range(2):
        copies[i][0].wait()
        kv_sum += late_dot(x_refs, wkv_buf, i)
    keys = turn(kv_sum[:, :HD] * inv_norm, cos_ref[...], sin_ref[...]).astype(BF16)
    values = (kv_sum[:, HD:] * inv_norm).astype(BF16)
    keys_ref[...] = keys
    values_ref[:, :HD] = values
    values_ref[:, HD:] = jnp.ones((ROWS, HD), BF16)
    row = lax.broadcasted_iota(jnp.int32, (2 * PAGE, 2 * PAGE), 0)
    column = lax.broadcasted_iota(jnp.int32, (2 * PAGE, 2 * PAGE), 1)
    picker = (column == (row >> 1) + (row & 1) * PAGE).astype(BF16)
    for page in range(NEW_PAGES):
        rows = slice(page * PAGE, (page + 1) * PAGE)
        both = jnp.concatenate([keys[rows], values[rows]], axis=0)
        mixed = jnp.dot(picker, both, preferred_element_type=F32).astype(BF16)
        send_ref[table_ref[PUSH, page]] = mixed


def project_keyval(table, halves, kv_sum, squares, cosine, sine, w_keyval):
    return pl.pallas_call(
        keyval_kernel,
        out_shape=[
            shape((ROWS, HD), BF16),
            shape((ROWS, 2 * HD), BF16),
            shape((ROWS, HD), F32),
            shape((POOL * PUSH_CAP, 2 * PAGE, HD), BF16),
        ],
        in_specs=[SMEM] + [VMEM] * 8 + [HBM],
        out_specs=[VMEM] * 4,
        scratch_shapes=[pltpu.VMEM((2, FEAT, KVW), BF16), pltpu.SemaphoreType.DMA((2,))],
        compiler_params=params(12),
        cost_estimate=cost(2 * ROWS * 2 * FEAT * KVW, 2 * FEAT * (KVW + ROWS) * 2),
        name="project_keyval",
    )(table, *halves, kv_sum, squares, cosine, sine, w_keyval)


def dot_nt(a, b):
    return lax.dot_general(a, b, (((1,), (1,)), ((), ())), preferred_element_type=F32)


def attend_kernel(*refs):
    x_refs = refs[:4]
    q_in, inv_ref, cos_ref, sin_ref, wq_ref = refs[4:9]
    keys_ref, values_ref, own_keys_ref, own_values_ref, out_ref, wq_buf, q_buf, sems = refs[9:]
    copies = weight_copies((wq_ref,), (wq_buf,), sems, LATE)
    q_sum = q_in[...]
    for i in range(2):
        copies[i][0].wait()
        q_sum += late_dot(x_refs, wq_buf, i)
    inv_norm = inv_ref[...]
    for head in range(HEADS):
        part = q_sum[:, head * HD : (head + 1) * HD] * inv_norm
        q_buf[head] = turn(part, cos_ref[...], sin_ref[...]).astype(BF16)
    block = 128
    allowed = lax.broadcasted_iota(jnp.int32, (block, block), 0) >= lax.broadcasted_iota(
        jnp.int32, (block, block), 1
    )

    def one_head(head, _):
        lanes = pl.ds(pl.multiple_of(head * HD, HD), HD)
        for b in range(ROWS // block):
            rows = slice(b * block, (b + 1) * block)
            queries = q_buf[head, rows, :]
            scores = dot_nt(queries, keys_ref[...])
            own = dot_nt(queries, own_keys_ref[: (b + 1) * block, :])
            last = jnp.where(allowed, own[:, b * block :], -1e30)
            own = last if b == 0 else jnp.concatenate([own[:, : b * block], last], axis=1)
            top = jnp.maximum(
                jnp.max(scores, axis=1, keepdims=True), jnp.max(own, axis=1, keepdims=True)
            )
            weights = jnp.exp2((scores - top) * SCALE).astype(BF16)
            own_weights = jnp.exp2((own - top) * SCALE).astype(BF16)
            both = jnp.dot(weights, values_ref[...], preferred_element_type=F32)
            both += jnp.dot(
                own_weights, own_values_ref[: (b + 1) * block, :], preferred_element_type=F32
            )
            out_ref[rows, lanes] = (both[:, :HD] / both[:, HD:]).astype(BF16)
        return 0

    lax.fori_loop(0, HEADS, one_head, 0)


def attend(halves, q_sum, inv_norm, cosine, sine, w_query, keys, values, own_keys, own_values):
    return pl.pallas_call(
        attend_kernel,
        out_shape=shape((ROWS, QW), BF16),
        in_specs=[VMEM] * 8 + [HBM] + [VMEM] * 4,
        out_specs=VMEM,
        scratch_shapes=[
            pltpu.VMEM((2, FEAT, QW), BF16),
            pltpu.VMEM((HEADS, ROWS, HD), BF16),
            pltpu.SemaphoreType.DMA((2,)),
        ],
        compiler_params=params(28),
        cost_estimate=cost(2 * ROWS * (4 * 2560 * 512 + 2 * FEAT * QW), 8 * MIB),
        name="attend",
    )(*halves, q_sum, inv_norm, cosine, sine, w_query, keys, values, own_keys, own_values)


def place_kernel(table_ref, received_ref, out_ref):
    height = out_ref.shape[0]
    base = pl.program_id(0) * height
    for i in range(height):
        source = table_ref[PLACE, base + i]
        page = received_ref[jnp.maximum(source - 1, 0)]
        out_ref[i] = jnp.where(source > 0, page, jnp.zeros_like(page))


def place_pages(table, received):
    height = 8
    return pl.pallas_call(
        place_kernel,
        grid=(SLOTS // height,),
        out_shape=shape((SLOTS, 2 * PAGE, HD), BF16),
        in_specs=[SMEM, VMEM],
        out_specs=pl.BlockSpec((height, 2 * PAGE, HD), lambda i: (i, 0, 0)),
        compiler_params=params(8),
        cost_estimate=cost(0, 2 * MIB),
        name="place_pages",
    )(table, received)


def shift(values, step):
    pairs = [(i, ((i // 2 + step) % 4) * 2 + i % 2) for i in range(8)]
    return lax.ppermute(values, "tp", pairs)


def swap(values):
    return lax.ppermute(values, "tp", [(i, i ^ 1) for i in range(8)])


def rope_tables(row_count, offset):
    half_dim = HD // 2
    frequency = 500000.0 ** (-(jnp.arange(half_dim, dtype=F32) * (2.0 / HD)))
    place = (offset + jnp.arange(row_count, dtype=jnp.int32)).astype(F32)
    angles = place[:, None] * frequency[None, :]
    cosine, sine = jnp.cos(angles), jnp.sin(angles)
    return jnp.concatenate([cosine, cosine], 1), jnp.concatenate([-sine, sine], 1)


def exchange(values):
    return lax.all_to_all(values, "pool", split_axis=0, concat_axis=0, tiled=True)


def body(hidden, w_query, w_keyval, store, page_owner, page_slot, new_owner):
    half = ROWS // 2
    ahead, behind = shift(hidden, 1), shift(hidden, -1)
    table = make_table(page_owner, page_slot, new_owner)
    pages = exchange(gather_pages(table, store.reshape(64, 2 * PAGE, HD)))
    cosine, sine = rope_tables(ROWS, PAGES * PAGE)
    top, bottom = shift(ahead[:half], 1), shift(behind[half:], -1)
    blocks = (hidden, swap(hidden), ahead, swap(ahead), behind, swap(behind))
    q_sum, kv_sum, squares = project_early(blocks, w_query, w_keyval)
    keys, values = split_pages(table, pages)
    halves = (top, bottom, swap(top), swap(bottom))
    own_keys, own_values, inv_norm, send = project_keyval(
        table, halves, kv_sum, squares, cosine, sine, w_keyval
    )
    received = exchange(send)
    attended = attend(
        halves, q_sum, inv_norm, cosine, sine, w_query, keys, values, own_keys, own_values
    )
    placed = place_pages(table, received)
    return attended, placed.reshape(SLOTS, 1, PAGE, 2, HD)


def solution(mesh):
    in_specs = (
        P("pool", "tp"),
        P(None, "tp"),
        P(None, "tp"),
        P("pool", "tp", None, None, None),
        P(),
        P(),
        P(),
    )
    out_specs = (P("pool", "tp"), P("pool", "tp", None, None, None))
    return jax.shard_map(body, mesh=mesh, in_specs=in_specs, out_specs=out_specs, check_vma=False)
```

time: 575 us -> 97.4 us (0.17)
  waiting for transfers between devices: 391 us -> 20.2 us
  matrix products: 55.9 us -> 0 us
  Pallas kernels: 0 us -> 29.5 us
  other arithmetic: 30.7 us -> 1.21 us
  blocking collectives: 23.3 us -> 0 us
  loops' own time: 16.5 us -> 0 us
  between operations: 14.4 us -> 0.9 us
  starting transfers between devices: 12.5 us -> 22.3 us
  local copies, waits for them, and re-layouts: 29.2 us -> 21.3 us
    all_gather x2 -> x0, waiting for transfers between devices: 261 us -> none  [the longest x1 207 us: body(): gathered = lax.all_gather(fresh_pages, 'pool', axis=0, tiled=True)]
    all_to_all x2, waiting for transfers between devices: 129 us -> 0.01 us  [exchange(): lax.all_to_all(values, 'pool', split_axis=0, concat_axis=0, tiled=True)]
    dot_general x18 -> x0, matrix products: 55.9 us -> none  [the longest x4 19.9 us: attend_one_head(): jnp.einsum('snk,skd->snd', weights.astype(jnp.bfloat16), value_rows, pref...]
    pallas_call x0 -> x7, Pallas kernels: none -> 29.5 us  [the longest x1 11.3 us: attend(): pl.pallas_call(attend_kernel, out_shape=shape((ROWS, QW), BF16), in_specs...]
    reduce_sum x15 -> x0, other arithmetic: 24.4 us -> none  [the longest x4 9.63 us: attend_one_head(): return (summed, row_max, jnp.sum(weights, axis=2))]
    all_to_all x2 -> x0, blocking collectives: 23.3 us -> none  [the longest x1 12.2 us: body(): lax.all_to_all(row_max, 'pool', split_axis=0, concat_axis=0, tiled=True)]
    ppermute x0 -> x9, waiting for transfers between devices: none -> 20.2 us  [the longest x4 20.2 us: shift(): return lax.ppermute(values, 'tp', pairs)]
    unnamed x16 -> x49, local copies, waits for them, and re-layouts: 2.41 us -> 20.2 us
  transfers between devices with their start and end apart: 4 -> 11, of which waited for: 4 -> 3; matrix products, arithmetic and copies ran while one was open for 7% -> 3% of each run, Pallas kernels for 0% -> 28%
where the time goes in v2:
time: 97.4 us; the launch traced here: 95.5 us
  Pallas kernels  29.5 us (30%)
  starting transfers between devices  22.3 us (23%)
  local copies, waits for them, and re-layouts  21.3 us (22%)
  waiting for transfers between devices  20.2 us (21%)
  other arithmetic  1.21 us (1%)
    ppermute x4, waiting for transfers between devices, shift(): return lax.ppermute(values, 'tp', pairs)  20.2 us
    unnamed x49, local copies, waits for them, and re-layouts  20.2 us
    all_to_all x2, starting transfers between devices, exchange(): lax.all_to_all(values, 'pool', split_axis=0, concat_axis=0, tiled=True)  14.1 us
    pallas_call x1, Pallas kernels, attend(): pl.pallas_call(attend_kernel, out_shape=shape((ROWS, QW), BF16), in_specs...  11.3 us
    pallas_call x1, Pallas kernels, project_early(): pl.pallas_call(early_kernel, out_shape=[shape((rows, QW), F32), shape((ro...  9.46 us
    ppermute x4, starting transfers between devices, shift(): return lax.ppermute(values, 'tp', pairs)  7.65 us
    pallas_call x1, Pallas kernels, place_pages(): pl.pallas_call(place_kernel, grid=(SLOTS // height,), out_shape=shape((SL...  2.45 us
    pallas_call x1, Pallas kernels, project_keyval(): pl.pallas_call(keyval_kernel, out_shape=[shape((ROWS, HD), BF16), shape((...  2.36 us
  transfers between devices with their start and end apart: 11, of which 3 were waited for; matrix products, arithmetic and copies ran while one was open for 3% of the time, Pallas kernels for 28%

profile of v2, /device:TPU:0, one launch (start us, length us, event | category | flops | bytes accessed | tf_op | source)
XLA Modules:
  0.0 95.5 jit_solution(7753083882660307141)
XLA Ops:
  0.6 2.1 %collective-permute-start = (bf16[512,1024]{1,0:T(8,128)(2,1)}, bf16[512,1024]{1,0:T(8,128)(2,1)S(1)}, u32[]{:S(2)}, u32[]{:S(2)}) collective-permute-start(bf16[512,1024]{1,0:T(8,128)(2,1)} %refs_0_.1), channel_id=1, source_target_pairs={{0,2},{1,3},{2,4},{3,5},{4,6},{5,7},{6,0},{7,1},{8,10},{9,11},{10,... | collective-permute-start | bytes 3145736 | tf_op jit(solution)/shard_map/ppermute | solution.py:376
  2.7 2.2 %collective-permute-start.2 = (bf16[512,1024]{1,0:T(8,128)(2,1)}, bf16[512,1024]{1,0:T(8,128)(2,1)}, u32[]{:S(2)}, u32[]{:S(2)}) collective-permute-start(bf16[512,1024]{1,0:T(8,128)(2,1)} %refs_0_.1), channel_id=1, source_target_pairs={{0,6},{1,7},{2,0},{3,1},{4,2},{5,3},{6,4},{7,5},{8,14},{9,15},{10,... | collective-permute-start | bytes 3145736 | tf_op jit(solution)/shard_map/ppermute | solution.py:376
  4.9 0.8 copy.9.new_owner_ref
  5.7 0.7 copy-done.16
  6.4 0.7 copy-done.17
  7.1 0.5 make_table.1.table_ref
  7.6 0.0 copy-start.3
  7.6 1.6 %copy-done.3 = bf16[64,1,64,2,128]{4,3,2,1,0:T(2,128)(2,1)S(1)} copy-done((bf16[64,1,64,2,128]{4,3,2,1,0:T(2,128)(2,1)S(1)}, bf16[64,1,64,2,128]{4,3,2,1,0:T(2,128)(2,1)}, u32[]{:S(2)}) %copy-start.3) | copy-done | bytes 2097176
  9.2 2.3 %gather_pages.1 = bf16[64,128,128]{2,1,0:T(8,128)(2,1)} custom-call(s32[24,128]{1,0:T(8,128)S(1)} %make_table.1.table_ref, bf16[64,128,128]{2,1,0:T(8,128)(2,1)S(1)} %bitcast.4), custom_call_target="tpu_custom_call" | custom-call | bytes 4194304 | tf_op jit(solution)/shard_map/gather_pages/pallas_call | solution.py:109
  11.5 7.0 %all-to-all-start = ((bf16[64,128,128]{2,1,0:T(8,128)(2,1)}), bf16[64,128,128]{2,1,0:T(8,128)(2,1)S(1)}, u32[]{:S(2)}, u32[]{:S(2)}) async-start(bf16[64,128,128]{2,1,0:T(8,128)(2,1)} %gather_pages.1), calls=%async_computation | async-start | bytes 4194304 | tf_op jit(solution)/shard_map/all_to_all | solution.py:393
  18.5 0.0 copy-start
  18.5 0.1 collective-permute-start.6
  18.6 9.6 %collective-permute-done.refs_2_ = bf16[512,1024]{1,0:T(8,128)(2,1)S(1)} collective-permute-done((bf16[512,1024]{1,0:T(8,128)(2,1)}, bf16[512,1024]{1,0:T(8,128)(2,1)S(1)}, u32[]{:S(2)}, u32[]{:S(2)}) %collective-permute-start) | collective-permute-done | bytes 1048608 | tf_op jit(solution)/shard_map/ppermute | solution.py:376
  28.2 0.5 collective-permute-start.8
  28.7 0.9 collective-permute-start.1
  29.7 1.1 %slice.9 = bf16[256,1024]{1,0:T(8,128)(2,1)S(1)} slice(bf16[512,1024]{1,0:T(8,128)(2,1)} %collective-permute-done.2.refs_4_), slice={[256:512], [0:1024]} | slice | bytes 1048576 | tf_op jit(solution)/shard_map/slice | solution.py:402
  30.7 2.5 %collective-permute-start.3 = (bf16[256,1024]{1,0:T(8,128)(2,1)S(1)}, bf16[256,1024]{1,0:T(8,128)(2,1)S(1)}, u32[]{:S(2)}, u32[]{:S(2)}) collective-permute-start(bf16[256,1024]{1,0:T(8,128)(2,1)S(1)} %slice.9), channel_id=1, source_target_pairs={{0,6},{1,7},{2,0},{3,1},{4,2},{5,3},{6,4},{7,5},{8,14},{9,15},{10,... | collective-permute-start | bytes 1572872 | tf_op jit(solution)/shard_map/ppermute | solution.py:376
  33.2 1.0 %fusion = (f32[512,64]{1,0:T(8,128)S(1)}, f32[512,64]{1,0:T(8,128)S(1)}, f32[512,64]{1,0:T(8,128)S(1)}) fusion(f32[64]{0:T(128)S(1)} %negate_power_fusion, f32[512]{0:T(512)S(1)} %add_convert_fusion), kind=kLoop, calls=%fused_computation.4 | loop fusion | flops 65536 | bytes 395520 | tf_op jit(solution)/shard_map/neg | solution.py:389
  34.2 9.8 %collective-permute-done.1.refs_0_ = bf16[256,1024]{1,0:T(8,128)(2,1)S(1)} collective-permute-done((bf16[256,1024]{1,0:T(8,128)(2,1)S(1)}, bf16[256,1024]{1,0:T(8,128)(2,1)S(1)}, u32[]{:S(2)}, u32[]{:S(2)}) %collective-permute-start.1) | collective-permute-done | bytes 524320 | tf_op jit(solution)/shard_map/ppermute | solution.py:376
  44.0 0.8 collective-permute-done.3.refs_1_
  44.9 0.0 collective-permute-start.5
  44.9 0.2 pad_maximum_fusion
  45.1 0.0 collective-permute-done.6.refs_1_
  45.1 0.0 collective-permute-done.7.refs_3_
  45.1 0.0 copy-start.1
  45.1 3.4 %copy-done.1 = bf16[8192,512]{1,0:T(8,128)(2,1)S(1)} copy-done((bf16[8192,512]{1,0:T(8,128)(2,1)S(1)}, bf16[8192,512]{1,0:T(8,128)(2,1)}, u32[]{:S(2)}) %copy-start.1) | copy-done | bytes 8388632
  48.6 1.2 %copy-done.4 = bf16[512,1024]{1,0:T(8,128)(2,1)S(1)} copy-done((bf16[512,1024]{1,0:T(8,128)(2,1)S(1)}, bf16[512,1024]{1,0:T(8,128)(2,1)}, u32[]{:S(2)}) %copy-start.4) | copy-done | bytes 1048600
  49.8 9.5 %project_early.1 = (f32[512,512]{1,0:T(8,128)S(1)}, f32[512,256]{1,0:T(8,128)S(1)}, f32[512,128]{1,0:T(8,128)S(1)}) custom-call(bf16[512,1024]{1,0:T(8,128)(2,1)S(1)} %copy-done.4, bf16[512,1024]{1,0:T(8,128)(2,1)S(1)} %collective-permute-done.6.refs_1_, bf16[512,1024]{1,0:T(8,128)(2,1)S(1)} %collective-permute-done.refs_2_, ...), custom_call_target="tpu_custom_call" | custom-call | flops 4831838208 | bytes 15728640 | tf_op jit(solution)/shard_map/project_early/pallas_call | solution.py:209
  59.3 0.0 copy-start.18
  59.3 1.0 %copy-done.18 = f32[512,512]{1,0:T(8,128)} copy-done((f32[512,512]{1,0:T(8,128)}, f32[512,512]{1,0:T(8,128)S(1)}, u32[]{:S(2)}) %copy-start.18) | copy-done | bytes 1048600
  60.2 0.0 collective-permute-done.4.refs_2_
  60.3 2.4 %project_keyval.1 = (bf16[512,128]{1,0:T(8,128)(2,1)S(1)}, bf16[512,256]{1,0:T(8,128)(2,1)S(1)}, f32[512,128]{1,0:T(8,128)S(1)}, bf16[32,128,128]{2,1,0:T(8,128)(2,1)S(1)}) custom-call(s32[24,128]{1,0:T(8,128)S(1)} %make_table.1.table_ref, bf16[256,1024]{1,0:T(8,128)(2,1)S(1)} %collective-permute-done.1.refs_0_, ...), custom_call_target="tpu_custom_call" | custom-call | flops 536870912 | bytes 3145728 | tf_op jit(solution)/shard_map/project_keyval/pallas_call | solution.py:271
  62.6 1.0 %copy-done.7 = bf16[32,128,128]{2,1,0:T(8,128)(2,1)} copy-done((bf16[32,128,128]{2,1,0:T(8,128)(2,1)}, bf16[32,128,128]{2,1,0:T(8,128)(2,1)S(1)}, u32[]{:S(2)}) %copy-start.7) | copy-done | bytes 1048600
  63.6 0.8 copy-done.12
  64.4 0.8 copy-done.14
  65.2 0.7 copy-done.20
  65.9 0.7 copy-done.22
  66.6 7.0 %all-to-all-start.1 = ((bf16[32,128,128]{2,1,0:T(8,128)(2,1)}), bf16[32,128,128]{2,1,0:T(8,128)(2,1)S(1)}, u32[]{:S(2)}, u32[]{:S(2)}) async-start(bf16[32,128,128]{2,1,0:T(8,128)(2,1)} %copy-done.7), calls=%async_computation.1 | async-start | bytes 2097152 | tf_op jit(solution)/shard_map/all_to_all | solution.py:393
  73.7 0.0 copy-start.9
  73.7 1.2 %split_pages.1 = (bf16[2048,128]{1,0:T(8,128)(2,1)S(1)}, bf16[2048,256]{1,0:T(8,128)(2,1)S(1)}) custom-call(s32[24,128]{1,0:T(8,128)S(1)} %make_table.1.table_ref, bf16[64,128,128]{2,1,0:T(8,128)(2,1)S(1)} %all-to-all-done.pages_ref), custom_call_target="tpu_custom_call" | custom-call | flops 134217728 | bytes 4194304 | tf_op jit(solution)/shard_map/split_pages/pallas_call | solution.py:134
  75.0 0.1 copy-done.13
  75.1 0.1 copy-done.21
  75.2 3.4 %copy-done.2 = bf16[8192,512]{1,0:T(8,128)(2,1)S(1)} copy-done((bf16[8192,512]{1,0:T(8,128)(2,1)S(1)}, bf16[8192,512]{1,0:T(8,128)(2,1)}, u32[]{:S(2)}) %copy-start.2) | copy-done | bytes 8388632
  78.6 1.0 %copy-done.15 = bf16[256,1024]{1,0:T(8,128)(2,1)S(1)} copy-done((bf16[256,1024]{1,0:T(8,128)(2,1)S(1)}, bf16[256,1024]{1,0:T(8,128)(2,1)}, u32[]{:S(2)}) %copy-start.15) | copy-done | bytes 524312
  79.6 1.2 %copy-done.19 = f32[512,512]{1,0:T(8,128)S(1)} copy-done((f32[512,512]{1,0:T(8,128)S(1)}, f32[512,512]{1,0:T(8,128)}, u32[]{:S(2)}) %copy-start.19) | copy-done | bytes 1048600
  80.8 0.9 copy-done.23
  81.8 11.3 %attend.1 = bf16[512,512]{1,0:T(8,128)(2,1)} custom-call(bf16[256,1024]{1,0:T(8,128)(2,1)S(1)} %copy-done.9, bf16[256,1024]{1,0:T(8,128)(2,1)S(1)} %copy-done.11, bf16[256,1024]{1,0:T(8,128)(2,1)S(1)} %copy-done.13, bf16[256,1024]{1,0:T(8,128)(2,1)S(1)} %copy-done.15, f32[512,512]{1,0:T(8,128)S(1)} %copy-done.19, f32[512,128]{1,0:T(8,128)S(1)} %copy-done.23, ...), custom_call_target="tpu_custom_call" | custom-call | flops 6442450944 | bytes 8388608 | tf_op jit(solution)/shard_map/attend/pallas_call | solution.py:335
  93.1 2.4 %place_pages.1 = bf16[32,128,128]{2,1,0:T(8,128)(2,1)} custom-call(s32[24,128]{1,0:T(8,128)S(1)} %make_table.1.table_ref, bf16[32,128,128]{2,1,0:T(8,128)(2,1)S(1)} %all-to-all-done.1.received_ref), custom_call_target="tpu_custom_call" | custom-call | bytes 2097152 | tf_op jit(solution)/shard_map/place_pages/pallas_call | solution.py:362
  (36 shorter events, 0.1 us)
Async XLA Ops:
  0.6 27.6 %collective-permute-start = (bf16[512,1024]{1,0:T(8,128)(2,1)}, bf16[512,1024]{1,0:T(8,128)(2,1)S(1)}, u32[]{:S(2)}, u32[]{:S(2)}) collective-permute-start(bf16[512,1024]{1,0:T(8,128)(2,1)} %refs_0_.1), channel_id=1, source_target_pairs={{0,2},{1,3},{2,4},{3,5},{4,6},{5,7},{6,0},{7,1},{8,10},{9,11},{10,... | collective-permute-start | bytes 3145736 | tf_op jit(solution)/shard_map/ppermute | solution.py:376
  2.7 25.5 %collective-permute-start.2 = (bf16[512,1024]{1,0:T(8,128)(2,1)}, bf16[512,1024]{1,0:T(8,128)(2,1)}, u32[]{:S(2)}, u32[]{:S(2)}) collective-permute-start(bf16[512,1024]{1,0:T(8,128)(2,1)} %refs_0_.1), channel_id=1, source_target_pairs={{0,6},{1,7},{2,0},{3,1},{4,2},{5,3},{6,4},{7,5},{8,14},{9,15},{10,... | collective-permute-start | bytes 3145736 | tf_op jit(solution)/shard_map/ppermute | solution.py:376
  5.7 0.7 copy-start.16
  6.4 0.7 copy-start.17
  7.6 1.6 %copy-start.3 = (bf16[64,1,64,2,128]{4,3,2,1,0:T(2,128)(2,1)S(1)}, bf16[64,1,64,2,128]{4,3,2,1,0:T(2,128)(2,1)}, u32[]{:S(2)}) copy-start(bf16[64,1,64,2,128]{4,3,2,1,0:T(2,128)(2,1)} %param.10) | copy-start | bytes 6291460
  11.5 55.2 %all-to-all-start = ((bf16[64,128,128]{2,1,0:T(8,128)(2,1)}), bf16[64,128,128]{2,1,0:T(8,128)(2,1)S(1)}, u32[]{:S(2)}, u32[]{:S(2)}) async-start(bf16[64,128,128]{2,1,0:T(8,128)(2,1)} %gather_pages.1), calls=%async_computation | async-start | bytes 4194304 | tf_op jit(solution)/shard_map/all_to_all | solution.py:393
  18.5 26.6 %copy-start = (bf16[8192,256]{1,0:T(8,128)(2,1)S(1)}, bf16[8192,256]{1,0:T(8,128)(2,1)}, u32[]{:S(2)}) copy-start(bf16[8192,256]{1,0:T(8,128)(2,1)} %refs_8_.2) | copy-start | bytes 12582916
  18.5 26.6 %collective-permute-start.6 = (bf16[512,1024]{1,0:T(8,128)(2,1)}, bf16[512,1024]{1,0:T(8,128)(2,1)S(1)}, u32[]{:S(2)}, u32[]{:S(2)}) collective-permute-start(bf16[512,1024]{1,0:T(8,128)(2,1)} %refs_0_.1), channel_id=1, source_target_pairs={{0,1},{1,0},{2,3},{3,2},{4,5},{5,4},{6,7},{7,6},{8,9},{9,8},{10,11... | collective-permute-start | bytes 3145736 | tf_op jit(solution)/shard_map/ppermute | solution.py:380
  28.2 16.9 %collective-permute-start.7 = (bf16[512,1024]{1,0:T(8,128)(2,1)S(1)}, bf16[512,1024]{1,0:T(8,128)(2,1)S(1)}, u32[]{:S(2)}, u32[]{:S(2)}) collective-permute-start(bf16[512,1024]{1,0:T(8,128)(2,1)S(1)} %collective-permute-done.refs_2_), channel_id=1, source_target_pairs={{0,1},{1,0},{2,3},{3,2},{4,5},{5,4},{6,7},{7,6},{8,9},{9,8},{10,11... | collective-permute-start | bytes 3145736 | tf_op jit(solution)/shard_map/ppermute | solution.py:380
  28.2 16.9 %collective-permute-start.8 = (bf16[512,1024]{1,0:T(8,128)(2,1)}, bf16[512,1024]{1,0:T(8,128)(2,1)S(1)}, u32[]{:S(2)}, u32[]{:S(2)}) collective-permute-start(bf16[512,1024]{1,0:T(8,128)(2,1)} %collective-permute-done.2.refs_4_), channel_id=1, source_target_pairs={{0,1},{1,0},{2,3},{3,2},{4,5},{5,4},{6,7},{7,6},{8,9},{9,8},{10,11... | collective-permute-start | bytes 3145736 | tf_op jit(solution)/shard_map/ppermute | solution.py:380
  28.7 15.3 %collective-permute-start.1 = (bf16[256,1024]{1,0:T(8,128)(2,1)S(1)}, bf16[256,1024]{1,0:T(8,128)(2,1)S(1)}, u32[]{:S(2)}, u32[]{:S(2)}) collective-permute-start(bf16[256,1024]{1,0:T(8,128)(2,1)S(1)} %slice.8), channel_id=1, source_target_pairs={{0,2},{1,3},{2,4},{3,5},{4,6},{5,7},{6,0},{7,1},{8,10},{9,11},{10,... | collective-permute-start | bytes 1572872 | tf_op jit(solution)/shard_map/ppermute | solution.py:376
  30.7 14.1 %collective-permute-start.3 = (bf16[256,1024]{1,0:T(8,128)(2,1)S(1)}, bf16[256,1024]{1,0:T(8,128)(2,1)S(1)}, u32[]{:S(2)}, u32[]{:S(2)}) collective-permute-start(bf16[256,1024]{1,0:T(8,128)(2,1)S(1)} %slice.9), channel_id=1, source_target_pairs={{0,6},{1,7},{2,0},{3,1},{4,2},{5,3},{6,4},{7,5},{8,14},{9,15},{10,... | collective-permute-start | bytes 1572872 | tf_op jit(solution)/shard_map/ppermute | solution.py:376
  44.0 16.2 %copy-start.8 = (bf16[256,1024]{1,0:T(8,128)(2,1)}, bf16[256,1024]{1,0:T(8,128)(2,1)S(1)}, u32[]{:S(2)}) copy-start(bf16[256,1024]{1,0:T(8,128)(2,1)S(1)} %collective-permute-done.1.refs_0_) | copy-start | bytes 1572868
  44.0 16.2 %collective-permute-start.4 = (bf16[256,1024]{1,0:T(8,128)(2,1)S(1)}, bf16[256,1024]{1,0:T(8,128)(2,1)S(1)}, u32[]{:S(2)}, u32[]{:S(2)}) collective-permute-start(bf16[256,1024]{1,0:T(8,128)(2,1)S(1)} %collective-permute-done.1.refs_0_), channel_id=1, source_target_pairs={{0,1},{1,0},{2,3},{3,2},{4,5},{5,4},{6,7},{7,6},{8,9},{9,8},{10,11... | collective-permute-start | bytes 1572872 | tf_op jit(solution)/shard_map/ppermute | solution.py:380
  44.9 15.4 %copy-start.10 = (bf16[256,1024]{1,0:T(8,128)(2,1)}, bf16[256,1024]{1,0:T(8,128)(2,1)S(1)}, u32[]{:S(2)}) copy-start(bf16[256,1024]{1,0:T(8,128)(2,1)S(1)} %collective-permute-done.3.refs_1_) | copy-start | bytes 1572868
  44.9 15.4 %collective-permute-start.5 = (bf16[256,1024]{1,0:T(8,128)(2,1)S(1)}, bf16[256,1024]{1,0:T(8,128)(2,1)S(1)}, u32[]{:S(2)}, u32[]{:S(2)}) collective-permute-start(bf16[256,1024]{1,0:T(8,128)(2,1)S(1)} %collective-permute-done.3.refs_1_), channel_id=1, source_target_pairs={{0,1},{1,0},{2,3},{3,2},{4,5},{5,4},{6,7},{7,6},{8,9},{9,8},{10,11... | collective-permute-start | bytes 1572872 | tf_op jit(solution)/shard_map/ppermute | solution.py:380
  45.1 15.2 %copy-start.5 = (f32[512,128]{1,0:T(8,128)}, f32[512,128]{1,0:T(8,128)S(1)}, u32[]{:S(2)}) copy-start(f32[512,128]{1,0:T(8,128)S(1)} %get-tuple-element.26.refs_7_) | copy-start | bytes 786436
  45.1 3.4 %copy-start.1 = (bf16[8192,512]{1,0:T(8,128)(2,1)S(1)}, bf16[8192,512]{1,0:T(8,128)(2,1)}, u32[]{:S(2)}) copy-start(bf16[8192,512]{1,0:T(8,128)(2,1)} %refs_8_.3) | copy-start | bytes 25165828
  48.6 1.2 %copy-start.4 = (bf16[512,1024]{1,0:T(8,128)(2,1)S(1)}, bf16[512,1024]{1,0:T(8,128)(2,1)}, u32[]{:S(2)}) copy-start(bf16[512,1024]{1,0:T(8,128)(2,1)} %refs_0_.1) | copy-start | bytes 3145732
  59.3 1.0 %copy-start.18 = (f32[512,512]{1,0:T(8,128)}, f32[512,512]{1,0:T(8,128)S(1)}, u32[]{:S(2)}) copy-start(f32[512,512]{1,0:T(8,128)S(1)} %get-tuple-element.11.refs_4_) | copy-start | bytes 3145732
  62.6 1.0 %copy-start.7 = (bf16[32,128,128]{2,1,0:T(8,128)(2,1)}, bf16[32,128,128]{2,1,0:T(8,128)(2,1)S(1)}, u32[]{:S(2)}) copy-start(bf16[32,128,128]{2,1,0:T(8,128)(2,1)S(1)} %get-tuple-element.19) | copy-start | bytes 3145732
  63.6 0.8 copy-start.12
  64.4 0.8 copy-start.14
  65.2 0.7 copy-start.20
  65.9 0.7 copy-start.22
  66.6 26.4 %all-to-all-start.1 = ((bf16[32,128,128]{2,1,0:T(8,128)(2,1)}), bf16[32,128,128]{2,1,0:T(8,128)(2,1)S(1)}, u32[]{:S(2)}, u32[]{:S(2)}) async-start(bf16[32,128,128]{2,1,0:T(8,128)(2,1)} %copy-done.7), calls=%async_computation.1 | async-start | bytes 2097152 | tf_op jit(solution)/shard_map/all_to_all | solution.py:393
  73.7 1.3 %copy-start.6 = (f32[512,128]{1,0:T(8,128)S(1)}, f32[512,128]{1,0:T(8,128)}, u32[]{:S(2)}) copy-start(f32[512,128]{1,0:T(8,128)} %copy-done.5) | copy-start | bytes 786436
  73.7 1.3 %copy-start.9 = (bf16[256,1024]{1,0:T(8,128)(2,1)S(1)}, bf16[256,1024]{1,0:T(8,128)(2,1)}, u32[]{:S(2)}) copy-start(bf16[256,1024]{1,0:T(8,128)(2,1)} %copy-done.8) | copy-start | bytes 1572868
  73.7 1.3 %copy-start.11 = (bf16[256,1024]{1,0:T(8,128)(2,1)S(1)}, bf16[256,1024]{1,0:T(8,128)(2,1)}, u32[]{:S(2)}) copy-start(bf16[256,1024]{1,0:T(8,128)(2,1)} %copy-done.10) | copy-start | bytes 1572868
  73.7 1.4 %copy-start.13 = (bf16[256,1024]{1,0:T(8,128)(2,1)S(1)}, bf16[256,1024]{1,0:T(8,128)(2,1)}, u32[]{:S(2)}) copy-start(bf16[256,1024]{1,0:T(8,128)(2,1)} %copy-done.12) | copy-start | bytes 1572868
  73.7 1.5 %copy-start.21 = (bf16[512,256]{1,0:T(8,128)(2,1)S(1)}, bf16[512,256]{1,0:T(8,128)(2,1)}, u32[]{:S(2)}) copy-start(bf16[512,256]{1,0:T(8,128)(2,1)} %copy-done.20) | copy-start | bytes 786436
  75.2 3.4 %copy-start.2 = (bf16[8192,512]{1,0:T(8,128)(2,1)S(1)}, bf16[8192,512]{1,0:T(8,128)(2,1)}, u32[]{:S(2)}) copy-start(bf16[8192,512]{1,0:T(8,128)(2,1)} %refs_8_.3) | copy-start | bytes 25165828
  78.6 1.0 %copy-start.15 = (bf16[256,1024]{1,0:T(8,128)(2,1)S(1)}, bf16[256,1024]{1,0:T(8,128)(2,1)}, u32[]{:S(2)}) copy-start(bf16[256,1024]{1,0:T(8,128)(2,1)} %copy-done.14) | copy-start | bytes 1572868
  79.6 1.2 %copy-start.19 = (f32[512,512]{1,0:T(8,128)S(1)}, f32[512,512]{1,0:T(8,128)}, u32[]{:S(2)}) copy-start(f32[512,512]{1,0:T(8,128)} %copy-done.18) | copy-start | bytes 3145732
  80.8 0.9 copy-start.23

commit v3 on v2

--- a/solution.py
+++ b/solution.py
@@ -27,6 +27,7 @@
 SCALE = math.log2(math.e) / math.sqrt(HD)
 F32 = jnp.float32
 BF16 = jnp.bfloat16
+ANY = pl.BlockSpec(memory_space=pl.ANY)
 HBM = pl.BlockSpec(memory_space=pltpu.HBM)
 VMEM = pl.BlockSpec(memory_space=pltpu.VMEM)
 SMEM = pl.BlockSpec(memory_space=pltpu.SMEM)
@@ -38,6 +39,10 @@
 
 def cost(flops, nbytes):
     return pl.CostEstimate(flops=flops, bytes_accessed=nbytes, transcendentals=0)
+
+
+def hbm(array):
+    return pltpu.with_memory_space_constraint(array, pltpu.HBM)
 
 
 def shape(dims, dtype):
@@ -177,143 +182,177 @@
     return copies
 
 
-EARLY = ((0, False), (0, True), (3, False), (3, True), (1, False), (1, True))
+EARLY = ((0, True), (3, False), (3, True), (1, False), (1, True), (0, False))
 LATE = ((2, False), (2, True))
+TILE = 128
 
 
 def early_kernel(*refs):
     count = len(EARLY)
-    x_refs = refs[:count]
-    wq_ref, wkv_ref, q_ref, kv_ref, sq_ref, wq_buf, wkv_buf, sems = refs[count:]
+    sources = (refs[0:1], refs[1:3], refs[3:5], refs[5:7], refs[7:9], None)
+    hidden_ref, wq_ref, wkv_ref = refs[9:12]
+    q_ref, kv_ref, sq_ref, late_q, late_kv, x_buf, wq_buf, wkv_buf, sems, late_sems, x_sem = refs[12:]
+    x_copy = pltpu.make_async_copy(hidden_ref, x_buf, x_sem)
     copies = weight_copies((wq_ref, wkv_ref), (wq_buf, wkv_buf), sems, EARLY)
+    x_copy.start()
+    late = weight_copies((wq_ref, wkv_ref), (late_q, late_kv), late_sems, LATE)
     for i in range(count):
         copies[i][0].wait()
         copies[i][1].wait()
-        rows = x_refs[i][...]
-        q_part = jnp.dot(rows, wq_buf[i], preferred_element_type=F32)
-        kv_part = jnp.dot(rows, wkv_buf[i], preferred_element_type=F32)
-        sq_part = squares_of(rows)
-        if i == 0:
-            q_ref[...] = q_part
-            kv_ref[...] = kv_part
-            sq_ref[...] = sq_part
-        else:
-            q_ref[...] += q_part
-            kv_ref[...] += kv_part
-            sq_ref[...] += sq_part
-
-
-def project_early(blocks, w_query, w_keyval):
-    rows = blocks[0].shape[0]
+        if i == count - 1:
+            x_copy.wait()
+        group = sources[i] or (x_buf,)
+        for r in range(0, ROWS, TILE):
+            height = ROWS // len(group)
+            start = r % height
+            x = group[r // height][start : start + TILE, :]
+            rows = slice(r, r + TILE)
+            q_part = jnp.dot(x, wq_buf[i], preferred_element_type=F32)
+            kv_part = jnp.dot(x, wkv_buf[i], preferred_element_type=F32)
+            sq_part = squares_of(x)
+            if i == 0:
+                q_ref[rows, :] = q_part
+                kv_ref[rows, :] = kv_part
+                sq_ref[rows, :] = sq_part
+            else:
+                q_ref[rows, :] += q_part
+                kv_ref[rows, :] += kv_part
+                sq_ref[rows, :] += sq_part
+    for group in late:
+        for copy in group:
+            copy.wait()
+
+
+def project_early(arrays, hidden, w_query, w_keyval):
     count = len(EARLY)
     return pl.pallas_call(
         early_kernel,
-        out_shape=[shape((rows, QW), F32), shape((rows, KVW), F32), shape((rows, HD), F32)],
-        in_specs=[VMEM] * count + [HBM] * 2,
-        out_specs=[VMEM] * 3,
+        out_shape=[
+            shape((ROWS, QW), F32),
+            shape((ROWS, KVW), F32),
+            shape((ROWS, HD), F32),
+            shape((2, FEAT, QW), BF16),
+            shape((2, FEAT, KVW), BF16),
+        ],
+        in_specs=[VMEM] * len(arrays) + [HBM] * 3,
+        out_specs=[VMEM] * 5,
         scratch_shapes=[
+            pltpu.VMEM((ROWS, FEAT), BF16),
             pltpu.VMEM((count, FEAT, QW), BF16),
             pltpu.VMEM((count, FEAT, KVW), BF16),
             pltpu.SemaphoreType.DMA((2 * count,)),
+            pltpu.SemaphoreType.DMA((4,)),
+            pltpu.SemaphoreType.DMA,
         ],
         compiler_params=params(16),
         cost_estimate=cost(
-            2 * rows * count * FEAT * (QW + KVW), count * FEAT * (QW + KVW + rows) * 2
+            2 * ROWS * count * FEAT * (QW + KVW), count * FEAT * (QW + KVW + ROWS) * 2
         ),
         name="project_early",
-    )(*blocks, w_query, w_keyval)
+    )(*arrays, hbm(hidden), hbm(w_query), hbm(w_keyval))
+
+
+def after_kernel(*refs):
+    pass
+
+
+def after(token, *arrays):
+    count = len(arrays)
+    return pl.pallas_call(
+        after_kernel,
+        out_shape=[shape(x.shape, x.dtype) for x in arrays],
+        in_specs=[ANY] * (count + 1),
+        out_specs=[ANY] * count,
+        input_output_aliases={i + 1: i for i in range(count)},
+        compiler_params=params(1),
+        cost_estimate=cost(0, 1024),
+        name="after",
+    )(token, *arrays)
 
 
 def turn(values, cosine, sine):
     return values * cosine + pltpu.roll(values, HD // 2, 1) * sine
 
 
-def late_dot(x_refs, buffers, index):
-    parts = [
-        jnp.dot(ref[...], buffers[index], preferred_element_type=F32)
-        for ref in x_refs[2 * index : 2 * index + 2]
-    ]
-    return jnp.concatenate(parts, axis=0)
-
-
-def keyval_kernel(table_ref, *refs):
-    x_refs = refs[:4]
-    kv_in, sq_in, cos_ref, sin_ref, wkv_ref = refs[4:9]
-    keys_ref, values_ref, inv_ref, send_ref, wkv_buf, sems = refs[9:]
-    copies = weight_copies((wkv_ref,), (wkv_buf,), sems, LATE)
-    squares = sq_in[...]
-    for i in range(2):
-        halves = [squares_of(ref[...]) for ref in x_refs[2 * i : 2 * i + 2]]
-        squares += jnp.concatenate(halves, axis=0)
-    mean = jnp.sum(squares, axis=1, keepdims=True) / D
-    inv_norm = jnp.broadcast_to(lax.rsqrt(mean + 1e-05), (ROWS, HD))
-    inv_ref[...] = inv_norm
-    kv_sum = kv_in[...]
-    for i in range(2):
-        copies[i][0].wait()
-        kv_sum += late_dot(x_refs, wkv_buf, i)
-    keys = turn(kv_sum[:, :HD] * inv_norm, cos_ref[...], sin_ref[...]).astype(BF16)
-    values = (kv_sum[:, HD:] * inv_norm).astype(BF16)
-    keys_ref[...] = keys
-    values_ref[:, :HD] = values
-    values_ref[:, HD:] = jnp.ones((ROWS, HD), BF16)
+def late_kernel(table_ref, *refs):
+    x_refs = (refs[0:2], refs[2:4])
+    q_in, kv_in, sq_in, late_q, late_kv, cos_ref, sin_ref = refs[4:11]
+    q_ref, keys_ref, values_ref, send_ref = refs[11:]
     row = lax.broadcasted_iota(jnp.int32, (2 * PAGE, 2 * PAGE), 0)
     column = lax.broadcasted_iota(jnp.int32, (2 * PAGE, 2 * PAGE), 1)
     picker = (column == (row >> 1) + (row & 1) * PAGE).astype(BF16)
-    for page in range(NEW_PAGES):
-        rows = slice(page * PAGE, (page + 1) * PAGE)
-        both = jnp.concatenate([keys[rows], values[rows]], axis=0)
-        mixed = jnp.dot(picker, both, preferred_element_type=F32).astype(BF16)
-        send_ref[table_ref[PUSH, page]] = mixed
-
-
-def project_keyval(table, halves, kv_sum, squares, cosine, sine, w_keyval):
-    return pl.pallas_call(
-        keyval_kernel,
+    half = ROWS // 2
+    for r in range(0, ROWS, TILE):
+        rows = slice(r, r + TILE)
+        start = r % half
+        x = [x_refs[i][r // half][start : start + TILE, :] for i in range(2)]
+        squares = sq_in[rows, :] + squares_of(x[0]) + squares_of(x[1])
+        mean = jnp.sum(squares, axis=1, keepdims=True) / D
+        inv_norm = jnp.broadcast_to(lax.rsqrt(mean + 1e-05), (TILE, HD))
+        kv_sum = kv_in[rows, :]
+        q_sum = q_in[rows, :]
+        for i in range(2):
+            kv_sum += jnp.dot(x[i], late_kv[i], preferred_element_type=F32)
+            q_sum += jnp.dot(x[i], late_q[i], preferred_element_type=F32)
+        cosine, sine = cos_ref[rows, :], sin_ref[rows, :]
+        for head in range(HEADS):
+            part = q_sum[:, head * HD : (head + 1) * HD] * inv_norm
+            q_ref[head, rows, :] = turn(part, cosine, sine).astype(BF16)
+        keys = turn(kv_sum[:, :HD] * inv_norm, cosine, sine).astype(BF16)
+        values = (kv_sum[:, HD:] * inv_norm).astype(BF16)
+        keys_ref[rows, :] = keys
+        values_ref[rows, :HD] = values
+        values_ref[rows, HD:] = jnp.ones((TILE, HD), BF16)
+        for p in range(0, TILE, PAGE):
+            both = jnp.concatenate([keys[p : p + PAGE], values[p : p + PAGE]], axis=0)
+            mixed = jnp.dot(picker, both, preferred_element_type=F32).astype(BF16)
+            send_ref[table_ref[PUSH, (r + p) // PAGE]] = mixed
+
+
+def project_late(table, halves, sums, late_weights, cosine, sine):
+    return pl.pallas_call(
+        late_kernel,
         out_shape=[
-            shape((ROWS, HD), BF16),
-            shape((ROWS, 2 * HD), BF16),
-            shape((ROWS, HD), F32),
-            shape((POOL * PUSH_CAP, 2 * PAGE, HD), BF16),
+            pltpu.HBM((HEADS, ROWS, HD), BF16),
+            pltpu.HBM((ROWS, HD), BF16),
+            pltpu.HBM((ROWS, 2 * HD), BF16),
+            pltpu.HBM((POOL * PUSH_CAP, 2 * PAGE, HD), BF16),
         ],
-        in_specs=[SMEM] + [VMEM] * 8 + [HBM],
+        in_specs=[SMEM] + [VMEM] * 11,
         out_specs=[VMEM] * 4,
-        scratch_shapes=[pltpu.VMEM((2, FEAT, KVW), BF16), pltpu.SemaphoreType.DMA((2,))],
         compiler_params=params(12),
-        cost_estimate=cost(2 * ROWS * 2 * FEAT * KVW, 2 * FEAT * (KVW + ROWS) * 2),
-        name="project_keyval",
-    )(table, *halves, kv_sum, squares, cosine, sine, w_keyval)
+        cost_estimate=cost(2 * ROWS * 2 * FEAT * (QW + KVW), 2 * FEAT * (QW + KVW + ROWS) * 2),
+        name="project_late",
+    )(table, *halves, *sums, *late_weights, cosine, sine)
 
 
 def dot_nt(a, b):
     return lax.dot_general(a, b, (((1,), (1,)), ((), ())), preferred_element_type=F32)
 
 
-def attend_kernel(*refs):
-    x_refs = refs[:4]
-    q_in, inv_ref, cos_ref, sin_ref, wq_ref = refs[4:9]
-    keys_ref, values_ref, own_keys_ref, own_values_ref, out_ref, wq_buf, q_buf, sems = refs[9:]
-    copies = weight_copies((wq_ref,), (wq_buf,), sems, LATE)
-    q_sum = q_in[...]
-    for i in range(2):
-        copies[i][0].wait()
-        q_sum += late_dot(x_refs, wq_buf, i)
-    inv_norm = inv_ref[...]
-    for head in range(HEADS):
-        part = q_sum[:, head * HD : (head + 1) * HD] * inv_norm
-        q_buf[head] = turn(part, cos_ref[...], sin_ref[...]).astype(BF16)
-    block = 128
+def attend_kernel(q_ref, own_keys_ref, own_values_ref, keys_ref, values_ref, out_ref, *scratch):
+    q_buf, own_keys, own_values, sems = scratch
+    copies = [
+        pltpu.make_async_copy(source, target, sems.at[i])
+        for i, (source, target) in enumerate(
+            ((q_ref, q_buf), (own_keys_ref, own_keys), (own_values_ref, own_values))
+        )
+    ]
+    for copy in copies:
+        copy.start()
+    for copy in copies:
+        copy.wait()
+    block = 256
     allowed = lax.broadcasted_iota(jnp.int32, (block, block), 0) >= lax.broadcasted_iota(
         jnp.int32, (block, block), 1
     )
-
-    def one_head(head, _):
-        lanes = pl.ds(pl.multiple_of(head * HD, HD), HD)
+    for head in range(HEADS):
+        lanes = slice(head * HD, (head + 1) * HD)
         for b in range(ROWS // block):
             rows = slice(b * block, (b + 1) * block)
             queries = q_buf[head, rows, :]
             scores = dot_nt(queries, keys_ref[...])
-            own = dot_nt(queries, own_keys_ref[: (b + 1) * block, :])
+            own = dot_nt(queries, own_keys[: (b + 1) * block, :])
             last = jnp.where(allowed, own[:, b * block :], -1e30)
             own = last if b == 0 else jnp.concatenate([own[:, : b * block], last], axis=1)
             top = jnp.maximum(
@@ -323,29 +362,27 @@
             own_weights = jnp.exp2((own - top) * SCALE).astype(BF16)
             both = jnp.dot(weights, values_ref[...], preferred_element_type=F32)
             both += jnp.dot(
-                own_weights, own_values_ref[: (b + 1) * block, :], preferred_element_type=F32
+                own_weights, own_values[: (b + 1) * block, :], preferred_element_type=F32
             )
             out_ref[rows, lanes] = (both[:, :HD] / both[:, HD:]).astype(BF16)
-        return 0
-
-    lax.fori_loop(0, HEADS, one_head, 0)
-
-
-def attend(halves, q_sum, inv_norm, cosine, sine, w_query, keys, values, own_keys, own_values):
+
+
+def attend(queries, own_keys, own_values, keys, values):
     return pl.pallas_call(
         attend_kernel,
         out_shape=shape((ROWS, QW), BF16),
-        in_specs=[VMEM] * 8 + [HBM] + [VMEM] * 4,
+        in_specs=[HBM] * 3 + [VMEM] * 2,
         out_specs=VMEM,
         scratch_shapes=[
-            pltpu.VMEM((2, FEAT, QW), BF16),
             pltpu.VMEM((HEADS, ROWS, HD), BF16),
-            pltpu.SemaphoreType.DMA((2,)),
+            pltpu.VMEM((ROWS, HD), BF16),
+            pltpu.VMEM((ROWS, 2 * HD), BF16),
+            pltpu.SemaphoreType.DMA((3,)),
         ],
-        compiler_params=params(28),
-        cost_estimate=cost(2 * ROWS * (4 * 2560 * 512 + 2 * FEAT * QW), 8 * MIB),
+        compiler_params=params(40),
+        cost_estimate=cost(2 * ROWS * 4 * 2560 * 512, 8 * MIB),
         name="attend",
-    )(*halves, q_sum, inv_norm, cosine, sine, w_query, keys, values, own_keys, own_values)
+    )(hbm(queries), hbm(own_keys), hbm(own_values), keys, values)
 
 
 def place_kernel(table_ref, received_ref, out_ref):
@@ -395,22 +432,31 @@
 
 def body(hidden, w_query, w_keyval, store, page_owner, page_slot, new_owner):
     half = ROWS // 2
-    ahead, behind = shift(hidden, 1), shift(hidden, -1)
+    upper, lower = hidden[:half], hidden[half:]
+    ahead_upper, behind_lower = shift(upper, 1), shift(lower, -1)
+    ahead_lower, behind_upper = shift(lower, 1), shift(upper, -1)
+    sibling = swap(hidden)
     table = make_table(page_owner, page_slot, new_owner)
     pages = exchange(gather_pages(table, store.reshape(64, 2 * PAGE, HD)))
     cosine, sine = rope_tables(ROWS, PAGES * PAGE)
-    top, bottom = shift(ahead[:half], 1), shift(behind[half:], -1)
-    blocks = (hidden, swap(hidden), ahead, swap(ahead), behind, swap(behind))
-    q_sum, kv_sum, squares = project_early(blocks, w_query, w_keyval)
-    keys, values = split_pages(table, pages)
-    halves = (top, bottom, swap(top), swap(bottom))
-    own_keys, own_values, inv_norm, send = project_keyval(
-        table, halves, kv_sum, squares, cosine, sine, w_keyval
+    far = (shift(ahead_upper, 1), shift(behind_lower, -1))
+    ahead, behind = (ahead_upper, ahead_lower), (behind_upper, behind_lower)
+    arrays = (
+        sibling,
+        *ahead,
+        *[swap(x) for x in ahead],
+        *behind,
+        *[swap(x) for x in behind],
+    )
+    early = project_early(arrays, hidden, w_query, w_keyval)
+    far = after(early[2], *far)
+    halves = (*far, *[swap(x) for x in far])
+    queries, own_keys, own_values, send = project_late(
+        table, halves, early[:3], early[3:], cosine, sine
     )
     received = exchange(send)
-    attended = attend(
-        halves, q_sum, inv_norm, cosine, sine, w_query, keys, values, own_keys, own_values
-    )
+    keys, values = split_pages(table, pages)
+    attended = attend(queries, own_keys, own_values, keys, values)
     placed = place_pages(table, received)
     return attended, placed.reshape(SLOTS, 1, PAGE, 2, HD)
 

time: 97.4 us -> 84.2 us (0.86); the launches traced: 95.5 us -> 83.9 us
  local copies, waits for them, and re-layouts: 21.3 us -> 2.47 us
  waiting for transfers between devices: 20.2 us -> 24.6 us
  starting transfers between devices: 22.3 us -> 25.5 us
    unnamed x49 -> x9, local copies, waits for them, and re-layouts: 20.2 us -> 0.09 us
    all_to_all x2, waiting for transfers between devices: 0.01 us -> 7.22 us  [exchange(): lax.all_to_all(values, 'pool', split_axis=0, concat_axis=0, tiled=True)]
    ppermute x4 -> x6, waiting for transfers between devices: 20.2 us -> 16.5 us  [shift(): return lax.ppermute(values, 'tp', pairs)]
    ppermute x4 -> x6, starting transfers between devices: 7.65 us -> 9.81 us  [shift(): return lax.ppermute(values, 'tp', pairs)]
    pallas_call x1, Pallas kernels: 11.3 us -> 9.35 us  [attend(): pl.pallas_call(attend_kernel, out_shape=shape((ROWS, QW), BF16), in_specs...]
    pallas_call x2 -> x3, Pallas kernels: 11.8 us -> 13.6 us  [the longest x1 8.66 us: project_early(): pl.pallas_call(early_kernel, out_shape=[shape((ROWS, QW), F32), shape((RO...]
    slice x2 -> x1, local copies, waits for them, and re-layouts: 1.11 us -> 2.39 us  [body(): upper, lower = (hidden[:half], hidden[half:])]
    ppermute x5 -> x7, starting transfers between devices: 0.6 us -> 1.61 us  [swap(): return lax.ppermute(values, 'tp', [(i, i ^ 1) for i in range(8)])]
  transfers between devices with their start and end apart: 11 -> 15, of which waited for: 3 -> 6; matrix products, arithmetic and copies ran while one was open for 3% -> 2% of each run, Pallas kernels for 28% -> 32%
where the time goes in v3:
time: 84.2 us; the launch traced here: 83.9 us
  Pallas kernels  29.4 us (35%)
  starting transfers between devices  25.5 us (30%)
  waiting for transfers between devices  24.6 us (29%)
  local copies, waits for them, and re-layouts  2.47 us (3%)
  other arithmetic  1.22 us (1%)
    ppermute x6, waiting for transfers between devices, shift(): return lax.ppermute(values, 'tp', pairs)  16.5 us
    all_to_all x2, starting transfers between devices, exchange(): lax.all_to_all(values, 'pool', split_axis=0, concat_axis=0, tiled=True)  14.1 us
    ppermute x6, starting transfers between devices, shift(): return lax.ppermute(values, 'tp', pairs)  9.81 us
    pallas_call x1, Pallas kernels, attend(): pl.pallas_call(attend_kernel, out_shape=shape((ROWS, QW), BF16), in_specs...  9.35 us
    pallas_call x1, Pallas kernels, project_early(): pl.pallas_call(early_kernel, out_shape=[shape((ROWS, QW), F32), shape((RO...  8.66 us
    all_to_all x2, waiting for transfers between devices, exchange(): lax.all_to_all(values, 'pool', split_axis=0, concat_axis=0, tiled=True)  7.22 us
    pallas_call x1, Pallas kernels, project_late(): pl.pallas_call(late_kernel, out_shape=[pltpu.HBM((HEADS, ROWS, HD), BF16)...  4.91 us
    pallas_call x1, Pallas kernels, place_pages(): pl.pallas_call(place_kernel, grid=(SLOTS // height,), out_shape=shape((SL...  2.42 us
  transfers between devices with their start and end apart: 15, of which 6 were waited for; matrix products, arithmetic and copies ran while one was open for 2% of the time, Pallas kernels for 32%

profile of v3, /device:TPU:0, one launch (start us, length us, event | category | flops | bytes accessed | tf_op | source)
XLA Modules:
  0.0 83.9 jit_solution(18325124552936970930)
XLA Ops:
  0.6 0.0 copy-start.3
  0.6 0.0 copy-start.1
  0.7 0.0 copy-start.2
  0.7 0.0 copy-start
  0.7 2.4 %fusion.1 = (bf16[256,1024]{1,0:T(8,128)(2,1)}, bf16[256,1024]{1,0:T(8,128)(2,1)}) fusion(bf16[512,1024]{1,0:T(8,128)(2,1)} %refs_9_.1), kind=kLoop, calls=%fused_computation.7 | loop fusion | bytes 2097152 | tf_op jit(solution)/shard_map/slice | solution.py:435
  3.1 2.0 %collective-permute-start.1 = (bf16[256,1024]{1,0:T(8,128)(2,1)}, bf16[256,1024]{1,0:T(8,128)(2,1)}, u32[]{:S(2)}, u32[]{:S(2)}) collective-permute-start(bf16[256,1024]{1,0:T(8,128)(2,1)} %get-tuple-element.31), channel_id=1, source_target_pairs={{0,2},{1,3},{2,4},{3,5},{4,6},{5,7},{6,0},{7,1},{8,10},{9,11},{10,... | collective-permute-start | bytes 1572872 | tf_op jit(solution)/shard_map/ppermute | solution.py:413
  5.1 2.1 %collective-permute-start.6 = (bf16[256,1024]{1,0:T(8,128)(2,1)}, bf16[256,1024]{1,0:T(8,128)(2,1)}, u32[]{:S(2)}, u32[]{:S(2)}) collective-permute-start(bf16[256,1024]{1,0:T(8,128)(2,1)} %get-tuple-element.30), channel_id=1, source_target_pairs={{0,6},{1,7},{2,0},{3,1},{4,2},{5,3},{6,4},{7,5},{8,14},{9,15},{10,... | collective-permute-start | bytes 1572872 | tf_op jit(solution)/shard_map/ppermute | solution.py:413
  7.2 0.0 collective-permute-start.2
  7.2 3.2 %collective-permute-start.5 = (bf16[256,1024]{1,0:T(8,128)(2,1)}, bf16[256,1024]{1,0:T(8,128)(2,1)}, u32[]{:S(2)}, u32[]{:S(2)}) collective-permute-start(bf16[256,1024]{1,0:T(8,128)(2,1)} %get-tuple-element.31), channel_id=1, source_target_pairs={{0,6},{1,7},{2,0},{3,1},{4,2},{5,3},{6,4},{7,5},{8,14},{9,15},{10,... | collective-permute-start | bytes 1572872 | tf_op jit(solution)/shard_map/ppermute | solution.py:413
  10.4 0.0 collective-permute-start
  10.4 0.0 copy-done.3
  10.4 0.1 copy.11.new_owner_ref
  10.5 0.0 copy-done.1
  10.5 0.5 make_table.1.table_ref
  11.0 0.0 copy-done
  11.0 2.3 %gather_pages.1 = bf16[64,128,128]{2,1,0:T(8,128)(2,1)} custom-call(s32[24,128]{1,0:T(8,128)S(1)} %make_table.1.table_ref, bf16[64,128,128]{2,1,0:T(8,128)(2,1)S(1)} %bitcast.4), custom_call_target="tpu_custom_call" | custom-call | bytes 4194304 | tf_op jit(solution)/shard_map/gather_pages/pallas_call | solution.py:114
  13.3 7.0 %all-to-all-start = ((bf16[64,128,128]{2,1,0:T(8,128)(2,1)}), bf16[64,128,128]{2,1,0:T(8,128)(2,1)S(1)}, u32[]{:S(2)}, u32[]{:S(2)}) async-start(bf16[64,128,128]{2,1,0:T(8,128)(2,1)} %gather_pages.1), calls=%async_computation | async-start | bytes 4194304 | tf_op jit(solution)/shard_map/all_to_all | solution.py:430
  20.4 0.0 collective-permute-done.1.refs_1_
  20.4 0.3 collective-permute-start.3
  20.7 0.0 collective-permute-done.6.refs_6_
  20.7 0.3 collective-permute-start.8
  21.0 9.7 %collective-permute-done.2.refs_2_ = bf16[256,1024]{1,0:T(8,128)(2,1)} collective-permute-done((bf16[256,1024]{1,0:T(8,128)(2,1)}, bf16[256,1024]{1,0:T(8,128)(2,1)}, u32[]{:S(2)}, u32[]{:S(2)}) %collective-permute-start.2) | collective-permute-done | bytes 524320 | tf_op jit(solution)/shard_map/ppermute | solution.py:413
  30.6 0.0 collective-permute-start.4
  30.7 0.0 collective-permute-done.5.refs_5_
  30.7 0.5 collective-permute-start.7
  31.2 0.0 collective-permute-done.3.refs_3_
  31.2 2.4 %collective-permute-start.10 = (bf16[256,1024]{1,0:T(8,128)(2,1)}, bf16[256,1024]{1,0:T(8,128)(2,1)S(1)}, u32[]{:S(2)}, u32[]{:S(2)}) collective-permute-start(bf16[256,1024]{1,0:T(8,128)(2,1)} %collective-permute-done.6.refs_6_), channel_id=1, source_target_pairs={{0,6},{1,7},{2,0},{3,1},{4,2},{5,3},{6,4},{7,5},{8,14},{9,15},{10,... | collective-permute-start | bytes 1572872 | tf_op jit(solution)/shard_map/ppermute | solution.py:413
  33.6 0.0 collective-permute-done.8.refs_8_
  33.6 0.0 collective-permute-start.9
  33.6 0.0 collective-permute-done.4.refs_4_
  33.6 0.0 collective-permute-done.7.refs_7_
  33.6 0.0 collective-permute-done.refs_0_
  33.6 8.7 %project_early.1 = (f32[512,512]{1,0:T(8,128)S(1)}, f32[512,256]{1,0:T(8,128)S(1)}, f32[512,128]{1,0:T(8,128)S(1)}, bf16[2,1024,512]{2,1,0:T(8,128)(2,1)S(1)}, bf16[2,1024,256]{2,1,0:T(8,128)(2,1)S(1)}) custom-call(bf16[512,1024]{1,0:T(8,128)(2,1)S(1)} %collective-permute-done.refs_0_, bf16[256,1024]{1,0:T(8,128)(2,1)} %collective-permute-done.1.refs_1_, ...), custom_call_target="tpu_custom_call" | custom-call | flops 4831838208 | bytes 15728640 | tf_op jit(solution)/shard_map/project_early/pallas_call | solution.py:228
  42.3 3.5 %collective-permute-done.10.refs_2_ = bf16[256,1024]{1,0:T(8,128)(2,1)S(1)} collective-permute-done((bf16[256,1024]{1,0:T(8,128)(2,1)}, bf16[256,1024]{1,0:T(8,128)(2,1)S(1)}, u32[]{:S(2)}, u32[]{:S(2)}) %collective-permute-start.10) | collective-permute-done | bytes 524320 | tf_op jit(solution)/shard_map/ppermute | solution.py:413
  45.8 3.3 %collective-permute-done.9.refs_1_ = bf16[256,1024]{1,0:T(8,128)(2,1)S(1)} collective-permute-done((bf16[256,1024]{1,0:T(8,128)(2,1)}, bf16[256,1024]{1,0:T(8,128)(2,1)S(1)}, u32[]{:S(2)}, u32[]{:S(2)}) %collective-permute-start.9) | collective-permute-done | bytes 524320 | tf_op jit(solution)/shard_map/ppermute | solution.py:413
  49.1 0.0 collective-permute-start.11
  49.1 0.5 collective-permute-start.12
  49.6 1.0 %fusion = (f32[512,64]{1,0:T(8,128)S(1)}, f32[512,64]{1,0:T(8,128)S(1)}, f32[512,64]{1,0:T(8,128)S(1)}) fusion(f32[64]{0:T(128)S(1)} %negate_power_fusion, f32[512]{0:T(512)S(1)} %add_convert_fusion), kind=kLoop, calls=%fused_computation.4 | loop fusion | flops 65536 | bytes 395520 | tf_op jit(solution)/shard_map/neg | solution.py:426
  50.6 0.2 pad_maximum_fusion
  50.8 0.2 collective-permute-done.11.refs_2_
  51.0 0.7 collective-permute-done.12.refs_3_
  51.8 4.9 %project_late.1 = (bf16[4,512,128]{2,1,0:T(8,128)(2,1)}, bf16[512,128]{1,0:T(8,128)(2,1)}, bf16[512,256]{1,0:T(8,128)(2,1)}, bf16[32,128,128]{2,1,0:T(8,128)(2,1)}) custom-call(s32[24,128]{1,0:T(8,128)S(1)} %make_table.1.table_ref, bf16[256,1024]{1,0:T(8,128)(2,1)S(1)} %get-tuple-element.16.refs_0_, bf16[256,1024]{1,0:T(8,128)(2,1)S(1)} %get-tuple-element.17.refs_1_, ...), custom_call_target="tpu_custom_call" | custom-call | flops 1610612736 | bytes 5242880 | tf_op jit(solution)/shard_map/project_late/pallas_call | solution.py:313
  56.7 0.0 all-to-all-done.pages_ref
  56.7 7.0 %all-to-all-start.1 = ((bf16[32,128,128]{2,1,0:T(8,128)(2,1)}), bf16[32,128,128]{2,1,0:T(8,128)(2,1)S(1)}, u32[]{:S(2)}, u32[]{:S(2)}) async-start(bf16[32,128,128]{2,1,0:T(8,128)(2,1)} %get-tuple-element.27), calls=%async_computation.1 | async-start | bytes 2097152 | tf_op jit(solution)/shard_map/all_to_all | solution.py:430
  63.7 1.2 %split_pages.1 = (bf16[2048,128]{1,0:T(8,128)(2,1)S(1)}, bf16[2048,256]{1,0:T(8,128)(2,1)S(1)}) custom-call(s32[24,128]{1,0:T(8,128)S(1)} %make_table.1.table_ref, bf16[64,128,128]{2,1,0:T(8,128)(2,1)S(1)} %all-to-all-done.pages_ref), custom_call_target="tpu_custom_call" | custom-call | flops 134217728 | bytes 4194304 | tf_op jit(solution)/shard_map/split_pages/pallas_call | solution.py:139
  64.9 9.3 %attend.1 = bf16[512,512]{1,0:T(8,128)(2,1)} custom-call(bf16[4,512,128]{2,1,0:T(8,128)(2,1)} %get-tuple-element.22.q_ref, bf16[512,128]{1,0:T(8,128)(2,1)} %get-tuple-element.23.own_keys_ref, bf16[512,256]{1,0:T(8,128)(2,1)} %get-tuple-element.24.own_values_ref, bf16[2048,128]{1,0:T(8,128)(2,1)S(1)} %get-tuple-element.25.keys_ref, ...), custom_call_target="tpu_custom_call" | custom-call | flops 5368709120 | bytes 8388608 | tf_op jit(solution)/shard_map/attend/pallas_call | solution.py:371
  74.3 7.2 %all-to-all-done.1.received_ref = bf16[32,128,128]{2,1,0:T(8,128)(2,1)S(1)} async-done(((bf16[32,128,128]{2,1,0:T(8,128)(2,1)}), bf16[32,128,128]{2,1,0:T(8,128)(2,1)S(1)}, u32[]{:S(2)}, u32[]{:S(2)}) %all-to-all-start.1) | async-done | bytes 1048608 | tf_op jit(solution)/shard_map/all_to_all | solution.py:430
  81.5 2.4 %place_pages.1 = bf16[32,128,128]{2,1,0:T(8,128)(2,1)} custom-call(s32[24,128]{1,0:T(8,128)S(1)} %make_table.1.table_ref, bf16[32,128,128]{2,1,0:T(8,128)(2,1)S(1)} %all-to-all-done.1.received_ref), custom_call_target="tpu_custom_call" | custom-call | bytes 2097152 | tf_op jit(solution)/shard_map/place_pages/pallas_call | solution.py:399
  (4 shorter events, 0.0 us)
Async XLA Ops:
  0.6 9.8 %copy-start.3 = (s32[16,8]{0,1:T(8,128)S(1)}, s32[16,8]{0,1:T(8,128)}, u32[]{:S(2)}) copy-start(s32[16,8]{0,1:T(8,128)} %param.13) | copy-start | bytes 1540
  0.6 9.9 %copy-start.1 = (s32[16,32]{1,0:T(8,128)S(1)}, s32[16,32]{1,0:T(8,128)}, u32[]{:S(2)}) copy-start(s32[16,32]{1,0:T(8,128)} %page_owner_ref.1) | copy-start | bytes 6148
  0.7 9.9 %copy-start.2 = (s32[16,32]{1,0:T(8,128)S(1)}, s32[16,32]{1,0:T(8,128)}, u32[]{:S(2)}) copy-start(s32[16,32]{1,0:T(8,128)} %page_slot_ref.1) | copy-start | bytes 6148
  0.7 10.3 %copy-start = (bf16[64,1,64,2,128]{4,3,2,1,0:T(2,128)(2,1)S(1)}, bf16[64,1,64,2,128]{4,3,2,1,0:T(2,128)(2,1)}, u32[]{:S(2)}) copy-start(bf16[64,1,64,2,128]{4,3,2,1,0:T(2,128)(2,1)} %param.10) | copy-start | bytes 6291460
  3.1 17.3 %collective-permute-start.1 = (bf16[256,1024]{1,0:T(8,128)(2,1)}, bf16[256,1024]{1,0:T(8,128)(2,1)}, u32[]{:S(2)}, u32[]{:S(2)}) collective-permute-start(bf16[256,1024]{1,0:T(8,128)(2,1)} %get-tuple-element.31), channel_id=1, source_target_pairs={{0,2},{1,3},{2,4},{3,5},{4,6},{5,7},{6,0},{7,1},{8,10},{9,11},{10,... | collective-permute-start | bytes 1572872 | tf_op jit(solution)/shard_map/ppermute | solution.py:413
  5.1 15.6 %collective-permute-start.6 = (bf16[256,1024]{1,0:T(8,128)(2,1)}, bf16[256,1024]{1,0:T(8,128)(2,1)}, u32[]{:S(2)}, u32[]{:S(2)}) collective-permute-start(bf16[256,1024]{1,0:T(8,128)(2,1)} %get-tuple-element.30), channel_id=1, source_target_pairs={{0,6},{1,7},{2,0},{3,1},{4,2},{5,3},{6,4},{7,5},{8,14},{9,15},{10,... | collective-permute-start | bytes 1572872 | tf_op jit(solution)/shard_map/ppermute | solution.py:413
  7.2 23.5 %collective-permute-start.2 = (bf16[256,1024]{1,0:T(8,128)(2,1)}, bf16[256,1024]{1,0:T(8,128)(2,1)}, u32[]{:S(2)}, u32[]{:S(2)}) collective-permute-start(bf16[256,1024]{1,0:T(8,128)(2,1)} %get-tuple-element.30), channel_id=1, source_target_pairs={{0,2},{1,3},{2,4},{3,5},{4,6},{5,7},{6,0},{7,1},{8,10},{9,11},{10,... | collective-permute-start | bytes 1572872 | tf_op jit(solution)/shard_map/ppermute | solution.py:413
  7.2 23.5 %collective-permute-start.5 = (bf16[256,1024]{1,0:T(8,128)(2,1)}, bf16[256,1024]{1,0:T(8,128)(2,1)}, u32[]{:S(2)}, u32[]{:S(2)}) collective-permute-start(bf16[256,1024]{1,0:T(8,128)(2,1)} %get-tuple-element.31), channel_id=1, source_target_pairs={{0,6},{1,7},{2,0},{3,1},{4,2},{5,3},{6,4},{7,5},{8,14},{9,15},{10,... | collective-permute-start | bytes 1572872 | tf_op jit(solution)/shard_map/ppermute | solution.py:413
  10.4 23.2 %collective-permute-start = (bf16[512,1024]{1,0:T(8,128)(2,1)}, bf16[512,1024]{1,0:T(8,128)(2,1)S(1)}, u32[]{:S(2)}, u32[]{:S(2)}) collective-permute-start(bf16[512,1024]{1,0:T(8,128)(2,1)} %refs_9_.1), channel_id=1, source_target_pairs={{0,1},{1,0},{2,3},{3,2},{4,5},{5,4},{6,7},{7,6},{8,9},{9,8},{10,11... | collective-permute-start | bytes 3145736 | tf_op jit(solution)/shard_map/ppermute | solution.py:417
  13.3 43.4 %all-to-all-start = ((bf16[64,128,128]{2,1,0:T(8,128)(2,1)}), bf16[64,128,128]{2,1,0:T(8,128)(2,1)S(1)}, u32[]{:S(2)}, u32[]{:S(2)}) async-start(bf16[64,128,128]{2,1,0:T(8,128)(2,1)} %gather_pages.1), calls=%async_computation | async-start | bytes 4194304 | tf_op jit(solution)/shard_map/all_to_all | solution.py:430
  20.4 10.8 %collective-permute-start.3 = (bf16[256,1024]{1,0:T(8,128)(2,1)}, bf16[256,1024]{1,0:T(8,128)(2,1)S(1)}, u32[]{:S(2)}, u32[]{:S(2)}) collective-permute-start(bf16[256,1024]{1,0:T(8,128)(2,1)} %collective-permute-done.1.refs_1_), channel_id=1, source_target_pairs={{0,1},{1,0},{2,3},{3,2},{4,5},{5,4},{6,7},{7,6},{8,9},{9,8},{10,11... | collective-permute-start | bytes 1572872 | tf_op jit(solution)/shard_map/ppermute | solution.py:417
  20.7 12.9 %collective-permute-start.8 = (bf16[256,1024]{1,0:T(8,128)(2,1)}, bf16[256,1024]{1,0:T(8,128)(2,1)S(1)}, u32[]{:S(2)}, u32[]{:S(2)}) collective-permute-start(bf16[256,1024]{1,0:T(8,128)(2,1)} %collective-permute-done.6.refs_6_), channel_id=1, source_target_pairs={{0,1},{1,0},{2,3},{3,2},{4,5},{5,4},{6,7},{7,6},{8,9},{9,8},{10,11... | collective-permute-start | bytes 1572872 | tf_op jit(solution)/shard_map/ppermute | solution.py:417
  30.6 3.0 %collective-permute-start.4 = (bf16[256,1024]{1,0:T(8,128)(2,1)}, bf16[256,1024]{1,0:T(8,128)(2,1)S(1)}, u32[]{:S(2)}, u32[]{:S(2)}) collective-permute-start(bf16[256,1024]{1,0:T(8,128)(2,1)} %collective-permute-done.2.refs_2_), channel_id=1, source_target_pairs={{0,1},{1,0},{2,3},{3,2},{4,5},{5,4},{6,7},{7,6},{8,9},{9,8},{10,11... | collective-permute-start | bytes 1572872 | tf_op jit(solution)/shard_map/ppermute | solution.py:417
  30.7 3.0 %collective-permute-start.7 = (bf16[256,1024]{1,0:T(8,128)(2,1)}, bf16[256,1024]{1,0:T(8,128)(2,1)S(1)}, u32[]{:S(2)}, u32[]{:S(2)}) collective-permute-start(bf16[256,1024]{1,0:T(8,128)(2,1)} %collective-permute-done.5.refs_5_), channel_id=1, source_target_pairs={{0,1},{1,0},{2,3},{3,2},{4,5},{5,4},{6,7},{7,6},{8,9},{9,8},{10,11... | collective-permute-start | bytes 1572872 | tf_op jit(solution)/shard_map/ppermute | solution.py:417
  31.2 14.6 %collective-permute-start.10 = (bf16[256,1024]{1,0:T(8,128)(2,1)}, bf16[256,1024]{1,0:T(8,128)(2,1)S(1)}, u32[]{:S(2)}, u32[]{:S(2)}) collective-permute-start(bf16[256,1024]{1,0:T(8,128)(2,1)} %collective-permute-done.6.refs_6_), channel_id=1, source_target_pairs={{0,6},{1,7},{2,0},{3,1},{4,2},{5,3},{6,4},{7,5},{8,14},{9,15},{10,... | collective-permute-start | bytes 1572872 | tf_op jit(solution)/shard_map/ppermute | solution.py:413
  33.6 15.5 %collective-permute-start.9 = (bf16[256,1024]{1,0:T(8,128)(2,1)}, bf16[256,1024]{1,0:T(8,128)(2,1)S(1)}, u32[]{:S(2)}, u32[]{:S(2)}) collective-permute-start(bf16[256,1024]{1,0:T(8,128)(2,1)} %collective-permute-done.1.refs_1_), channel_id=1, source_target_pairs={{0,2},{1,3},{2,4},{3,5},{4,6},{5,7},{6,0},{7,1},{8,10},{9,11},{10,... | collective-permute-start | bytes 1572872 | tf_op jit(solution)/shard_map/ppermute | solution.py:413
  49.1 1.9 %collective-permute-start.11 = (bf16[256,1024]{1,0:T(8,128)(2,1)S(1)}, bf16[256,1024]{1,0:T(8,128)(2,1)S(1)}, u32[]{:S(2)}, u32[]{:S(2)}) collective-permute-start(bf16[256,1024]{1,0:T(8,128)(2,1)S(1)} %get-tuple-element.16.refs_0_), channel_id=1, source_target_pairs={{0,1},{1,0},{2,3},{3,2},{4,5},{5,4},{6,7},{7,6},{8,9},{9,8},{10,11... | collective-permute-start | bytes 1572872 | tf_op jit(solution)/shard_map/ppermute | solution.py:417
  49.1 2.7 %collective-permute-start.12 = (bf16[256,1024]{1,0:T(8,128)(2,1)S(1)}, bf16[256,1024]{1,0:T(8,128)(2,1)S(1)}, u32[]{:S(2)}, u32[]{:S(2)}) collective-permute-start(bf16[256,1024]{1,0:T(8,128)(2,1)S(1)} %get-tuple-element.17.refs_1_), channel_id=1, source_target_pairs={{0,1},{1,0},{2,3},{3,2},{4,5},{5,4},{6,7},{7,6},{8,9},{9,8},{10,11... | collective-permute-start | bytes 1572872 | tf_op jit(solution)/shard_map/ppermute | solution.py:417
  56.7 24.8 %all-to-all-start.1 = ((bf16[32,128,128]{2,1,0:T(8,128)(2,1)}), bf16[32,128,128]{2,1,0:T(8,128)(2,1)S(1)}, u32[]{:S(2)}, u32[]{:S(2)}) async-start(bf16[32,128,128]{2,1,0:T(8,128)(2,1)} %get-tuple-element.27), calls=%async_computation.1 | async-start | bytes 2097152 | tf_op jit(solution)/shard_map/all_to_all | solution.py:430

commit v4 on v3

--- a/solution.py
+++ b/solution.py
@@ -150,11 +150,13 @@
     )(table, pages)
 
 
-def block_index(z_step, other_core):
+def block_index(steps, other_core):
     index = lax.axis_index("tp")
-    z = lax.rem(index // 2 + z_step, 4)
     core = lax.rem(index, 2)
-    return 2 * z + (1 - core if other_core else core)
+    if other_core:
+        core = 1 - core
+    z = lax.rem(index // 2 + jnp.where(core == 0, steps[0], steps[1]), 4)
+    return 2 * z + core
 
 
 def squares_of(rows):
@@ -168,8 +170,8 @@
 
 def weight_copies(refs, buffers, sems, blocks):
     copies = []
-    for i, (z_step, other) in enumerate(blocks):
-        rows = pl.ds(pl.multiple_of(block_index(z_step, other) * FEAT, FEAT), FEAT)
+    for i, (steps, other) in enumerate(blocks):
+        rows = pl.ds(pl.multiple_of(block_index(steps, other) * FEAT, FEAT), FEAT)
         copies.append(
             [
                 pltpu.make_async_copy(ref.at[rows, :], buffer.at[i], sems.at[len(refs) * i + j])
@@ -182,16 +184,17 @@
     return copies
 
 
-EARLY = ((0, True), (3, False), (3, True), (1, False), (1, True), (0, False))
-LATE = ((2, False), (2, True))
+OWN, NEAR, BACK, FAR = (0, 0), (3, 1), (1, 3), (2, 2)
+EARLY = ((OWN, True), (NEAR, False), (NEAR, True), (BACK, False), (BACK, True), (OWN, False))
+LATE = ((FAR, False), (FAR, True))
 TILE = 128
 
 
 def early_kernel(*refs):
     count = len(EARLY)
-    sources = (refs[0:1], refs[1:3], refs[3:5], refs[5:7], refs[7:9], None)
-    hidden_ref, wq_ref, wkv_ref = refs[9:12]
-    q_ref, kv_ref, sq_ref, late_q, late_kv, x_buf, wq_buf, wkv_buf, sems, late_sems, x_sem = refs[12:]
+    hidden_ref, wq_ref, wkv_ref = refs[5:8]
+    q_ref, kv_ref, sq_ref, late_q, late_kv, x_buf, wq_buf, wkv_buf, sems, late_sems, x_sem = refs[8:]
+    sources = (*refs[:5], x_buf)
     x_copy = pltpu.make_async_copy(hidden_ref, x_buf, x_sem)
     copies = weight_copies((wq_ref, wkv_ref), (wq_buf, wkv_buf), sems, EARLY)
     x_copy.start()
@@ -201,12 +204,9 @@
         copies[i][1].wait()
         if i == count - 1:
             x_copy.wait()
-        group = sources[i] or (x_buf,)
         for r in range(0, ROWS, TILE):
-            height = ROWS // len(group)
-            start = r % height
-            x = group[r // height][start : start + TILE, :]
             rows = slice(r, r + TILE)
+            x = sources[i][rows, :]
             q_part = jnp.dot(x, wq_buf[i], preferred_element_type=F32)
             kv_part = jnp.dot(x, wkv_buf[i], preferred_element_type=F32)
             sq_part = squares_of(x)
@@ -245,9 +245,7 @@
             pltpu.SemaphoreType.DMA,
         ],
         compiler_params=params(16),
-        cost_estimate=cost(
-            2 * ROWS * count * FEAT * (QW + KVW), count * FEAT * (QW + KVW + ROWS) * 2
-        ),
+        cost_estimate=cost(0, 1),
         name="project_early",
     )(*arrays, hbm(hidden), hbm(w_query), hbm(w_keyval))
 
@@ -256,18 +254,18 @@
     pass
 
 
-def after(token, *arrays):
-    count = len(arrays)
+def after(tokens, *arrays):
+    count, skip = len(arrays), len(tokens)
     return pl.pallas_call(
         after_kernel,
         out_shape=[shape(x.shape, x.dtype) for x in arrays],
-        in_specs=[ANY] * (count + 1),
+        in_specs=[ANY] * (count + skip),
         out_specs=[ANY] * count,
-        input_output_aliases={i + 1: i for i in range(count)},
+        input_output_aliases={i + skip: i for i in range(count)},
         compiler_params=params(1),
         cost_estimate=cost(0, 1024),
         name="after",
-    )(token, *arrays)
+    )(*tokens, *arrays)
 
 
 def turn(values, cosine, sine):
@@ -275,17 +273,15 @@
 
 
 def late_kernel(table_ref, *refs):
-    x_refs = (refs[0:2], refs[2:4])
-    q_in, kv_in, sq_in, late_q, late_kv, cos_ref, sin_ref = refs[4:11]
-    q_ref, keys_ref, values_ref, send_ref = refs[11:]
+    x_refs = refs[:2]
+    q_in, kv_in, sq_in, late_q, late_kv, cos_ref, sin_ref = refs[2:9]
+    q_ref, keys_ref, values_ref, send_ref = refs[9:]
     row = lax.broadcasted_iota(jnp.int32, (2 * PAGE, 2 * PAGE), 0)
     column = lax.broadcasted_iota(jnp.int32, (2 * PAGE, 2 * PAGE), 1)
     picker = (column == (row >> 1) + (row & 1) * PAGE).astype(BF16)
-    half = ROWS // 2
     for r in range(0, ROWS, TILE):
         rows = slice(r, r + TILE)
-        start = r % half
-        x = [x_refs[i][r // half][start : start + TILE, :] for i in range(2)]
+        x = [ref[rows, :] for ref in x_refs]
         squares = sq_in[rows, :] + squares_of(x[0]) + squares_of(x[1])
         mean = jnp.sum(squares, axis=1, keepdims=True) / D
         inv_norm = jnp.broadcast_to(lax.rsqrt(mean + 1e-05), (TILE, HD))
@@ -309,7 +305,7 @@
             send_ref[table_ref[PUSH, (r + p) // PAGE]] = mixed
 
 
-def project_late(table, halves, sums, late_weights, cosine, sine):
+def project_late(table, blocks, sums, late_weights, cosine, sine):
     return pl.pallas_call(
         late_kernel,
         out_shape=[
@@ -318,12 +314,12 @@
             pltpu.HBM((ROWS, 2 * HD), BF16),
             pltpu.HBM((POOL * PUSH_CAP, 2 * PAGE, HD), BF16),
         ],
-        in_specs=[SMEM] + [VMEM] * 11,
+        in_specs=[SMEM] + [VMEM] * 9,
         out_specs=[VMEM] * 4,
         compiler_params=params(12),
-        cost_estimate=cost(2 * ROWS * 2 * FEAT * (QW + KVW), 2 * FEAT * (QW + KVW + ROWS) * 2),
+        cost_estimate=cost(0, 1),
         name="project_late",
-    )(table, *halves, *sums, *late_weights, cosine, sine)
+    )(table, *blocks, *sums, *late_weights, cosine, sine)
 
 
 def dot_nt(a, b):
@@ -351,19 +347,18 @@
         for b in range(ROWS // block):
             rows = slice(b * block, (b + 1) * block)
             queries = q_buf[head, rows, :]
-            scores = dot_nt(queries, keys_ref[...])
             own = dot_nt(queries, own_keys[: (b + 1) * block, :])
-            last = jnp.where(allowed, own[:, b * block :], -1e30)
-            own = last if b == 0 else jnp.concatenate([own[:, : b * block], last], axis=1)
-            top = jnp.maximum(
-                jnp.max(scores, axis=1, keepdims=True), jnp.max(own, axis=1, keepdims=True)
-            )
-            weights = jnp.exp2((scores - top) * SCALE).astype(BF16)
-            own_weights = jnp.exp2((own - top) * SCALE).astype(BF16)
-            both = jnp.dot(weights, values_ref[...], preferred_element_type=F32)
-            both += jnp.dot(
-                own_weights, own_values[: (b + 1) * block, :], preferred_element_type=F32
-            )
+            diagonal = jnp.where(allowed, own[:, b * block :], -1e30)
+            parts = [(diagonal, own_values[rows, :])]
+            if b:
+                parts.append((own[:, : b * block], own_values[: b * block, :]))
+            parts.append((dot_nt(queries, keys_ref[...]), values_ref[...]))
+            tops = [jnp.max(scores, axis=1, keepdims=True) for scores, _ in parts]
+            top = functools.reduce(jnp.maximum, tops)
+            both = jnp.zeros((block, 2 * HD), F32)
+            for scores, held in parts:
+                weights = jnp.exp2((scores - top) * SCALE).astype(BF16)
+                both += jnp.dot(weights, held, preferred_element_type=F32)
             out_ref[rows, lanes] = (both[:, :HD] / both[:, HD:]).astype(BF16)
 
 
@@ -385,31 +380,42 @@
     )(hbm(queries), hbm(own_keys), hbm(own_values), keys, values)
 
 
-def place_kernel(table_ref, received_ref, out_ref):
-    height = out_ref.shape[0]
-    base = pl.program_id(0) * height
-    for i in range(height):
-        source = table_ref[PLACE, base + i]
+def place_kernel(table_ref, received_ref, out_ref, buffer, sems):
+    group = 4
+    copies = []
+    for i in range(SLOTS):
+        source = table_ref[PLACE, i]
         page = received_ref[jnp.maximum(source - 1, 0)]
-        out_ref[i] = jnp.where(source > 0, page, jnp.zeros_like(page))
+        buffer[i] = jnp.where(source > 0, page, jnp.zeros_like(page))
+        if i % group == group - 1:
+            slots = pl.ds(i + 1 - group, group)
+            copy = pltpu.make_async_copy(
+                buffer.at[slots], out_ref.at[slots], sems.at[i // group]
+            )
+            copy.start()
+            copies.append(copy)
+    for copy in copies:
+        copy.wait()
 
 
 def place_pages(table, received):
-    height = 8
     return pl.pallas_call(
         place_kernel,
-        grid=(SLOTS // height,),
-        out_shape=shape((SLOTS, 2 * PAGE, HD), BF16),
+        out_shape=pltpu.HBM((SLOTS, 2 * PAGE, HD), BF16),
         in_specs=[SMEM, VMEM],
-        out_specs=pl.BlockSpec((height, 2 * PAGE, HD), lambda i: (i, 0, 0)),
+        out_specs=HBM,
+        scratch_shapes=[
+            pltpu.VMEM((SLOTS, 2 * PAGE, HD), BF16),
+            pltpu.SemaphoreType.DMA((SLOTS // 4,)),
+        ],
         compiler_params=params(8),
         cost_estimate=cost(0, 2 * MIB),
         name="place_pages",
     )(table, received)
 
 
-def shift(values, step):
-    pairs = [(i, ((i // 2 + step) % 4) * 2 + i % 2) for i in range(8)]
+def shift(values, steps):
+    pairs = [(i, ((i // 2 + steps[i % 2]) % 4) * 2 + i % 2) for i in range(8)]
     return lax.ppermute(values, "tp", pairs)
 
 
@@ -431,28 +437,16 @@
 
 
 def body(hidden, w_query, w_keyval, store, page_owner, page_slot, new_owner):
-    half = ROWS // 2
-    upper, lower = hidden[:half], hidden[half:]
-    ahead_upper, behind_lower = shift(upper, 1), shift(lower, -1)
-    ahead_lower, behind_upper = shift(lower, 1), shift(upper, -1)
-    sibling = swap(hidden)
+    near, back = shift(hidden, (1, -1)), shift(hidden, (-1, 1))
+    far = shift(near, (1, -1))
     table = make_table(page_owner, page_slot, new_owner)
     pages = exchange(gather_pages(table, store.reshape(64, 2 * PAGE, HD)))
     cosine, sine = rope_tables(ROWS, PAGES * PAGE)
-    far = (shift(ahead_upper, 1), shift(behind_lower, -1))
-    ahead, behind = (ahead_upper, ahead_lower), (behind_upper, behind_lower)
-    arrays = (
-        sibling,
-        *ahead,
-        *[swap(x) for x in ahead],
-        *behind,
-        *[swap(x) for x in behind],
-    )
+    arrays = (swap(hidden), near, swap(near), back, swap(back))
     early = project_early(arrays, hidden, w_query, w_keyval)
-    far = after(early[2], *far)
-    halves = (*far, *[swap(x) for x in far])
+    (far,) = after((early[2], pages), far)
     queries, own_keys, own_values, send = project_late(
-        table, halves, early[:3], early[3:], cosine, sine
+        table, (far, swap(far)), early[:3], early[3:], cosine, sine
     )
     received = exchange(send)
     keys, values = split_pages(table, pages)

time: 84.2 us -> 82.7 us (0.982)
  the two profiles are of different devices: /device:TPU:0 before, /device:TPU:96 now
where the time goes in v4:
time: 82.7 us; the launch traced here: 82.2 us
  waiting for transfers between devices  29.2 us (35%)
  Pallas kernels  27.3 us (33%)
  starting transfers between devices  14.5 us (18%)
  local copies, waits for them, and re-layouts  9.1 us (11%)
  other arithmetic  1.21 us (1%)
  between operations  0.95 us (1%)
    all_to_all x2, waiting for transfers between devices, exchange(): lax.all_to_all(values, 'pool', split_axis=0, concat_axis=0, tiled=True)  15.1 us
    all_to_all x2, starting transfers between devices, exchange(): lax.all_to_all(values, 'pool', split_axis=0, concat_axis=0, tiled=True)  10.9 us
    ppermute x3, waiting for transfers between devices, shift(): return lax.ppermute(values, 'tp', pairs)  10.5 us
    pallas_call x1, Pallas kernels, attend(): pl.pallas_call(attend_kernel, out_shape=shape((ROWS, QW), BF16), in_specs...  9.3 us
    unnamed x25, local copies, waits for them, and re-layouts  9.1 us
    pallas_call x1, Pallas kernels, project_early(): pl.pallas_call(early_kernel, out_shape=[shape((ROWS, QW), F32), shape((RO...  8.67 us
    pallas_call x1, Pallas kernels, project_late(): pl.pallas_call(late_kernel, out_shape=[pltpu.HBM((HEADS, ROWS, HD), BF16)...  4.85 us
    ppermute x4, waiting for transfers between devices, swap(): return lax.ppermute(values, 'tp', [(i, i ^ 1) for i in range(8)])  3.54 us
  transfers between devices with their start and end apart: 9, of which 7 were waited for; matrix products, arithmetic and copies ran while one was open for 2% of the time, Pallas kernels for 25%

profile of v4, /device:TPU:96, one launch (start us, length us, event | category | flops | bytes accessed | tf_op | source)
XLA Modules:
  0.0 82.2 jit_solution(380455348769124444)
XLA Ops:
  0.6 0.1 collective-permute-start.1
  0.7 2.0 %collective-permute-start.3 = (bf16[512,1024]{1,0:T(8,128)(2,1)}, bf16[512,1024]{1,0:T(8,128)(2,1)}, u32[]{:S(2)}, u32[]{:S(2)}) collective-permute-start(bf16[512,1024]{1,0:T(8,128)(2,1)} %refs_5_.1), channel_id=1, source_target_pairs={{0,6},{1,3},{2,0},{3,5},{4,2},{5,7},{6,4},{7,1},{8,14},{9,11},{10,... | collective-permute-start | bytes 3145736 | tf_op jit(solution)/shard_map/ppermute | solution.py:419
  2.7 0.8 copy.10.new_owner_ref
  3.5 0.0 copy-start.10
  3.5 0.7 copy-done.10
  4.2 0.0 copy-start.11
  4.2 0.7 copy-done.11
  4.9 0.5 make_table.1.table_ref
  5.4 0.0 copy-start.1
  5.4 1.6 %copy-done.1 = bf16[64,1,64,2,128]{4,3,2,1,0:T(2,128)(2,1)S(1)} copy-done((bf16[64,1,64,2,128]{4,3,2,1,0:T(2,128)(2,1)S(1)}, bf16[64,1,64,2,128]{4,3,2,1,0:T(2,128)(2,1)}, u32[]{:S(2)}) %copy-start.1) | copy-done | bytes 2097176
  7.0 1.0 %gather_pages.1 = bf16[64,128,128]{2,1,0:T(8,128)(2,1)S(1)} custom-call(s32[24,128]{1,0:T(8,128)S(1)} %make_table.1.table_ref, bf16[64,128,128]{2,1,0:T(8,128)(2,1)S(1)} %bitcast.4), custom_call_target="tpu_custom_call" | custom-call | bytes 4194304 | tf_op jit(solution)/shard_map/gather_pages/pallas_call | solution.py:114
  8.0 0.0 copy-start
  8.0 1.3 %copy-done = bf16[64,128,128]{2,1,0:T(8,128)(2,1)} copy-done((bf16[64,128,128]{2,1,0:T(8,128)(2,1)}, bf16[64,128,128]{2,1,0:T(8,128)(2,1)S(1)}, u32[]{:S(2)}) %copy-start) | copy-done | bytes 2097176
  9.2 7.0 %all-to-all-start = ((bf16[64,128,128]{2,1,0:T(8,128)(2,1)}), bf16[64,128,128]{2,1,0:T(8,128)(2,1)S(1)}, u32[]{:S(2)}, u32[]{:S(2)}) async-start(bf16[64,128,128]{2,1,0:T(8,128)(2,1)} %copy-done), calls=%async_computation | async-start | bytes 4194304 | tf_op jit(solution)/shard_map/all_to_all | solution.py:436
  16.3 0.3 collective-permute-start
  16.6 9.5 %collective-permute-done.1.refs_1_ = bf16[512,1024]{1,0:T(8,128)(2,1)} collective-permute-done((bf16[512,1024]{1,0:T(8,128)(2,1)}, bf16[512,1024]{1,0:T(8,128)(2,1)}, u32[]{:S(2)}, u32[]{:S(2)}) %collective-permute-start.1) | collective-permute-done | bytes 1048608 | tf_op jit(solution)/shard_map/ppermute | solution.py:419
  26.0 0.0 collective-permute-start.2
  26.0 1.1 %collective-permute-done.3.refs_3_ = bf16[512,1024]{1,0:T(8,128)(2,1)} collective-permute-done((bf16[512,1024]{1,0:T(8,128)(2,1)}, bf16[512,1024]{1,0:T(8,128)(2,1)}, u32[]{:S(2)}, u32[]{:S(2)}) %collective-permute-start.3) | collective-permute-done | bytes 1048608 | tf_op jit(solution)/shard_map/ppermute | solution.py:419
  27.1 0.0 collective-permute-start.4
  27.1 1.2 %collective-permute-start.5 = (bf16[512,1024]{1,0:T(8,128)(2,1)}, bf16[512,1024]{1,0:T(8,128)(2,1)S(1)}, u32[]{:S(2)}, u32[]{:S(2)}) collective-permute-start(bf16[512,1024]{1,0:T(8,128)(2,1)} %collective-permute-done.1.refs_1_), channel_id=1, source_target_pairs={{0,2},{1,7},{2,4},{3,1},{4,6},{5,3},{6,0},{7,5},{8,10},{9,15},{10,... | collective-permute-start | bytes 3145736 | tf_op jit(solution)/shard_map/ppermute | solution.py:419
  28.3 0.0 collective-permute-done.refs_0_
  28.3 0.6 collective-permute-done.2.refs_2_
  28.9 1.5 %collective-permute-done.4.refs_4_ = bf16[512,1024]{1,0:T(8,128)(2,1)S(1)} collective-permute-done((bf16[512,1024]{1,0:T(8,128)(2,1)}, bf16[512,1024]{1,0:T(8,128)(2,1)S(1)}, u32[]{:S(2)}, u32[]{:S(2)}) %collective-permute-start.4) | collective-permute-done | bytes 1048608 | tf_op jit(solution)/shard_map/ppermute | solution.py:423
  30.4 8.7 %project_early.1 = (f32[512,512]{1,0:T(8,128)S(1)}, f32[512,256]{1,0:T(8,128)S(1)}, f32[512,128]{1,0:T(8,128)S(1)}, bf16[2,1024,512]{2,1,0:T(8,128)(2,1)S(1)}, bf16[2,1024,256]{2,1,0:T(8,128)(2,1)S(1)}) custom-call(bf16[512,1024]{1,0:T(8,128)(2,1)S(1)} %collective-permute-done.refs_0_, bf16[512,1024]{1,0:T(8,128)(2,1)} %collective-permute-done.1.refs_1_, ...), custom_call_target="tpu_custom_call" | custom-call | bytes 1 | tf_op jit(solution)/shard_map/project_early/pallas_call | solution.py:228
  39.1 0.0 copy-start.2
  39.1 1.3 %copy-done.2 = bf16[2,1024,512]{2,1,0:T(8,128)(2,1)} copy-done((bf16[2,1024,512]{2,1,0:T(8,128)(2,1)}, bf16[2,1024,512]{2,1,0:T(8,128)(2,1)S(1)}, u32[]{:S(2)}) %copy-start.2) | copy-done | bytes 2097176
  40.4 0.0 copy-start.4
  40.4 1.0 %copy-done.4 = f32[512,512]{1,0:T(8,128)} copy-done((f32[512,512]{1,0:T(8,128)}, f32[512,512]{1,0:T(8,128)S(1)}, u32[]{:S(2)}) %copy-start.4) | copy-done | bytes 1048600
  41.4 0.0 copy-start.6
  41.4 1.0 %copy-done.6 = bf16[2,1024,256]{2,1,0:T(8,128)(2,1)} copy-done((bf16[2,1024,256]{2,1,0:T(8,128)(2,1)}, bf16[2,1024,256]{2,1,0:T(8,128)(2,1)S(1)}, u32[]{:S(2)}) %copy-start.6) | copy-done | bytes 1048600
  42.4 0.8 copy-done.8
  43.2 7.3 %all-to-all-done.refs_1_.pages_ref = bf16[64,128,128]{2,1,0:T(8,128)(2,1)S(1)} async-done(((bf16[64,128,128]{2,1,0:T(8,128)(2,1)}), bf16[64,128,128]{2,1,0:T(8,128)(2,1)S(1)}, u32[]{:S(2)}, u32[]{:S(2)}) %all-to-all-start) | async-done | bytes 2097184 | tf_op jit(solution)/shard_map/all_to_all | solution.py:436
  50.4 0.0 collective-permute-done.5.refs_2_
  50.5 0.0 copy-start.3
  50.5 0.1 collective-permute-start.6
  50.6 1.0 %fusion = (f32[512,64]{1,0:T(8,128)S(1)}, f32[512,64]{1,0:T(8,128)S(1)}, f32[512,64]{1,0:T(8,128)S(1)}) fusion(f32[64]{0:T(128)S(1)} %negate_power_fusion, f32[512]{0:T(512)S(1)} %add_convert_fusion), kind=kLoop, calls=%fused_computation.4 | loop fusion | flops 65536 | bytes 395520 | tf_op jit(solution)/shard_map/neg | solution.py:432
  51.6 0.2 pad_maximum_fusion
  51.8 1.4 %collective-permute-done.6.refs_1_ = bf16[512,1024]{1,0:T(8,128)(2,1)S(1)} collective-permute-done((bf16[512,1024]{1,0:T(8,128)(2,1)S(1)}, bf16[512,1024]{1,0:T(8,128)(2,1)S(1)}, u32[]{:S(2)}, u32[]{:S(2)}) %collective-permute-start.6) | collective-permute-done | bytes 1048608 | tf_op jit(solution)/shard_map/ppermute | solution.py:423
  53.2 0.0 copy-done.5
  53.2 0.0 copy-done.7
  53.2 0.0 copy-done.9
  53.2 0.0 copy-done.3
  53.2 4.9 %project_late.1 = (bf16[4,512,128]{2,1,0:T(8,128)(2,1)}, bf16[512,128]{1,0:T(8,128)(2,1)}, bf16[512,256]{1,0:T(8,128)(2,1)}, bf16[32,128,128]{2,1,0:T(8,128)(2,1)}) custom-call(s32[24,128]{1,0:T(8,128)S(1)} %make_table.1.table_ref, bf16[512,1024]{1,0:T(8,128)(2,1)S(1)} %after.1.refs_0_, bf16[512,1024]{1,0:T(8,128)(2,1)S(1)} %collective-permute-done.6.refs_1_, ...), custom_call_target="tpu_custom_call" | custom-call | bytes 1 | tf_op jit(solution)/shard_map/project_late/pallas_call | solution.py:309
  58.1 3.8 %all-to-all-start.1 = ((bf16[32,128,128]{2,1,0:T(8,128)(2,1)}), bf16[32,128,128]{2,1,0:T(8,128)(2,1)S(1)}, u32[]{:S(2)}, u32[]{:S(2)}) async-start(bf16[32,128,128]{2,1,0:T(8,128)(2,1)} %get-tuple-element.23), calls=%async_computation.1 | async-start | bytes 2097152 | tf_op jit(solution)/shard_map/all_to_all | solution.py:436
  61.9 1.2 %split_pages.1 = (bf16[2048,128]{1,0:T(8,128)(2,1)S(1)}, bf16[2048,256]{1,0:T(8,128)(2,1)S(1)}) custom-call(s32[24,128]{1,0:T(8,128)S(1)} %make_table.1.table_ref, bf16[64,128,128]{2,1,0:T(8,128)(2,1)S(1)} %all-to-all-done.refs_1_.pages_ref), custom_call_target="tpu_custom_call" | custom-call | flops 134217728 | bytes 4194304 | tf_op jit(solution)/shard_map/split_pages/pallas_call | solution.py:139
  63.2 9.3 %attend.1 = bf16[512,512]{1,0:T(8,128)(2,1)} custom-call(bf16[4,512,128]{2,1,0:T(8,128)(2,1)} %get-tuple-element.18.q_ref, bf16[512,128]{1,0:T(8,128)(2,1)} %get-tuple-element.19.own_keys_ref, bf16[512,256]{1,0:T(8,128)(2,1)} %get-tuple-element.20.own_values_ref, bf16[2048,128]{1,0:T(8,128)(2,1)S(1)} %get-tuple-element.21.keys_ref, ...), custom_call_target="tpu_custom_call" | custom-call | flops 5368709120 | bytes 8388608 | tf_op jit(solution)/shard_map/attend/pallas_call | solution.py:366
  72.5 7.8 %all-to-all-done.1.received_ref = bf16[32,128,128]{2,1,0:T(8,128)(2,1)S(1)} async-done(((bf16[32,128,128]{2,1,0:T(8,128)(2,1)}), bf16[32,128,128]{2,1,0:T(8,128)(2,1)S(1)}, u32[]{:S(2)}, u32[]{:S(2)}) %all-to-all-start.1) | async-done | bytes 1048608 | tf_op jit(solution)/shard_map/all_to_all | solution.py:436
  80.3 1.8 %place_pages.1 = bf16[32,128,128]{2,1,0:T(8,128)(2,1)} custom-call(s32[24,128]{1,0:T(8,128)S(1)} %make_table.1.table_ref, bf16[32,128,128]{2,1,0:T(8,128)(2,1)S(1)} %all-to-all-done.1.received_ref), custom_call_target="tpu_custom_call" | custom-call | bytes 2097152 | tf_op jit(solution)/shard_map/place_pages/pallas_call | solution.py:402
  (7 shorter events, 0.0 us)
Async XLA Ops:
  0.6 25.4 %collective-permute-start.1 = (bf16[512,1024]{1,0:T(8,128)(2,1)}, bf16[512,1024]{1,0:T(8,128)(2,1)}, u32[]{:S(2)}, u32[]{:S(2)}) collective-permute-start(bf16[512,1024]{1,0:T(8,128)(2,1)} %refs_5_.1), channel_id=1, source_target_pairs={{0,2},{1,7},{2,4},{3,1},{4,6},{5,3},{6,0},{7,5},{8,10},{9,15},{10,... | collective-permute-start | bytes 3145736 | tf_op jit(solution)/shard_map/ppermute | solution.py:419
  0.7 26.4 %collective-permute-start.3 = (bf16[512,1024]{1,0:T(8,128)(2,1)}, bf16[512,1024]{1,0:T(8,128)(2,1)}, u32[]{:S(2)}, u32[]{:S(2)}) collective-permute-start(bf16[512,1024]{1,0:T(8,128)(2,1)} %refs_5_.1), channel_id=1, source_target_pairs={{0,6},{1,3},{2,0},{3,5},{4,2},{5,7},{6,4},{7,1},{8,14},{9,11},{10,... | collective-permute-start | bytes 3145736 | tf_op jit(solution)/shard_map/ppermute | solution.py:419
  3.5 0.7 copy-start.10
  4.2 0.7 copy-start.11
  5.4 1.6 %copy-start.1 = (bf16[64,1,64,2,128]{4,3,2,1,0:T(2,128)(2,1)S(1)}, bf16[64,1,64,2,128]{4,3,2,1,0:T(2,128)(2,1)}, u32[]{:S(2)}) copy-start(bf16[64,1,64,2,128]{4,3,2,1,0:T(2,128)(2,1)} %param.10) | copy-start | bytes 6291460
  8.0 1.3 %copy-start = (bf16[64,128,128]{2,1,0:T(8,128)(2,1)}, bf16[64,128,128]{2,1,0:T(8,128)(2,1)S(1)}, u32[]{:S(2)}) copy-start(bf16[64,128,128]{2,1,0:T(8,128)(2,1)S(1)} %gather_pages.1) | copy-start | bytes 6291460
  9.2 41.2 %all-to-all-start = ((bf16[64,128,128]{2,1,0:T(8,128)(2,1)}), bf16[64,128,128]{2,1,0:T(8,128)(2,1)S(1)}, u32[]{:S(2)}, u32[]{:S(2)}) async-start(bf16[64,128,128]{2,1,0:T(8,128)(2,1)} %copy-done), calls=%async_computation | async-start | bytes 4194304 | tf_op jit(solution)/shard_map/all_to_all | solution.py:436
  16.3 12.0 %collective-permute-start = (bf16[512,1024]{1,0:T(8,128)(2,1)}, bf16[512,1024]{1,0:T(8,128)(2,1)S(1)}, u32[]{:S(2)}, u32[]{:S(2)}) collective-permute-start(bf16[512,1024]{1,0:T(8,128)(2,1)} %refs_5_.1), channel_id=1, source_target_pairs={{0,1},{1,0},{2,3},{3,2},{4,5},{5,4},{6,7},{7,6},{8,9},{9,8},{10,11... | collective-permute-start | bytes 3145736 | tf_op jit(solution)/shard_map/ppermute | solution.py:423
  26.0 2.9 %collective-permute-start.2 = (bf16[512,1024]{1,0:T(8,128)(2,1)}, bf16[512,1024]{1,0:T(8,128)(2,1)S(1)}, u32[]{:S(2)}, u32[]{:S(2)}) collective-permute-start(bf16[512,1024]{1,0:T(8,128)(2,1)} %collective-permute-done.1.refs_1_), channel_id=1, source_target_pairs={{0,1},{1,0},{2,3},{3,2},{4,5},{5,4},{6,7},{7,6},{8,9},{9,8},{10,11... | collective-permute-start | bytes 3145736 | tf_op jit(solution)/shard_map/ppermute | solution.py:423
  27.1 3.3 %collective-permute-start.4 = (bf16[512,1024]{1,0:T(8,128)(2,1)}, bf16[512,1024]{1,0:T(8,128)(2,1)S(1)}, u32[]{:S(2)}, u32[]{:S(2)}) collective-permute-start(bf16[512,1024]{1,0:T(8,128)(2,1)} %collective-permute-done.3.refs_3_), channel_id=1, source_target_pairs={{0,1},{1,0},{2,3},{3,2},{4,5},{5,4},{6,7},{7,6},{8,9},{9,8},{10,11... | collective-permute-start | bytes 3145736 | tf_op jit(solution)/shard_map/ppermute | solution.py:423
  27.1 23.3 %collective-permute-start.5 = (bf16[512,1024]{1,0:T(8,128)(2,1)}, bf16[512,1024]{1,0:T(8,128)(2,1)S(1)}, u32[]{:S(2)}, u32[]{:S(2)}) collective-permute-start(bf16[512,1024]{1,0:T(8,128)(2,1)} %collective-permute-done.1.refs_1_), channel_id=1, source_target_pairs={{0,2},{1,7},{2,4},{3,1},{4,6},{5,3},{6,0},{7,5},{8,10},{9,15},{10,... | collective-permute-start | bytes 3145736 | tf_op jit(solution)/shard_map/ppermute | solution.py:419
  39.1 1.3 %copy-start.2 = (bf16[2,1024,512]{2,1,0:T(8,128)(2,1)}, bf16[2,1024,512]{2,1,0:T(8,128)(2,1)S(1)}, u32[]{:S(2)}) copy-start(bf16[2,1024,512]{2,1,0:T(8,128)(2,1)S(1)} %get-tuple-element.16.refs_5_) | copy-start | bytes 6291460
  40.4 1.0 %copy-start.4 = (f32[512,512]{1,0:T(8,128)}, f32[512,512]{1,0:T(8,128)S(1)}, u32[]{:S(2)}) copy-start(f32[512,512]{1,0:T(8,128)S(1)} %get-tuple-element.14.refs_2_) | copy-start | bytes 3145732
  41.4 1.0 %copy-start.6 = (bf16[2,1024,256]{2,1,0:T(8,128)(2,1)}, bf16[2,1024,256]{2,1,0:T(8,128)(2,1)S(1)}, u32[]{:S(2)}) copy-start(bf16[2,1024,256]{2,1,0:T(8,128)(2,1)S(1)} %get-tuple-element.17.refs_6_) | copy-start | bytes 3145732
  42.4 0.8 copy-start.8
  50.5 2.8 %copy-start.5 = (f32[512,512]{1,0:T(8,128)S(1)}, f32[512,512]{1,0:T(8,128)}, u32[]{:S(2)}) copy-start(f32[512,512]{1,0:T(8,128)} %copy-done.4) | copy-start | bytes 3145732
  50.5 2.8 %copy-start.7 = (bf16[2,1024,256]{2,1,0:T(8,128)(2,1)S(1)}, bf16[2,1024,256]{2,1,0:T(8,128)(2,1)}, u32[]{:S(2)}) copy-start(bf16[2,1024,256]{2,1,0:T(8,128)(2,1)} %copy-done.6) | copy-start | bytes 3145732
  50.5 2.8 %copy-start.9 = (f32[512,256]{1,0:T(8,128)S(1)}, f32[512,256]{1,0:T(8,128)}, u32[]{:S(2)}) copy-start(f32[512,256]{1,0:T(8,128)} %copy-done.8) | copy-start | bytes 1572868
  50.5 2.8 %copy-start.3 = (bf16[2,1024,512]{2,1,0:T(8,128)(2,1)S(1)}, bf16[2,1024,512]{2,1,0:T(8,128)(2,1)}, u32[]{:S(2)}) copy-start(bf16[2,1024,512]{2,1,0:T(8,128)(2,1)} %copy-done.2) | copy-start | bytes 6291460
  50.5 2.7 %collective-permute-start.6 = (bf16[512,1024]{1,0:T(8,128)(2,1)S(1)}, bf16[512,1024]{1,0:T(8,128)(2,1)S(1)}, u32[]{:S(2)}, u32[]{:S(2)}) collective-permute-start(bf16[512,1024]{1,0:T(8,128)(2,1)S(1)} %after.1.refs_0_), channel_id=1, source_target_pairs={{0,1},{1,0},{2,3},{3,2},{4,5},{5,4},{6,7},{7,6},{8,9},{9,8},{10,11... | collective-permute-start | bytes 3145736 | tf_op jit(solution)/shard_map/ppermute | solution.py:423
  58.1 22.2 %all-to-all-start.1 = ((bf16[32,128,128]{2,1,0:T(8,128)(2,1)}), bf16[32,128,128]{2,1,0:T(8,128)(2,1)S(1)}, u32[]{:S(2)}, u32[]{:S(2)}) async-start(bf16[32,128,128]{2,1,0:T(8,128)(2,1)} %get-tuple-element.23), calls=%async_computation.1 | async-start | bytes 2097152 | tf_op jit(solution)/shard_map/all_to_all | solution.py:436

commit v5 on v4

--- a/solution.py
+++ b/solution.py
@@ -22,9 +22,10 @@
 NEW_PAGES = 8
 SLOTS = 32
 ROWS = 512
-TAKE, PUSH, PLACE = 16, 17, 18
+PUSH, TAKE, PLACE = 4, 16, 17
 MIB = 1024 * 1024
 SCALE = math.log2(math.e) / math.sqrt(HD)
+PIN = 30_000_000_000
 F32 = jnp.float32
 BF16 = jnp.bfloat16
 ANY = pl.BlockSpec(memory_space=pl.ANY)
@@ -49,77 +50,93 @@
     return jax.ShapeDtypeStruct(dims, dtype)
 
 
-def ranks_of(owners, lanes):
-    ranks = jnp.zeros_like(owners)
-    for j in range(owners.shape[1]):
-        ranks += ((owners == owners[:, j : j + 1]) & (lanes > j)).astype(jnp.int32)
-    return ranks
-
-
-def table_kernel(page_owner_ref, page_slot_ref, new_owner_ref, out_ref):
+def fill_table(owners, slots, targets, out_ref):
     me = lax.axis_index("pool")
     out_ref[...] = jnp.zeros_like(out_ref)
-    owners, slots = page_owner_ref[...], page_slot_ref[...]
     lanes = lax.broadcasted_iota(jnp.int32, owners.shape, 1)
     rows = lax.broadcasted_iota(jnp.int32, owners.shape, 0)
-    ranks = ranks_of(owners, lanes)
+    ranks = jnp.zeros_like(owners)
+    for j in range(PAGES):
+        ranks += ((owners == owners[:, j : j + 1]) & (lanes > j)).astype(jnp.int32)
     for k in range(CAP):
         chosen = jnp.where((owners == me) & (ranks == k), slots, 0)
         out_ref[:POOL, k : k + 1] = jnp.sum(chosen, axis=1, keepdims=True)
     mine = jnp.where(rows == me, owners * CAP + ranks, 0)
     out_ref[TAKE : TAKE + 1, :PAGES] = jnp.sum(mine, axis=0, keepdims=True)
-    targets = new_owner_ref[...]
-    target_lanes = lax.broadcasted_iota(jnp.int32, targets.shape, 1)
-    target_rows = lax.broadcasted_iota(jnp.int32, targets.shape, 0)
-    ranks = ranks_of(targets, target_lanes)
-    mine = jnp.where(target_rows == me, targets * PUSH_CAP + ranks, 0)
-    out_ref[PUSH : PUSH + 1, :NEW_PAGES] = jnp.sum(mine, axis=0, keepdims=True)
+    lanes = lax.broadcasted_iota(jnp.int32, targets.shape, 1)
+    rows = lax.broadcasted_iota(jnp.int32, targets.shape, 0)
     kept = (targets == me).astype(jnp.int32)
+    ranks = jnp.zeros_like(targets)
     slot = jnp.zeros_like(targets)
     for j in range(NEW_PAGES):
-        slot += jnp.where(target_lanes > j, kept[:, j : j + 1], 0)
-    in_row = jnp.sum(kept, axis=1, keepdims=True)
+        later = rows > j
+        ranks += ((targets == targets[j : j + 1, :]) & later).astype(jnp.int32)
+        slot += jnp.where(later, kept[j : j + 1, :], 0)
+    mine = jnp.where(lanes == me, targets * PUSH_CAP + ranks, 0)
+    out_ref[:NEW_PAGES, PUSH : PUSH + 1] = jnp.sum(mine, axis=1, keepdims=True)
+    of_request = jnp.sum(kept, axis=0, keepdims=True)
     for r in range(POOL):
-        slot += jnp.where(target_rows > r, in_row[r : r + 1, :], 0)
-    source = jnp.zeros((POOL, SLOTS), jnp.int32)
+        slot += jnp.where(lanes > r, of_request[:, r : r + 1], 0)
+    source = jnp.zeros((NEW_PAGES, SLOTS), jnp.int32)
     slot_lanes = lax.broadcasted_iota(jnp.int32, source.shape, 1)
-    slot_rows = lax.broadcasted_iota(jnp.int32, source.shape, 0)
-    for j in range(NEW_PAGES):
-        hit = (kept[:, j : j + 1] > 0) & (slot[:, j : j + 1] == slot_lanes)
-        source += jnp.where(hit, slot_rows * PUSH_CAP + ranks[:, j : j + 1] + 1, 0)
+    for r in range(POOL):
+        hit = (kept[:, r : r + 1] > 0) & (slot[:, r : r + 1] == slot_lanes)
+        source += jnp.where(hit, r * PUSH_CAP + ranks[:, r : r + 1] + 1, 0)
     out_ref[PLACE : PLACE + 1, :SLOTS] = jnp.sum(source, axis=0, keepdims=True)
 
 
-def make_table(page_owner, page_slot, new_owner):
-    return pl.pallas_call(
-        table_kernel,
-        out_shape=shape((24, HD), jnp.int32),
-        in_specs=[VMEM] * 3,
-        out_specs=VMEM,
-        compiler_params=params(4),
-        cost_estimate=cost(0, 16384),
-        name="make_table",
-    )(page_owner, page_slot, new_owner)
-
-
-def gather_kernel(table_ref, store_ref, out_ref):
-    def one(index, _):
-        out_ref[index] = store_ref[table_ref[index >> 2, index & 3]]
-        return 0
-
-    lax.fori_loop(0, POOL * CAP, one, 0, unroll=8)
-
-
-def gather_pages(table, store):
-    return pl.pallas_call(
-        gather_kernel,
-        out_shape=shape((POOL * CAP, 2 * PAGE, HD), BF16),
-        in_specs=[SMEM, VMEM],
-        out_specs=VMEM,
+def prelude_kernel(owner_in, slot_in, target_in, store_in, table_ref, out_ref, *scratch):
+    owner_ref, slot_ref, target_ref, store_ref, index_ref, sems, page_sems = scratch
+    pairs = (
+        (owner_in, owner_ref),
+        (slot_in, slot_ref),
+        (target_in, target_ref),
+        (store_in, store_ref),
+    )
+    copies = [pltpu.make_async_copy(x, y, sems.at[i]) for i, (x, y) in enumerate(pairs)]
+    for copy in copies:
+        copy.start()
+    for copy in copies[:3]:
+        copy.wait()
+    fill_table(owner_ref[...], slot_ref[...], target_ref[...], table_ref)
+    indices = pltpu.make_async_copy(table_ref, index_ref, sems.at[4])
+    indices.start()
+    indices.wait()
+    copies[3].wait()
+    pages = [
+        pltpu.make_async_copy(
+            store_ref.at[index_ref[i // CAP, i % CAP]], out_ref.at[i], page_sems.at[i]
+        )
+        for i in range(POOL * CAP)
+    ]
+    for page in pages:
+        page.start()
+    for page in pages:
+        page.wait()
+
+
+def prelude(page_owner, page_slot, new_owner, store):
+    return pl.pallas_call(
+        prelude_kernel,
+        out_shape=[
+            shape((24, HD), jnp.int32),
+            pltpu.HBM((POOL * CAP, 2 * PAGE, HD), BF16),
+        ],
+        in_specs=[HBM] * 4,
+        out_specs=[VMEM, HBM],
+        scratch_shapes=[
+            pltpu.VMEM((POOL, PAGES), jnp.int32),
+            pltpu.VMEM((POOL, PAGES), jnp.int32),
+            pltpu.VMEM((NEW_PAGES, POOL), jnp.int32),
+            pltpu.VMEM(store.shape, BF16),
+            pltpu.SMEM((24, HD), jnp.int32),
+            pltpu.SemaphoreType.DMA((5,)),
+            pltpu.SemaphoreType.DMA((POOL * CAP,)),
+        ],
         compiler_params=params(8),
-        cost_estimate=cost(0, 4 * MIB),
-        name="gather_pages",
-    )(table, store)
+        cost_estimate=cost(0, 1),
+        name="prelude",
+    )(hbm(page_owner), hbm(page_slot), hbm(new_owner.T), hbm(store))
 
 
 def split_kernel(table_ref, pages_ref, keys_ref, values_ref):
@@ -185,28 +202,27 @@
 
 
 OWN, NEAR, BACK, FAR = (0, 0), (3, 1), (1, 3), (2, 2)
-EARLY = ((OWN, True), (NEAR, False), (NEAR, True), (BACK, False), (BACK, True), (OWN, False))
+EARLY = ((OWN, True), (NEAR, True), (BACK, True), (OWN, False), (NEAR, False), (BACK, False))
 LATE = ((FAR, False), (FAR, True))
 TILE = 128
 
 
 def early_kernel(*refs):
     count = len(EARLY)
-    hidden_ref, wq_ref, wkv_ref = refs[5:8]
-    q_ref, kv_ref, sq_ref, late_q, late_kv, x_buf, wq_buf, wkv_buf, sems, late_sems, x_sem = refs[8:]
-    sources = (*refs[:5], x_buf)
-    x_copy = pltpu.make_async_copy(hidden_ref, x_buf, x_sem)
+    wq_ref, wkv_ref = refs[6:8]
+    q_ref, kv_ref, sq_ref, x_buf, wq_buf, wkv_buf, sems, x_sems = refs[8:]
+    x_copies = [pltpu.make_async_copy(refs[3 + i], x_buf.at[i], x_sems.at[i]) for i in range(3)]
     copies = weight_copies((wq_ref, wkv_ref), (wq_buf, wkv_buf), sems, EARLY)
-    x_copy.start()
-    late = weight_copies((wq_ref, wkv_ref), (late_q, late_kv), late_sems, LATE)
+    for copy in x_copies:
+        copy.start()
     for i in range(count):
         copies[i][0].wait()
         copies[i][1].wait()
-        if i == count - 1:
-            x_copy.wait()
+        if i >= 3:
+            x_copies[i - 3].wait()
         for r in range(0, ROWS, TILE):
             rows = slice(r, r + TILE)
-            x = sources[i][rows, :]
+            x = refs[i][rows, :] if i < 3 else x_buf[i - 3, rows, :]
             q_part = jnp.dot(x, wq_buf[i], preferred_element_type=F32)
             kv_part = jnp.dot(x, wkv_buf[i], preferred_element_type=F32)
             sq_part = squares_of(x)
@@ -218,54 +234,48 @@
                 q_ref[rows, :] += q_part
                 kv_ref[rows, :] += kv_part
                 sq_ref[rows, :] += sq_part
-    for group in late:
-        for copy in group:
-            copy.wait()
-
-
-def project_early(arrays, hidden, w_query, w_keyval):
+
+
+def project_early(swapped, direct, w_query, w_keyval):
     count = len(EARLY)
     return pl.pallas_call(
         early_kernel,
         out_shape=[
-            shape((ROWS, QW), F32),
-            shape((ROWS, KVW), F32),
-            shape((ROWS, HD), F32),
-            shape((2, FEAT, QW), BF16),
-            shape((2, FEAT, KVW), BF16),
-        ],
-        in_specs=[VMEM] * len(arrays) + [HBM] * 3,
-        out_specs=[VMEM] * 5,
+            pltpu.HBM((ROWS, QW), F32),
+            pltpu.HBM((ROWS, KVW), F32),
+            pltpu.HBM((ROWS, HD), F32),
+        ],
+        in_specs=[VMEM] * 3 + [HBM] * 5,
+        out_specs=[VMEM] * 3,
         scratch_shapes=[
-            pltpu.VMEM((ROWS, FEAT), BF16),
+            pltpu.VMEM((3, ROWS, FEAT), BF16),
             pltpu.VMEM((count, FEAT, QW), BF16),
             pltpu.VMEM((count, FEAT, KVW), BF16),
             pltpu.SemaphoreType.DMA((2 * count,)),
-            pltpu.SemaphoreType.DMA((4,)),
-            pltpu.SemaphoreType.DMA,
+            pltpu.SemaphoreType.DMA((3,)),
         ],
         compiler_params=params(16),
         cost_estimate=cost(0, 1),
         name="project_early",
-    )(*arrays, hbm(hidden), hbm(w_query), hbm(w_keyval))
+    )(*swapped, *[hbm(x) for x in (*direct, w_query, w_keyval)])
 
 
 def after_kernel(*refs):
     pass
 
 
-def after(tokens, *arrays):
+def after(tokens, *arrays, flops=0):
     count, skip = len(arrays), len(tokens)
     return pl.pallas_call(
         after_kernel,
         out_shape=[shape(x.shape, x.dtype) for x in arrays],
-        in_specs=[ANY] * (count + skip),
+        in_specs=[HBM] * skip + [ANY] * count,
         out_specs=[ANY] * count,
         input_output_aliases={i + skip: i for i in range(count)},
         compiler_params=params(1),
-        cost_estimate=cost(0, 1024),
+        cost_estimate=cost(flops, 1),
         name="after",
-    )(*tokens, *arrays)
+    )(*[hbm(token) for token in tokens], *arrays)
 
 
 def turn(values, cosine, sine):
@@ -274,52 +284,82 @@
 
 def late_kernel(table_ref, *refs):
     x_refs = refs[:2]
-    q_in, kv_in, sq_in, late_q, late_kv, cos_ref, sin_ref = refs[2:9]
-    q_ref, keys_ref, values_ref, send_ref = refs[9:]
+    q_in, kv_in, sq_in, cos_ref, sin_ref, wq_ref, wkv_ref, _ = refs[2:10]
+    q_out, keys_out, values_out, send_out = refs[10:14]
+    wq_buf, wkv_buf, q_buf, keys_buf, values_buf, page_buf, w_sems, sems, page_sems = refs[14:]
+    weights = weight_copies((wq_ref, wkv_ref), (wq_buf, wkv_buf), w_sems, LATE)
     row = lax.broadcasted_iota(jnp.int32, (2 * PAGE, 2 * PAGE), 0)
     column = lax.broadcasted_iota(jnp.int32, (2 * PAGE, 2 * PAGE), 1)
     picker = (column == (row >> 1) + (row & 1) * PAGE).astype(BF16)
+    values_buf[:, HD:] = jnp.ones((ROWS, HD), BF16)
+    inv_norms = []
     for r in range(0, ROWS, TILE):
         rows = slice(r, r + TILE)
-        x = [ref[rows, :] for ref in x_refs]
-        squares = sq_in[rows, :] + squares_of(x[0]) + squares_of(x[1])
+        squares = sq_in[rows, :] + squares_of(x_refs[0][rows, :]) + squares_of(x_refs[1][rows, :])
         mean = jnp.sum(squares, axis=1, keepdims=True) / D
-        inv_norm = jnp.broadcast_to(lax.rsqrt(mean + 1e-05), (TILE, HD))
+        inv_norms.append(jnp.broadcast_to(lax.rsqrt(mean + 1e-05), (TILE, HD)))
+    copies = []
+    for group in weights:
+        for copy in group:
+            copy.wait()
+    for r in range(0, ROWS, TILE):
+        rows = slice(r, r + TILE)
+        inv_norm = inv_norms[r // TILE]
         kv_sum = kv_in[rows, :]
         q_sum = q_in[rows, :]
         for i in range(2):
-            kv_sum += jnp.dot(x[i], late_kv[i], preferred_element_type=F32)
-            q_sum += jnp.dot(x[i], late_q[i], preferred_element_type=F32)
+            x = x_refs[i][rows, :]
+            kv_sum += jnp.dot(x, wkv_buf[i], preferred_element_type=F32)
+            q_sum += jnp.dot(x, wq_buf[i], preferred_element_type=F32)
         cosine, sine = cos_ref[rows, :], sin_ref[rows, :]
+        keys = turn(kv_sum[:, :HD] * inv_norm, cosine, sine).astype(BF16)
+        values = (kv_sum[:, HD:] * inv_norm).astype(BF16)
+        keys_buf[rows, :] = keys
+        values_buf[rows, :HD] = values
+        for p in range(0, TILE, PAGE):
+            page = (r + p) // PAGE
+            both = jnp.concatenate([keys[p : p + PAGE], values[p : p + PAGE]], axis=0)
+            page_buf[page] = jnp.dot(picker, both, preferred_element_type=F32).astype(BF16)
+            target = send_out.at[table_ref[page, PUSH]]
+            copies.append(pltpu.make_async_copy(page_buf.at[page], target, page_sems.at[page]))
+            copies[-1].start()
         for head in range(HEADS):
             part = q_sum[:, head * HD : (head + 1) * HD] * inv_norm
-            q_ref[head, rows, :] = turn(part, cosine, sine).astype(BF16)
-        keys = turn(kv_sum[:, :HD] * inv_norm, cosine, sine).astype(BF16)
-        values = (kv_sum[:, HD:] * inv_norm).astype(BF16)
-        keys_ref[rows, :] = keys
-        values_ref[rows, :HD] = values
-        values_ref[rows, HD:] = jnp.ones((TILE, HD), BF16)
-        for p in range(0, TILE, PAGE):
-            both = jnp.concatenate([keys[p : p + PAGE], values[p : p + PAGE]], axis=0)
-            mixed = jnp.dot(picker, both, preferred_element_type=F32).astype(BF16)
-            send_ref[table_ref[PUSH, (r + p) // PAGE]] = mixed
-
-
-def project_late(table, blocks, sums, late_weights, cosine, sine):
+            q_buf[head, rows, :] = turn(part, cosine, sine).astype(BF16)
+        span = pl.ds(r, TILE)
+        results = (
+            (q_buf.at[:, span, :], q_out.at[:, span, :]),
+            (keys_buf.at[span, :], keys_out.at[span, :]),
+            (values_buf.at[span, :], values_out.at[span, :]),
+        )
+        for i, (source, target) in enumerate(results):
+            copies.append(pltpu.make_async_copy(source, target, sems.at[3 * (r // TILE) + i]))
+            copies[-1].start()
+    for copy in copies:
+        copy.wait()
+
+
+def project_late(table, blocks, sums, cosine, sine, w_query, w_keyval, token):
+    results = [(HEADS, ROWS, HD), (ROWS, HD), (ROWS, 2 * HD)]
     return pl.pallas_call(
         late_kernel,
-        out_shape=[
-            pltpu.HBM((HEADS, ROWS, HD), BF16),
-            pltpu.HBM((ROWS, HD), BF16),
-            pltpu.HBM((ROWS, 2 * HD), BF16),
-            pltpu.HBM((POOL * PUSH_CAP, 2 * PAGE, HD), BF16),
-        ],
-        in_specs=[SMEM] + [VMEM] * 9,
-        out_specs=[VMEM] * 4,
-        compiler_params=params(12),
+        out_shape=[pltpu.HBM(x, BF16) for x in results]
+        + [pltpu.HBM((POOL * PUSH_CAP, 2 * PAGE, HD), BF16)],
+        in_specs=[SMEM] + [VMEM] * 7 + [HBM] * 2 + [ANY],
+        out_specs=[HBM] * 4,
+        scratch_shapes=[
+            pltpu.VMEM((2, FEAT, QW), BF16),
+            pltpu.VMEM((2, FEAT, KVW), BF16),
+            *[pltpu.VMEM(x, BF16) for x in results],
+            pltpu.VMEM((NEW_PAGES, 2 * PAGE, HD), BF16),
+            pltpu.SemaphoreType.DMA((4,)),
+            pltpu.SemaphoreType.DMA((3 * ROWS // TILE,)),
+            pltpu.SemaphoreType.DMA((NEW_PAGES,)),
+        ],
+        compiler_params=params(16),
         cost_estimate=cost(0, 1),
         name="project_late",
-    )(table, *blocks, *sums, *late_weights, cosine, sine)
+    )(table, *blocks, *sums, cosine, sine, hbm(w_query), hbm(w_keyval), token)
 
 
 def dot_nt(a, b):
@@ -439,14 +479,14 @@
 def body(hidden, w_query, w_keyval, store, page_owner, page_slot, new_owner):
     near, back = shift(hidden, (1, -1)), shift(hidden, (-1, 1))
     far = shift(near, (1, -1))
-    table = make_table(page_owner, page_slot, new_owner)
-    pages = exchange(gather_pages(table, store.reshape(64, 2 * PAGE, HD)))
+    table, packed = prelude(page_owner, page_slot, new_owner, store.reshape(64, 2 * PAGE, HD))
+    (pages,) = after((), exchange(packed), flops=PIN)
     cosine, sine = rope_tables(ROWS, PAGES * PAGE)
-    arrays = (swap(hidden), near, swap(near), back, swap(back))
-    early = project_early(arrays, hidden, w_query, w_keyval)
-    (far,) = after((early[2], pages), far)
+    direct = (hidden, near, back)
+    sums = project_early([swap(x) for x in direct], direct, w_query, w_keyval)
+    (far,) = after((sums[2],), far)
     queries, own_keys, own_values, send = project_late(
-        table, (far, swap(far)), early[:3], early[3:], cosine, sine
+        table, (far, swap(far)), sums, cosine, sine, w_query, w_keyval, pages
     )
     received = exchange(send)
     keys, values = split_pages(table, pages)

time: 82.7 us -> 82.5 us (level)
  the two profiles are of different devices: /device:TPU:96 before, /device:TPU:0 now
where the time goes in v5:
time: 82.5 us; the launch traced here: 82.2 us
  Pallas kernels  31.7 us (38%)
  waiting for transfers between devices  27.7 us (34%)
  starting transfers between devices  19.9 us (24%)
  other arithmetic  1.92 us (2%)
  between operations  0.9 us (1%)
    ppermute x3, waiting for transfers between devices, shift(): return lax.ppermute(values, 'tp', pairs)  17.1 us
    all_to_all x2, starting transfers between devices, exchange(): lax.all_to_all(values, 'pool', split_axis=0, concat_axis=0, tiled=True)  13.9 us
    pallas_call x1, Pallas kernels, attend(): pl.pallas_call(attend_kernel, out_shape=shape((ROWS, QW), BF16), in_specs...  9.3 us
    all_to_all x2, waiting for transfers between devices, exchange(): lax.all_to_all(values, 'pool', split_axis=0, concat_axis=0, tiled=True)  8.32 us
    pallas_call x1, Pallas kernels, project_early(): pl.pallas_call(early_kernel, out_shape=[pltpu.HBM((ROWS, QW), F32), pltpu...  8.31 us
    pallas_call x1, Pallas kernels, project_late(): pl.pallas_call(late_kernel, out_shape=[pltpu.HBM(x, BF16) for x in result...  7.3 us
    ppermute x3, starting transfers between devices, shift(): return lax.ppermute(values, 'tp', pairs)  4.28 us
    pallas_call x1, Pallas kernels, prelude(): pl.pallas_call(prelude_kernel, out_shape=[shape((24, HD), jnp.int32), plt...  3.82 us
  transfers between devices with their start and end apart: 9, of which 7 were waited for; matrix products, arithmetic and copies ran while one was open for 2% of the time, Pallas kernels for 28%

profile of v5, /device:TPU:0, one launch (start us, length us, event | category | flops | bytes accessed | tf_op | source)
XLA Modules:
  0.0 82.2 jit_solution(6083748018356631037)
XLA Ops:
  0.6 2.1 %collective-permute-start.1 = (bf16[512,1024]{1,0:T(8,128)(2,1)}, bf16[512,1024]{1,0:T(8,128)(2,1)}, u32[]{:S(2)}, u32[]{:S(2)}) collective-permute-start(bf16[512,1024]{1,0:T(8,128)(2,1)} %refs_3_.1), channel_id=1, source_target_pairs={{0,2},{1,7},{2,4},{3,1},{4,6},{5,3},{6,0},{7,5},{8,10},{9,15},{10,... | collective-permute-start | bytes 3145736 | tf_op jit(solution)/shard_map/ppermute | solution.py:459
  2.7 2.2 %collective-permute-start.3 = (bf16[512,1024]{1,0:T(8,128)(2,1)}, bf16[512,1024]{1,0:T(8,128)(2,1)}, u32[]{:S(2)}, u32[]{:S(2)}) collective-permute-start(bf16[512,1024]{1,0:T(8,128)(2,1)} %refs_3_.1), channel_id=1, source_target_pairs={{0,6},{1,3},{2,0},{3,5},{4,2},{5,7},{6,4},{7,1},{8,14},{9,11},{10,... | collective-permute-start | bytes 3145736 | tf_op jit(solution)/shard_map/ppermute | solution.py:459
  4.9 3.8 %prelude.1 = (s32[24,128]{1,0:T(8,128)S(1)}, bf16[64,128,128]{2,1,0:T(8,128)(2,1)}) custom-call(s32[16,32]{1,0:T(8,128)} %owner_in.1, s32[16,32]{1,0:T(8,128)} %slot_in.1, s32[8,16]{1,0:T(8,128)} %bitcast.7, bf16[64,128,128]{2,1,0:T(8,128)(2,1)} %bitcast.5), custom_call_target="tpu_custom_call" | custom-call | bytes 1 | tf_op jit(solution)/shard_map/prelude/pallas_call | solution.py:119
  8.7 7.0 %all-to-all-start = ((bf16[64,128,128]{2,1,0:T(8,128)(2,1)}), bf16[64,128,128]{2,1,0:T(8,128)(2,1)S(1)}, u32[]{:S(2)}, u32[]{:S(2)}) async-start(bf16[64,128,128]{2,1,0:T(8,128)(2,1)} %get-tuple-element.17), calls=%async_computation | async-start | bytes 4194304 | tf_op jit(solution)/shard_map/all_to_all | solution.py:476
  15.8 0.1 collective-permute-start
  15.9 11.4 %collective-permute-done.1.refs_4_ = bf16[512,1024]{1,0:T(8,128)(2,1)} collective-permute-done((bf16[512,1024]{1,0:T(8,128)(2,1)}, bf16[512,1024]{1,0:T(8,128)(2,1)}, u32[]{:S(2)}, u32[]{:S(2)}) %collective-permute-start.1) | collective-permute-done | bytes 1048608 | tf_op jit(solution)/shard_map/ppermute | solution.py:459
  27.3 0.0 collective-permute-start.2
  27.3 0.3 collective-permute-done.3.refs_5_
  27.6 1.6 %collective-permute-start.4 = (bf16[512,1024]{1,0:T(8,128)(2,1)}, bf16[512,1024]{1,0:T(8,128)(2,1)S(1)}, u32[]{:S(2)}, u32[]{:S(2)}) collective-permute-start(bf16[512,1024]{1,0:T(8,128)(2,1)} %collective-permute-done.3.refs_5_), channel_id=1, source_target_pairs={{0,1},{1,0},{2,3},{3,2},{4,5},{5,4},{6,7},{7,6},{8,9},{9,8},{10,11... | collective-permute-start | bytes 3145736 | tf_op jit(solution)/shard_map/ppermute | solution.py:463
  29.2 0.0 collective-permute-start.5
  29.2 1.0 %fusion = (f32[512,64]{1,0:T(8,128)S(1)}, f32[512,64]{1,0:T(8,128)S(1)}, f32[512,64]{1,0:T(8,128)S(1)}) fusion(f32[64]{0:T(128)S(1)} %negate_power_fusion, f32[512]{0:T(512)S(1)} %add_convert_fusion), kind=kLoop, calls=%fused_computation.4 | loop fusion | flops 65536 | bytes 395520 | tf_op jit(solution)/shard_map/neg | solution.py:472
  30.2 0.9 %pad_maximum_fusion = (f32[512,128]{1,0:T(8,128)S(1)}, f32[512,128]{1,0:T(8,128)}) fusion(f32[512,64]{1,0:T(8,128)S(1)} %get-tuple-element.28, f32[512,64]{1,0:T(8,128)S(1)} %get-tuple-element.27, f32[512,64]{1,0:T(8,128)S(1)} %get-tuple-element.26), kind=kLoop, calls=%fused_computation.2 | loop fusion | flops 131072 | bytes 917504 | tf_op jit(solution)/shard_map/concatenate | solution.py:472
  31.1 0.0 collective-permute-done.refs_0_
  31.1 0.0 collective-permute-done.2.refs_1_
  31.1 0.6 collective-permute-done.4.refs_2_
  31.7 8.3 %project_early.1 = (f32[512,512]{1,0:T(8,128)}, f32[512,256]{1,0:T(8,128)}, f32[512,128]{1,0:T(8,128)}) custom-call(bf16[512,1024]{1,0:T(8,128)(2,1)S(1)} %collective-permute-done.refs_0_, bf16[512,1024]{1,0:T(8,128)(2,1)S(1)} %collective-permute-done.2.refs_1_, bf16[512,1024]{1,0:T(8,128)(2,1)S(1)} %collective-permute-done.4.refs_2_, ...), custom_call_target="tpu_custom_call" | custom-call | bytes 1 | tf_op jit(solution)/shard_map/project_early/pallas_call | solution.py:241
  40.0 5.4 %collective-permute-done.5.refs_1_ = bf16[512,1024]{1,0:T(8,128)(2,1)S(1)} collective-permute-done((bf16[512,1024]{1,0:T(8,128)(2,1)}, bf16[512,1024]{1,0:T(8,128)(2,1)S(1)}, u32[]{:S(2)}, u32[]{:S(2)}) %collective-permute-start.5) | collective-permute-done | bytes 1048608 | tf_op jit(solution)/shard_map/ppermute | solution.py:459
  45.4 0.0 collective-permute-start.6
  45.4 1.0 %all-to-all-done.refs_0_ = bf16[64,128,128]{2,1,0:T(8,128)(2,1)S(1)} async-done(((bf16[64,128,128]{2,1,0:T(8,128)(2,1)}), bf16[64,128,128]{2,1,0:T(8,128)(2,1)S(1)}, u32[]{:S(2)}, u32[]{:S(2)}) %all-to-all-start) | async-done | bytes 2097184 | tf_op jit(solution)/shard_map/all_to_all | solution.py:476
  46.4 0.0 copy-start
  46.4 0.0 copy-start.1
  46.4 0.0 copy-start.2
  46.4 0.0 copy-start.3
  46.5 1.7 %collective-permute-done.6.refs_1_ = bf16[512,1024]{1,0:T(8,128)(2,1)} collective-permute-done((bf16[512,1024]{1,0:T(8,128)(2,1)S(1)}, bf16[512,1024]{1,0:T(8,128)(2,1)}, u32[]{:S(2)}, u32[]{:S(2)}) %collective-permute-start.6) | collective-permute-done | bytes 1048608 | tf_op jit(solution)/shard_map/ppermute | solution.py:463
  48.2 0.0 copy-done
  48.2 0.0 copy-done.1
  48.2 0.0 copy-done.2
  48.2 0.0 copy-done.3
  48.2 7.3 %project_late.1 = (bf16[4,512,128]{2,1,0:T(8,128)(2,1)}, bf16[512,128]{1,0:T(8,128)(2,1)}, bf16[512,256]{1,0:T(8,128)(2,1)}, bf16[32,128,128]{2,1,0:T(8,128)(2,1)}) custom-call(s32[24,128]{1,0:T(8,128)S(1)} %get-tuple-element.13.table_ref, bf16[512,1024]{1,0:T(8,128)(2,1)S(1)} %after.2.refs_0_, bf16[512,1024]{1,0:T(8,128)(2,1)} %collective-permute-done.6.refs_1_, ...), custom_call_target="tpu_custom_call" | custom-call | bytes 1 | tf_op jit(solution)/shard_map/project_late/pallas_call | solution.py:344
  55.5 6.9 %all-to-all-start.1 = ((bf16[32,128,128]{2,1,0:T(8,128)(2,1)}), bf16[32,128,128]{2,1,0:T(8,128)(2,1)S(1)}, u32[]{:S(2)}, u32[]{:S(2)}) async-start(bf16[32,128,128]{2,1,0:T(8,128)(2,1)} %get-tuple-element.23), calls=%async_computation.1 | async-start | bytes 2097152 | tf_op jit(solution)/shard_map/all_to_all | solution.py:476
  62.4 1.2 %split_pages.1 = (bf16[2048,128]{1,0:T(8,128)(2,1)S(1)}, bf16[2048,256]{1,0:T(8,128)(2,1)S(1)}) custom-call(s32[24,128]{1,0:T(8,128)S(1)} %get-tuple-element.13.table_ref, bf16[64,128,128]{2,1,0:T(8,128)(2,1)S(1)} %after.3.refs_9_.pages_ref), custom_call_target="tpu_custom_call" | custom-call | flops 134217728 | bytes 4194304 | tf_op jit(solution)/shard_map/split_pages/pallas_call | solution.py:156
  63.6 9.3 %attend.1 = bf16[512,512]{1,0:T(8,128)(2,1)} custom-call(bf16[4,512,128]{2,1,0:T(8,128)(2,1)} %get-tuple-element.18.q_ref, bf16[512,128]{1,0:T(8,128)(2,1)} %get-tuple-element.19.own_keys_ref, bf16[512,256]{1,0:T(8,128)(2,1)} %get-tuple-element.20.own_values_ref, bf16[2048,128]{1,0:T(8,128)(2,1)S(1)} %get-tuple-element.21.keys_ref, ...), custom_call_target="tpu_custom_call" | custom-call | flops 5368709120 | bytes 8388608 | tf_op jit(solution)/shard_map/attend/pallas_call | solution.py:406
  72.9 7.3 %all-to-all-done.1.received_ref = bf16[32,128,128]{2,1,0:T(8,128)(2,1)S(1)} async-done(((bf16[32,128,128]{2,1,0:T(8,128)(2,1)}), bf16[32,128,128]{2,1,0:T(8,128)(2,1)S(1)}, u32[]{:S(2)}, u32[]{:S(2)}) %all-to-all-start.1) | async-done | bytes 1048608 | tf_op jit(solution)/shard_map/all_to_all | solution.py:476
  80.2 1.8 %place_pages.1 = bf16[32,128,128]{2,1,0:T(8,128)(2,1)} custom-call(s32[24,128]{1,0:T(8,128)S(1)} %get-tuple-element.13.table_ref, bf16[32,128,128]{2,1,0:T(8,128)(2,1)S(1)} %all-to-all-done.1.received_ref), custom_call_target="tpu_custom_call" | custom-call | bytes 2097152 | tf_op jit(solution)/shard_map/place_pages/pallas_call | solution.py:442
  (4 shorter events, 0.0 us)
Async XLA Ops:
  0.6 26.6 %collective-permute-start.1 = (bf16[512,1024]{1,0:T(8,128)(2,1)}, bf16[512,1024]{1,0:T(8,128)(2,1)}, u32[]{:S(2)}, u32[]{:S(2)}) collective-permute-start(bf16[512,1024]{1,0:T(8,128)(2,1)} %refs_3_.1), channel_id=1, source_target_pairs={{0,2},{1,7},{2,4},{3,1},{4,6},{5,3},{6,0},{7,5},{8,10},{9,15},{10,... | collective-permute-start | bytes 3145736 | tf_op jit(solution)/shard_map/ppermute | solution.py:459
  2.7 24.9 %collective-permute-start.3 = (bf16[512,1024]{1,0:T(8,128)(2,1)}, bf16[512,1024]{1,0:T(8,128)(2,1)}, u32[]{:S(2)}, u32[]{:S(2)}) collective-permute-start(bf16[512,1024]{1,0:T(8,128)(2,1)} %refs_3_.1), channel_id=1, source_target_pairs={{0,6},{1,3},{2,0},{3,5},{4,2},{5,7},{6,4},{7,1},{8,14},{9,11},{10,... | collective-permute-start | bytes 3145736 | tf_op jit(solution)/shard_map/ppermute | solution.py:459
  8.7 37.7 %all-to-all-start = ((bf16[64,128,128]{2,1,0:T(8,128)(2,1)}), bf16[64,128,128]{2,1,0:T(8,128)(2,1)S(1)}, u32[]{:S(2)}, u32[]{:S(2)}) async-start(bf16[64,128,128]{2,1,0:T(8,128)(2,1)} %get-tuple-element.17), calls=%async_computation | async-start | bytes 4194304 | tf_op jit(solution)/shard_map/all_to_all | solution.py:476
  15.8 15.3 %collective-permute-start = (bf16[512,1024]{1,0:T(8,128)(2,1)}, bf16[512,1024]{1,0:T(8,128)(2,1)S(1)}, u32[]{:S(2)}, u32[]{:S(2)}) collective-permute-start(bf16[512,1024]{1,0:T(8,128)(2,1)} %refs_3_.1), channel_id=1, source_target_pairs={{0,1},{1,0},{2,3},{3,2},{4,5},{5,4},{6,7},{7,6},{8,9},{9,8},{10,11... | collective-permute-start | bytes 3145736 | tf_op jit(solution)/shard_map/ppermute | solution.py:463
  27.3 3.8 %collective-permute-start.2 = (bf16[512,1024]{1,0:T(8,128)(2,1)}, bf16[512,1024]{1,0:T(8,128)(2,1)S(1)}, u32[]{:S(2)}, u32[]{:S(2)}) collective-permute-start(bf16[512,1024]{1,0:T(8,128)(2,1)} %collective-permute-done.1.refs_4_), channel_id=1, source_target_pairs={{0,1},{1,0},{2,3},{3,2},{4,5},{5,4},{6,7},{7,6},{8,9},{9,8},{10,11... | collective-permute-start | bytes 3145736 | tf_op jit(solution)/shard_map/ppermute | solution.py:463
  27.6 4.1 %collective-permute-start.4 = (bf16[512,1024]{1,0:T(8,128)(2,1)}, bf16[512,1024]{1,0:T(8,128)(2,1)S(1)}, u32[]{:S(2)}, u32[]{:S(2)}) collective-permute-start(bf16[512,1024]{1,0:T(8,128)(2,1)} %collective-permute-done.3.refs_5_), channel_id=1, source_target_pairs={{0,1},{1,0},{2,3},{3,2},{4,5},{5,4},{6,7},{7,6},{8,9},{9,8},{10,11... | collective-permute-start | bytes 3145736 | tf_op jit(solution)/shard_map/ppermute | solution.py:463
  29.2 16.2 %collective-permute-start.5 = (bf16[512,1024]{1,0:T(8,128)(2,1)}, bf16[512,1024]{1,0:T(8,128)(2,1)S(1)}, u32[]{:S(2)}, u32[]{:S(2)}) collective-permute-start(bf16[512,1024]{1,0:T(8,128)(2,1)} %collective-permute-done.1.refs_4_), channel_id=1, source_target_pairs={{0,2},{1,7},{2,4},{3,1},{4,6},{5,3},{6,0},{7,5},{8,10},{9,15},{10,... | collective-permute-start | bytes 3145736 | tf_op jit(solution)/shard_map/ppermute | solution.py:459
  45.4 2.8 %collective-permute-start.6 = (bf16[512,1024]{1,0:T(8,128)(2,1)S(1)}, bf16[512,1024]{1,0:T(8,128)(2,1)}, u32[]{:S(2)}, u32[]{:S(2)}) collective-permute-start(bf16[512,1024]{1,0:T(8,128)(2,1)S(1)} %after.2.refs_0_), channel_id=1, source_target_pairs={{0,1},{1,0},{2,3},{3,2},{4,5},{5,4},{6,7},{7,6},{8,9},{9,8},{10,11... | collective-permute-start | bytes 3145736 | tf_op jit(solution)/shard_map/ppermute | solution.py:463
  46.4 1.7 %copy-start = (f32[512,128]{1,0:T(8,128)S(1)}, f32[512,128]{1,0:T(8,128)}, u32[]{:S(2)}) copy-start(f32[512,128]{1,0:T(8,128)} %get-tuple-element.30.refs_6_) | copy-start | bytes 786436
  46.4 1.7 %copy-start.1 = (f32[512,128]{1,0:T(8,128)S(1)}, f32[512,128]{1,0:T(8,128)}, u32[]{:S(2)}) copy-start(f32[512,128]{1,0:T(8,128)} %get-tuple-element.14.refs_0_.refs_4_) | copy-start | bytes 786436
  46.4 1.7 %copy-start.2 = (f32[512,512]{1,0:T(8,128)S(1)}, f32[512,512]{1,0:T(8,128)}, u32[]{:S(2)}) copy-start(f32[512,512]{1,0:T(8,128)} %get-tuple-element.15.refs_2_) | copy-start | bytes 3145732
  46.4 1.7 %copy-start.3 = (f32[512,256]{1,0:T(8,128)S(1)}, f32[512,256]{1,0:T(8,128)}, u32[]{:S(2)}) copy-start(f32[512,256]{1,0:T(8,128)} %get-tuple-element.16.refs_3_) | copy-start | bytes 1572868
  55.5 24.7 %all-to-all-start.1 = ((bf16[32,128,128]{2,1,0:T(8,128)(2,1)}), bf16[32,128,128]{2,1,0:T(8,128)(2,1)S(1)}, u32[]{:S(2)}, u32[]{:S(2)}) async-start(bf16[32,128,128]{2,1,0:T(8,128)(2,1)} %get-tuple-element.23), calls=%async_computation.1 | async-start | bytes 2097152 | tf_op jit(solution)/shard_map/all_to_all | solution.py:476

commit v6 on v5

--- a/solution.py
+++ b/solution.py
@@ -25,7 +25,7 @@
 PUSH, TAKE, PLACE = 4, 16, 17
 MIB = 1024 * 1024
 SCALE = math.log2(math.e) / math.sqrt(HD)
-PIN = 30_000_000_000
+HIDES = 20_000_000_000
 F32 = jnp.float32
 BF16 = jnp.bfloat16
 ANY = pl.BlockSpec(memory_space=pl.ANY)
@@ -202,62 +202,74 @@
 
 
 OWN, NEAR, BACK, FAR = (0, 0), (3, 1), (1, 3), (2, 2)
-EARLY = ((OWN, True), (NEAR, True), (BACK, True), (OWN, False), (NEAR, False), (BACK, False))
-LATE = ((FAR, False), (FAR, True))
 TILE = 128
 
 
-def early_kernel(*refs):
-    count = len(EARLY)
-    wq_ref, wkv_ref = refs[6:8]
-    q_ref, kv_ref, sq_ref, x_buf, wq_buf, wkv_buf, sems, x_sems = refs[8:]
-    x_copies = [pltpu.make_async_copy(refs[3 + i], x_buf.at[i], x_sems.at[i]) for i in range(3)]
-    copies = weight_copies((wq_ref, wkv_ref), (wq_buf, wkv_buf), sems, EARLY)
-    for copy in x_copies:
-        copy.start()
+def project_kernel(blocks, held, has_sums, tokens, ahead, *refs):
+    count = len(blocks)
+    x_refs, refs = refs[:count], refs[count:]
+    wq_ref, wkv_ref, refs = refs[0], refs[1], refs[2:]
+    before, refs = (refs[:3], refs[3:]) if has_sums else (None, refs)
+    refs = refs[tokens:]
+    sums, refs = refs[:3], refs[3:]
+    fetched, refs = (refs[:2], refs[2:]) if ahead else (None, refs)
+    x_buf, wq_buf, wkv_buf, sems, x_sems, ahead_sems = refs
+    copies = weight_copies((wq_ref, wkv_ref), (wq_buf, wkv_buf), sems, blocks)
+    x_copies = {}
+    for i in range(held, count):
+        x_copies[i] = pltpu.make_async_copy(x_refs[i], x_buf.at[i - held], x_sems.at[i - held])
+        x_copies[i].start()
+    later = weight_copies((wq_ref, wkv_ref), fetched, ahead_sems, ahead) if ahead else []
     for i in range(count):
         copies[i][0].wait()
         copies[i][1].wait()
-        if i >= 3:
-            x_copies[i - 3].wait()
+        if i in x_copies:
+            x_copies[i].wait()
         for r in range(0, ROWS, TILE):
             rows = slice(r, r + TILE)
-            x = refs[i][rows, :] if i < 3 else x_buf[i - 3, rows, :]
-            q_part = jnp.dot(x, wq_buf[i], preferred_element_type=F32)
-            kv_part = jnp.dot(x, wkv_buf[i], preferred_element_type=F32)
-            sq_part = squares_of(x)
-            if i == 0:
-                q_ref[rows, :] = q_part
-                kv_ref[rows, :] = kv_part
-                sq_ref[rows, :] = sq_part
-            else:
-                q_ref[rows, :] += q_part
-                kv_ref[rows, :] += kv_part
-                sq_ref[rows, :] += sq_part
-
-
-def project_early(swapped, direct, w_query, w_keyval):
-    count = len(EARLY)
-    return pl.pallas_call(
-        early_kernel,
-        out_shape=[
-            pltpu.HBM((ROWS, QW), F32),
-            pltpu.HBM((ROWS, KVW), F32),
-            pltpu.HBM((ROWS, HD), F32),
-        ],
-        in_specs=[VMEM] * 3 + [HBM] * 5,
-        out_specs=[VMEM] * 3,
+            x = x_refs[i][rows, :] if i < held else x_buf[i - held, rows, :]
+            parts = (
+                jnp.dot(x, wq_buf[i], preferred_element_type=F32),
+                jnp.dot(x, wkv_buf[i], preferred_element_type=F32),
+                squares_of(x),
+            )
+            for j, part in enumerate(parts):
+                if i > 0:
+                    sums[j][rows, :] += part
+                elif has_sums:
+                    sums[j][rows, :] = before[j][rows, :] + part
+                else:
+                    sums[j][rows, :] = part
+    for group in later:
+        for copy in group:
+            copy.wait()
+
+
+def project(blocks, held, direct, w_query, w_keyval, sums=(), ahead=(), tokens=(), flops=0):
+    count = len(blocks)
+    shapes = [shape((ROWS, w), F32) for w in (QW, KVW, HD)]
+    if ahead:
+        shapes += [shape((len(ahead), FEAT, w), BF16) for w in (QW, KVW)]
+    return pl.pallas_call(
+        functools.partial(project_kernel, blocks, len(held), bool(sums), len(tokens), ahead),
+        out_shape=shapes,
+        in_specs=[VMEM] * len(held)
+        + [HBM] * (len(direct) + 2)
+        + [VMEM] * len(sums)
+        + [ANY] * len(tokens),
+        out_specs=[VMEM] * len(shapes),
         scratch_shapes=[
-            pltpu.VMEM((3, ROWS, FEAT), BF16),
+            pltpu.VMEM((max(len(direct), 1), ROWS, FEAT), BF16),
             pltpu.VMEM((count, FEAT, QW), BF16),
             pltpu.VMEM((count, FEAT, KVW), BF16),
             pltpu.SemaphoreType.DMA((2 * count,)),
-            pltpu.SemaphoreType.DMA((3,)),
-        ],
-        compiler_params=params(16),
-        cost_estimate=cost(0, 1),
-        name="project_early",
-    )(*swapped, *[hbm(x) for x in (*direct, w_query, w_keyval)])
+            pltpu.SemaphoreType.DMA((max(len(direct), 1),)),
+            pltpu.SemaphoreType.DMA((max(2 * len(ahead), 1),)),
+        ],
+        compiler_params=params(24),
+        cost_estimate=cost(flops, 1),
+        name="project",
+    )(*held, *[hbm(x) for x in (*direct, w_query, w_keyval)], *sums, *tokens)
 
 
 def after_kernel(*refs):
@@ -269,48 +281,35 @@
     return pl.pallas_call(
         after_kernel,
         out_shape=[shape(x.shape, x.dtype) for x in arrays],
-        in_specs=[HBM] * skip + [ANY] * count,
+        in_specs=[ANY] * (count + skip),
         out_specs=[ANY] * count,
         input_output_aliases={i + skip: i for i in range(count)},
         compiler_params=params(1),
         cost_estimate=cost(flops, 1),
         name="after",
-    )(*[hbm(token) for token in tokens], *arrays)
+    )(*tokens, *arrays)
 
 
 def turn(values, cosine, sine):
     return values * cosine + pltpu.roll(values, HD // 2, 1) * sine
 
 
-def late_kernel(table_ref, *refs):
-    x_refs = refs[:2]
-    q_in, kv_in, sq_in, cos_ref, sin_ref, wq_ref, wkv_ref, _ = refs[2:10]
-    q_out, keys_out, values_out, send_out = refs[10:14]
-    wq_buf, wkv_buf, q_buf, keys_buf, values_buf, page_buf, w_sems, sems, page_sems = refs[14:]
-    weights = weight_copies((wq_ref, wkv_ref), (wq_buf, wkv_buf), w_sems, LATE)
+def late_kernel(table_ref, x_ref, q_in, kv_in, sq_in, wq_ref, wkv_ref, cos_ref, sin_ref, *refs):
+    q_out, keys_out, values_out, send_out = refs[:4]
+    q_buf, keys_buf, values_buf, page_buf, sems, page_sems = refs[4:]
     row = lax.broadcasted_iota(jnp.int32, (2 * PAGE, 2 * PAGE), 0)
     column = lax.broadcasted_iota(jnp.int32, (2 * PAGE, 2 * PAGE), 1)
     picker = (column == (row >> 1) + (row & 1) * PAGE).astype(BF16)
     values_buf[:, HD:] = jnp.ones((ROWS, HD), BF16)
-    inv_norms = []
+    copies = []
     for r in range(0, ROWS, TILE):
         rows = slice(r, r + TILE)
-        squares = sq_in[rows, :] + squares_of(x_refs[0][rows, :]) + squares_of(x_refs[1][rows, :])
+        x = x_ref[rows, :]
+        kv_sum = kv_in[rows, :] + jnp.dot(x, wkv_ref[0], preferred_element_type=F32)
+        q_sum = q_in[rows, :] + jnp.dot(x, wq_ref[0], preferred_element_type=F32)
+        squares = sq_in[rows, :] + squares_of(x)
         mean = jnp.sum(squares, axis=1, keepdims=True) / D
-        inv_norms.append(jnp.broadcast_to(lax.rsqrt(mean + 1e-05), (TILE, HD)))
-    copies = []
-    for group in weights:
-        for copy in group:
-            copy.wait()
-    for r in range(0, ROWS, TILE):
-        rows = slice(r, r + TILE)
-        inv_norm = inv_norms[r // TILE]
-        kv_sum = kv_in[rows, :]
-        q_sum = q_in[rows, :]
-        for i in range(2):
-            x = x_refs[i][rows, :]
-            kv_sum += jnp.dot(x, wkv_buf[i], preferred_element_type=F32)
-            q_sum += jnp.dot(x, wq_buf[i], preferred_element_type=F32)
+        inv_norm = jnp.broadcast_to(lax.rsqrt(mean + 1e-05), (TILE, HD))
         cosine, sine = cos_ref[rows, :], sin_ref[rows, :]
         keys = turn(kv_sum[:, :HD] * inv_norm, cosine, sine).astype(BF16)
         values = (kv_sum[:, HD:] * inv_norm).astype(BF16)
@@ -339,27 +338,24 @@
         copy.wait()
 
 
-def project_late(table, blocks, sums, cosine, sine, w_query, w_keyval, token):
+def project_late(table, block, sums, cosine, sine):
     results = [(HEADS, ROWS, HD), (ROWS, HD), (ROWS, 2 * HD)]
     return pl.pallas_call(
         late_kernel,
         out_shape=[pltpu.HBM(x, BF16) for x in results]
         + [pltpu.HBM((POOL * PUSH_CAP, 2 * PAGE, HD), BF16)],
-        in_specs=[SMEM] + [VMEM] * 7 + [HBM] * 2 + [ANY],
+        in_specs=[SMEM] + [VMEM] * 8,
         out_specs=[HBM] * 4,
         scratch_shapes=[
-            pltpu.VMEM((2, FEAT, QW), BF16),
-            pltpu.VMEM((2, FEAT, KVW), BF16),
             *[pltpu.VMEM(x, BF16) for x in results],
             pltpu.VMEM((NEW_PAGES, 2 * PAGE, HD), BF16),
-            pltpu.SemaphoreType.DMA((4,)),
             pltpu.SemaphoreType.DMA((3 * ROWS // TILE,)),
             pltpu.SemaphoreType.DMA((NEW_PAGES,)),
         ],
         compiler_params=params(16),
         cost_estimate=cost(0, 1),
         name="project_late",
-    )(table, *blocks, *sums, cosine, sine, hbm(w_query), hbm(w_keyval), token)
+    )(table, block, *sums, cosine, sine)
 
 
 def dot_nt(a, b):
@@ -480,14 +476,20 @@
     near, back = shift(hidden, (1, -1)), shift(hidden, (-1, 1))
     far = shift(near, (1, -1))
     table, packed = prelude(page_owner, page_slot, new_owner, store.reshape(64, 2 * PAGE, HD))
-    (pages,) = after((), exchange(packed), flops=PIN)
+    pages = exchange(packed)
     cosine, sine = rope_tables(ROWS, PAGES * PAGE)
-    direct = (hidden, near, back)
-    sums = project_early([swap(x) for x in direct], direct, w_query, w_keyval)
+    weights = (w_query, w_keyval)
+    blocks = ((OWN, True), (OWN, False), (NEAR, False), (BACK, False))
+    tables = (cosine, sine)
+    sums = project(
+        blocks, [swap(hidden)], [hidden, near, back], *weights, tokens=tables, flops=HIDES
+    )
+    blocks = ((NEAR, True), (BACK, True))
+    sums = project(blocks, [swap(near), swap(back)], [], *weights, sums)
     (far,) = after((sums[2],), far)
-    queries, own_keys, own_values, send = project_late(
-        table, (far, swap(far)), sums, cosine, sine, w_query, w_keyval, pages
-    )
+    other = swap(far)
+    sums = project(((FAR, False),), [far], [], *weights, sums, ((FAR, True),))
+    queries, own_keys, own_values, send = project_late(table, other, sums, cosine, sine)
     received = exchange(send)
     keys, values = split_pages(table, pages)
     attended = attend(queries, own_keys, own_values, keys, values)

time: 82.5 us -> 77.8 us (0.943)
  waiting for transfers between devices: 27.7 us -> 23.4 us
    pallas_call x1, Pallas kernels: 7.3 us -> 3.41 us  [project_late(): pl.pallas_call(late_kernel, out_shape=[pltpu.HBM(x, BF16) for x in result...]
    pallas_call x1 -> x3, Pallas kernels: 8.31 us -> 11.7 us  [project(): pl.pallas_call(functools.partial(project_kernel, blocks, len(held), bool(...]
    ppermute x4, waiting for transfers between devices: 2.28 us -> 0.01 us  [swap(): return lax.ppermute(values, 'tp', [(i, i ^ 1) for i in range(8)])]
    ppermute x3, waiting for transfers between devices: 17.1 us -> 15 us  [shift(): return lax.ppermute(values, 'tp', pairs)]
  transfers between devices with their start and end apart: 9 -> 9, of which waited for: 7 -> 4; matrix products, arithmetic and copies ran while one was open for 2% -> 2% of each run, Pallas kernels for 28% -> 38%
where the time goes in v6:
time: 77.8 us; the launch traced here: 77.5 us
  Pallas kernels  31.2 us (40%)
  waiting for transfers between devices  23.4 us (30%)
  starting transfers between devices  20.7 us (27%)
  other arithmetic  1.21 us (2%)
  between operations  0.92 us (1%)
    ppermute x3, waiting for transfers between devices, shift(): return lax.ppermute(values, 'tp', pairs)  15 us
    all_to_all x2, starting transfers between devices, exchange(): lax.all_to_all(values, 'pool', split_axis=0, concat_axis=0, tiled=True)  13.8 us
    pallas_call x3, Pallas kernels, project(): pl.pallas_call(functools.partial(project_kernel, blocks, len(held), bool(...  11.7 us
    pallas_call x1, Pallas kernels, attend(): pl.pallas_call(attend_kernel, out_shape=shape((ROWS, QW), BF16), in_specs...  9.3 us
    all_to_all x2, waiting for transfers between devices, exchange(): lax.all_to_all(values, 'pool', split_axis=0, concat_axis=0, tiled=True)  8.41 us
    ppermute x3, starting transfers between devices, shift(): return lax.ppermute(values, 'tp', pairs)  5.03 us
    pallas_call x1, Pallas kernels, prelude(): pl.pallas_call(prelude_kernel, out_shape=[shape((24, HD), jnp.int32), plt...  3.82 us
    pallas_call x1, Pallas kernels, project_late(): pl.pallas_call(late_kernel, out_shape=[pltpu.HBM(x, BF16) for x in result...  3.41 us
  transfers between devices with their start and end apart: 9, of which 4 were waited for; matrix products, arithmetic and copies ran while one was open for 2% of the time, Pallas kernels for 38%

profile of v6, /device:TPU:0, one launch (start us, length us, event | category | flops | bytes accessed | tf_op | source)
XLA Modules:
  0.0 77.5 jit_solution(444706901474119520)
XLA Ops:
  0.6 2.1 %collective-permute-start = (bf16[512,1024]{1,0:T(8,128)(2,1)}, bf16[512,1024]{1,0:T(8,128)(2,1)}, u32[]{:S(2)}, u32[]{:S(2)}) collective-permute-start(bf16[512,1024]{1,0:T(8,128)(2,1)} %refs_1_.2), channel_id=1, source_target_pairs={{0,2},{1,7},{2,4},{3,1},{4,6},{5,3},{6,0},{7,5},{8,10},{9,15},{10,... | collective-permute-start | bytes 3145736 | tf_op jit(solution)/shard_map/ppermute | solution.py:455
  2.7 2.2 %collective-permute-start.2 = (bf16[512,1024]{1,0:T(8,128)(2,1)}, bf16[512,1024]{1,0:T(8,128)(2,1)}, u32[]{:S(2)}, u32[]{:S(2)}) collective-permute-start(bf16[512,1024]{1,0:T(8,128)(2,1)} %refs_1_.2), channel_id=1, source_target_pairs={{0,6},{1,3},{2,0},{3,5},{4,2},{5,7},{6,4},{7,1},{8,14},{9,11},{10,... | collective-permute-start | bytes 3145736 | tf_op jit(solution)/shard_map/ppermute | solution.py:455
  4.9 0.0 collective-permute-start.4
  4.9 3.8 %prelude.1 = (s32[24,128]{1,0:T(8,128)S(1)}, bf16[64,128,128]{2,1,0:T(8,128)(2,1)}) custom-call(s32[16,32]{1,0:T(8,128)} %owner_in.1, s32[16,32]{1,0:T(8,128)} %slot_in.1, s32[8,16]{1,0:T(8,128)} %bitcast.7, bf16[64,128,128]{2,1,0:T(8,128)(2,1)} %bitcast.5), custom_call_target="tpu_custom_call" | custom-call | bytes 1 | tf_op jit(solution)/shard_map/prelude/pallas_call | solution.py:119
  8.7 7.0 %all-to-all-start = ((bf16[64,128,128]{2,1,0:T(8,128)(2,1)}), bf16[64,128,128]{2,1,0:T(8,128)(2,1)S(1)}, u32[]{:S(2)}, u32[]{:S(2)}) async-start(bf16[64,128,128]{2,1,0:T(8,128)(2,1)} %get-tuple-element.36), calls=%async_computation | async-start | bytes 4194304 | tf_op jit(solution)/shard_map/all_to_all | solution.py:472
  15.8 1.0 %fusion = (f32[512,64]{1,0:T(8,128)S(1)}, f32[512,64]{1,0:T(8,128)S(1)}, f32[512,64]{1,0:T(8,128)S(1)}) fusion(f32[64]{0:T(128)S(1)} %negate_power_fusion, f32[512]{0:T(512)S(1)} %add_convert_fusion), kind=kLoop, calls=%fused_computation.4 | loop fusion | flops 65536 | bytes 395520 | tf_op jit(solution)/shard_map/neg | solution.py:468
  16.8 0.2 pad_maximum_fusion
  17.0 10.2 %collective-permute-done.refs_2_ = bf16[512,1024]{1,0:T(8,128)(2,1)} collective-permute-done((bf16[512,1024]{1,0:T(8,128)(2,1)}, bf16[512,1024]{1,0:T(8,128)(2,1)}, u32[]{:S(2)}, u32[]{:S(2)}) %collective-permute-start) | collective-permute-done | bytes 1048608 | tf_op jit(solution)/shard_map/ppermute | solution.py:455
  27.3 0.8 collective-permute-start.5
  28.0 1.8 %collective-permute-start.1 = (bf16[512,1024]{1,0:T(8,128)(2,1)}, bf16[512,1024]{1,0:T(8,128)(2,1)S(1)}, u32[]{:S(2)}, u32[]{:S(2)}) collective-permute-start(bf16[512,1024]{1,0:T(8,128)(2,1)} %collective-permute-done.refs_2_), channel_id=1, source_target_pairs={{0,1},{1,0},{2,3},{3,2},{4,5},{5,4},{6,7},{7,6},{8,9},{9,8},{10,11... | collective-permute-start | bytes 3145736 | tf_op jit(solution)/shard_map/ppermute | solution.py:459
  29.8 0.0 collective-permute-done.2.refs_3_
  29.8 0.0 collective-permute-start.3
  29.8 0.0 collective-permute-done.4.refs_0_
  29.8 5.2 %project.3 = (f32[512,512]{1,0:T(8,128)S(1)}, f32[512,256]{1,0:T(8,128)S(1)}, f32[512,128]{1,0:T(8,128)S(1)}) custom-call(bf16[512,1024]{1,0:T(8,128)(2,1)S(1)} %collective-permute-done.4.refs_0_, bf16[512,1024]{1,0:T(8,128)(2,1)} %refs_1_.2, bf16[512,1024]{1,0:T(8,128)(2,1)} %collective-permute-done.refs_2_, ...), custom_call_target="tpu_custom_call" | custom-call | flops 20000000000 | bytes 1 | tf_op jit(solution)/shard_map/project/pallas_call | solution.py:253
  35.1 0.0 collective-permute-done.3.refs_1_
  35.1 0.0 collective-permute-done.1.refs_0_
  35.1 3.6 %project.4 = (f32[512,512]{1,0:T(8,128)S(1)}, f32[512,256]{1,0:T(8,128)S(1)}, f32[512,128]{1,0:T(8,128)S(1)}) custom-call(bf16[512,1024]{1,0:T(8,128)(2,1)S(1)} %collective-permute-done.1.refs_0_, bf16[512,1024]{1,0:T(8,128)(2,1)S(1)} %collective-permute-done.3.refs_1_, bf16[8192,512]{1,0:T(8,128)(2,1)} %refs_1_.3, bf16[8192,256]{1,0:T(8,128)(2,1)} %refs_2_.3, ...), custom_call_target="tpu_custom_call" | custom-call | bytes 1 | tf_op jit(solution)/shard_map/project/pallas_call | solution.py:253
  38.7 4.8 %collective-permute-done.5.refs_1_ = bf16[512,1024]{1,0:T(8,128)(2,1)S(1)} collective-permute-done((bf16[512,1024]{1,0:T(8,128)(2,1)}, bf16[512,1024]{1,0:T(8,128)(2,1)S(1)}, u32[]{:S(2)}, u32[]{:S(2)}) %collective-permute-start.5) | collective-permute-done | bytes 1048608 | tf_op jit(solution)/shard_map/ppermute | solution.py:455
  43.5 0.0 collective-permute-start.6
  43.5 2.8 %project.5 = (f32[512,512]{1,0:T(8,128)S(1)}, f32[512,256]{1,0:T(8,128)S(1)}, f32[512,128]{1,0:T(8,128)S(1)}, bf16[1,1024,512]{2,1,0:T(8,128)(2,1)S(1)}, bf16[1,1024,256]{2,1,0:T(8,128)(2,1)S(1)}) custom-call(bf16[512,1024]{1,0:T(8,128)(2,1)S(1)} %after.1.refs_0_, bf16[8192,512]{1,0:T(8,128)(2,1)} %refs_1_.3, bf16[8192,256]{1,0:T(8,128)(2,1)} %refs_2_.3, ...), custom_call_target="tpu_custom_call" | custom-call | bytes 1 | tf_op jit(solution)/shard_map/project/pallas_call | solution.py:253
  46.4 0.0 collective-permute-done.6.x_ref
  46.4 3.4 %project_late.1 = (bf16[4,512,128]{2,1,0:T(8,128)(2,1)}, bf16[512,128]{1,0:T(8,128)(2,1)}, bf16[512,256]{1,0:T(8,128)(2,1)}, bf16[32,128,128]{2,1,0:T(8,128)(2,1)}) custom-call(s32[24,128]{1,0:T(8,128)S(1)} %get-tuple-element.21.table_ref, bf16[512,1024]{1,0:T(8,128)(2,1)S(1)} %collective-permute-done.6.x_ref, f32[512,512]{1,0:T(8,128)S(1)} %get-tuple-element.28.q_in, ...), custom_call_target="tpu_custom_call" | custom-call | bytes 1 | tf_op jit(solution)/shard_map/project_late/pallas_call | solution.py:343
  49.8 0.3 all-to-all-done.pages_ref
  50.0 6.8 %all-to-all-start.1 = ((bf16[32,128,128]{2,1,0:T(8,128)(2,1)}), bf16[32,128,128]{2,1,0:T(8,128)(2,1)S(1)}, u32[]{:S(2)}, u32[]{:S(2)}) async-start(bf16[32,128,128]{2,1,0:T(8,128)(2,1)} %get-tuple-element.39), calls=%async_computation.1 | async-start | bytes 2097152 | tf_op jit(solution)/shard_map/all_to_all | solution.py:472
  56.8 1.2 %split_pages.1 = (bf16[2048,128]{1,0:T(8,128)(2,1)S(1)}, bf16[2048,256]{1,0:T(8,128)(2,1)S(1)}) custom-call(s32[24,128]{1,0:T(8,128)S(1)} %get-tuple-element.21.table_ref, bf16[64,128,128]{2,1,0:T(8,128)(2,1)S(1)} %all-to-all-done.pages_ref), custom_call_target="tpu_custom_call" | custom-call | flops 134217728 | bytes 4194304 | tf_op jit(solution)/shard_map/split_pages/pallas_call | solution.py:156
  58.1 9.3 %attend.1 = bf16[512,512]{1,0:T(8,128)(2,1)} custom-call(bf16[4,512,128]{2,1,0:T(8,128)(2,1)} %get-tuple-element.33.q_ref, bf16[512,128]{1,0:T(8,128)(2,1)} %get-tuple-element.34.own_keys_ref, bf16[512,256]{1,0:T(8,128)(2,1)} %get-tuple-element.35.own_values_ref, bf16[2048,128]{1,0:T(8,128)(2,1)S(1)} %get-tuple-element.37.keys_ref, ...), custom_call_target="tpu_custom_call" | custom-call | flops 5368709120 | bytes 8388608 | tf_op jit(solution)/shard_map/attend/pallas_call | solution.py:402
  67.4 8.2 %all-to-all-done.1.received_ref = bf16[32,128,128]{2,1,0:T(8,128)(2,1)S(1)} async-done(((bf16[32,128,128]{2,1,0:T(8,128)(2,1)}), bf16[32,128,128]{2,1,0:T(8,128)(2,1)S(1)}, u32[]{:S(2)}, u32[]{:S(2)}) %all-to-all-start.1) | async-done | bytes 1048608 | tf_op jit(solution)/shard_map/all_to_all | solution.py:472
  75.5 1.8 %place_pages.1 = bf16[32,128,128]{2,1,0:T(8,128)(2,1)} custom-call(s32[24,128]{1,0:T(8,128)S(1)} %get-tuple-element.21.table_ref, bf16[32,128,128]{2,1,0:T(8,128)(2,1)S(1)} %all-to-all-done.1.received_ref), custom_call_target="tpu_custom_call" | custom-call | bytes 2097152 | tf_op jit(solution)/shard_map/place_pages/pallas_call | solution.py:438
  (3 shorter events, 0.0 us)
Async XLA Ops:
  0.6 26.6 %collective-permute-start = (bf16[512,1024]{1,0:T(8,128)(2,1)}, bf16[512,1024]{1,0:T(8,128)(2,1)}, u32[]{:S(2)}, u32[]{:S(2)}) collective-permute-start(bf16[512,1024]{1,0:T(8,128)(2,1)} %refs_1_.2), channel_id=1, source_target_pairs={{0,2},{1,7},{2,4},{3,1},{4,6},{5,3},{6,0},{7,5},{8,10},{9,15},{10,... | collective-permute-start | bytes 3145736 | tf_op jit(solution)/shard_map/ppermute | solution.py:455
  2.7 27.1 %collective-permute-start.2 = (bf16[512,1024]{1,0:T(8,128)(2,1)}, bf16[512,1024]{1,0:T(8,128)(2,1)}, u32[]{:S(2)}, u32[]{:S(2)}) collective-permute-start(bf16[512,1024]{1,0:T(8,128)(2,1)} %refs_1_.2), channel_id=1, source_target_pairs={{0,6},{1,3},{2,0},{3,5},{4,2},{5,7},{6,4},{7,1},{8,14},{9,11},{10,... | collective-permute-start | bytes 3145736 | tf_op jit(solution)/shard_map/ppermute | solution.py:455
  4.9 24.9 %collective-permute-start.4 = (bf16[512,1024]{1,0:T(8,128)(2,1)}, bf16[512,1024]{1,0:T(8,128)(2,1)S(1)}, u32[]{:S(2)}, u32[]{:S(2)}) collective-permute-start(bf16[512,1024]{1,0:T(8,128)(2,1)} %refs_1_.2), channel_id=1, source_target_pairs={{0,1},{1,0},{2,3},{3,2},{4,5},{5,4},{6,7},{7,6},{8,9},{9,8},{10,11... | collective-permute-start | bytes 3145736 | tf_op jit(solution)/shard_map/ppermute | solution.py:459
  8.7 41.3 %all-to-all-start = ((bf16[64,128,128]{2,1,0:T(8,128)(2,1)}), bf16[64,128,128]{2,1,0:T(8,128)(2,1)S(1)}, u32[]{:S(2)}, u32[]{:S(2)}) async-start(bf16[64,128,128]{2,1,0:T(8,128)(2,1)} %get-tuple-element.36), calls=%async_computation | async-start | bytes 4194304 | tf_op jit(solution)/shard_map/all_to_all | solution.py:472
  27.3 16.2 %collective-permute-start.5 = (bf16[512,1024]{1,0:T(8,128)(2,1)}, bf16[512,1024]{1,0:T(8,128)(2,1)S(1)}, u32[]{:S(2)}, u32[]{:S(2)}) collective-permute-start(bf16[512,1024]{1,0:T(8,128)(2,1)} %collective-permute-done.refs_2_), channel_id=1, source_target_pairs={{0,2},{1,7},{2,4},{3,1},{4,6},{5,3},{6,0},{7,5},{8,10},{9,15},{10,... | collective-permute-start | bytes 3145736 | tf_op jit(solution)/shard_map/ppermute | solution.py:455
  28.0 7.1 %collective-permute-start.1 = (bf16[512,1024]{1,0:T(8,128)(2,1)}, bf16[512,1024]{1,0:T(8,128)(2,1)S(1)}, u32[]{:S(2)}, u32[]{:S(2)}) collective-permute-start(bf16[512,1024]{1,0:T(8,128)(2,1)} %collective-permute-done.refs_2_), channel_id=1, source_target_pairs={{0,1},{1,0},{2,3},{3,2},{4,5},{5,4},{6,7},{7,6},{8,9},{9,8},{10,11... | collective-permute-start | bytes 3145736 | tf_op jit(solution)/shard_map/ppermute | solution.py:459
  29.8 5.3 %collective-permute-start.3 = (bf16[512,1024]{1,0:T(8,128)(2,1)}, bf16[512,1024]{1,0:T(8,128)(2,1)S(1)}, u32[]{:S(2)}, u32[]{:S(2)}) collective-permute-start(bf16[512,1024]{1,0:T(8,128)(2,1)} %collective-permute-done.2.refs_3_), channel_id=1, source_target_pairs={{0,1},{1,0},{2,3},{3,2},{4,5},{5,4},{6,7},{7,6},{8,9},{9,8},{10,11... | collective-permute-start | bytes 3145736 | tf_op jit(solution)/shard_map/ppermute | solution.py:459
  43.5 2.9 %collective-permute-start.6 = (bf16[512,1024]{1,0:T(8,128)(2,1)S(1)}, bf16[512,1024]{1,0:T(8,128)(2,1)S(1)}, u32[]{:S(2)}, u32[]{:S(2)}) collective-permute-start(bf16[512,1024]{1,0:T(8,128)(2,1)S(1)} %after.1.refs_0_), channel_id=1, source_target_pairs={{0,1},{1,0},{2,3},{3,2},{4,5},{5,4},{6,7},{7,6},{8,9},{9,8},{10,11... | collective-permute-start | bytes 3145736 | tf_op jit(solution)/shard_map/ppermute | solution.py:459
  50.0 25.5 %all-to-all-start.1 = ((bf16[32,128,128]{2,1,0:T(8,128)(2,1)}), bf16[32,128,128]{2,1,0:T(8,128)(2,1)S(1)}, u32[]{:S(2)}, u32[]{:S(2)}) async-start(bf16[32,128,128]{2,1,0:T(8,128)(2,1)} %get-tuple-element.39), calls=%async_computation.1 | async-start | bytes 2097152 | tf_op jit(solution)/shard_map/all_to_all | solution.py:472

commit v7 on v6

--- a/solution.py
+++ b/solution.py
@@ -85,13 +85,15 @@
     out_ref[PLACE : PLACE + 1, :SLOTS] = jnp.sum(source, axis=0, keepdims=True)
 
 
-def prelude_kernel(owner_in, slot_in, target_in, store_in, table_ref, out_ref, *scratch):
-    owner_ref, slot_ref, target_ref, store_ref, index_ref, sems, page_sems = scratch
+def prelude_kernel(*refs):
+    owner_in, slot_in, target_in, store_in, hidden_in, table_ref, out_ref, hidden_out = refs[:8]
+    owner_ref, slot_ref, target_ref, store_ref, hidden_ref, index_ref, sems, page_sems = refs[8:]
     pairs = (
         (owner_in, owner_ref),
         (slot_in, slot_ref),
         (target_in, target_ref),
         (store_in, store_ref),
+        (hidden_in, hidden_ref),
     )
     copies = [pltpu.make_async_copy(x, y, sems.at[i]) for i, (x, y) in enumerate(pairs)]
     for copy in copies:
@@ -99,8 +101,11 @@
     for copy in copies[:3]:
         copy.wait()
     fill_table(owner_ref[...], slot_ref[...], target_ref[...], table_ref)
-    indices = pltpu.make_async_copy(table_ref, index_ref, sems.at[4])
+    indices = pltpu.make_async_copy(table_ref, index_ref, sems.at[5])
     indices.start()
+    copies[4].wait()
+    hidden_copy = pltpu.make_async_copy(hidden_ref, hidden_out, sems.at[6])
+    hidden_copy.start()
     indices.wait()
     copies[3].wait()
     pages = [
@@ -113,30 +118,33 @@
         page.start()
     for page in pages:
         page.wait()
-
-
-def prelude(page_owner, page_slot, new_owner, store):
+    hidden_copy.wait()
+
+
+def prelude(page_owner, page_slot, new_owner, store, hidden):
     return pl.pallas_call(
         prelude_kernel,
         out_shape=[
             shape((24, HD), jnp.int32),
             pltpu.HBM((POOL * CAP, 2 * PAGE, HD), BF16),
-        ],
-        in_specs=[HBM] * 4,
-        out_specs=[VMEM, HBM],
+            pltpu.HBM(hidden.shape, BF16),
+        ],
+        in_specs=[HBM] * 5,
+        out_specs=[VMEM, HBM, HBM],
         scratch_shapes=[
             pltpu.VMEM((POOL, PAGES), jnp.int32),
             pltpu.VMEM((POOL, PAGES), jnp.int32),
             pltpu.VMEM((NEW_PAGES, POOL), jnp.int32),
             pltpu.VMEM(store.shape, BF16),
+            pltpu.VMEM(hidden.shape, BF16),
             pltpu.SMEM((24, HD), jnp.int32),
-            pltpu.SemaphoreType.DMA((5,)),
+            pltpu.SemaphoreType.DMA((7,)),
             pltpu.SemaphoreType.DMA((POOL * CAP,)),
         ],
         compiler_params=params(8),
         cost_estimate=cost(0, 1),
         name="prelude",
-    )(hbm(page_owner), hbm(page_slot), hbm(new_owner.T), hbm(store))
+    )(*[hbm(x) for x in (page_owner, page_slot, new_owner.T, store, hidden)])
 
 
 def split_kernel(table_ref, pages_ref, keys_ref, values_ref):
@@ -272,6 +280,28 @@
     )(*held, *[hbm(x) for x in (*direct, w_query, w_keyval)], *sums, *tokens)
 
 
+def far_kernel(x_ref, wq_ref, wkv_ref, *refs):
+    before, sums = refs[:3], refs[3:]
+    for r in range(0, ROWS, TILE):
+        rows = slice(r, r + TILE)
+        x = x_ref[rows, :]
+        sums[0][rows, :] = before[0][rows, :] + jnp.dot(x, wq_ref[0], preferred_element_type=F32)
+        sums[1][rows, :] = before[1][rows, :] + jnp.dot(x, wkv_ref[0], preferred_element_type=F32)
+        sums[2][rows, :] = before[2][rows, :] + squares_of(x)
+
+
+def project_far(block, weights, sums):
+    return pl.pallas_call(
+        far_kernel,
+        out_shape=[shape((ROWS, w), F32) for w in (QW, KVW, HD)],
+        in_specs=[VMEM] * 6,
+        out_specs=[VMEM] * 3,
+        compiler_params=params(16),
+        cost_estimate=cost(0, 1),
+        name="project_far",
+    )(block, *weights, *sums)
+
+
 def after_kernel(*refs):
     pass
 
@@ -296,7 +326,9 @@
 
 def late_kernel(table_ref, x_ref, q_in, kv_in, sq_in, wq_ref, wkv_ref, cos_ref, sin_ref, *refs):
     q_out, keys_out, values_out, send_out = refs[:4]
-    q_buf, keys_buf, values_buf, page_buf, sems, page_sems = refs[4:]
+    q_buf, keys_buf, values_buf, page_buf, index_ref, index_sem, sems, page_sems = refs[4:]
+    indices = pltpu.make_async_copy(table_ref, index_ref, index_sem)
+    indices.start()
     row = lax.broadcasted_iota(jnp.int32, (2 * PAGE, 2 * PAGE), 0)
     column = lax.broadcasted_iota(jnp.int32, (2 * PAGE, 2 * PAGE), 1)
     picker = (column == (row >> 1) + (row & 1) * PAGE).astype(BF16)
@@ -305,8 +337,8 @@
     for r in range(0, ROWS, TILE):
         rows = slice(r, r + TILE)
         x = x_ref[rows, :]
-        kv_sum = kv_in[rows, :] + jnp.dot(x, wkv_ref[0], preferred_element_type=F32)
-        q_sum = q_in[rows, :] + jnp.dot(x, wq_ref[0], preferred_element_type=F32)
+        kv_sum = kv_in[rows, :] + jnp.dot(x, wkv_ref[1], preferred_element_type=F32)
+        q_sum = q_in[rows, :] + jnp.dot(x, wq_ref[1], preferred_element_type=F32)
         squares = sq_in[rows, :] + squares_of(x)
         mean = jnp.sum(squares, axis=1, keepdims=True) / D
         inv_norm = jnp.broadcast_to(lax.rsqrt(mean + 1e-05), (TILE, HD))
@@ -315,11 +347,13 @@
         values = (kv_sum[:, HD:] * inv_norm).astype(BF16)
         keys_buf[rows, :] = keys
         values_buf[rows, :HD] = values
+        if r == 0:
+            indices.wait()
         for p in range(0, TILE, PAGE):
             page = (r + p) // PAGE
             both = jnp.concatenate([keys[p : p + PAGE], values[p : p + PAGE]], axis=0)
             page_buf[page] = jnp.dot(picker, both, preferred_element_type=F32).astype(BF16)
-            target = send_out.at[table_ref[page, PUSH]]
+            target = send_out.at[index_ref[page, PUSH]]
             copies.append(pltpu.make_async_copy(page_buf.at[page], target, page_sems.at[page]))
             copies[-1].start()
         for head in range(HEADS):
@@ -338,24 +372,26 @@
         copy.wait()
 
 
-def project_late(table, block, sums, cosine, sine):
+def project_late(table, block, sums, weights, cosine, sine):
     results = [(HEADS, ROWS, HD), (ROWS, HD), (ROWS, 2 * HD)]
     return pl.pallas_call(
         late_kernel,
         out_shape=[pltpu.HBM(x, BF16) for x in results]
         + [pltpu.HBM((POOL * PUSH_CAP, 2 * PAGE, HD), BF16)],
-        in_specs=[SMEM] + [VMEM] * 8,
+        in_specs=[VMEM] * 9,
         out_specs=[HBM] * 4,
         scratch_shapes=[
             *[pltpu.VMEM(x, BF16) for x in results],
             pltpu.VMEM((NEW_PAGES, 2 * PAGE, HD), BF16),
+            pltpu.SMEM((24, HD), jnp.int32),
+            pltpu.SemaphoreType.DMA,
             pltpu.SemaphoreType.DMA((3 * ROWS // TILE,)),
             pltpu.SemaphoreType.DMA((NEW_PAGES,)),
         ],
         compiler_params=params(16),
         cost_estimate=cost(0, 1),
         name="project_late",
-    )(table, block, *sums, cosine, sine)
+    )(table, block, *sums, *weights, cosine, sine)
 
 
 def dot_nt(a, b):
@@ -473,23 +509,29 @@
 
 
 def body(hidden, w_query, w_keyval, store, page_owner, page_slot, new_owner):
-    near, back = shift(hidden, (1, -1)), shift(hidden, (-1, 1))
+    near = shift(hidden, (1, -1))
+    table, packed, again = prelude(
+        page_owner, page_slot, new_owner, store.reshape(64, 2 * PAGE, HD), hidden
+    )
+    pages = exchange(packed)
+    back = shift(again, (-1, 1))
+    tables = rope_tables(ROWS, PAGES * PAGE)
+    weights = (w_query, w_keyval)
+    blocks = ((OWN, True), (OWN, False))
+    sums = project(blocks, [swap(hidden)], [hidden], *weights, tokens=tables)
+    (near,) = after((sums[2],), near)
     far = shift(near, (1, -1))
-    table, packed = prelude(page_owner, page_slot, new_owner, store.reshape(64, 2 * PAGE, HD))
-    pages = exchange(packed)
-    cosine, sine = rope_tables(ROWS, PAGES * PAGE)
-    weights = (w_query, w_keyval)
-    blocks = ((OWN, True), (OWN, False), (NEAR, False), (BACK, False))
-    tables = (cosine, sine)
-    sums = project(
-        blocks, [swap(hidden)], [hidden, near, back], *weights, tokens=tables, flops=HIDES
-    )
-    blocks = ((NEAR, True), (BACK, True))
-    sums = project(blocks, [swap(near), swap(back)], [], *weights, sums)
+    blocks = ((NEAR, False), (BACK, False))
+    sums = project(blocks, [], [near, back], *weights, sums, flops=HIDES)
+    blocks, ahead = ((NEAR, True), (BACK, True)), ((FAR, False), (FAR, True))
+    held = [swap(near), swap(back)]
+    *sums, last_q, last_kv = project(blocks, held, [], *weights, sums, ahead)
     (far,) = after((sums[2],), far)
     other = swap(far)
-    sums = project(((FAR, False),), [far], [], *weights, sums, ((FAR, True),))
-    queries, own_keys, own_values, send = project_late(table, other, sums, cosine, sine)
+    sums = project_far(far, (last_q, last_kv), sums)
+    queries, own_keys, own_values, send = project_late(
+        table, other, sums, (last_q, last_kv), *tables
+    )
     received = exchange(send)
     keys, values = split_pages(table, pages)
     attended = attend(queries, own_keys, own_values, keys, values)

time: 77.8 us -> 73.3 us (0.942)
  waiting for transfers between devices: 23.4 us -> 17.3 us
  Pallas kernels: 31.2 us -> 33.1 us
    ppermute x3, waiting for transfers between devices: 15 us -> 5.39 us  [shift(): return lax.ppermute(values, 'tp', pairs)]
    all_to_all x2, starting transfers between devices: 13.8 us -> 11 us  [exchange(): lax.all_to_all(values, 'pool', split_axis=0, concat_axis=0, tiled=True)]
    all_to_all x2, waiting for transfers between devices: 8.41 us -> 10.3 us  [exchange(): lax.all_to_all(values, 'pool', split_axis=0, concat_axis=0, tiled=True)]
    ppermute x3, starting transfers between devices: 5.03 us -> 6.66 us  [shift(): return lax.ppermute(values, 'tp', pairs)]
    ppermute x4, waiting for transfers between devices: 0.01 us -> 1.61 us  [swap(): return lax.ppermute(values, 'tp', [(i, i ^ 1) for i in range(8)])]
    pallas_call x0 -> x1, Pallas kernels: none -> 1.05 us  [project_far(): pl.pallas_call(far_kernel, out_shape=[shape((ROWS, w), F32) for w in (QW,...]
    ppermute x4, starting transfers between devices: 1.81 us -> 2.66 us  [swap(): return lax.ppermute(values, 'tp', [(i, i ^ 1) for i in range(8)])]
    pallas_call x3, Pallas kernels: 11.7 us -> 12.5 us  [project(): pl.pallas_call(functools.partial(project_kernel, blocks, len(held), bool(...]
  transfers between devices with their start and end apart: 9 -> 9, of which waited for: 4 -> 6; matrix products, arithmetic and copies ran while one was open for 2% -> 2% of each run, Pallas kernels for 38% -> 43%
where the time goes in v7:
time: 73.3 us; the launch traced here: 72.9 us
  Pallas kernels  33.1 us (45%)
  starting transfers between devices  20.4 us (28%)
  waiting for transfers between devices  17.3 us (24%)
  other arithmetic  1.21 us (2%)
  between operations  0.93 us (1%)
    pallas_call x3, Pallas kernels, project(): pl.pallas_call(functools.partial(project_kernel, blocks, len(held), bool(...  12.5 us
    all_to_all x2, starting transfers between devices, exchange(): lax.all_to_all(values, 'pool', split_axis=0, concat_axis=0, tiled=True)  11 us
    all_to_all x2, waiting for transfers between devices, exchange(): lax.all_to_all(values, 'pool', split_axis=0, concat_axis=0, tiled=True)  10.3 us
    pallas_call x1, Pallas kernels, attend(): pl.pallas_call(attend_kernel, out_shape=shape((ROWS, QW), BF16), in_specs...  9.3 us
    ppermute x3, starting transfers between devices, shift(): return lax.ppermute(values, 'tp', pairs)  6.66 us
    ppermute x3, waiting for transfers between devices, shift(): return lax.ppermute(values, 'tp', pairs)  5.39 us
    pallas_call x1, Pallas kernels, prelude(): pl.pallas_call(prelude_kernel, out_shape=[shape((24, HD), jnp.int32), plt...  4.15 us
    pallas_call x1, Pallas kernels, project_late(): pl.pallas_call(late_kernel, out_shape=[pltpu.HBM(x, BF16) for x in result...  3.07 us
  transfers between devices with their start and end apart: 9, of which 6 were waited for; matrix products, arithmetic and copies ran while one was open for 2% of the time, Pallas kernels for 43%

profile of v7, /device:TPU:0, one launch (start us, length us, event | category | flops | bytes accessed | tf_op | source)
XLA Modules:
  0.0 72.9 jit_solution(5438806938704060275)
XLA Ops:
  0.6 0.1 collective-permute-start
  0.7 2.1 %collective-permute-start.1 = (bf16[512,1024]{1,0:T(8,128)(2,1)}, bf16[512,1024]{1,0:T(8,128)(2,1)S(1)}, u32[]{:S(2)}, u32[]{:S(2)}) collective-permute-start(bf16[512,1024]{1,0:T(8,128)(2,1)} %refs_1_.3), channel_id=1, source_target_pairs={{0,2},{1,7},{2,4},{3,1},{4,6},{5,3},{6,0},{7,5},{8,10},{9,15},{10,... | collective-permute-start | bytes 3145736 | tf_op jit(solution)/shard_map/ppermute | solution.py:491
  2.8 4.2 %prelude.1 = (s32[24,128]{1,0:T(8,128)S(1)}, bf16[64,128,128]{2,1,0:T(8,128)(2,1)}, bf16[512,1024]{1,0:T(8,128)(2,1)}) custom-call(s32[16,32]{1,0:T(8,128)} %refs_0_.1, s32[16,32]{1,0:T(8,128)} %refs_1_.2, s32[8,16]{1,0:T(8,128)} %bitcast.7, bf16[64,128,128]{2,1,0:T(8,128)(2,1)} %bitcast.5, bf16[512,1024]{1,0:T(8,128)(2,1)} %refs_1_.3), custom_call_target="tpu_custom_call" | custom-call | bytes 1 | tf_op jit(solution)/shard_map/prelude/pallas_call | solution.py:125
  7.0 2.2 %collective-permute-start.3 = (bf16[512,1024]{1,0:T(8,128)(2,1)}, bf16[512,1024]{1,0:T(8,128)(2,1)}, u32[]{:S(2)}, u32[]{:S(2)}) collective-permute-start(bf16[512,1024]{1,0:T(8,128)(2,1)} %get-tuple-element.27), channel_id=1, source_target_pairs={{0,6},{1,3},{2,0},{3,5},{4,2},{5,7},{6,4},{7,1},{8,14},{9,11},{10,... | collective-permute-start | bytes 3145736 | tf_op jit(solution)/shard_map/ppermute | solution.py:491
  9.2 7.0 %all-to-all-start = ((bf16[64,128,128]{2,1,0:T(8,128)(2,1)}), bf16[64,128,128]{2,1,0:T(8,128)(2,1)S(1)}, u32[]{:S(2)}, u32[]{:S(2)}) async-start(bf16[64,128,128]{2,1,0:T(8,128)(2,1)} %get-tuple-element.44), calls=%async_computation | async-start | bytes 4194304 | tf_op jit(solution)/shard_map/all_to_all | solution.py:508
  16.2 1.0 %fusion = (f32[512,64]{1,0:T(8,128)S(1)}, f32[512,64]{1,0:T(8,128)S(1)}, f32[512,64]{1,0:T(8,128)S(1)}) fusion(f32[64]{0:T(128)S(1)} %negate_power_fusion, f32[512]{0:T(512)S(1)} %add_convert_fusion), kind=kLoop, calls=%fused_computation.4 | loop fusion | flops 65536 | bytes 395520 | tf_op jit(solution)/shard_map/neg | solution.py:504
  17.2 0.2 pad_maximum_fusion
  17.4 0.0 collective-permute-done.refs_0_
  17.4 4.9 %project.3 = (f32[512,512]{1,0:T(8,128)S(1)}, f32[512,256]{1,0:T(8,128)S(1)}, f32[512,128]{1,0:T(8,128)S(1)}) custom-call(bf16[512,1024]{1,0:T(8,128)(2,1)} %collective-permute-done.refs_0_, bf16[512,1024]{1,0:T(8,128)(2,1)} %refs_1_.3, bf16[8192,512]{1,0:T(8,128)(2,1)} %refs_2_.5, bf16[8192,256]{1,0:T(8,128)(2,1)} %refs_3_.5, ...), custom_call_target="tpu_custom_call" | custom-call | bytes 1 | tf_op jit(solution)/shard_map/project/pallas_call | solution.py:261
  22.3 0.1 collective-permute-done.1.refs_1_
  22.4 0.0 copy-start
  22.4 2.4 %collective-permute-start.5 = (bf16[512,1024]{1,0:T(8,128)(2,1)S(1)}, bf16[512,1024]{1,0:T(8,128)(2,1)S(1)}, u32[]{:S(2)}, u32[]{:S(2)}) collective-permute-start(bf16[512,1024]{1,0:T(8,128)(2,1)S(1)} %after.2.refs_0_), channel_id=1, source_target_pairs={{0,2},{1,7},{2,4},{3,1},{4,6},{5,3},{6,0},{7,5},{8,10},{9,15},{10,... | collective-permute-start | bytes 3145736 | tf_op jit(solution)/shard_map/ppermute | solution.py:491
  24.8 2.1 %collective-permute-start.2 = (bf16[512,1024]{1,0:T(8,128)(2,1)S(1)}, bf16[512,1024]{1,0:T(8,128)(2,1)S(1)}, u32[]{:S(2)}, u32[]{:S(2)}) collective-permute-start(bf16[512,1024]{1,0:T(8,128)(2,1)S(1)} %after.2.refs_0_), channel_id=1, source_target_pairs={{0,1},{1,0},{2,3},{3,2},{4,5},{5,4},{6,7},{7,6},{8,9},{9,8},{10,11... | collective-permute-start | bytes 3145736 | tf_op jit(solution)/shard_map/ppermute | solution.py:495
  26.9 2.1 %collective-permute-done.3.refs_1_ = bf16[512,1024]{1,0:T(8,128)(2,1)} collective-permute-done((bf16[512,1024]{1,0:T(8,128)(2,1)}, bf16[512,1024]{1,0:T(8,128)(2,1)}, u32[]{:S(2)}, u32[]{:S(2)}) %collective-permute-start.3) | collective-permute-done | bytes 1048608 | tf_op jit(solution)/shard_map/ppermute | solution.py:491
  29.0 0.5 collective-permute-start.4
  29.5 0.0 copy-done
  29.5 3.8 %project.4 = (f32[512,512]{1,0:T(8,128)S(1)}, f32[512,256]{1,0:T(8,128)S(1)}, f32[512,128]{1,0:T(8,128)S(1)}) custom-call(bf16[512,1024]{1,0:T(8,128)(2,1)} %copy-done, bf16[512,1024]{1,0:T(8,128)(2,1)} %collective-permute-done.3.refs_1_, bf16[8192,512]{1,0:T(8,128)(2,1)} %refs_2_.5, bf16[8192,256]{1,0:T(8,128)(2,1)} %refs_3_.5, ...), custom_call_target="tpu_custom_call" | custom-call | flops 20000000000 | bytes 1 | tf_op jit(solution)/shard_map/project/pallas_call | solution.py:261
  33.3 0.0 collective-permute-done.2.refs_0_
  33.3 0.0 collective-permute-done.4.refs_1_
  33.4 3.9 %project.5 = (f32[512,512]{1,0:T(8,128)S(1)}, f32[512,256]{1,0:T(8,128)S(1)}, f32[512,128]{1,0:T(8,128)S(1)}, bf16[2,1024,512]{2,1,0:T(8,128)(2,1)S(1)}, bf16[2,1024,256]{2,1,0:T(8,128)(2,1)S(1)}) custom-call(bf16[512,1024]{1,0:T(8,128)(2,1)S(1)} %collective-permute-done.2.refs_0_, bf16[512,1024]{1,0:T(8,128)(2,1)S(1)} %collective-permute-done.4.refs_1_, ...), custom_call_target="tpu_custom_call" | custom-call | bytes 1 | tf_op jit(solution)/shard_map/project/pallas_call | solution.py:261
  37.2 3.2 %collective-permute-done.5.refs_1_ = bf16[512,1024]{1,0:T(8,128)(2,1)S(1)} collective-permute-done((bf16[512,1024]{1,0:T(8,128)(2,1)S(1)}, bf16[512,1024]{1,0:T(8,128)(2,1)S(1)}, u32[]{:S(2)}, u32[]{:S(2)}) %collective-permute-start.5) | collective-permute-done | bytes 1048608 | tf_op jit(solution)/shard_map/ppermute | solution.py:491
  40.4 0.0 collective-permute-start.6
  40.4 1.1 %project_far.1 = (f32[512,512]{1,0:T(8,128)S(1)}, f32[512,256]{1,0:T(8,128)S(1)}, f32[512,128]{1,0:T(8,128)S(1)}) custom-call(bf16[512,1024]{1,0:T(8,128)(2,1)S(1)} %after.3.x_ref, bf16[2,1024,512]{2,1,0:T(8,128)(2,1)S(1)} %get-tuple-element.34.wq_ref, bf16[2,1024,256]{2,1,0:T(8,128)(2,1)S(1)} %get-tuple-element.35.wkv_ref, ...), custom_call_target="tpu_custom_call" | custom-call | bytes 1 | tf_op jit(solution)/shard_map/project_far/pallas_call | solution.py:294
  41.4 1.6 %collective-permute-done.6.x_ref = bf16[512,1024]{1,0:T(8,128)(2,1)S(1)} collective-permute-done((bf16[512,1024]{1,0:T(8,128)(2,1)S(1)}, bf16[512,1024]{1,0:T(8,128)(2,1)S(1)}, u32[]{:S(2)}, u32[]{:S(2)}) %collective-permute-start.6) | collective-permute-done | bytes 1048608 | tf_op jit(solution)/shard_map/ppermute | solution.py:495
  43.0 3.1 %project_late.1 = (bf16[4,512,128]{2,1,0:T(8,128)(2,1)}, bf16[512,128]{1,0:T(8,128)(2,1)}, bf16[512,256]{1,0:T(8,128)(2,1)}, bf16[32,128,128]{2,1,0:T(8,128)(2,1)}) custom-call(s32[24,128]{1,0:T(8,128)S(1)} %get-tuple-element.25.table_ref, bf16[512,1024]{1,0:T(8,128)(2,1)S(1)} %collective-permute-done.6.x_ref, f32[512,512]{1,0:T(8,128)S(1)} %get-tuple-element.38.q_in, ...), custom_call_target="tpu_custom_call" | custom-call | bytes 1 | tf_op jit(solution)/shard_map/project_late/pallas_call | solution.py:377
  46.1 3.1 %all-to-all-done.pages_ref = bf16[64,128,128]{2,1,0:T(8,128)(2,1)S(1)} async-done(((bf16[64,128,128]{2,1,0:T(8,128)(2,1)}), bf16[64,128,128]{2,1,0:T(8,128)(2,1)S(1)}, u32[]{:S(2)}, u32[]{:S(2)}) %all-to-all-start) | async-done | bytes 2097184 | tf_op jit(solution)/shard_map/all_to_all | solution.py:508
  49.2 4.0 %all-to-all-start.1 = ((bf16[32,128,128]{2,1,0:T(8,128)(2,1)}), bf16[32,128,128]{2,1,0:T(8,128)(2,1)S(1)}, u32[]{:S(2)}, u32[]{:S(2)}) async-start(bf16[32,128,128]{2,1,0:T(8,128)(2,1)} %get-tuple-element.47), calls=%async_computation.1 | async-start | bytes 2097152 | tf_op jit(solution)/shard_map/all_to_all | solution.py:508
  53.2 1.2 %split_pages.1 = (bf16[2048,128]{1,0:T(8,128)(2,1)S(1)}, bf16[2048,256]{1,0:T(8,128)(2,1)S(1)}) custom-call(s32[24,128]{1,0:T(8,128)S(1)} %get-tuple-element.25.table_ref, bf16[64,128,128]{2,1,0:T(8,128)(2,1)S(1)} %all-to-all-done.pages_ref), custom_call_target="tpu_custom_call" | custom-call | flops 134217728 | bytes 4194304 | tf_op jit(solution)/shard_map/split_pages/pallas_call | solution.py:164
  54.4 9.3 %attend.1 = bf16[512,512]{1,0:T(8,128)(2,1)} custom-call(bf16[4,512,128]{2,1,0:T(8,128)(2,1)} %get-tuple-element.41.q_ref, bf16[512,128]{1,0:T(8,128)(2,1)} %get-tuple-element.42.own_keys_ref, bf16[512,256]{1,0:T(8,128)(2,1)} %get-tuple-element.43.own_values_ref, bf16[2048,128]{1,0:T(8,128)(2,1)S(1)} %get-tuple-element.45.keys_ref, ...), custom_call_target="tpu_custom_call" | custom-call | flops 5368709120 | bytes 8388608 | tf_op jit(solution)/shard_map/attend/pallas_call | solution.py:438
  63.7 7.3 %all-to-all-done.1.received_ref = bf16[32,128,128]{2,1,0:T(8,128)(2,1)S(1)} async-done(((bf16[32,128,128]{2,1,0:T(8,128)(2,1)}), bf16[32,128,128]{2,1,0:T(8,128)(2,1)S(1)}, u32[]{:S(2)}, u32[]{:S(2)}) %all-to-all-start.1) | async-done | bytes 1048608 | tf_op jit(solution)/shard_map/all_to_all | solution.py:508
  71.0 1.8 %place_pages.1 = bf16[32,128,128]{2,1,0:T(8,128)(2,1)} custom-call(s32[24,128]{1,0:T(8,128)S(1)} %get-tuple-element.25.table_ref, bf16[32,128,128]{2,1,0:T(8,128)(2,1)S(1)} %all-to-all-done.1.received_ref), custom_call_target="tpu_custom_call" | custom-call | bytes 2097152 | tf_op jit(solution)/shard_map/place_pages/pallas_call | solution.py:474
  (4 shorter events, 0.0 us)
Async XLA Ops:
  0.6 16.8 %collective-permute-start = (bf16[512,1024]{1,0:T(8,128)(2,1)}, bf16[512,1024]{1,0:T(8,128)(2,1)}, u32[]{:S(2)}, u32[]{:S(2)}) collective-permute-start(bf16[512,1024]{1,0:T(8,128)(2,1)} %refs_1_.3), channel_id=1, source_target_pairs={{0,1},{1,0},{2,3},{3,2},{4,5},{5,4},{6,7},{7,6},{8,9},{9,8},{10,11... | collective-permute-start | bytes 3145736 | tf_op jit(solution)/shard_map/ppermute | solution.py:495
  0.7 21.7 %collective-permute-start.1 = (bf16[512,1024]{1,0:T(8,128)(2,1)}, bf16[512,1024]{1,0:T(8,128)(2,1)S(1)}, u32[]{:S(2)}, u32[]{:S(2)}) collective-permute-start(bf16[512,1024]{1,0:T(8,128)(2,1)} %refs_1_.3), channel_id=1, source_target_pairs={{0,2},{1,7},{2,4},{3,1},{4,6},{5,3},{6,0},{7,5},{8,10},{9,15},{10,... | collective-permute-start | bytes 3145736 | tf_op jit(solution)/shard_map/ppermute | solution.py:491
  7.0 22.0 %collective-permute-start.3 = (bf16[512,1024]{1,0:T(8,128)(2,1)}, bf16[512,1024]{1,0:T(8,128)(2,1)}, u32[]{:S(2)}, u32[]{:S(2)}) collective-permute-start(bf16[512,1024]{1,0:T(8,128)(2,1)} %get-tuple-element.27), channel_id=1, source_target_pairs={{0,6},{1,3},{2,0},{3,5},{4,2},{5,7},{6,4},{7,1},{8,14},{9,11},{10,... | collective-permute-start | bytes 3145736 | tf_op jit(solution)/shard_map/ppermute | solution.py:491
  9.2 40.0 %all-to-all-start = ((bf16[64,128,128]{2,1,0:T(8,128)(2,1)}), bf16[64,128,128]{2,1,0:T(8,128)(2,1)S(1)}, u32[]{:S(2)}, u32[]{:S(2)}) async-start(bf16[64,128,128]{2,1,0:T(8,128)(2,1)} %get-tuple-element.44), calls=%async_computation | async-start | bytes 4194304 | tf_op jit(solution)/shard_map/all_to_all | solution.py:508
  22.4 7.1 %copy-start = (bf16[512,1024]{1,0:T(8,128)(2,1)}, bf16[512,1024]{1,0:T(8,128)(2,1)S(1)}, u32[]{:S(2)}) copy-start(bf16[512,1024]{1,0:T(8,128)(2,1)S(1)} %after.2.refs_0_) | copy-start | bytes 3145732
  22.4 17.9 %collective-permute-start.5 = (bf16[512,1024]{1,0:T(8,128)(2,1)S(1)}, bf16[512,1024]{1,0:T(8,128)(2,1)S(1)}, u32[]{:S(2)}, u32[]{:S(2)}) collective-permute-start(bf16[512,1024]{1,0:T(8,128)(2,1)S(1)} %after.2.refs_0_), channel_id=1, source_target_pairs={{0,2},{1,7},{2,4},{3,1},{4,6},{5,3},{6,0},{7,5},{8,10},{9,15},{10,... | collective-permute-start | bytes 3145736 | tf_op jit(solution)/shard_map/ppermute | solution.py:491
  24.8 8.5 %collective-permute-start.2 = (bf16[512,1024]{1,0:T(8,128)(2,1)S(1)}, bf16[512,1024]{1,0:T(8,128)(2,1)S(1)}, u32[]{:S(2)}, u32[]{:S(2)}) collective-permute-start(bf16[512,1024]{1,0:T(8,128)(2,1)S(1)} %after.2.refs_0_), channel_id=1, source_target_pairs={{0,1},{1,0},{2,3},{3,2},{4,5},{5,4},{6,7},{7,6},{8,9},{9,8},{10,11... | collective-permute-start | bytes 3145736 | tf_op jit(solution)/shard_map/ppermute | solution.py:495
  29.0 4.3 %collective-permute-start.4 = (bf16[512,1024]{1,0:T(8,128)(2,1)}, bf16[512,1024]{1,0:T(8,128)(2,1)S(1)}, u32[]{:S(2)}, u32[]{:S(2)}) collective-permute-start(bf16[512,1024]{1,0:T(8,128)(2,1)} %collective-permute-done.3.refs_1_), channel_id=1, source_target_pairs={{0,1},{1,0},{2,3},{3,2},{4,5},{5,4},{6,7},{7,6},{8,9},{9,8},{10,11... | collective-permute-start | bytes 3145736 | tf_op jit(solution)/shard_map/ppermute | solution.py:495
  40.4 2.7 %collective-permute-start.6 = (bf16[512,1024]{1,0:T(8,128)(2,1)S(1)}, bf16[512,1024]{1,0:T(8,128)(2,1)S(1)}, u32[]{:S(2)}, u32[]{:S(2)}) collective-permute-start(bf16[512,1024]{1,0:T(8,128)(2,1)S(1)} %after.3.x_ref), channel_id=1, source_target_pairs={{0,1},{1,0},{2,3},{3,2},{4,5},{5,4},{6,7},{7,6},{8,9},{9,8},{10,11... | collective-permute-start | bytes 3145736 | tf_op jit(solution)/shard_map/ppermute | solution.py:495
  49.2 21.8 %all-to-all-start.1 = ((bf16[32,128,128]{2,1,0:T(8,128)(2,1)}), bf16[32,128,128]{2,1,0:T(8,128)(2,1)S(1)}, u32[]{:S(2)}, u32[]{:S(2)}) async-start(bf16[32,128,128]{2,1,0:T(8,128)(2,1)} %get-tuple-element.47), calls=%async_computation.1 | async-start | bytes 2097152 | tf_op jit(solution)/shard_map/all_to_all | solution.py:508

commit v8 on v7

--- a/solution.py
+++ b/solution.py
@@ -145,34 +145,6 @@
         cost_estimate=cost(0, 1),
         name="prelude",
     )(*[hbm(x) for x in (page_owner, page_slot, new_owner.T, store, hidden)])
-
-
-def split_kernel(table_ref, pages_ref, keys_ref, values_ref):
-    row = lax.broadcasted_iota(jnp.int32, (2 * PAGE, 2 * PAGE), 0)
-    column = lax.broadcasted_iota(jnp.int32, (2 * PAGE, 2 * PAGE), 1)
-    wanted = jnp.where(row < PAGE, 2 * row, 2 * (row - PAGE) + 1)
-    picker = (column == wanted).astype(BF16)
-    values_ref[:, HD:] = jnp.ones((PAGES * PAGE, HD), BF16)
-    for page in range(PAGES):
-        both = jnp.dot(picker, pages_ref[table_ref[TAKE, page]], preferred_element_type=F32)
-        rows = pl.ds(page * PAGE, PAGE)
-        keys_ref[rows, :] = both[:PAGE].astype(BF16)
-        values_ref[rows, :HD] = both[PAGE:].astype(BF16)
-
-
-def split_pages(table, pages):
-    return pl.pallas_call(
-        split_kernel,
-        out_shape=[
-            shape((PAGES * PAGE, HD), BF16),
-            shape((PAGES * PAGE, 2 * HD), BF16),
-        ],
-        in_specs=[SMEM, VMEM],
-        out_specs=[VMEM, VMEM],
-        compiler_params=params(8),
-        cost_estimate=cost(2 * 2048 * 128 * 256, 4 * MIB),
-        name="split_pages",
-    )(table, pages)
 
 
 def block_index(steps, other_core):
@@ -293,7 +265,7 @@
 def project_far(block, weights, sums):
     return pl.pallas_call(
         far_kernel,
-        out_shape=[shape((ROWS, w), F32) for w in (QW, KVW, HD)],
+        out_shape=[pltpu.HBM((ROWS, QW), F32)] + [shape((ROWS, w), F32) for w in (KVW, HD)],
         in_specs=[VMEM] * 6,
         out_specs=[VMEM] * 3,
         compiler_params=params(16),
@@ -324,26 +296,26 @@
     return values * cosine + pltpu.roll(values, HD // 2, 1) * sine
 
 
-def late_kernel(table_ref, x_ref, q_in, kv_in, sq_in, wq_ref, wkv_ref, cos_ref, sin_ref, *refs):
-    q_out, keys_out, values_out, send_out = refs[:4]
-    q_buf, keys_buf, values_buf, page_buf, index_ref, index_sem, sems, page_sems = refs[4:]
-    indices = pltpu.make_async_copy(table_ref, index_ref, index_sem)
+def keyval_kernel(table_ref, x_ref, kv_in, sq_in, wkv_ref, cos_ref, sin_ref, *refs):
+    keys_out, values_out, inv_out, x_out, send_out = refs[:5]
+    keys_buf, values_buf, inv_buf, page_buf, index_ref, sems, page_sems = refs[5:]
+    indices = pltpu.make_async_copy(table_ref, index_ref, sems.at[0])
     indices.start()
+    copies = [pltpu.make_async_copy(x_ref, x_out, sems.at[1])]
+    copies[0].start()
     row = lax.broadcasted_iota(jnp.int32, (2 * PAGE, 2 * PAGE), 0)
     column = lax.broadcasted_iota(jnp.int32, (2 * PAGE, 2 * PAGE), 1)
     picker = (column == (row >> 1) + (row & 1) * PAGE).astype(BF16)
     values_buf[:, HD:] = jnp.ones((ROWS, HD), BF16)
-    copies = []
     for r in range(0, ROWS, TILE):
         rows = slice(r, r + TILE)
         x = x_ref[rows, :]
         kv_sum = kv_in[rows, :] + jnp.dot(x, wkv_ref[1], preferred_element_type=F32)
-        q_sum = q_in[rows, :] + jnp.dot(x, wq_ref[1], preferred_element_type=F32)
         squares = sq_in[rows, :] + squares_of(x)
         mean = jnp.sum(squares, axis=1, keepdims=True) / D
         inv_norm = jnp.broadcast_to(lax.rsqrt(mean + 1e-05), (TILE, HD))
-        cosine, sine = cos_ref[rows, :], sin_ref[rows, :]
-        keys = turn(kv_sum[:, :HD] * inv_norm, cosine, sine).astype(BF16)
+        inv_buf[rows, :] = inv_norm
+        keys = turn(kv_sum[:, :HD] * inv_norm, cos_ref[rows, :], sin_ref[rows, :]).astype(BF16)
         values = (kv_sum[:, HD:] * inv_norm).astype(BF16)
         keys_buf[rows, :] = keys
         values_buf[rows, :HD] = values
@@ -356,60 +328,69 @@
             target = send_out.at[index_ref[page, PUSH]]
             copies.append(pltpu.make_async_copy(page_buf.at[page], target, page_sems.at[page]))
             copies[-1].start()
-        for head in range(HEADS):
-            part = q_sum[:, head * HD : (head + 1) * HD] * inv_norm
-            q_buf[head, rows, :] = turn(part, cosine, sine).astype(BF16)
-        span = pl.ds(r, TILE)
-        results = (
-            (q_buf.at[:, span, :], q_out.at[:, span, :]),
-            (keys_buf.at[span, :], keys_out.at[span, :]),
-            (values_buf.at[span, :], values_out.at[span, :]),
-        )
-        for i, (source, target) in enumerate(results):
-            copies.append(pltpu.make_async_copy(source, target, sems.at[3 * (r // TILE) + i]))
-            copies[-1].start()
+    results = ((keys_buf, keys_out), (values_buf, values_out), (inv_buf, inv_out))
+    for i, (source, target) in enumerate(results):
+        copies.append(pltpu.make_async_copy(source, target, sems.at[2 + i]))
+        copies[-1].start()
     for copy in copies:
         copy.wait()
 
 
-def project_late(table, block, sums, weights, cosine, sine):
-    results = [(HEADS, ROWS, HD), (ROWS, HD), (ROWS, 2 * HD)]
-    return pl.pallas_call(
-        late_kernel,
-        out_shape=[pltpu.HBM(x, BF16) for x in results]
-        + [pltpu.HBM((POOL * PUSH_CAP, 2 * PAGE, HD), BF16)],
-        in_specs=[VMEM] * 9,
-        out_specs=[HBM] * 4,
+def project_keyval(table, block, sums, weights, cosine, sine):
+    kept = [((ROWS, HD), BF16), ((ROWS, 2 * HD), BF16), ((ROWS, HD), F32)]
+    sent = (POOL * PUSH_CAP, 2 * PAGE, HD)
+    return pl.pallas_call(
+        keyval_kernel,
+        out_shape=[pltpu.HBM(*x) for x in (*kept, ((ROWS, FEAT), BF16), (sent, BF16))],
+        in_specs=[VMEM] * 7,
+        out_specs=[HBM] * 5,
         scratch_shapes=[
-            *[pltpu.VMEM(x, BF16) for x in results],
+            *[pltpu.VMEM(*x) for x in kept],
             pltpu.VMEM((NEW_PAGES, 2 * PAGE, HD), BF16),
             pltpu.SMEM((24, HD), jnp.int32),
-            pltpu.SemaphoreType.DMA,
-            pltpu.SemaphoreType.DMA((3 * ROWS // TILE,)),
+            pltpu.SemaphoreType.DMA((5,)),
             pltpu.SemaphoreType.DMA((NEW_PAGES,)),
         ],
         compiler_params=params(16),
         cost_estimate=cost(0, 1),
-        name="project_late",
-    )(table, block, *sums, *weights, cosine, sine)
+        name="project_keyval",
+    )(table, block, *sums, weights, cosine, sine)
 
 
 def dot_nt(a, b):
     return lax.dot_general(a, b, (((1,), (1,)), ((), ())), preferred_element_type=F32)
 
 
-def attend_kernel(q_ref, own_keys_ref, own_values_ref, keys_ref, values_ref, out_ref, *scratch):
-    q_buf, own_keys, own_values, sems = scratch
-    copies = [
-        pltpu.make_async_copy(source, target, sems.at[i])
-        for i, (source, target) in enumerate(
-            ((q_ref, q_buf), (own_keys_ref, own_keys), (own_values_ref, own_values))
-        )
-    ]
+def attend_kernel(table_ref, pages_ref, *refs):
+    sources, wq_ref, out_ref, refs = refs[:7], refs[7], refs[8], refs[9:]
+    targets, wq_buf, index_ref, q_buf, keys, values, sems = refs[:7], *refs[7:]
+    q_sum, x, inv_norm, cosine, sine, own_keys, own_values = targets
+    indices = pltpu.make_async_copy(table_ref, index_ref, sems.at[8])
+    indices.start()
+    copies = [pltpu.make_async_copy(a, b, sems.at[i]) for i, (a, b) in enumerate(zip(sources, targets))]
+    rows = pl.ds(pl.multiple_of(block_index(FAR, True) * FEAT, FEAT), FEAT)
+    copies.insert(0, pltpu.make_async_copy(wq_ref.at[rows, :], wq_buf, sems.at[7]))
     for copy in copies:
         copy.start()
+    row = lax.broadcasted_iota(jnp.int32, (2 * PAGE, 2 * PAGE), 0)
+    column = lax.broadcasted_iota(jnp.int32, (2 * PAGE, 2 * PAGE), 1)
+    wanted = jnp.where(row < PAGE, 2 * row, 2 * (row - PAGE) + 1)
+    picker = (column == wanted).astype(BF16)
+    values[:, HD:] = jnp.ones((PAGES * PAGE, HD), BF16)
+    indices.wait()
+    for page in range(PAGES):
+        both = jnp.dot(picker, pages_ref[index_ref[TAKE, page]], preferred_element_type=F32)
+        rows = slice(page * PAGE, (page + 1) * PAGE)
+        keys[rows, :] = both[:PAGE].astype(BF16)
+        values[rows, :HD] = both[PAGE:].astype(BF16)
     for copy in copies:
         copy.wait()
+    for r in range(0, ROWS, TILE):
+        rows = slice(r, r + TILE)
+        total = q_sum[rows, :] + jnp.dot(x[rows, :], wq_buf[...], preferred_element_type=F32)
+        for head in range(HEADS):
+            part = total[:, head * HD : (head + 1) * HD] * inv_norm[rows, :]
+            q_buf[head, rows, :] = turn(part, cosine[rows, :], sine[rows, :]).astype(BF16)
     block = 256
     allowed = lax.broadcasted_iota(jnp.int32, (block, block), 0) >= lax.broadcasted_iota(
         jnp.int32, (block, block), 1
@@ -424,7 +405,7 @@
             parts = [(diagonal, own_values[rows, :])]
             if b:
                 parts.append((own[:, : b * block], own_values[: b * block, :]))
-            parts.append((dot_nt(queries, keys_ref[...]), values_ref[...]))
+            parts.append((dot_nt(queries, keys[...]), values[...]))
             tops = [jnp.max(scores, axis=1, keepdims=True) for scores, _ in parts]
             top = functools.reduce(jnp.maximum, tops)
             both = jnp.zeros((block, 2 * HD), F32)
@@ -434,22 +415,25 @@
             out_ref[rows, lanes] = (both[:, :HD] / both[:, HD:]).astype(BF16)
 
 
-def attend(queries, own_keys, own_values, keys, values):
+def attend(table, pages, sources, w_query):
     return pl.pallas_call(
         attend_kernel,
         out_shape=shape((ROWS, QW), BF16),
-        in_specs=[HBM] * 3 + [VMEM] * 2,
+        in_specs=[VMEM] * 2 + [HBM] * (len(sources) + 1),
         out_specs=VMEM,
         scratch_shapes=[
+            *[pltpu.VMEM(x.shape, x.dtype) for x in sources],
+            pltpu.VMEM((FEAT, QW), BF16),
+            pltpu.SMEM((24, HD), jnp.int32),
             pltpu.VMEM((HEADS, ROWS, HD), BF16),
-            pltpu.VMEM((ROWS, HD), BF16),
-            pltpu.VMEM((ROWS, 2 * HD), BF16),
-            pltpu.SemaphoreType.DMA((3,)),
+            pltpu.VMEM((PAGES * PAGE, HD), BF16),
+            pltpu.VMEM((PAGES * PAGE, 2 * HD), BF16),
+            pltpu.SemaphoreType.DMA((9,)),
         ],
         compiler_params=params(40),
         cost_estimate=cost(2 * ROWS * 4 * 2560 * 512, 8 * MIB),
         name="attend",
-    )(hbm(queries), hbm(own_keys), hbm(own_values), keys, values)
+    )(table, pages, *[hbm(x) for x in (*sources, w_query)])
 
 
 def place_kernel(table_ref, received_ref, out_ref, buffer, sems):
@@ -518,23 +502,23 @@
     tables = rope_tables(ROWS, PAGES * PAGE)
     weights = (w_query, w_keyval)
     blocks = ((OWN, True), (OWN, False))
-    sums = project(blocks, [swap(hidden)], [hidden], *weights, tokens=tables)
+    sums = project(blocks, [swap(hidden)], [hidden], *weights, tokens=tables, flops=HIDES)
     (near,) = after((sums[2],), near)
     far = shift(near, (1, -1))
     blocks = ((NEAR, False), (BACK, False))
-    sums = project(blocks, [], [near, back], *weights, sums, flops=HIDES)
+    sums = project(blocks, [near, back], [], *weights, sums, flops=HIDES)
     blocks, ahead = ((NEAR, True), (BACK, True)), ((FAR, False), (FAR, True))
     held = [swap(near), swap(back)]
     *sums, last_q, last_kv = project(blocks, held, [], *weights, sums, ahead)
     (far,) = after((sums[2],), far)
     other = swap(far)
     sums = project_far(far, (last_q, last_kv), sums)
-    queries, own_keys, own_values, send = project_late(
-        table, other, sums, (last_q, last_kv), *tables
+    own_keys, own_values, inv_norm, other, send = project_keyval(
+        table, other, sums[1:], last_kv, *tables
     )
     received = exchange(send)
-    keys, values = split_pages(table, pages)
-    attended = attend(queries, own_keys, own_values, keys, values)
+    sources = (sums[0], other, inv_norm, *tables, own_keys, own_values)
+    attended = attend(table, pages, sources, w_query)
     placed = place_pages(table, received)
     return attended, placed.reshape(SLOTS, 1, PAGE, 2, HD)
 

time: 73.3 us -> 76.1 us (1.038); the launches traced: 72.9 us -> 74.6 us
  starting transfers between devices: 20.4 us -> 23 us
  waiting for transfers between devices: 17.3 us -> 15.7 us
    all_to_all x2, waiting for transfers between devices: 10.3 us -> 7.14 us  [exchange(): lax.all_to_all(values, 'pool', split_axis=0, concat_axis=0, tiled=True)]
    all_to_all x2, starting transfers between devices: 11 us -> 13.7 us  [exchange(): lax.all_to_all(values, 'pool', split_axis=0, concat_axis=0, tiled=True)]
    ppermute x3, waiting for transfers between devices: 5.39 us -> 7.93 us  [shift(): return lax.ppermute(values, 'tp', pairs)]
    ppermute x3, starting transfers between devices: 6.66 us -> 4.35 us  [shift(): return lax.ppermute(values, 'tp', pairs)]
    ppermute x4, starting transfers between devices: 2.66 us -> 4.94 us  [swap(): return lax.ppermute(values, 'tp', [(i, i ^ 1) for i in range(8)])]
    pallas_call x1, Pallas kernels: 9.3 us -> 10.6 us  [attend(): pl.pallas_call(attend_kernel, out_shape=shape((ROWS, QW), BF16), in_specs...]
    ppermute x4, waiting for transfers between devices: 1.61 us -> 0.63 us  [swap(): return lax.ppermute(values, 'tp', [(i, i ^ 1) for i in range(8)])]
    pallas_call x3 -> x2, Pallas kernels: 5.33 us -> 4.7 us  [the longest x1 2.67 us: project_keyval(): pl.pallas_call(keyval_kernel, out_shape=[pltpu.HBM(*x) for x in (*kept, (...]
  transfers between devices with their start and end apart: 9 -> 9, of which waited for: 6 -> 3; matrix products, arithmetic and copies ran while one was open for 2% -> 2% of each run, Pallas kernels for 43% -> 43%
where the time goes in v8:
time: 76.1 us; the launch traced here: 74.6 us
  Pallas kernels  33.7 us (44%)
  starting transfers between devices  23 us (30%)
  waiting for transfers between devices  15.7 us (21%)
  other arithmetic  1.22 us (2%)
  between operations  0.98 us (1%)
    all_to_all x2, starting transfers between devices, exchange(): lax.all_to_all(values, 'pool', split_axis=0, concat_axis=0, tiled=True)  13.7 us
    pallas_call x3, Pallas kernels, project(): pl.pallas_call(functools.partial(project_kernel, blocks, len(held), bool(...  12.5 us
    pallas_call x1, Pallas kernels, attend(): pl.pallas_call(attend_kernel, out_shape=shape((ROWS, QW), BF16), in_specs...  10.6 us
    ppermute x3, waiting for transfers between devices, shift(): return lax.ppermute(values, 'tp', pairs)  7.93 us
    all_to_all x2, waiting for transfers between devices, exchange(): lax.all_to_all(values, 'pool', split_axis=0, concat_axis=0, tiled=True)  7.14 us
    ppermute x4, starting transfers between devices, swap(): return lax.ppermute(values, 'tp', [(i, i ^ 1) for i in range(8)])  4.94 us
    ppermute x3, starting transfers between devices, shift(): return lax.ppermute(values, 'tp', pairs)  4.35 us
    pallas_call x1, Pallas kernels, prelude(): pl.pallas_call(prelude_kernel, out_shape=[shape((24, HD), jnp.int32), plt...  4.15 us
  transfers between devices with their start and end apart: 9, of which 3 were waited for; matrix products, arithmetic and copies ran while one was open for 2% of the time, Pallas kernels for 43%

profile of v8, /device:TPU:0, one launch (start us, length us, event | category | flops | bytes accessed | tf_op | source)
XLA Modules:
  0.0 74.6 jit_solution(11611123360991531729)
XLA Ops:
  0.6 0.1 collective-permute-start
  0.7 2.1 %collective-permute-start.1 = (bf16[512,1024]{1,0:T(8,128)(2,1)}, bf16[512,1024]{1,0:T(8,128)(2,1)S(1)}, u32[]{:S(2)}, u32[]{:S(2)}) collective-permute-start(bf16[512,1024]{1,0:T(8,128)(2,1)} %refs_1_.3), channel_id=1, source_target_pairs={{0,2},{1,7},{2,4},{3,1},{4,6},{5,3},{6,0},{7,5},{8,10},{9,15},{10,... | collective-permute-start | bytes 3145736 | tf_op jit(solution)/shard_map/ppermute | solution.py:475
  2.8 4.2 %prelude.1 = (s32[24,128]{1,0:T(8,128)S(1)}, bf16[64,128,128]{2,1,0:T(8,128)(2,1)}, bf16[512,1024]{1,0:T(8,128)(2,1)}) custom-call(s32[16,32]{1,0:T(8,128)} %refs_0_.1, s32[16,32]{1,0:T(8,128)} %refs_1_.2, s32[8,16]{1,0:T(8,128)} %bitcast.7, bf16[64,128,128]{2,1,0:T(8,128)(2,1)} %bitcast.5, bf16[512,1024]{1,0:T(8,128)(2,1)} %refs_1_.3), custom_call_target="tpu_custom_call" | custom-call | bytes 1 | tf_op jit(solution)/shard_map/prelude/pallas_call | solution.py:125
  7.0 7.0 %all-to-all-start = ((bf16[64,128,128]{2,1,0:T(8,128)(2,1)}), bf16[64,128,128]{2,1,0:T(8,128)(2,1)S(1)}, u32[]{:S(2)}, u32[]{:S(2)}) async-start(bf16[64,128,128]{2,1,0:T(8,128)(2,1)} %get-tuple-element.25), calls=%async_computation | async-start | bytes 4194304 | tf_op jit(solution)/shard_map/all_to_all | solution.py:492
  14.0 2.2 %collective-permute-start.3 = (bf16[512,1024]{1,0:T(8,128)(2,1)}, bf16[512,1024]{1,0:T(8,128)(2,1)S(1)}, u32[]{:S(2)}, u32[]{:S(2)}) collective-permute-start(bf16[512,1024]{1,0:T(8,128)(2,1)} %get-tuple-element.27), channel_id=1, source_target_pairs={{0,6},{1,3},{2,0},{3,5},{4,2},{5,7},{6,4},{7,1},{8,14},{9,11},{10,... | collective-permute-start | bytes 3145736 | tf_op jit(solution)/shard_map/ppermute | solution.py:475
  16.2 1.0 %fusion = (f32[512,64]{1,0:T(8,128)S(1)}, f32[512,64]{1,0:T(8,128)S(1)}, f32[512,64]{1,0:T(8,128)S(1)}) fusion(f32[64]{0:T(128)S(1)} %negate_power_fusion, f32[512]{0:T(512)S(1)} %add_convert_fusion), kind=kLoop, calls=%fused_computation.4 | loop fusion | flops 65536 | bytes 395520 | tf_op jit(solution)/shard_map/neg | solution.py:488
  17.2 0.2 pad_maximum_fusion
  17.4 0.0 copy-start
  17.5 0.0 copy-start.1
  17.5 0.0 collective-permute-done.refs_0_
  17.5 5.0 %project.3 = (f32[512,512]{1,0:T(8,128)S(1)}, f32[512,256]{1,0:T(8,128)S(1)}, f32[512,128]{1,0:T(8,128)S(1)}) custom-call(bf16[512,1024]{1,0:T(8,128)(2,1)} %collective-permute-done.refs_0_, bf16[512,1024]{1,0:T(8,128)(2,1)} %refs_1_.3, bf16[8192,512]{1,0:T(8,128)(2,1)} %refs_7_.1, bf16[8192,256]{1,0:T(8,128)(2,1)} %refs_3_.5, ...), custom_call_target="tpu_custom_call" | custom-call | flops 20000000000 | bytes 1 | tf_op jit(solution)/shard_map/project/pallas_call | solution.py:233
  22.5 0.0 collective-permute-done.1.refs_1_
  22.5 0.1 collective-permute-start.5
  22.6 2.5 %collective-permute-start.2 = (bf16[512,1024]{1,0:T(8,128)(2,1)S(1)}, bf16[512,1024]{1,0:T(8,128)(2,1)S(1)}, u32[]{:S(2)}, u32[]{:S(2)}) collective-permute-start(bf16[512,1024]{1,0:T(8,128)(2,1)S(1)} %after.2.refs_0_), channel_id=1, source_target_pairs={{0,1},{1,0},{2,3},{3,2},{4,5},{5,4},{6,7},{7,6},{8,9},{9,8},{10,11... | collective-permute-start | bytes 3145736 | tf_op jit(solution)/shard_map/ppermute | solution.py:479
  25.1 7.9 %collective-permute-done.3.refs_1_ = bf16[512,1024]{1,0:T(8,128)(2,1)S(1)} collective-permute-done((bf16[512,1024]{1,0:T(8,128)(2,1)}, bf16[512,1024]{1,0:T(8,128)(2,1)S(1)}, u32[]{:S(2)}, u32[]{:S(2)}) %collective-permute-start.3) | collective-permute-done | bytes 1048608 | tf_op jit(solution)/shard_map/ppermute | solution.py:475
  33.1 2.3 %collective-permute-start.4 = (bf16[512,1024]{1,0:T(8,128)(2,1)S(1)}, bf16[512,1024]{1,0:T(8,128)(2,1)S(1)}, u32[]{:S(2)}, u32[]{:S(2)}) collective-permute-start(bf16[512,1024]{1,0:T(8,128)(2,1)S(1)} %collective-permute-done.3.refs_1_), channel_id=1, source_target_pairs={{0,1},{1,0},{2,3},{3,2},{4,5},{5,4},{6,7},{7,6},{8,9},{9,8},{10,11... | collective-permute-start | bytes 3145736 | tf_op jit(solution)/shard_map/ppermute | solution.py:479
  35.3 3.6 %project.4 = (f32[512,512]{1,0:T(8,128)S(1)}, f32[512,256]{1,0:T(8,128)S(1)}, f32[512,128]{1,0:T(8,128)S(1)}) custom-call(bf16[512,1024]{1,0:T(8,128)(2,1)S(1)} %after.2.refs_0_, bf16[512,1024]{1,0:T(8,128)(2,1)S(1)} %collective-permute-done.3.refs_1_, bf16[8192,512]{1,0:T(8,128)(2,1)} %refs_7_.1, bf16[8192,256]{1,0:T(8,128)(2,1)} %refs_3_.5, ...), custom_call_target="tpu_custom_call" | custom-call | flops 20000000000 | bytes 1 | tf_op jit(solution)/shard_map/project/pallas_call | solution.py:233
  38.9 0.0 collective-permute-done.2.refs_0_
  38.9 0.0 collective-permute-done.4.refs_1_
  38.9 3.9 %project.5 = (f32[512,512]{1,0:T(8,128)S(1)}, f32[512,256]{1,0:T(8,128)S(1)}, f32[512,128]{1,0:T(8,128)S(1)}, bf16[2,1024,512]{2,1,0:T(8,128)(2,1)S(1)}, bf16[2,1024,256]{2,1,0:T(8,128)(2,1)S(1)}) custom-call(bf16[512,1024]{1,0:T(8,128)(2,1)S(1)} %collective-permute-done.2.refs_0_, bf16[512,1024]{1,0:T(8,128)(2,1)S(1)} %collective-permute-done.4.refs_1_, ...), custom_call_target="tpu_custom_call" | custom-call | bytes 1 | tf_op jit(solution)/shard_map/project/pallas_call | solution.py:233
  42.8 0.0 collective-permute-done.5.refs_1_
  42.8 0.1 collective-permute-start.6
  42.9 2.0 %project_far.1 = (f32[512,512]{1,0:T(8,128)}, f32[512,256]{1,0:T(8,128)S(1)}, f32[512,128]{1,0:T(8,128)S(1)}) custom-call(bf16[512,1024]{1,0:T(8,128)(2,1)S(1)} %after.3.x_ref, bf16[2,1024,512]{2,1,0:T(8,128)(2,1)S(1)} %get-tuple-element.34.wq_ref, bf16[2,1024,256]{2,1,0:T(8,128)(2,1)S(1)} %get-tuple-element.35.wkv_ref, ...), custom_call_target="tpu_custom_call" | custom-call | bytes 1 | tf_op jit(solution)/shard_map/project_far/pallas_call | solution.py:266
  44.9 0.6 collective-permute-done.6.x_ref
  45.5 0.0 copy-done
  45.5 0.0 copy-done.1
  45.5 2.7 %project_keyval.1 = (bf16[512,128]{1,0:T(8,128)(2,1)}, bf16[512,256]{1,0:T(8,128)(2,1)}, f32[512,128]{1,0:T(8,128)}, bf16[512,1024]{1,0:T(8,128)(2,1)}, bf16[32,128,128]{2,1,0:T(8,128)(2,1)}) custom-call(s32[24,128]{1,0:T(8,128)S(1)} %get-tuple-element.24.table_ref, bf16[512,1024]{1,0:T(8,128)(2,1)S(1)} %collective-permute-done.6.x_ref, ...), custom_call_target="tpu_custom_call" | custom-call | bytes 1 | tf_op jit(solution)/shard_map/project_keyval/pallas_call | solution.py:342
  48.2 0.0 all-to-all-done.pages_ref
  48.2 6.6 %all-to-all-start.1 = ((bf16[32,128,128]{2,1,0:T(8,128)(2,1)}), bf16[32,128,128]{2,1,0:T(8,128)(2,1)S(1)}, u32[]{:S(2)}, u32[]{:S(2)}) async-start(bf16[32,128,128]{2,1,0:T(8,128)(2,1)} %get-tuple-element.45), calls=%async_computation.1 | async-start | bytes 2097152 | tf_op jit(solution)/shard_map/all_to_all | solution.py:492
  54.9 10.6 %attend.1 = bf16[512,512]{1,0:T(8,128)(2,1)} custom-call(s32[24,128]{1,0:T(8,128)S(1)} %get-tuple-element.24.table_ref, bf16[64,128,128]{2,1,0:T(8,128)(2,1)S(1)} %all-to-all-done.pages_ref, f32[512,512]{1,0:T(8,128)} %get-tuple-element.38.refs_0_, bf16[512,1024]{1,0:T(8,128)(2,1)} %get-tuple-element.41.refs_1_, f32[512,128]{1,0:T(8,128)} %get-tuple-element.42.refs_2_, ...), custom_call_target="tpu_custom_call" | custom-call | flops 5368709120 | bytes 8388608 | tf_op jit(solution)/shard_map/attend/pallas_call | solution.py:419
  65.5 7.1 %all-to-all-done.1.received_ref = bf16[32,128,128]{2,1,0:T(8,128)(2,1)S(1)} async-done(((bf16[32,128,128]{2,1,0:T(8,128)(2,1)}), bf16[32,128,128]{2,1,0:T(8,128)(2,1)S(1)}, u32[]{:S(2)}, u32[]{:S(2)}) %all-to-all-start.1) | async-done | bytes 1048608 | tf_op jit(solution)/shard_map/all_to_all | solution.py:492
  72.7 1.8 %place_pages.1 = bf16[32,128,128]{2,1,0:T(8,128)(2,1)} custom-call(s32[24,128]{1,0:T(8,128)S(1)} %get-tuple-element.24.table_ref, bf16[32,128,128]{2,1,0:T(8,128)(2,1)S(1)} %all-to-all-done.1.received_ref), custom_call_target="tpu_custom_call" | custom-call | bytes 2097152 | tf_op jit(solution)/shard_map/place_pages/pallas_call | solution.py:458
  (4 shorter events, 0.0 us)
Async XLA Ops:
  0.6 16.8 %collective-permute-start = (bf16[512,1024]{1,0:T(8,128)(2,1)}, bf16[512,1024]{1,0:T(8,128)(2,1)}, u32[]{:S(2)}, u32[]{:S(2)}) collective-permute-start(bf16[512,1024]{1,0:T(8,128)(2,1)} %refs_1_.3), channel_id=1, source_target_pairs={{0,1},{1,0},{2,3},{3,2},{4,5},{5,4},{6,7},{7,6},{8,9},{9,8},{10,11... | collective-permute-start | bytes 3145736 | tf_op jit(solution)/shard_map/ppermute | solution.py:479
  0.7 21.8 %collective-permute-start.1 = (bf16[512,1024]{1,0:T(8,128)(2,1)}, bf16[512,1024]{1,0:T(8,128)(2,1)S(1)}, u32[]{:S(2)}, u32[]{:S(2)}) collective-permute-start(bf16[512,1024]{1,0:T(8,128)(2,1)} %refs_1_.3), channel_id=1, source_target_pairs={{0,2},{1,7},{2,4},{3,1},{4,6},{5,3},{6,0},{7,5},{8,10},{9,15},{10,... | collective-permute-start | bytes 3145736 | tf_op jit(solution)/shard_map/ppermute | solution.py:475
  7.0 41.3 %all-to-all-start = ((bf16[64,128,128]{2,1,0:T(8,128)(2,1)}), bf16[64,128,128]{2,1,0:T(8,128)(2,1)S(1)}, u32[]{:S(2)}, u32[]{:S(2)}) async-start(bf16[64,128,128]{2,1,0:T(8,128)(2,1)} %get-tuple-element.25), calls=%async_computation | async-start | bytes 4194304 | tf_op jit(solution)/shard_map/all_to_all | solution.py:492
  14.0 19.0 %collective-permute-start.3 = (bf16[512,1024]{1,0:T(8,128)(2,1)}, bf16[512,1024]{1,0:T(8,128)(2,1)S(1)}, u32[]{:S(2)}, u32[]{:S(2)}) collective-permute-start(bf16[512,1024]{1,0:T(8,128)(2,1)} %get-tuple-element.27), channel_id=1, source_target_pairs={{0,6},{1,3},{2,0},{3,5},{4,2},{5,7},{6,4},{7,1},{8,14},{9,11},{10,... | collective-permute-start | bytes 3145736 | tf_op jit(solution)/shard_map/ppermute | solution.py:475
  17.4 28.1 %copy-start = (f32[512,128]{1,0:T(8,128)}, f32[512,128]{1,0:T(8,128)S(1)}, u32[]{:S(2)}) copy-start(f32[512,128]{1,0:T(8,128)S(1)} %get-tuple-element.51.refs_4_.cos_ref.refs_3_) | copy-start | bytes 786436
  17.5 28.1 %copy-start.1 = (f32[512,128]{1,0:T(8,128)}, f32[512,128]{1,0:T(8,128)S(1)}, u32[]{:S(2)}) copy-start(f32[512,128]{1,0:T(8,128)S(1)} %get-tuple-element.52.refs_5_.sin_ref.refs_4_) | copy-start | bytes 786436
  22.5 20.2 %collective-permute-start.5 = (bf16[512,1024]{1,0:T(8,128)(2,1)S(1)}, bf16[512,1024]{1,0:T(8,128)(2,1)S(1)}, u32[]{:S(2)}, u32[]{:S(2)}) collective-permute-start(bf16[512,1024]{1,0:T(8,128)(2,1)S(1)} %after.2.refs_0_), channel_id=1, source_target_pairs={{0,2},{1,7},{2,4},{3,1},{4,6},{5,3},{6,0},{7,5},{8,10},{9,15},{10,... | collective-permute-start | bytes 3145736 | tf_op jit(solution)/shard_map/ppermute | solution.py:475
  22.6 16.3 %collective-permute-start.2 = (bf16[512,1024]{1,0:T(8,128)(2,1)S(1)}, bf16[512,1024]{1,0:T(8,128)(2,1)S(1)}, u32[]{:S(2)}, u32[]{:S(2)}) collective-permute-start(bf16[512,1024]{1,0:T(8,128)(2,1)S(1)} %after.2.refs_0_), channel_id=1, source_target_pairs={{0,1},{1,0},{2,3},{3,2},{4,5},{5,4},{6,7},{7,6},{8,9},{9,8},{10,11... | collective-permute-start | bytes 3145736 | tf_op jit(solution)/shard_map/ppermute | solution.py:479
  33.1 5.9 %collective-permute-start.4 = (bf16[512,1024]{1,0:T(8,128)(2,1)S(1)}, bf16[512,1024]{1,0:T(8,128)(2,1)S(1)}, u32[]{:S(2)}, u32[]{:S(2)}) collective-permute-start(bf16[512,1024]{1,0:T(8,128)(2,1)S(1)} %collective-permute-done.3.refs_1_), channel_id=1, source_target_pairs={{0,1},{1,0},{2,3},{3,2},{4,5},{5,4},{6,7},{7,6},{8,9},{9,8},{10,11... | collective-permute-start | bytes 3145736 | tf_op jit(solution)/shard_map/ppermute | solution.py:479
  42.8 2.7 %collective-permute-start.6 = (bf16[512,1024]{1,0:T(8,128)(2,1)S(1)}, bf16[512,1024]{1,0:T(8,128)(2,1)S(1)}, u32[]{:S(2)}, u32[]{:S(2)}) collective-permute-start(bf16[512,1024]{1,0:T(8,128)(2,1)S(1)} %after.3.x_ref), channel_id=1, source_target_pairs={{0,1},{1,0},{2,3},{3,2},{4,5},{5,4},{6,7},{7,6},{8,9},{9,8},{10,11... | collective-permute-start | bytes 3145736 | tf_op jit(solution)/shard_map/ppermute | solution.py:479
  48.2 24.4 %all-to-all-start.1 = ((bf16[32,128,128]{2,1,0:T(8,128)(2,1)}), bf16[32,128,128]{2,1,0:T(8,128)(2,1)S(1)}, u32[]{:S(2)}, u32[]{:S(2)}) async-start(bf16[32,128,128]{2,1,0:T(8,128)(2,1)} %get-tuple-element.45), calls=%async_computation.1 | async-start | bytes 2097152 | tf_op jit(solution)/shard_map/all_to_all | solution.py:492

commit v9 on v8

--- a/solution.py
+++ b/solution.py
@@ -436,11 +436,14 @@
     )(table, pages, *[hbm(x) for x in (*sources, w_query)])
 
 
-def place_kernel(table_ref, received_ref, out_ref, buffer, sems):
+def place_kernel(table_ref, received_ref, out_ref, buffer, index_ref, index_sem, sems):
+    indices = pltpu.make_async_copy(table_ref, index_ref, index_sem)
+    indices.start()
+    indices.wait()
     group = 4
     copies = []
     for i in range(SLOTS):
-        source = table_ref[PLACE, i]
+        source = index_ref[PLACE, i]
         page = received_ref[jnp.maximum(source - 1, 0)]
         buffer[i] = jnp.where(source > 0, page, jnp.zeros_like(page))
         if i % group == group - 1:
@@ -458,10 +461,12 @@
     return pl.pallas_call(
         place_kernel,
         out_shape=pltpu.HBM((SLOTS, 2 * PAGE, HD), BF16),
-        in_specs=[SMEM, VMEM],
+        in_specs=[VMEM, VMEM],
         out_specs=HBM,
         scratch_shapes=[
             pltpu.VMEM((SLOTS, 2 * PAGE, HD), BF16),
+            pltpu.SMEM((24, HD), jnp.int32),
+            pltpu.SemaphoreType.DMA,
             pltpu.SemaphoreType.DMA((SLOTS // 4,)),
         ],
         compiler_params=params(8),
@@ -502,7 +507,7 @@
     tables = rope_tables(ROWS, PAGES * PAGE)
     weights = (w_query, w_keyval)
     blocks = ((OWN, True), (OWN, False))
-    sums = project(blocks, [swap(hidden)], [hidden], *weights, tokens=tables, flops=HIDES)
+    sums = project(blocks, [swap(hidden)], [hidden], *weights, tokens=tables)
     (near,) = after((sums[2],), near)
     far = shift(near, (1, -1))
     blocks = ((NEAR, False), (BACK, False))

time: 76.1 us -> 73.4 us (0.965)
  starting transfers between devices: 23 us -> 20.4 us
  Pallas kernels: 33.7 us -> 35.3 us
  waiting for transfers between devices: 15.7 us -> 14.8 us
    all_to_all x2, starting transfers between devices: 13.7 us -> 10.9 us  [exchange(): lax.all_to_all(values, 'pool', split_axis=0, concat_axis=0, tiled=True)]
    ppermute x3, waiting for transfers between devices: 7.93 us -> 5.29 us  [shift(): return lax.ppermute(values, 'tp', pairs)]
    ppermute x3, starting transfers between devices: 4.35 us -> 6.66 us  [shift(): return lax.ppermute(values, 'tp', pairs)]
    ppermute x4, starting transfers between devices: 4.94 us -> 2.77 us  [swap(): return lax.ppermute(values, 'tp', [(i, i ^ 1) for i in range(8)])]
    all_to_all x2, waiting for transfers between devices: 7.14 us -> 8.89 us  [exchange(): lax.all_to_all(values, 'pool', split_axis=0, concat_axis=0, tiled=True)]
    pallas_call x1, Pallas kernels: 10.6 us -> 12.2 us  [attend(): pl.pallas_call(attend_kernel, out_shape=shape((ROWS, QW), BF16), in_specs...]
  transfers between devices with their start and end apart: 9 -> 9, of which waited for: 3 -> 6; matrix products, arithmetic and copies ran while one was open for 2% -> 2% of each run, Pallas kernels for 43% -> 46%
where the time goes in v9:
time: 73.4 us; the launch traced here: 72.7 us
  Pallas kernels  35.3 us (48%)
  starting transfers between devices  20.4 us (28%)
  waiting for transfers between devices  14.8 us (20%)
  other arithmetic  1.21 us (2%)
  between operations  0.93 us (1%)
    pallas_call x3, Pallas kernels, project(): pl.pallas_call(functools.partial(project_kernel, blocks, len(held), bool(...  12.4 us
    pallas_call x1, Pallas kernels, attend(): pl.pallas_call(attend_kernel, out_shape=shape((ROWS, QW), BF16), in_specs...  12.2 us
    all_to_all x2, starting transfers between devices, exchange(): lax.all_to_all(values, 'pool', split_axis=0, concat_axis=0, tiled=True)  10.9 us
    all_to_all x2, waiting for transfers between devices, exchange(): lax.all_to_all(values, 'pool', split_axis=0, concat_axis=0, tiled=True)  8.89 us
    ppermute x3, starting transfers between devices, shift(): return lax.ppermute(values, 'tp', pairs)  6.66 us
    ppermute x3, waiting for transfers between devices, shift(): return lax.ppermute(values, 'tp', pairs)  5.29 us
    pallas_call x1, Pallas kernels, prelude(): pl.pallas_call(prelude_kernel, out_shape=[shape((24, HD), jnp.int32), plt...  4.15 us
    ppermute x4, starting transfers between devices, swap(): return lax.ppermute(values, 'tp', [(i, i ^ 1) for i in range(8)])  2.77 us
  transfers between devices with their start and end apart: 9, of which 6 were waited for; matrix products, arithmetic and copies ran while one was open for 2% of the time, Pallas kernels for 46%

profile of v9, /device:TPU:0, one launch (start us, length us, event | category | flops | bytes accessed | tf_op | source)
XLA Modules:
  0.0 72.7 jit_solution(5391298631019033461)
XLA Ops:
  0.6 0.1 collective-permute-start
  0.7 2.1 %collective-permute-start.1 = (bf16[512,1024]{1,0:T(8,128)(2,1)}, bf16[512,1024]{1,0:T(8,128)(2,1)S(1)}, u32[]{:S(2)}, u32[]{:S(2)}) collective-permute-start(bf16[512,1024]{1,0:T(8,128)(2,1)} %refs_1_.3), channel_id=1, source_target_pairs={{0,2},{1,7},{2,4},{3,1},{4,6},{5,3},{6,0},{7,5},{8,10},{9,15},{10,... | collective-permute-start | bytes 3145736 | tf_op jit(solution)/shard_map/ppermute | solution.py:480
  2.8 4.2 %prelude.1 = (s32[24,128]{1,0:T(8,128)S(1)}, bf16[64,128,128]{2,1,0:T(8,128)(2,1)}, bf16[512,1024]{1,0:T(8,128)(2,1)}) custom-call(s32[16,32]{1,0:T(8,128)} %refs_0_.1, s32[16,32]{1,0:T(8,128)} %refs_1_.2, s32[8,16]{1,0:T(8,128)} %bitcast.7, bf16[64,128,128]{2,1,0:T(8,128)(2,1)} %bitcast.5, bf16[512,1024]{1,0:T(8,128)(2,1)} %refs_1_.3), custom_call_target="tpu_custom_call" | custom-call | bytes 1 | tf_op jit(solution)/shard_map/prelude/pallas_call | solution.py:125
  7.0 2.2 %collective-permute-start.3 = (bf16[512,1024]{1,0:T(8,128)(2,1)}, bf16[512,1024]{1,0:T(8,128)(2,1)}, u32[]{:S(2)}, u32[]{:S(2)}) collective-permute-start(bf16[512,1024]{1,0:T(8,128)(2,1)} %get-tuple-element.27), channel_id=1, source_target_pairs={{0,6},{1,3},{2,0},{3,5},{4,2},{5,7},{6,4},{7,1},{8,14},{9,11},{10,... | collective-permute-start | bytes 3145736 | tf_op jit(solution)/shard_map/ppermute | solution.py:480
  9.2 7.1 %all-to-all-start = ((bf16[64,128,128]{2,1,0:T(8,128)(2,1)}), bf16[64,128,128]{2,1,0:T(8,128)(2,1)}, u32[]{:S(2)}, u32[]{:S(2)}) async-start(bf16[64,128,128]{2,1,0:T(8,128)(2,1)} %get-tuple-element.25), calls=%async_computation | async-start | bytes 4194304 | tf_op jit(solution)/shard_map/all_to_all | solution.py:497
  16.3 1.0 %fusion = (f32[512,64]{1,0:T(8,128)S(1)}, f32[512,64]{1,0:T(8,128)S(1)}, f32[512,64]{1,0:T(8,128)S(1)}) fusion(f32[64]{0:T(128)S(1)} %negate_power_fusion, f32[512]{0:T(512)S(1)} %add_convert_fusion), kind=kLoop, calls=%fused_computation.4 | loop fusion | flops 65536 | bytes 395520 | tf_op jit(solution)/shard_map/neg | solution.py:493
  17.3 0.2 pad_maximum_fusion
  17.5 0.0 copy-start
  17.5 0.0 copy-start.1
  17.5 0.0 collective-permute-done.refs_0_
  17.5 3.8 %project.3 = (f32[512,512]{1,0:T(8,128)S(1)}, f32[512,256]{1,0:T(8,128)S(1)}, f32[512,128]{1,0:T(8,128)S(1)}) custom-call(bf16[512,1024]{1,0:T(8,128)(2,1)S(1)} %collective-permute-done.refs_0_, bf16[512,1024]{1,0:T(8,128)(2,1)} %refs_1_.3, bf16[8192,512]{1,0:T(8,128)(2,1)} %refs_7_.1, bf16[8192,256]{1,0:T(8,128)(2,1)} %refs_3_.5, ...), custom_call_target="tpu_custom_call" | custom-call | bytes 1 | tf_op jit(solution)/shard_map/project/pallas_call | solution.py:233
  21.4 1.1 %collective-permute-done.1.refs_1_ = bf16[512,1024]{1,0:T(8,128)(2,1)S(1)} collective-permute-done((bf16[512,1024]{1,0:T(8,128)(2,1)}, bf16[512,1024]{1,0:T(8,128)(2,1)S(1)}, u32[]{:S(2)}, u32[]{:S(2)}) %collective-permute-start.1) | collective-permute-done | bytes 1048608 | tf_op jit(solution)/shard_map/ppermute | solution.py:480
  22.4 2.4 %collective-permute-start.5 = (bf16[512,1024]{1,0:T(8,128)(2,1)S(1)}, bf16[512,1024]{1,0:T(8,128)(2,1)S(1)}, u32[]{:S(2)}, u32[]{:S(2)}) collective-permute-start(bf16[512,1024]{1,0:T(8,128)(2,1)S(1)} %after.2.refs_0_), channel_id=1, source_target_pairs={{0,2},{1,7},{2,4},{3,1},{4,6},{5,3},{6,0},{7,5},{8,10},{9,15},{10,... | collective-permute-start | bytes 3145736 | tf_op jit(solution)/shard_map/ppermute | solution.py:480
  24.8 2.1 %collective-permute-start.2 = (bf16[512,1024]{1,0:T(8,128)(2,1)S(1)}, bf16[512,1024]{1,0:T(8,128)(2,1)S(1)}, u32[]{:S(2)}, u32[]{:S(2)}) collective-permute-start(bf16[512,1024]{1,0:T(8,128)(2,1)S(1)} %after.2.refs_0_), channel_id=1, source_target_pairs={{0,1},{1,0},{2,3},{3,2},{4,5},{5,4},{6,7},{7,6},{8,9},{9,8},{10,11... | collective-permute-start | bytes 3145736 | tf_op jit(solution)/shard_map/ppermute | solution.py:484
  26.9 2.1 %collective-permute-done.3.refs_1_ = bf16[512,1024]{1,0:T(8,128)(2,1)} collective-permute-done((bf16[512,1024]{1,0:T(8,128)(2,1)}, bf16[512,1024]{1,0:T(8,128)(2,1)}, u32[]{:S(2)}, u32[]{:S(2)}) %collective-permute-start.3) | collective-permute-done | bytes 1048608 | tf_op jit(solution)/shard_map/ppermute | solution.py:480
  29.0 0.6 collective-permute-start.4
  29.6 4.7 %project.4 = (f32[512,512]{1,0:T(8,128)S(1)}, f32[512,256]{1,0:T(8,128)S(1)}, f32[512,128]{1,0:T(8,128)S(1)}) custom-call(bf16[512,1024]{1,0:T(8,128)(2,1)S(1)} %after.2.refs_0_, bf16[512,1024]{1,0:T(8,128)(2,1)} %collective-permute-done.3.refs_1_, bf16[8192,512]{1,0:T(8,128)(2,1)} %refs_7_.1, bf16[8192,256]{1,0:T(8,128)(2,1)} %refs_3_.5, ...), custom_call_target="tpu_custom_call" | custom-call | flops 20000000000 | bytes 1 | tf_op jit(solution)/shard_map/project/pallas_call | solution.py:233
  34.4 0.0 collective-permute-done.2.refs_0_
  34.4 0.0 collective-permute-done.4.refs_1_
  34.4 3.9 %project.5 = (f32[512,512]{1,0:T(8,128)S(1)}, f32[512,256]{1,0:T(8,128)S(1)}, f32[512,128]{1,0:T(8,128)S(1)}, bf16[2,1024,512]{2,1,0:T(8,128)(2,1)S(1)}, bf16[2,1024,256]{2,1,0:T(8,128)(2,1)S(1)}) custom-call(bf16[512,1024]{1,0:T(8,128)(2,1)S(1)} %collective-permute-done.2.refs_0_, bf16[512,1024]{1,0:T(8,128)(2,1)S(1)} %collective-permute-done.4.refs_1_, ...), custom_call_target="tpu_custom_call" | custom-call | bytes 1 | tf_op jit(solution)/shard_map/project/pallas_call | solution.py:233
  38.2 2.1 %collective-permute-done.5.refs_1_ = bf16[512,1024]{1,0:T(8,128)(2,1)S(1)} collective-permute-done((bf16[512,1024]{1,0:T(8,128)(2,1)S(1)}, bf16[512,1024]{1,0:T(8,128)(2,1)S(1)}, u32[]{:S(2)}, u32[]{:S(2)}) %collective-permute-start.5) | collective-permute-done | bytes 1048608 | tf_op jit(solution)/shard_map/ppermute | solution.py:480
  40.4 0.0 collective-permute-start.6
  40.4 2.0 %project_far.1 = (f32[512,512]{1,0:T(8,128)}, f32[512,256]{1,0:T(8,128)S(1)}, f32[512,128]{1,0:T(8,128)S(1)}) custom-call(bf16[512,1024]{1,0:T(8,128)(2,1)S(1)} %after.3.x_ref, bf16[2,1024,512]{2,1,0:T(8,128)(2,1)S(1)} %get-tuple-element.34.wq_ref, bf16[2,1024,256]{2,1,0:T(8,128)(2,1)S(1)} %get-tuple-element.35.wkv_ref, ...), custom_call_target="tpu_custom_call" | custom-call | bytes 1 | tf_op jit(solution)/shard_map/project_far/pallas_call | solution.py:266
  42.4 0.6 collective-permute-done.6.x_ref
  43.0 0.0 copy-done
  43.0 0.0 copy-done.1
  43.0 2.7 %project_keyval.1 = (bf16[512,128]{1,0:T(8,128)(2,1)}, bf16[512,256]{1,0:T(8,128)(2,1)}, f32[512,128]{1,0:T(8,128)}, bf16[512,1024]{1,0:T(8,128)(2,1)}, bf16[32,128,128]{2,1,0:T(8,128)(2,1)}) custom-call(s32[24,128]{1,0:T(8,128)S(1)} %get-tuple-element.24.table_ref, bf16[512,1024]{1,0:T(8,128)(2,1)S(1)} %collective-permute-done.6.x_ref, ...), custom_call_target="tpu_custom_call" | custom-call | bytes 1 | tf_op jit(solution)/shard_map/project_keyval/pallas_call | solution.py:342
  45.7 3.6 %all-to-all-done.pages_ref = bf16[64,128,128]{2,1,0:T(8,128)(2,1)} async-done(((bf16[64,128,128]{2,1,0:T(8,128)(2,1)}), bf16[64,128,128]{2,1,0:T(8,128)(2,1)}, u32[]{:S(2)}, u32[]{:S(2)}) %all-to-all-start) | async-done | bytes 2097184 | tf_op jit(solution)/shard_map/all_to_all | solution.py:497
  49.3 3.8 %all-to-all-start.1 = ((bf16[32,128,128]{2,1,0:T(8,128)(2,1)}), bf16[32,128,128]{2,1,0:T(8,128)(2,1)S(1)}, u32[]{:S(2)}, u32[]{:S(2)}) async-start(bf16[32,128,128]{2,1,0:T(8,128)(2,1)} %get-tuple-element.45), calls=%async_computation.1 | async-start | bytes 2097152 | tf_op jit(solution)/shard_map/all_to_all | solution.py:497
  53.1 12.2 %attend.1 = bf16[512,512]{1,0:T(8,128)(2,1)} custom-call(s32[24,128]{1,0:T(8,128)S(1)} %get-tuple-element.24.table_ref, bf16[64,128,128]{2,1,0:T(8,128)(2,1)} %all-to-all-done.pages_ref, f32[512,512]{1,0:T(8,128)} %get-tuple-element.38.refs_0_, bf16[512,1024]{1,0:T(8,128)(2,1)} %get-tuple-element.41.refs_1_, f32[512,128]{1,0:T(8,128)} %get-tuple-element.42.refs_2_, ...), custom_call_target="tpu_custom_call" | custom-call | flops 5368709120 | bytes 8388608 | tf_op jit(solution)/shard_map/attend/pallas_call | solution.py:419
  65.4 5.3 %all-to-all-done.1.received_ref = bf16[32,128,128]{2,1,0:T(8,128)(2,1)S(1)} async-done(((bf16[32,128,128]{2,1,0:T(8,128)(2,1)}), bf16[32,128,128]{2,1,0:T(8,128)(2,1)S(1)}, u32[]{:S(2)}, u32[]{:S(2)}) %all-to-all-start.1) | async-done | bytes 1048608 | tf_op jit(solution)/shard_map/all_to_all | solution.py:497
  70.7 1.8 %place_pages.1 = bf16[32,128,128]{2,1,0:T(8,128)(2,1)} custom-call(s32[24,128]{1,0:T(8,128)S(1)} %get-tuple-element.24.table_ref, bf16[32,128,128]{2,1,0:T(8,128)(2,1)S(1)} %all-to-all-done.1.received_ref), custom_call_target="tpu_custom_call" | custom-call | bytes 2097152 | tf_op jit(solution)/shard_map/place_pages/pallas_call | solution.py:461
  (4 shorter events, 0.0 us)
Async XLA Ops:
  0.6 16.9 %collective-permute-start = (bf16[512,1024]{1,0:T(8,128)(2,1)}, bf16[512,1024]{1,0:T(8,128)(2,1)S(1)}, u32[]{:S(2)}, u32[]{:S(2)}) collective-permute-start(bf16[512,1024]{1,0:T(8,128)(2,1)} %refs_1_.3), channel_id=1, source_target_pairs={{0,1},{1,0},{2,3},{3,2},{4,5},{5,4},{6,7},{7,6},{8,9},{9,8},{10,11... | collective-permute-start | bytes 3145736 | tf_op jit(solution)/shard_map/ppermute | solution.py:484
  0.7 21.7 %collective-permute-start.1 = (bf16[512,1024]{1,0:T(8,128)(2,1)}, bf16[512,1024]{1,0:T(8,128)(2,1)S(1)}, u32[]{:S(2)}, u32[]{:S(2)}) collective-permute-start(bf16[512,1024]{1,0:T(8,128)(2,1)} %refs_1_.3), channel_id=1, source_target_pairs={{0,2},{1,7},{2,4},{3,1},{4,6},{5,3},{6,0},{7,5},{8,10},{9,15},{10,... | collective-permute-start | bytes 3145736 | tf_op jit(solution)/shard_map/ppermute | solution.py:480
  7.0 22.1 %collective-permute-start.3 = (bf16[512,1024]{1,0:T(8,128)(2,1)}, bf16[512,1024]{1,0:T(8,128)(2,1)}, u32[]{:S(2)}, u32[]{:S(2)}) collective-permute-start(bf16[512,1024]{1,0:T(8,128)(2,1)} %get-tuple-element.27), channel_id=1, source_target_pairs={{0,6},{1,3},{2,0},{3,5},{4,2},{5,7},{6,4},{7,1},{8,14},{9,11},{10,... | collective-permute-start | bytes 3145736 | tf_op jit(solution)/shard_map/ppermute | solution.py:480
  9.2 40.1 %all-to-all-start = ((bf16[64,128,128]{2,1,0:T(8,128)(2,1)}), bf16[64,128,128]{2,1,0:T(8,128)(2,1)}, u32[]{:S(2)}, u32[]{:S(2)}) async-start(bf16[64,128,128]{2,1,0:T(8,128)(2,1)} %get-tuple-element.25), calls=%async_computation | async-start | bytes 4194304 | tf_op jit(solution)/shard_map/all_to_all | solution.py:497
  17.5 25.6 %copy-start = (f32[512,128]{1,0:T(8,128)}, f32[512,128]{1,0:T(8,128)S(1)}, u32[]{:S(2)}) copy-start(f32[512,128]{1,0:T(8,128)S(1)} %get-tuple-element.51.refs_4_.cos_ref.refs_3_) | copy-start | bytes 786436
  17.5 25.5 %copy-start.1 = (f32[512,128]{1,0:T(8,128)}, f32[512,128]{1,0:T(8,128)S(1)}, u32[]{:S(2)}) copy-start(f32[512,128]{1,0:T(8,128)S(1)} %get-tuple-element.52.refs_5_.sin_ref.refs_4_) | copy-start | bytes 786436
  22.4 17.9 %collective-permute-start.5 = (bf16[512,1024]{1,0:T(8,128)(2,1)S(1)}, bf16[512,1024]{1,0:T(8,128)(2,1)S(1)}, u32[]{:S(2)}, u32[]{:S(2)}) collective-permute-start(bf16[512,1024]{1,0:T(8,128)(2,1)S(1)} %after.2.refs_0_), channel_id=1, source_target_pairs={{0,2},{1,7},{2,4},{3,1},{4,6},{5,3},{6,0},{7,5},{8,10},{9,15},{10,... | collective-permute-start | bytes 3145736 | tf_op jit(solution)/shard_map/ppermute | solution.py:480
  24.8 9.5 %collective-permute-start.2 = (bf16[512,1024]{1,0:T(8,128)(2,1)S(1)}, bf16[512,1024]{1,0:T(8,128)(2,1)S(1)}, u32[]{:S(2)}, u32[]{:S(2)}) collective-permute-start(bf16[512,1024]{1,0:T(8,128)(2,1)S(1)} %after.2.refs_0_), channel_id=1, source_target_pairs={{0,1},{1,0},{2,3},{3,2},{4,5},{5,4},{6,7},{7,6},{8,9},{9,8},{10,11... | collective-permute-start | bytes 3145736 | tf_op jit(solution)/shard_map/ppermute | solution.py:484
  29.0 5.4 %collective-permute-start.4 = (bf16[512,1024]{1,0:T(8,128)(2,1)}, bf16[512,1024]{1,0:T(8,128)(2,1)S(1)}, u32[]{:S(2)}, u32[]{:S(2)}) collective-permute-start(bf16[512,1024]{1,0:T(8,128)(2,1)} %collective-permute-done.3.refs_1_), channel_id=1, source_target_pairs={{0,1},{1,0},{2,3},{3,2},{4,5},{5,4},{6,7},{7,6},{8,9},{9,8},{10,11... | collective-permute-start | bytes 3145736 | tf_op jit(solution)/shard_map/ppermute | solution.py:484
  40.4 2.7 %collective-permute-start.6 = (bf16[512,1024]{1,0:T(8,128)(2,1)S(1)}, bf16[512,1024]{1,0:T(8,128)(2,1)S(1)}, u32[]{:S(2)}, u32[]{:S(2)}) collective-permute-start(bf16[512,1024]{1,0:T(8,128)(2,1)S(1)} %after.3.x_ref), channel_id=1, source_target_pairs={{0,1},{1,0},{2,3},{3,2},{4,5},{5,4},{6,7},{7,6},{8,9},{9,8},{10,11... | collective-permute-start | bytes 3145736 | tf_op jit(solution)/shard_map/ppermute | solution.py:484
  49.3 21.4 %all-to-all-start.1 = ((bf16[32,128,128]{2,1,0:T(8,128)(2,1)}), bf16[32,128,128]{2,1,0:T(8,128)(2,1)S(1)}, u32[]{:S(2)}, u32[]{:S(2)}) async-start(bf16[32,128,128]{2,1,0:T(8,128)(2,1)} %get-tuple-element.45), calls=%async_computation.1 | async-start | bytes 2097152 | tf_op jit(solution)/shard_map/all_to_all | solution.py:497

commit v10 on v9

--- a/solution.py
+++ b/solution.py
@@ -86,14 +86,13 @@
 
 
 def prelude_kernel(*refs):
-    owner_in, slot_in, target_in, store_in, hidden_in, table_ref, out_ref, hidden_out = refs[:8]
-    owner_ref, slot_ref, target_ref, store_ref, hidden_ref, index_ref, sems, page_sems = refs[8:]
+    owner_in, slot_in, target_in, store_in, table_ref, out_ref = refs[:6]
+    owner_ref, slot_ref, target_ref, store_ref, index_ref, sems, page_sems = refs[6:]
     pairs = (
         (owner_in, owner_ref),
         (slot_in, slot_ref),
         (target_in, target_ref),
         (store_in, store_ref),
-        (hidden_in, hidden_ref),
     )
     copies = [pltpu.make_async_copy(x, y, sems.at[i]) for i, (x, y) in enumerate(pairs)]
     for copy in copies:
@@ -101,11 +100,8 @@
     for copy in copies[:3]:
         copy.wait()
     fill_table(owner_ref[...], slot_ref[...], target_ref[...], table_ref)
-    indices = pltpu.make_async_copy(table_ref, index_ref, sems.at[5])
+    indices = pltpu.make_async_copy(table_ref, index_ref, sems.at[4])
     indices.start()
-    copies[4].wait()
-    hidden_copy = pltpu.make_async_copy(hidden_ref, hidden_out, sems.at[6])
-    hidden_copy.start()
     indices.wait()
     copies[3].wait()
     pages = [
@@ -118,33 +114,30 @@
         page.start()
     for page in pages:
         page.wait()
-    hidden_copy.wait()
-
-
-def prelude(page_owner, page_slot, new_owner, store, hidden):
+
+
+def prelude(page_owner, page_slot, new_owner, store):
     return pl.pallas_call(
         prelude_kernel,
         out_shape=[
             shape((24, HD), jnp.int32),
             pltpu.HBM((POOL * CAP, 2 * PAGE, HD), BF16),
-            pltpu.HBM(hidden.shape, BF16),
         ],
-        in_specs=[HBM] * 5,
-        out_specs=[VMEM, HBM, HBM],
+        in_specs=[HBM] * 4,
+        out_specs=[VMEM, HBM],
         scratch_shapes=[
             pltpu.VMEM((POOL, PAGES), jnp.int32),
             pltpu.VMEM((POOL, PAGES), jnp.int32),
             pltpu.VMEM((NEW_PAGES, POOL), jnp.int32),
             pltpu.VMEM(store.shape, BF16),
-            pltpu.VMEM(hidden.shape, BF16),
             pltpu.SMEM((24, HD), jnp.int32),
-            pltpu.SemaphoreType.DMA((7,)),
+            pltpu.SemaphoreType.DMA((5,)),
             pltpu.SemaphoreType.DMA((POOL * CAP,)),
         ],
         compiler_params=params(8),
         cost_estimate=cost(0, 1),
         name="prelude",
-    )(*[hbm(x) for x in (page_owner, page_slot, new_owner.T, store, hidden)])
+    )(*[hbm(x) for x in (page_owner, page_slot, new_owner.T, store)])
 
 
 def block_index(steps, other_core):
@@ -361,9 +354,9 @@
     return lax.dot_general(a, b, (((1,), (1,)), ((), ())), preferred_element_type=F32)
 
 
-def attend_kernel(table_ref, pages_ref, *refs):
-    sources, wq_ref, out_ref, refs = refs[:7], refs[7], refs[8], refs[9:]
-    targets, wq_buf, index_ref, q_buf, keys, values, sems = refs[:7], *refs[7:]
+def attend_kernel(table_ref, *refs):
+    sources, wq_ref, pages_ref, out_ref, refs = refs[:7], refs[7], refs[8], refs[9], refs[10:]
+    targets, wq_buf, index_ref, page_buf, q_buf, keys, values, sems, page_sems = refs[:7], *refs[7:]
     q_sum, x, inv_norm, cosine, sine, own_keys, own_values = targets
     indices = pltpu.make_async_copy(table_ref, index_ref, sems.at[8])
     indices.start()
@@ -378,8 +371,17 @@
     picker = (column == wanted).astype(BF16)
     values[:, HD:] = jnp.ones((PAGES * PAGE, HD), BF16)
     indices.wait()
+    fetches = [
+        pltpu.make_async_copy(
+            pages_ref.at[index_ref[TAKE, page]], page_buf.at[page], page_sems.at[page]
+        )
+        for page in range(PAGES)
+    ]
+    for fetch in fetches:
+        fetch.start()
     for page in range(PAGES):
-        both = jnp.dot(picker, pages_ref[index_ref[TAKE, page]], preferred_element_type=F32)
+        fetches[page].wait()
+        both = jnp.dot(picker, page_buf[page], preferred_element_type=F32)
         rows = slice(page * PAGE, (page + 1) * PAGE)
         keys[rows, :] = both[:PAGE].astype(BF16)
         values[rows, :HD] = both[PAGE:].astype(BF16)
@@ -419,21 +421,23 @@
     return pl.pallas_call(
         attend_kernel,
         out_shape=shape((ROWS, QW), BF16),
-        in_specs=[VMEM] * 2 + [HBM] * (len(sources) + 1),
+        in_specs=[VMEM] + [HBM] * (len(sources) + 2),
         out_specs=VMEM,
         scratch_shapes=[
             *[pltpu.VMEM(x.shape, x.dtype) for x in sources],
             pltpu.VMEM((FEAT, QW), BF16),
             pltpu.SMEM((24, HD), jnp.int32),
+            pltpu.VMEM((PAGES, 2 * PAGE, HD), BF16),
             pltpu.VMEM((HEADS, ROWS, HD), BF16),
             pltpu.VMEM((PAGES * PAGE, HD), BF16),
             pltpu.VMEM((PAGES * PAGE, 2 * HD), BF16),
             pltpu.SemaphoreType.DMA((9,)),
+            pltpu.SemaphoreType.DMA((PAGES,)),
         ],
         compiler_params=params(40),
         cost_estimate=cost(2 * ROWS * 4 * 2560 * 512, 8 * MIB),
         name="attend",
-    )(table, pages, *[hbm(x) for x in (*sources, w_query)])
+    )(table, *[hbm(x) for x in (*sources, w_query, pages)])
 
 
 def place_kernel(table_ref, received_ref, out_ref, buffer, index_ref, index_sem, sems):
@@ -499,20 +503,20 @@
 
 def body(hidden, w_query, w_keyval, store, page_owner, page_slot, new_owner):
     near = shift(hidden, (1, -1))
-    table, packed, again = prelude(
-        page_owner, page_slot, new_owner, store.reshape(64, 2 * PAGE, HD), hidden
-    )
+    table, packed = prelude(page_owner, page_slot, new_owner, store.reshape(64, 2 * PAGE, HD))
     pages = exchange(packed)
-    back = shift(again, (-1, 1))
+    sibling = swap(hidden)
+    (sibling,) = after((table,), sibling)
+    back = shift(sibling, (1, -1))
     tables = rope_tables(ROWS, PAGES * PAGE)
     weights = (w_query, w_keyval)
     blocks = ((OWN, True), (OWN, False))
-    sums = project(blocks, [swap(hidden)], [hidden], *weights, tokens=tables)
+    sums = project(blocks, [sibling], [hidden], *weights, tokens=tables)
     (near,) = after((sums[2],), near)
     far = shift(near, (1, -1))
-    blocks = ((NEAR, False), (BACK, False))
+    blocks = ((NEAR, False), (BACK, True))
     sums = project(blocks, [near, back], [], *weights, sums, flops=HIDES)
-    blocks, ahead = ((NEAR, True), (BACK, True)), ((FAR, False), (FAR, True))
+    blocks, ahead = ((NEAR, True), (BACK, False)), ((FAR, False), (FAR, True))
     held = [swap(near), swap(back)]
     *sums, last_q, last_kv = project(blocks, held, [], *weights, sums, ahead)
     (far,) = after((sums[2],), far)

time: 73.4 us -> 73.4 us (level)
  starting transfers between devices: 20.4 us -> 16.8 us
  Pallas kernels: 35.3 us -> 38.5 us
  waiting for transfers between devices: 14.8 us -> 15.7 us
    ppermute x3, waiting for transfers between devices: 5.29 us -> 9.17 us  [shift(): return lax.ppermute(values, 'tp', pairs)]
    pallas_call x1, Pallas kernels: 12.2 us -> 15.7 us  [attend(): pl.pallas_call(attend_kernel, out_shape=shape((ROWS, QW), BF16), in_specs...]
    all_to_all x2, waiting for transfers between devices: 8.89 us -> 5.89 us  [exchange(): lax.all_to_all(values, 'pool', split_axis=0, concat_axis=0, tiled=True)]
    ppermute x4, starting transfers between devices: 2.77 us -> 0.1 us  [swap(): return lax.ppermute(values, 'tp', [(i, i ^ 1) for i in range(8)])]
    ppermute x3, starting transfers between devices: 6.66 us -> 5.75 us  [shift(): return lax.ppermute(values, 'tp', pairs)]
  transfers between devices with their start and end apart: 9 -> 9, of which waited for: 6 -> 5; matrix products, arithmetic and copies ran while one was open for 2% -> 2% of each run, Pallas kernels for 46% -> 50%
where the time goes in v10:
time: 73.4 us; the launch traced here: 73.1 us
  Pallas kernels  38.5 us (52%)
  starting transfers between devices  16.8 us (23%)
  waiting for transfers between devices  15.7 us (21%)
  other arithmetic  1.21 us (2%)
  between operations  0.96 us (1%)
    pallas_call x1, Pallas kernels, attend(): pl.pallas_call(attend_kernel, out_shape=shape((ROWS, QW), BF16), in_specs...  15.7 us
    pallas_call x3, Pallas kernels, project(): pl.pallas_call(functools.partial(project_kernel, blocks, len(held), bool(...  12.5 us
    all_to_all x2, starting transfers between devices, exchange(): lax.all_to_all(values, 'pool', split_axis=0, concat_axis=0, tiled=True)  10.9 us
    ppermute x3, waiting for transfers between devices, shift(): return lax.ppermute(values, 'tp', pairs)  9.17 us
    all_to_all x2, waiting for transfers between devices, exchange(): lax.all_to_all(values, 'pool', split_axis=0, concat_axis=0, tiled=True)  5.89 us
    ppermute x3, starting transfers between devices, shift(): return lax.ppermute(values, 'tp', pairs)  5.75 us
    pallas_call x1, Pallas kernels, prelude(): pl.pallas_call(prelude_kernel, out_shape=[shape((24, HD), jnp.int32), plt...  3.82 us
    pallas_call x1, Pallas kernels, project_keyval(): pl.pallas_call(keyval_kernel, out_shape=[pltpu.HBM(*x) for x in (*kept, (...  2.67 us
  transfers between devices with their start and end apart: 9, of which 5 were waited for; matrix products, arithmetic and copies ran while one was open for 2% of the time, Pallas kernels for 50%

profile of v10, /device:TPU:0, one launch (start us, length us, event | category | flops | bytes accessed | tf_op | source)
XLA Modules:
  0.0 73.1 jit_solution(15053232433494440476)
XLA Ops:
  0.6 0.1 collective-permute-start
  0.7 2.1 %collective-permute-start.1 = (bf16[512,1024]{1,0:T(8,128)(2,1)}, bf16[512,1024]{1,0:T(8,128)(2,1)S(1)}, u32[]{:S(2)}, u32[]{:S(2)}) collective-permute-start(bf16[512,1024]{1,0:T(8,128)(2,1)} %refs_1_.3), channel_id=1, source_target_pairs={{0,2},{1,7},{2,4},{3,1},{4,6},{5,3},{6,0},{7,5},{8,10},{9,15},{10,... | collective-permute-start | bytes 3145736 | tf_op jit(solution)/shard_map/ppermute | solution.py:484
  2.8 3.8 %prelude.1 = (s32[24,128]{1,0:T(8,128)S(1)}, bf16[64,128,128]{2,1,0:T(8,128)(2,1)}) custom-call(s32[16,32]{1,0:T(8,128)} %refs_0_.1, s32[16,32]{1,0:T(8,128)} %refs_1_.2, s32[8,16]{1,0:T(8,128)} %bitcast.7, bf16[64,128,128]{2,1,0:T(8,128)(2,1)} %bitcast.5), custom_call_target="tpu_custom_call" | custom-call | bytes 1 | tf_op jit(solution)/shard_map/prelude/pallas_call | solution.py:120
  6.6 0.0 collective-permute-done.refs_1_
  6.6 2.0 %collective-permute-start.3 = (bf16[512,1024]{1,0:T(8,128)(2,1)S(1)}, bf16[512,1024]{1,0:T(8,128)(2,1)}, u32[]{:S(2)}, u32[]{:S(2)}) collective-permute-start(bf16[512,1024]{1,0:T(8,128)(2,1)S(1)} %after.3.refs_0_), channel_id=1, source_target_pairs={{0,2},{1,7},{2,4},{3,1},{4,6},{5,3},{6,0},{7,5},{8,10},{9,15},{10,... | collective-permute-start | bytes 3145736 | tf_op jit(solution)/shard_map/ppermute | solution.py:484
  8.6 7.1 %all-to-all-start = ((bf16[64,128,128]{2,1,0:T(8,128)(2,1)}), bf16[64,128,128]{2,1,0:T(8,128)(2,1)}, u32[]{:S(2)}, u32[]{:S(2)}) async-start(bf16[64,128,128]{2,1,0:T(8,128)(2,1)} %get-tuple-element.42), calls=%async_computation | async-start | bytes 4194304 | tf_op jit(solution)/shard_map/all_to_all | solution.py:501
  15.8 1.0 %fusion = (f32[512,64]{1,0:T(8,128)S(1)}, f32[512,64]{1,0:T(8,128)S(1)}, f32[512,64]{1,0:T(8,128)S(1)}) fusion(f32[64]{0:T(128)S(1)} %negate_power_fusion, f32[512]{0:T(512)S(1)} %add_convert_fusion), kind=kLoop, calls=%fused_computation.4 | loop fusion | flops 65536 | bytes 395520 | tf_op jit(solution)/shard_map/neg | solution.py:497
  16.8 0.2 pad_maximum_fusion
  17.0 0.0 copy-start
  17.0 0.0 copy-start.1
  17.0 3.9 %project.3 = (f32[512,512]{1,0:T(8,128)S(1)}, f32[512,256]{1,0:T(8,128)S(1)}, f32[512,128]{1,0:T(8,128)S(1)}) custom-call(bf16[512,1024]{1,0:T(8,128)(2,1)S(1)} %after.3.refs_0_, bf16[512,1024]{1,0:T(8,128)(2,1)} %refs_1_.3, bf16[8192,512]{1,0:T(8,128)(2,1)} %refs_7_.1, bf16[8192,256]{1,0:T(8,128)(2,1)} %refs_3_.5, ...), custom_call_target="tpu_custom_call" | custom-call | bytes 1 | tf_op jit(solution)/shard_map/project/pallas_call | solution.py:226
  20.8 0.0 collective-permute-done.1.refs_1_
  20.9 1.7 %collective-permute-start.5 = (bf16[512,1024]{1,0:T(8,128)(2,1)S(1)}, bf16[512,1024]{1,0:T(8,128)(2,1)S(1)}, u32[]{:S(2)}, u32[]{:S(2)}) collective-permute-start(bf16[512,1024]{1,0:T(8,128)(2,1)S(1)} %after.4.refs_0_), channel_id=1, source_target_pairs={{0,2},{1,7},{2,4},{3,1},{4,6},{5,3},{6,0},{7,5},{8,10},{9,15},{10,... | collective-permute-start | bytes 3145736 | tf_op jit(solution)/shard_map/ppermute | solution.py:484
  22.6 0.0 collective-permute-start.2
  22.6 6.7 %collective-permute-done.3.refs_1_ = bf16[512,1024]{1,0:T(8,128)(2,1)} collective-permute-done((bf16[512,1024]{1,0:T(8,128)(2,1)S(1)}, bf16[512,1024]{1,0:T(8,128)(2,1)}, u32[]{:S(2)}, u32[]{:S(2)}) %collective-permute-start.3) | collective-permute-done | bytes 1048608 | tf_op jit(solution)/shard_map/ppermute | solution.py:484
  29.2 0.0 collective-permute-start.4
  29.3 4.7 %project.4 = (f32[512,512]{1,0:T(8,128)S(1)}, f32[512,256]{1,0:T(8,128)S(1)}, f32[512,128]{1,0:T(8,128)S(1)}) custom-call(bf16[512,1024]{1,0:T(8,128)(2,1)S(1)} %after.4.refs_0_, bf16[512,1024]{1,0:T(8,128)(2,1)} %collective-permute-done.3.refs_1_, bf16[8192,512]{1,0:T(8,128)(2,1)} %refs_7_.1, bf16[8192,256]{1,0:T(8,128)(2,1)} %refs_3_.5, ...), custom_call_target="tpu_custom_call" | custom-call | flops 20000000000 | bytes 1 | tf_op jit(solution)/shard_map/project/pallas_call | solution.py:226
  34.0 0.0 collective-permute-done.2.refs_0_
  34.0 0.0 collective-permute-done.4.refs_1_
  34.0 3.9 %project.5 = (f32[512,512]{1,0:T(8,128)S(1)}, f32[512,256]{1,0:T(8,128)S(1)}, f32[512,128]{1,0:T(8,128)S(1)}, bf16[2,1024,512]{2,1,0:T(8,128)(2,1)S(1)}, bf16[2,1024,256]{2,1,0:T(8,128)(2,1)S(1)}) custom-call(bf16[512,1024]{1,0:T(8,128)(2,1)S(1)} %collective-permute-done.2.refs_0_, bf16[512,1024]{1,0:T(8,128)(2,1)S(1)} %collective-permute-done.4.refs_1_, ...), custom_call_target="tpu_custom_call" | custom-call | bytes 1 | tf_op jit(solution)/shard_map/project/pallas_call | solution.py:226
  37.9 2.5 %collective-permute-done.5.refs_1_ = bf16[512,1024]{1,0:T(8,128)(2,1)S(1)} collective-permute-done((bf16[512,1024]{1,0:T(8,128)(2,1)S(1)}, bf16[512,1024]{1,0:T(8,128)(2,1)S(1)}, u32[]{:S(2)}, u32[]{:S(2)}) %collective-permute-start.5) | collective-permute-done | bytes 1048608 | tf_op jit(solution)/shard_map/ppermute | solution.py:484
  40.4 0.0 collective-permute-start.6
  40.4 2.0 %project_far.1 = (f32[512,512]{1,0:T(8,128)}, f32[512,256]{1,0:T(8,128)S(1)}, f32[512,128]{1,0:T(8,128)S(1)}) custom-call(bf16[512,1024]{1,0:T(8,128)(2,1)S(1)} %after.5.x_ref, bf16[2,1024,512]{2,1,0:T(8,128)(2,1)S(1)} %get-tuple-element.31.wq_ref, bf16[2,1024,256]{2,1,0:T(8,128)(2,1)S(1)} %get-tuple-element.32.wkv_ref, ...), custom_call_target="tpu_custom_call" | custom-call | bytes 1 | tf_op jit(solution)/shard_map/project_far/pallas_call | solution.py:259
  42.4 0.6 collective-permute-done.6.x_ref
  43.0 0.0 copy-done
  43.0 0.0 copy-done.1
  43.0 2.7 %project_keyval.1 = (bf16[512,128]{1,0:T(8,128)(2,1)}, bf16[512,256]{1,0:T(8,128)(2,1)}, f32[512,128]{1,0:T(8,128)}, bf16[512,1024]{1,0:T(8,128)(2,1)}, bf16[32,128,128]{2,1,0:T(8,128)(2,1)}) custom-call(s32[24,128]{1,0:T(8,128)S(1)} %get-tuple-element.23.refs_0_.table_ref, bf16[512,1024]{1,0:T(8,128)(2,1)S(1)} %collective-permute-done.6.x_ref, ...), custom_call_target="tpu_custom_call" | custom-call | bytes 1 | tf_op jit(solution)/shard_map/project_keyval/pallas_call | solution.py:335
  45.7 4.2 %all-to-all-done.refs_8_ = bf16[64,128,128]{2,1,0:T(8,128)(2,1)} async-done(((bf16[64,128,128]{2,1,0:T(8,128)(2,1)}), bf16[64,128,128]{2,1,0:T(8,128)(2,1)}, u32[]{:S(2)}, u32[]{:S(2)}) %all-to-all-start) | async-done | bytes 2097184 | tf_op jit(solution)/shard_map/all_to_all | solution.py:501
  49.9 3.8 %all-to-all-start.1 = ((bf16[32,128,128]{2,1,0:T(8,128)(2,1)}), bf16[32,128,128]{2,1,0:T(8,128)(2,1)S(1)}, u32[]{:S(2)}, u32[]{:S(2)}) async-start(bf16[32,128,128]{2,1,0:T(8,128)(2,1)} %get-tuple-element.43), calls=%async_computation.1 | async-start | bytes 2097152 | tf_op jit(solution)/shard_map/all_to_all | solution.py:501
  53.7 15.7 %attend.1 = bf16[512,512]{1,0:T(8,128)(2,1)} custom-call(s32[24,128]{1,0:T(8,128)S(1)} %get-tuple-element.23.refs_0_.table_ref, f32[512,512]{1,0:T(8,128)} %get-tuple-element.35.refs_0_, bf16[512,1024]{1,0:T(8,128)(2,1)} %get-tuple-element.38.refs_1_, f32[512,128]{1,0:T(8,128)} %get-tuple-element.39.refs_2_, f32[512,128]{1,0:T(8,128)} %copy-done, ...), custom_call_target="tpu_custom_call" | custom-call | flops 5368709120 | bytes 8388608 | tf_op jit(solution)/shard_map/attend/pallas_call | solution.py:421
  69.4 1.7 %all-to-all-done.1.received_ref = bf16[32,128,128]{2,1,0:T(8,128)(2,1)S(1)} async-done(((bf16[32,128,128]{2,1,0:T(8,128)(2,1)}), bf16[32,128,128]{2,1,0:T(8,128)(2,1)S(1)}, u32[]{:S(2)}, u32[]{:S(2)}) %all-to-all-start.1) | async-done | bytes 1048608 | tf_op jit(solution)/shard_map/all_to_all | solution.py:501
  71.1 1.8 %place_pages.1 = bf16[32,128,128]{2,1,0:T(8,128)(2,1)} custom-call(s32[24,128]{1,0:T(8,128)S(1)} %get-tuple-element.23.refs_0_.table_ref, bf16[32,128,128]{2,1,0:T(8,128)(2,1)S(1)} %all-to-all-done.1.received_ref), custom_call_target="tpu_custom_call" | custom-call | bytes 2097152 | tf_op jit(solution)/shard_map/place_pages/pallas_call | solution.py:465
  (5 shorter events, 0.0 us)
Async XLA Ops:
  0.6 6.0 %collective-permute-start = (bf16[512,1024]{1,0:T(8,128)(2,1)}, bf16[512,1024]{1,0:T(8,128)(2,1)S(1)}, u32[]{:S(2)}, u32[]{:S(2)}) collective-permute-start(bf16[512,1024]{1,0:T(8,128)(2,1)} %refs_1_.3), channel_id=1, source_target_pairs={{0,1},{1,0},{2,3},{3,2},{4,5},{5,4},{6,7},{7,6},{8,9},{9,8},{10,11... | collective-permute-start | bytes 3145736 | tf_op jit(solution)/shard_map/ppermute | solution.py:488
  0.7 20.1 %collective-permute-start.1 = (bf16[512,1024]{1,0:T(8,128)(2,1)}, bf16[512,1024]{1,0:T(8,128)(2,1)S(1)}, u32[]{:S(2)}, u32[]{:S(2)}) collective-permute-start(bf16[512,1024]{1,0:T(8,128)(2,1)} %refs_1_.3), channel_id=1, source_target_pairs={{0,2},{1,7},{2,4},{3,1},{4,6},{5,3},{6,0},{7,5},{8,10},{9,15},{10,... | collective-permute-start | bytes 3145736 | tf_op jit(solution)/shard_map/ppermute | solution.py:484
  6.6 22.6 %collective-permute-start.3 = (bf16[512,1024]{1,0:T(8,128)(2,1)S(1)}, bf16[512,1024]{1,0:T(8,128)(2,1)}, u32[]{:S(2)}, u32[]{:S(2)}) collective-permute-start(bf16[512,1024]{1,0:T(8,128)(2,1)S(1)} %after.3.refs_0_), channel_id=1, source_target_pairs={{0,2},{1,7},{2,4},{3,1},{4,6},{5,3},{6,0},{7,5},{8,10},{9,15},{10,... | collective-permute-start | bytes 3145736 | tf_op jit(solution)/shard_map/ppermute | solution.py:484
  8.6 41.3 %all-to-all-start = ((bf16[64,128,128]{2,1,0:T(8,128)(2,1)}), bf16[64,128,128]{2,1,0:T(8,128)(2,1)}, u32[]{:S(2)}, u32[]{:S(2)}) async-start(bf16[64,128,128]{2,1,0:T(8,128)(2,1)} %get-tuple-element.42), calls=%async_computation | async-start | bytes 4194304 | tf_op jit(solution)/shard_map/all_to_all | solution.py:501
  17.0 26.1 %copy-start = (f32[512,128]{1,0:T(8,128)}, f32[512,128]{1,0:T(8,128)S(1)}, u32[]{:S(2)}) copy-start(f32[512,128]{1,0:T(8,128)S(1)} %get-tuple-element.49.refs_4_.cos_ref.refs_3_) | copy-start | bytes 786436
  17.0 26.1 %copy-start.1 = (f32[512,128]{1,0:T(8,128)}, f32[512,128]{1,0:T(8,128)S(1)}, u32[]{:S(2)}) copy-start(f32[512,128]{1,0:T(8,128)S(1)} %get-tuple-element.50.refs_5_.sin_ref.refs_4_) | copy-start | bytes 786436
  20.9 19.5 %collective-permute-start.5 = (bf16[512,1024]{1,0:T(8,128)(2,1)S(1)}, bf16[512,1024]{1,0:T(8,128)(2,1)S(1)}, u32[]{:S(2)}, u32[]{:S(2)}) collective-permute-start(bf16[512,1024]{1,0:T(8,128)(2,1)S(1)} %after.4.refs_0_), channel_id=1, source_target_pairs={{0,2},{1,7},{2,4},{3,1},{4,6},{5,3},{6,0},{7,5},{8,10},{9,15},{10,... | collective-permute-start | bytes 3145736 | tf_op jit(solution)/shard_map/ppermute | solution.py:484
  22.6 11.4 %collective-permute-start.2 = (bf16[512,1024]{1,0:T(8,128)(2,1)S(1)}, bf16[512,1024]{1,0:T(8,128)(2,1)S(1)}, u32[]{:S(2)}, u32[]{:S(2)}) collective-permute-start(bf16[512,1024]{1,0:T(8,128)(2,1)S(1)} %after.4.refs_0_), channel_id=1, source_target_pairs={{0,1},{1,0},{2,3},{3,2},{4,5},{5,4},{6,7},{7,6},{8,9},{9,8},{10,11... | collective-permute-start | bytes 3145736 | tf_op jit(solution)/shard_map/ppermute | solution.py:488
  29.2 4.8 %collective-permute-start.4 = (bf16[512,1024]{1,0:T(8,128)(2,1)}, bf16[512,1024]{1,0:T(8,128)(2,1)S(1)}, u32[]{:S(2)}, u32[]{:S(2)}) collective-permute-start(bf16[512,1024]{1,0:T(8,128)(2,1)} %collective-permute-done.3.refs_1_), channel_id=1, source_target_pairs={{0,1},{1,0},{2,3},{3,2},{4,5},{5,4},{6,7},{7,6},{8,9},{9,8},{10,11... | collective-permute-start | bytes 3145736 | tf_op jit(solution)/shard_map/ppermute | solution.py:488
  40.4 2.7 %collective-permute-start.6 = (bf16[512,1024]{1,0:T(8,128)(2,1)S(1)}, bf16[512,1024]{1,0:T(8,128)(2,1)S(1)}, u32[]{:S(2)}, u32[]{:S(2)}) collective-permute-start(bf16[512,1024]{1,0:T(8,128)(2,1)S(1)} %after.5.x_ref), channel_id=1, source_target_pairs={{0,1},{1,0},{2,3},{3,2},{4,5},{5,4},{6,7},{7,6},{8,9},{9,8},{10,11... | collective-permute-start | bytes 3145736 | tf_op jit(solution)/shard_map/ppermute | solution.py:488
  49.9 21.2 %all-to-all-start.1 = ((bf16[32,128,128]{2,1,0:T(8,128)(2,1)}), bf16[32,128,128]{2,1,0:T(8,128)(2,1)S(1)}, u32[]{:S(2)}, u32[]{:S(2)}) async-start(bf16[32,128,128]{2,1,0:T(8,128)(2,1)} %get-tuple-element.43), calls=%async_computation.1 | async-start | bytes 2097152 | tf_op jit(solution)/shard_map/all_to_all | solution.py:501

commit v11 on v10

--- a/solution.py
+++ b/solution.py
@@ -258,7 +258,7 @@
 def project_far(block, weights, sums):
     return pl.pallas_call(
         far_kernel,
-        out_shape=[pltpu.HBM((ROWS, QW), F32)] + [shape((ROWS, w), F32) for w in (KVW, HD)],
+        out_shape=[shape((ROWS, w), F32) for w in (QW, KVW, HD)],
         in_specs=[VMEM] * 6,
         out_specs=[VMEM] * 3,
         compiler_params=params(16),
@@ -289,26 +289,26 @@
     return values * cosine + pltpu.roll(values, HD // 2, 1) * sine
 
 
-def keyval_kernel(table_ref, x_ref, kv_in, sq_in, wkv_ref, cos_ref, sin_ref, *refs):
-    keys_out, values_out, inv_out, x_out, send_out = refs[:5]
-    keys_buf, values_buf, inv_buf, page_buf, index_ref, sems, page_sems = refs[5:]
-    indices = pltpu.make_async_copy(table_ref, index_ref, sems.at[0])
+def late_kernel(table_ref, x_ref, q_in, kv_in, sq_in, wq_ref, wkv_ref, cos_ref, sin_ref, *refs):
+    q_out, keys_out, values_out, send_out = refs[:4]
+    q_buf, keys_buf, values_buf, page_buf, index_ref, index_sem, sems, page_sems = refs[4:]
+    indices = pltpu.make_async_copy(table_ref, index_ref, index_sem)
     indices.start()
-    copies = [pltpu.make_async_copy(x_ref, x_out, sems.at[1])]
-    copies[0].start()
     row = lax.broadcasted_iota(jnp.int32, (2 * PAGE, 2 * PAGE), 0)
     column = lax.broadcasted_iota(jnp.int32, (2 * PAGE, 2 * PAGE), 1)
     picker = (column == (row >> 1) + (row & 1) * PAGE).astype(BF16)
     values_buf[:, HD:] = jnp.ones((ROWS, HD), BF16)
+    copies = []
     for r in range(0, ROWS, TILE):
         rows = slice(r, r + TILE)
         x = x_ref[rows, :]
         kv_sum = kv_in[rows, :] + jnp.dot(x, wkv_ref[1], preferred_element_type=F32)
+        q_sum = q_in[rows, :] + jnp.dot(x, wq_ref[1], preferred_element_type=F32)
         squares = sq_in[rows, :] + squares_of(x)
         mean = jnp.sum(squares, axis=1, keepdims=True) / D
         inv_norm = jnp.broadcast_to(lax.rsqrt(mean + 1e-05), (TILE, HD))
-        inv_buf[rows, :] = inv_norm
-        keys = turn(kv_sum[:, :HD] * inv_norm, cos_ref[rows, :], sin_ref[rows, :]).astype(BF16)
+        cosine, sine = cos_ref[rows, :], sin_ref[rows, :]
+        keys = turn(kv_sum[:, :HD] * inv_norm, cosine, sine).astype(BF16)
         values = (kv_sum[:, HD:] * inv_norm).astype(BF16)
         keys_buf[rows, :] = keys
         values_buf[rows, :HD] = values
@@ -321,33 +321,42 @@
             target = send_out.at[index_ref[page, PUSH]]
             copies.append(pltpu.make_async_copy(page_buf.at[page], target, page_sems.at[page]))
             copies[-1].start()
-    results = ((keys_buf, keys_out), (values_buf, values_out), (inv_buf, inv_out))
-    for i, (source, target) in enumerate(results):
-        copies.append(pltpu.make_async_copy(source, target, sems.at[2 + i]))
-        copies[-1].start()
+        for head in range(HEADS):
+            part = q_sum[:, head * HD : (head + 1) * HD] * inv_norm
+            q_buf[head, rows, :] = turn(part, cosine, sine).astype(BF16)
+        span = pl.ds(r, TILE)
+        results = (
+            (q_buf.at[:, span, :], q_out.at[:, span, :]),
+            (keys_buf.at[span, :], keys_out.at[span, :]),
+            (values_buf.at[span, :], values_out.at[span, :]),
+        )
+        for i, (source, target) in enumerate(results):
+            copies.append(pltpu.make_async_copy(source, target, sems.at[3 * (r // TILE) + i]))
+            copies[-1].start()
     for copy in copies:
         copy.wait()
 
 
-def project_keyval(table, block, sums, weights, cosine, sine):
-    kept = [((ROWS, HD), BF16), ((ROWS, 2 * HD), BF16), ((ROWS, HD), F32)]
-    sent = (POOL * PUSH_CAP, 2 * PAGE, HD)
-    return pl.pallas_call(
-        keyval_kernel,
-        out_shape=[pltpu.HBM(*x) for x in (*kept, ((ROWS, FEAT), BF16), (sent, BF16))],
-        in_specs=[VMEM] * 7,
-        out_specs=[HBM] * 5,
+def project_late(table, block, sums, weights, cosine, sine):
+    results = [(HEADS, ROWS, HD), (ROWS, HD), (ROWS, 2 * HD)]
+    return pl.pallas_call(
+        late_kernel,
+        out_shape=[pltpu.HBM(x, BF16) for x in results]
+        + [pltpu.HBM((POOL * PUSH_CAP, 2 * PAGE, HD), BF16)],
+        in_specs=[VMEM] * 9,
+        out_specs=[HBM] * 4,
         scratch_shapes=[
-            *[pltpu.VMEM(*x) for x in kept],
+            *[pltpu.VMEM(x, BF16) for x in results],
             pltpu.VMEM((NEW_PAGES, 2 * PAGE, HD), BF16),
             pltpu.SMEM((24, HD), jnp.int32),
-            pltpu.SemaphoreType.DMA((5,)),
+            pltpu.SemaphoreType.DMA,
+            pltpu.SemaphoreType.DMA((3 * ROWS // TILE,)),
             pltpu.SemaphoreType.DMA((NEW_PAGES,)),
         ],
         compiler_params=params(16),
         cost_estimate=cost(0, 1),
-        name="project_keyval",
-    )(table, block, *sums, weights, cosine, sine)
+        name="project_late",
+    )(table, block, *sums, *weights, cosine, sine)
 
 
 def dot_nt(a, b):
@@ -355,14 +364,11 @@
 
 
 def attend_kernel(table_ref, *refs):
-    sources, wq_ref, pages_ref, out_ref, refs = refs[:7], refs[7], refs[8], refs[9], refs[10:]
-    targets, wq_buf, index_ref, page_buf, q_buf, keys, values, sems, page_sems = refs[:7], *refs[7:]
-    q_sum, x, inv_norm, cosine, sine, own_keys, own_values = targets
-    indices = pltpu.make_async_copy(table_ref, index_ref, sems.at[8])
+    sources, out_ref, targets, (index_ref, keys, values, sems) = refs[:4], refs[4], refs[5:9], refs[9:]
+    page_buf, q_buf, own_keys, own_values = targets
+    indices = pltpu.make_async_copy(table_ref, index_ref, sems.at[4])
     indices.start()
     copies = [pltpu.make_async_copy(a, b, sems.at[i]) for i, (a, b) in enumerate(zip(sources, targets))]
-    rows = pl.ds(pl.multiple_of(block_index(FAR, True) * FEAT, FEAT), FEAT)
-    copies.insert(0, pltpu.make_async_copy(wq_ref.at[rows, :], wq_buf, sems.at[7]))
     for copy in copies:
         copy.start()
     row = lax.broadcasted_iota(jnp.int32, (2 * PAGE, 2 * PAGE), 0)
@@ -371,28 +377,14 @@
     picker = (column == wanted).astype(BF16)
     values[:, HD:] = jnp.ones((PAGES * PAGE, HD), BF16)
     indices.wait()
-    fetches = [
-        pltpu.make_async_copy(
-            pages_ref.at[index_ref[TAKE, page]], page_buf.at[page], page_sems.at[page]
-        )
-        for page in range(PAGES)
-    ]
-    for fetch in fetches:
-        fetch.start()
+    copies[0].wait()
     for page in range(PAGES):
-        fetches[page].wait()
-        both = jnp.dot(picker, page_buf[page], preferred_element_type=F32)
+        both = jnp.dot(picker, page_buf[index_ref[TAKE, page]], preferred_element_type=F32)
         rows = slice(page * PAGE, (page + 1) * PAGE)
         keys[rows, :] = both[:PAGE].astype(BF16)
         values[rows, :HD] = both[PAGE:].astype(BF16)
-    for copy in copies:
+    for copy in copies[1:]:
         copy.wait()
-    for r in range(0, ROWS, TILE):
-        rows = slice(r, r + TILE)
-        total = q_sum[rows, :] + jnp.dot(x[rows, :], wq_buf[...], preferred_element_type=F32)
-        for head in range(HEADS):
-            part = total[:, head * HD : (head + 1) * HD] * inv_norm[rows, :]
-            q_buf[head, rows, :] = turn(part, cosine[rows, :], sine[rows, :]).astype(BF16)
     block = 256
     allowed = lax.broadcasted_iota(jnp.int32, (block, block), 0) >= lax.broadcasted_iota(
         jnp.int32, (block, block), 1
@@ -417,27 +409,23 @@
             out_ref[rows, lanes] = (both[:, :HD] / both[:, HD:]).astype(BF16)
 
 
-def attend(table, pages, sources, w_query):
+def attend(table, *sources):
     return pl.pallas_call(
         attend_kernel,
         out_shape=shape((ROWS, QW), BF16),
-        in_specs=[VMEM] + [HBM] * (len(sources) + 2),
+        in_specs=[VMEM] + [HBM] * len(sources),
         out_specs=VMEM,
         scratch_shapes=[
             *[pltpu.VMEM(x.shape, x.dtype) for x in sources],
-            pltpu.VMEM((FEAT, QW), BF16),
             pltpu.SMEM((24, HD), jnp.int32),
-            pltpu.VMEM((PAGES, 2 * PAGE, HD), BF16),
-            pltpu.VMEM((HEADS, ROWS, HD), BF16),
             pltpu.VMEM((PAGES * PAGE, HD), BF16),
             pltpu.VMEM((PAGES * PAGE, 2 * HD), BF16),
-            pltpu.SemaphoreType.DMA((9,)),
-            pltpu.SemaphoreType.DMA((PAGES,)),
+            pltpu.SemaphoreType.DMA((5,)),
         ],
         compiler_params=params(40),
         cost_estimate=cost(2 * ROWS * 4 * 2560 * 512, 8 * MIB),
         name="attend",
-    )(table, *[hbm(x) for x in (*sources, w_query, pages)])
+    )(table, *[hbm(x) for x in sources])
 
 
 def place_kernel(table_ref, received_ref, out_ref, buffer, index_ref, index_sem, sems):
@@ -522,12 +510,11 @@
     (far,) = after((sums[2],), far)
     other = swap(far)
     sums = project_far(far, (last_q, last_kv), sums)
-    own_keys, own_values, inv_norm, other, send = project_keyval(
-        table, other, sums[1:], last_kv, *tables
+    queries, own_keys, own_values, send = project_late(
+        table, other, sums, (last_q, last_kv), *tables
     )
     received = exchange(send)
-    sources = (sums[0], other, inv_norm, *tables, own_keys, own_values)
-    attended = attend(table, pages, sources, w_query)
+    attended = attend(table, pages, queries, own_keys, own_values)
     placed = place_pages(table, received)
     return attended, placed.reshape(SLOTS, 1, PAGE, 2, HD)
 

time: 73.4 us -> 73.4 us (level)
  waiting for transfers between devices: 15.7 us -> 23.7 us
  Pallas kernels: 38.5 us -> 30.6 us
    pallas_call x1, Pallas kernels: 15.7 us -> 9.81 us  [attend(): pl.pallas_call(attend_kernel, out_shape=shape((ROWS, QW), BF16), in_specs...]
    all_to_all x2, waiting for transfers between devices: 5.89 us -> 11.5 us  [exchange(): lax.all_to_all(values, 'pool', split_axis=0, concat_axis=0, tiled=True)]
    ppermute x3, waiting for transfers between devices: 9.17 us -> 10.6 us  [shift(): return lax.ppermute(values, 'tp', pairs)]
    pallas_call x3, Pallas kernels: 12.5 us -> 11.1 us  [project(): pl.pallas_call(functools.partial(project_kernel, blocks, len(held), bool(...]
    ppermute x4, waiting for transfers between devices: 0.64 us -> 1.61 us  [swap(): return lax.ppermute(values, 'tp', [(i, i ^ 1) for i in range(8)])]
  transfers between devices with their start and end apart: 9 -> 9, of which waited for: 5 -> 5; matrix products, arithmetic and copies ran while one was open for 2% -> 2% of each run, Pallas kernels for 50% -> 39%
where the time goes in v11:
time: 73.4 us; the launch traced here: 73.1 us
  Pallas kernels  30.6 us (42%)
  waiting for transfers between devices  23.7 us (32%)
  starting transfers between devices  16.6 us (23%)
  other arithmetic  1.21 us (2%)
  between operations  0.95 us (1%)
    all_to_all x2, waiting for transfers between devices, exchange(): lax.all_to_all(values, 'pool', split_axis=0, concat_axis=0, tiled=True)  11.5 us
    pallas_call x3, Pallas kernels, project(): pl.pallas_call(functools.partial(project_kernel, blocks, len(held), bool(...  11.1 us
    all_to_all x2, starting transfers between devices, exchange(): lax.all_to_all(values, 'pool', split_axis=0, concat_axis=0, tiled=True)  10.7 us
    ppermute x3, waiting for transfers between devices, shift(): return lax.ppermute(values, 'tp', pairs)  10.6 us
    pallas_call x1, Pallas kernels, attend(): pl.pallas_call(attend_kernel, out_shape=shape((ROWS, QW), BF16), in_specs...  9.81 us
    ppermute x3, starting transfers between devices, shift(): return lax.ppermute(values, 'tp', pairs)  5.75 us
    pallas_call x1, Pallas kernels, prelude(): pl.pallas_call(prelude_kernel, out_shape=[shape((24, HD), jnp.int32), plt...  3.81 us
    pallas_call x1, Pallas kernels, project_late(): pl.pallas_call(late_kernel, out_shape=[pltpu.HBM(x, BF16) for x in result...  3.07 us
  transfers between devices with their start and end apart: 9, of which 5 were waited for; matrix products, arithmetic and copies ran while one was open for 2% of the time, Pallas kernels for 39%

profile of v11, /device:TPU:0, one launch (start us, length us, event | category | flops | bytes accessed | tf_op | source)
XLA Modules:
  0.0 73.1 jit_solution(9462033901400643470)
XLA Ops:
  0.6 0.1 collective-permute-start
  0.7 2.1 %collective-permute-start.1 = (bf16[512,1024]{1,0:T(8,128)(2,1)}, bf16[512,1024]{1,0:T(8,128)(2,1)S(1)}, u32[]{:S(2)}, u32[]{:S(2)}) collective-permute-start(bf16[512,1024]{1,0:T(8,128)(2,1)} %refs_1_.3), channel_id=1, source_target_pairs={{0,2},{1,7},{2,4},{3,1},{4,6},{5,3},{6,0},{7,5},{8,10},{9,15},{10,... | collective-permute-start | bytes 3145736 | tf_op jit(solution)/shard_map/ppermute | solution.py:472
  2.8 3.8 %prelude.1 = (s32[24,128]{1,0:T(8,128)S(1)}, bf16[64,128,128]{2,1,0:T(8,128)(2,1)}) custom-call(s32[16,32]{1,0:T(8,128)} %refs_0_.1, s32[16,32]{1,0:T(8,128)} %refs_1_.2, s32[8,16]{1,0:T(8,128)} %bitcast.7, bf16[64,128,128]{2,1,0:T(8,128)(2,1)} %bitcast.5), custom_call_target="tpu_custom_call" | custom-call | bytes 1 | tf_op jit(solution)/shard_map/prelude/pallas_call | solution.py:120
  6.6 0.0 collective-permute-done.refs_1_
  6.6 2.0 %collective-permute-start.3 = (bf16[512,1024]{1,0:T(8,128)(2,1)S(1)}, bf16[512,1024]{1,0:T(8,128)(2,1)S(1)}, u32[]{:S(2)}, u32[]{:S(2)}) collective-permute-start(bf16[512,1024]{1,0:T(8,128)(2,1)S(1)} %after.3.refs_0_), channel_id=1, source_target_pairs={{0,2},{1,7},{2,4},{3,1},{4,6},{5,3},{6,0},{7,5},{8,10},{9,15},{10,... | collective-permute-start | bytes 3145736 | tf_op jit(solution)/shard_map/ppermute | solution.py:472
  8.6 7.1 %all-to-all-start = ((bf16[64,128,128]{2,1,0:T(8,128)(2,1)}), bf16[64,128,128]{2,1,0:T(8,128)(2,1)}, u32[]{:S(2)}, u32[]{:S(2)}) async-start(bf16[64,128,128]{2,1,0:T(8,128)(2,1)} %get-tuple-element.23), calls=%async_computation | async-start | bytes 4194304 | tf_op jit(solution)/shard_map/all_to_all | solution.py:489
  15.7 1.0 %fusion = (f32[512,64]{1,0:T(8,128)S(1)}, f32[512,64]{1,0:T(8,128)S(1)}, f32[512,64]{1,0:T(8,128)S(1)}) fusion(f32[64]{0:T(128)S(1)} %negate_power_fusion, f32[512]{0:T(512)S(1)} %add_convert_fusion), kind=kLoop, calls=%fused_computation.4 | loop fusion | flops 65536 | bytes 395520 | tf_op jit(solution)/shard_map/neg | solution.py:485
  16.7 0.2 pad_maximum_fusion
  16.9 3.7 %project.3 = (f32[512,512]{1,0:T(8,128)S(1)}, f32[512,256]{1,0:T(8,128)S(1)}, f32[512,128]{1,0:T(8,128)S(1)}) custom-call(bf16[512,1024]{1,0:T(8,128)(2,1)S(1)} %after.3.refs_0_, bf16[512,1024]{1,0:T(8,128)(2,1)} %refs_1_.3, bf16[8192,512]{1,0:T(8,128)(2,1)} %refs_2_.5, bf16[8192,256]{1,0:T(8,128)(2,1)} %refs_3_.5, ...), custom_call_target="tpu_custom_call" | custom-call | bytes 1 | tf_op jit(solution)/shard_map/project/pallas_call | solution.py:226
  20.6 0.0 collective-permute-done.1.refs_1_
  20.6 1.7 %collective-permute-start.5 = (bf16[512,1024]{1,0:T(8,128)(2,1)S(1)}, bf16[512,1024]{1,0:T(8,128)(2,1)S(1)}, u32[]{:S(2)}, u32[]{:S(2)}) collective-permute-start(bf16[512,1024]{1,0:T(8,128)(2,1)S(1)} %after.4.refs_0_), channel_id=1, source_target_pairs={{0,2},{1,7},{2,4},{3,1},{4,6},{5,3},{6,0},{7,5},{8,10},{9,15},{10,... | collective-permute-start | bytes 3145736 | tf_op jit(solution)/shard_map/ppermute | solution.py:472
  22.3 0.0 collective-permute-start.2
  22.3 6.8 %collective-permute-done.3.refs_1_ = bf16[512,1024]{1,0:T(8,128)(2,1)S(1)} collective-permute-done((bf16[512,1024]{1,0:T(8,128)(2,1)S(1)}, bf16[512,1024]{1,0:T(8,128)(2,1)S(1)}, u32[]{:S(2)}, u32[]{:S(2)}) %collective-permute-start.3) | collective-permute-done | bytes 1048608 | tf_op jit(solution)/shard_map/ppermute | solution.py:472
  29.1 0.0 collective-permute-start.4
  29.1 3.6 %project.4 = (f32[512,512]{1,0:T(8,128)S(1)}, f32[512,256]{1,0:T(8,128)S(1)}, f32[512,128]{1,0:T(8,128)S(1)}) custom-call(bf16[512,1024]{1,0:T(8,128)(2,1)S(1)} %after.4.refs_0_, bf16[512,1024]{1,0:T(8,128)(2,1)S(1)} %collective-permute-done.3.refs_1_, bf16[8192,512]{1,0:T(8,128)(2,1)} %refs_2_.5, bf16[8192,256]{1,0:T(8,128)(2,1)} %refs_3_.5, ...), custom_call_target="tpu_custom_call" | custom-call | flops 20000000000 | bytes 1 | tf_op jit(solution)/shard_map/project/pallas_call | solution.py:226
  32.7 0.0 collective-permute-done.2.refs_0_
  32.7 0.0 collective-permute-done.4.refs_1_
  32.8 3.9 %project.5 = (f32[512,512]{1,0:T(8,128)S(1)}, f32[512,256]{1,0:T(8,128)S(1)}, f32[512,128]{1,0:T(8,128)S(1)}, bf16[2,1024,512]{2,1,0:T(8,128)(2,1)S(1)}, bf16[2,1024,256]{2,1,0:T(8,128)(2,1)S(1)}) custom-call(bf16[512,1024]{1,0:T(8,128)(2,1)S(1)} %collective-permute-done.2.refs_0_, bf16[512,1024]{1,0:T(8,128)(2,1)S(1)} %collective-permute-done.4.refs_1_, ...), custom_call_target="tpu_custom_call" | custom-call | bytes 1 | tf_op jit(solution)/shard_map/project/pallas_call | solution.py:226
  36.6 3.8 %collective-permute-done.5.refs_1_ = bf16[512,1024]{1,0:T(8,128)(2,1)S(1)} collective-permute-done((bf16[512,1024]{1,0:T(8,128)(2,1)S(1)}, bf16[512,1024]{1,0:T(8,128)(2,1)S(1)}, u32[]{:S(2)}, u32[]{:S(2)}) %collective-permute-start.5) | collective-permute-done | bytes 1048608 | tf_op jit(solution)/shard_map/ppermute | solution.py:472
  40.4 0.0 collective-permute-start.6
  40.4 1.0 %project_far.1 = (f32[512,512]{1,0:T(8,128)S(1)}, f32[512,256]{1,0:T(8,128)S(1)}, f32[512,128]{1,0:T(8,128)S(1)}) custom-call(bf16[512,1024]{1,0:T(8,128)(2,1)S(1)} %after.5.x_ref, bf16[2,1024,512]{2,1,0:T(8,128)(2,1)S(1)} %get-tuple-element.31.wq_ref, bf16[2,1024,256]{2,1,0:T(8,128)(2,1)S(1)} %get-tuple-element.32.wkv_ref, ...), custom_call_target="tpu_custom_call" | custom-call | bytes 1 | tf_op jit(solution)/shard_map/project_far/pallas_call | solution.py:259
  41.4 1.6 %collective-permute-done.6.x_ref = bf16[512,1024]{1,0:T(8,128)(2,1)S(1)} collective-permute-done((bf16[512,1024]{1,0:T(8,128)(2,1)S(1)}, bf16[512,1024]{1,0:T(8,128)(2,1)S(1)}, u32[]{:S(2)}, u32[]{:S(2)}) %collective-permute-start.6) | collective-permute-done | bytes 1048608 | tf_op jit(solution)/shard_map/ppermute | solution.py:476
  43.0 3.1 %project_late.1 = (bf16[4,512,128]{2,1,0:T(8,128)(2,1)}, bf16[512,128]{1,0:T(8,128)(2,1)}, bf16[512,256]{1,0:T(8,128)(2,1)}, bf16[32,128,128]{2,1,0:T(8,128)(2,1)}) custom-call(s32[24,128]{1,0:T(8,128)S(1)} %get-tuple-element.22.refs_0_.table_ref, bf16[512,1024]{1,0:T(8,128)(2,1)S(1)} %collective-permute-done.6.x_ref, ...), custom_call_target="tpu_custom_call" | custom-call | bytes 1 | tf_op jit(solution)/shard_map/project_late/pallas_call | solution.py:342
  46.1 3.8 %all-to-all-done.refs_0_ = bf16[64,128,128]{2,1,0:T(8,128)(2,1)} async-done(((bf16[64,128,128]{2,1,0:T(8,128)(2,1)}), bf16[64,128,128]{2,1,0:T(8,128)(2,1)}, u32[]{:S(2)}, u32[]{:S(2)}) %all-to-all-start) | async-done | bytes 2097184 | tf_op jit(solution)/shard_map/all_to_all | solution.py:489
  49.9 3.7 %all-to-all-start.1 = ((bf16[32,128,128]{2,1,0:T(8,128)(2,1)}), bf16[32,128,128]{2,1,0:T(8,128)(2,1)S(1)}, u32[]{:S(2)}, u32[]{:S(2)}) async-start(bf16[32,128,128]{2,1,0:T(8,128)(2,1)} %get-tuple-element.41), calls=%async_computation.1 | async-start | bytes 2097152 | tf_op jit(solution)/shard_map/all_to_all | solution.py:489
  53.5 9.8 %attend.1 = bf16[512,512]{1,0:T(8,128)(2,1)} custom-call(s32[24,128]{1,0:T(8,128)S(1)} %get-tuple-element.22.refs_0_.table_ref, bf16[64,128,128]{2,1,0:T(8,128)(2,1)} %all-to-all-done.refs_0_, bf16[4,512,128]{2,1,0:T(8,128)(2,1)} %get-tuple-element.38.refs_1_, bf16[512,128]{1,0:T(8,128)(2,1)} %get-tuple-element.39.refs_2_, ...), custom_call_target="tpu_custom_call" | custom-call | flops 5368709120 | bytes 8388608 | tf_op jit(solution)/shard_map/attend/pallas_call | solution.py:413
  63.4 7.8 %all-to-all-done.1.received_ref = bf16[32,128,128]{2,1,0:T(8,128)(2,1)S(1)} async-done(((bf16[32,128,128]{2,1,0:T(8,128)(2,1)}), bf16[32,128,128]{2,1,0:T(8,128)(2,1)S(1)}, u32[]{:S(2)}, u32[]{:S(2)}) %all-to-all-start.1) | async-done | bytes 1048608 | tf_op jit(solution)/shard_map/all_to_all | solution.py:489
  71.1 1.8 %place_pages.1 = bf16[32,128,128]{2,1,0:T(8,128)(2,1)} custom-call(s32[24,128]{1,0:T(8,128)S(1)} %get-tuple-element.22.refs_0_.table_ref, bf16[32,128,128]{2,1,0:T(8,128)(2,1)S(1)} %all-to-all-done.1.received_ref), custom_call_target="tpu_custom_call" | custom-call | bytes 2097152 | tf_op jit(solution)/shard_map/place_pages/pallas_call | solution.py:453
  (5 shorter events, 0.0 us)
Async XLA Ops:
  0.6 6.0 %collective-permute-start = (bf16[512,1024]{1,0:T(8,128)(2,1)}, bf16[512,1024]{1,0:T(8,128)(2,1)S(1)}, u32[]{:S(2)}, u32[]{:S(2)}) collective-permute-start(bf16[512,1024]{1,0:T(8,128)(2,1)} %refs_1_.3), channel_id=1, source_target_pairs={{0,1},{1,0},{2,3},{3,2},{4,5},{5,4},{6,7},{7,6},{8,9},{9,8},{10,11... | collective-permute-start | bytes 3145736 | tf_op jit(solution)/shard_map/ppermute | solution.py:476
  0.7 19.9 %collective-permute-start.1 = (bf16[512,1024]{1,0:T(8,128)(2,1)}, bf16[512,1024]{1,0:T(8,128)(2,1)S(1)}, u32[]{:S(2)}, u32[]{:S(2)}) collective-permute-start(bf16[512,1024]{1,0:T(8,128)(2,1)} %refs_1_.3), channel_id=1, source_target_pairs={{0,2},{1,7},{2,4},{3,1},{4,6},{5,3},{6,0},{7,5},{8,10},{9,15},{10,... | collective-permute-start | bytes 3145736 | tf_op jit(solution)/shard_map/ppermute | solution.py:472
  6.6 22.5 %collective-permute-start.3 = (bf16[512,1024]{1,0:T(8,128)(2,1)S(1)}, bf16[512,1024]{1,0:T(8,128)(2,1)S(1)}, u32[]{:S(2)}, u32[]{:S(2)}) collective-permute-start(bf16[512,1024]{1,0:T(8,128)(2,1)S(1)} %after.3.refs_0_), channel_id=1, source_target_pairs={{0,2},{1,7},{2,4},{3,1},{4,6},{5,3},{6,0},{7,5},{8,10},{9,15},{10,... | collective-permute-start | bytes 3145736 | tf_op jit(solution)/shard_map/ppermute | solution.py:472
  8.6 41.3 %all-to-all-start = ((bf16[64,128,128]{2,1,0:T(8,128)(2,1)}), bf16[64,128,128]{2,1,0:T(8,128)(2,1)}, u32[]{:S(2)}, u32[]{:S(2)}) async-start(bf16[64,128,128]{2,1,0:T(8,128)(2,1)} %get-tuple-element.23), calls=%async_computation | async-start | bytes 4194304 | tf_op jit(solution)/shard_map/all_to_all | solution.py:489
  20.6 19.7 %collective-permute-start.5 = (bf16[512,1024]{1,0:T(8,128)(2,1)S(1)}, bf16[512,1024]{1,0:T(8,128)(2,1)S(1)}, u32[]{:S(2)}, u32[]{:S(2)}) collective-permute-start(bf16[512,1024]{1,0:T(8,128)(2,1)S(1)} %after.4.refs_0_), channel_id=1, source_target_pairs={{0,2},{1,7},{2,4},{3,1},{4,6},{5,3},{6,0},{7,5},{8,10},{9,15},{10,... | collective-permute-start | bytes 3145736 | tf_op jit(solution)/shard_map/ppermute | solution.py:472
  22.3 10.4 %collective-permute-start.2 = (bf16[512,1024]{1,0:T(8,128)(2,1)S(1)}, bf16[512,1024]{1,0:T(8,128)(2,1)S(1)}, u32[]{:S(2)}, u32[]{:S(2)}) collective-permute-start(bf16[512,1024]{1,0:T(8,128)(2,1)S(1)} %after.4.refs_0_), channel_id=1, source_target_pairs={{0,1},{1,0},{2,3},{3,2},{4,5},{5,4},{6,7},{7,6},{8,9},{9,8},{10,11... | collective-permute-start | bytes 3145736 | tf_op jit(solution)/shard_map/ppermute | solution.py:476
  29.1 3.6 %collective-permute-start.4 = (bf16[512,1024]{1,0:T(8,128)(2,1)S(1)}, bf16[512,1024]{1,0:T(8,128)(2,1)S(1)}, u32[]{:S(2)}, u32[]{:S(2)}) collective-permute-start(bf16[512,1024]{1,0:T(8,128)(2,1)S(1)} %collective-permute-done.3.refs_1_), channel_id=1, source_target_pairs={{0,1},{1,0},{2,3},{3,2},{4,5},{5,4},{6,7},{7,6},{8,9},{9,8},{10,11... | collective-permute-start | bytes 3145736 | tf_op jit(solution)/shard_map/ppermute | solution.py:476
  40.4 2.7 %collective-permute-start.6 = (bf16[512,1024]{1,0:T(8,128)(2,1)S(1)}, bf16[512,1024]{1,0:T(8,128)(2,1)S(1)}, u32[]{:S(2)}, u32[]{:S(2)}) collective-permute-start(bf16[512,1024]{1,0:T(8,128)(2,1)S(1)} %after.5.x_ref), channel_id=1, source_target_pairs={{0,1},{1,0},{2,3},{3,2},{4,5},{5,4},{6,7},{7,6},{8,9},{9,8},{10,11... | collective-permute-start | bytes 3145736 | tf_op jit(solution)/shard_map/ppermute | solution.py:476
  49.9 21.2 %all-to-all-start.1 = ((bf16[32,128,128]{2,1,0:T(8,128)(2,1)}), bf16[32,128,128]{2,1,0:T(8,128)(2,1)S(1)}, u32[]{:S(2)}, u32[]{:S(2)}) async-start(bf16[32,128,128]{2,1,0:T(8,128)(2,1)} %get-tuple-element.41), calls=%async_computation.1 | async-start | bytes 2097152 | tf_op jit(solution)/shard_map/all_to_all | solution.py:489

commit v12 on v11

--- a/solution.py
+++ b/solution.py
@@ -494,19 +494,18 @@
     table, packed = prelude(page_owner, page_slot, new_owner, store.reshape(64, 2 * PAGE, HD))
     pages = exchange(packed)
     sibling = swap(hidden)
-    (sibling,) = after((table,), sibling)
     back = shift(sibling, (1, -1))
     tables = rope_tables(ROWS, PAGES * PAGE)
     weights = (w_query, w_keyval)
     blocks = ((OWN, True), (OWN, False))
-    sums = project(blocks, [sibling], [hidden], *weights, tokens=tables)
+    sums = project(blocks, [sibling], [hidden], *weights, tokens=tables, flops=HIDES)
+    blocks = ((NEAR, True), (NEAR, False))
+    sums = project(blocks, [swap(near), near], [], *weights, sums, flops=HIDES)
     (near,) = after((sums[2],), near)
     far = shift(near, (1, -1))
-    blocks = ((NEAR, False), (BACK, True))
-    sums = project(blocks, [near, back], [], *weights, sums, flops=HIDES)
-    blocks, ahead = ((NEAR, True), (BACK, False)), ((FAR, False), (FAR, True))
-    held = [swap(near), swap(back)]
-    *sums, last_q, last_kv = project(blocks, held, [], *weights, sums, ahead)
+    sums = project(((BACK, True),), [back], [], *weights, sums, flops=HIDES)
+    blocks, ahead = ((BACK, False),), ((FAR, False), (FAR, True))
+    *sums, last_q, last_kv = project(blocks, [swap(back)], [], *weights, sums, ahead)
     (far,) = after((sums[2],), far)
     other = swap(far)
     sums = project_far(far, (last_q, last_kv), sums)

time: 73.4 us -> 75.3 us (1.026)
  waiting for transfers between devices: 23.7 us -> 20.8 us
  starting transfers between devices: 16.6 us -> 19.4 us
  Pallas kernels: 30.6 us -> 32.7 us
    all_to_all x2, waiting for transfers between devices: 11.5 us -> 7.99 us  [exchange(): lax.all_to_all(values, 'pool', split_axis=0, concat_axis=0, tiled=True)]
    all_to_all x2, starting transfers between devices: 10.7 us -> 14.3 us  [exchange(): lax.all_to_all(values, 'pool', split_axis=0, concat_axis=0, tiled=True)]
    pallas_call x3 -> x4, Pallas kernels: 11.1 us -> 13.1 us  [project(): pl.pallas_call(functools.partial(project_kernel, blocks, len(held), bool(...]
    ppermute x3, starting transfers between devices: 5.75 us -> 4.97 us  [shift(): return lax.ppermute(values, 'tp', pairs)]
  transfers between devices with their start and end apart: 9 -> 9, of which waited for: 5 -> 6; matrix products, arithmetic and copies ran while one was open for 2% -> 2% of each run, Pallas kernels for 39% -> 41%
where the time goes in v12:
time: 75.3 us; the launch traced here: 75 us
  Pallas kernels  32.7 us (43%)
  waiting for transfers between devices  20.8 us (28%)
  starting transfers between devices  19.4 us (26%)
  other arithmetic  1.21 us (2%)
  between operations  0.94 us (1%)
    all_to_all x2, starting transfers between devices, exchange(): lax.all_to_all(values, 'pool', split_axis=0, concat_axis=0, tiled=True)  14.3 us
    pallas_call x4, Pallas kernels, project(): pl.pallas_call(functools.partial(project_kernel, blocks, len(held), bool(...  13.1 us
    ppermute x3, waiting for transfers between devices, shift(): return lax.ppermute(values, 'tp', pairs)  11.1 us
    pallas_call x1, Pallas kernels, attend(): pl.pallas_call(attend_kernel, out_shape=shape((ROWS, QW), BF16), in_specs...  9.81 us
    all_to_all x2, waiting for transfers between devices, exchange(): lax.all_to_all(values, 'pool', split_axis=0, concat_axis=0, tiled=True)  7.99 us
    ppermute x3, starting transfers between devices, shift(): return lax.ppermute(values, 'tp', pairs)  4.97 us
    pallas_call x1, Pallas kernels, prelude(): pl.pallas_call(prelude_kernel, out_shape=[shape((24, HD), jnp.int32), plt...  3.8 us
    pallas_call x1, Pallas kernels, project_late(): pl.pallas_call(late_kernel, out_shape=[pltpu.HBM(x, BF16) for x in result...  3.07 us
  transfers between devices with their start and end apart: 9, of which 6 were waited for; matrix products, arithmetic and copies ran while one was open for 2% of the time, Pallas kernels for 41%

profile of v12, /device:TPU:0, one launch (start us, length us, event | category | flops | bytes accessed | tf_op | source)
XLA Modules:
  0.0 75.0 jit_solution(2500561438372459766)
XLA Ops:
  0.6 0.1 collective-permute-start
  0.7 2.1 %collective-permute-start.3 = (bf16[512,1024]{1,0:T(8,128)(2,1)}, bf16[512,1024]{1,0:T(8,128)(2,1)S(1)}, u32[]{:S(2)}, u32[]{:S(2)}) collective-permute-start(bf16[512,1024]{1,0:T(8,128)(2,1)} %refs_1_.5), channel_id=1, source_target_pairs={{0,2},{1,7},{2,4},{3,1},{4,6},{5,3},{6,0},{7,5},{8,10},{9,15},{10,... | collective-permute-start | bytes 3145736 | tf_op jit(solution)/shard_map/ppermute | solution.py:472
  2.8 3.8 %prelude.1 = (s32[24,128]{1,0:T(8,128)S(1)}, bf16[64,128,128]{2,1,0:T(8,128)(2,1)}) custom-call(s32[16,32]{1,0:T(8,128)} %refs_0_.1, s32[16,32]{1,0:T(8,128)} %refs_1_.4, s32[8,16]{1,0:T(8,128)} %bitcast.7, bf16[64,128,128]{2,1,0:T(8,128)(2,1)} %bitcast.5), custom_call_target="tpu_custom_call" | custom-call | bytes 1 | tf_op jit(solution)/shard_map/prelude/pallas_call | solution.py:120
  6.6 7.1 %all-to-all-start = ((bf16[64,128,128]{2,1,0:T(8,128)(2,1)}), bf16[64,128,128]{2,1,0:T(8,128)(2,1)}, u32[]{:S(2)}, u32[]{:S(2)}) async-start(bf16[64,128,128]{2,1,0:T(8,128)(2,1)} %get-tuple-element.26), calls=%async_computation | async-start | bytes 4194304 | tf_op jit(solution)/shard_map/all_to_all | solution.py:489
  13.7 1.0 %fusion = (f32[512,64]{1,0:T(8,128)S(1)}, f32[512,64]{1,0:T(8,128)S(1)}, f32[512,64]{1,0:T(8,128)S(1)}) fusion(f32[64]{0:T(128)S(1)} %negate_power_fusion, f32[512]{0:T(512)S(1)} %add_convert_fusion), kind=kLoop, calls=%fused_computation.4 | loop fusion | flops 65536 | bytes 395520 | tf_op jit(solution)/shard_map/neg | solution.py:485
  14.7 0.2 pad_maximum_fusion
  14.9 0.0 collective-permute-done.refs_0_
  15.0 2.0 %collective-permute-start.1 = (bf16[512,1024]{1,0:T(8,128)(2,1)S(1)}, bf16[512,1024]{1,0:T(8,128)(2,1)S(1)}, u32[]{:S(2)}, u32[]{:S(2)}) collective-permute-start(bf16[512,1024]{1,0:T(8,128)(2,1)S(1)} %collective-permute-done.refs_0_), channel_id=1, source_target_pairs={{0,2},{1,7},{2,4},{3,1},{4,6},{5,3},{6,0},{7,5},{8,10},{9,15},{10,... | collective-permute-start | bytes 3145736 | tf_op jit(solution)/shard_map/ppermute | solution.py:472
  16.9 1.0 %collective-permute-done.3.refs_1_ = bf16[512,1024]{1,0:T(8,128)(2,1)S(1)} collective-permute-done((bf16[512,1024]{1,0:T(8,128)(2,1)}, bf16[512,1024]{1,0:T(8,128)(2,1)S(1)}, u32[]{:S(2)}, u32[]{:S(2)}) %collective-permute-start.3) | collective-permute-done | bytes 1048608 | tf_op jit(solution)/shard_map/ppermute | solution.py:472
  17.9 0.0 collective-permute-start.4
  17.9 3.7 %project.4 = (f32[512,512]{1,0:T(8,128)S(1)}, f32[512,256]{1,0:T(8,128)S(1)}, f32[512,128]{1,0:T(8,128)S(1)}) custom-call(bf16[512,1024]{1,0:T(8,128)(2,1)S(1)} %collective-permute-done.refs_0_, bf16[512,1024]{1,0:T(8,128)(2,1)} %refs_1_.5, bf16[8192,512]{1,0:T(8,128)(2,1)} %refs_1_.7, bf16[8192,256]{1,0:T(8,128)(2,1)} %refs_2_.7, ...), custom_call_target="tpu_custom_call" | custom-call | flops 20000000000 | bytes 1 | tf_op jit(solution)/shard_map/project/pallas_call | solution.py:226
  21.6 0.0 collective-permute-done.4.refs_0_
  21.6 3.6 %project.5 = (f32[512,512]{1,0:T(8,128)S(1)}, f32[512,256]{1,0:T(8,128)S(1)}, f32[512,128]{1,0:T(8,128)S(1)}) custom-call(bf16[512,1024]{1,0:T(8,128)(2,1)S(1)} %collective-permute-done.4.refs_0_, bf16[512,1024]{1,0:T(8,128)(2,1)S(1)} %collective-permute-done.3.refs_1_, bf16[8192,512]{1,0:T(8,128)(2,1)} %refs_1_.7, bf16[8192,256]{1,0:T(8,128)(2,1)} %refs_2_.7, ...), custom_call_target="tpu_custom_call" | custom-call | flops 20000000000 | bytes 1 | tf_op jit(solution)/shard_map/project/pallas_call | solution.py:226
  25.2 0.9 %collective-permute-start.5 = (bf16[512,1024]{1,0:T(8,128)(2,1)S(1)}, bf16[512,1024]{1,0:T(8,128)(2,1)S(1)}, u32[]{:S(2)}, u32[]{:S(2)}) collective-permute-start(bf16[512,1024]{1,0:T(8,128)(2,1)S(1)} %after.2), channel_id=1, source_target_pairs={{0,2},{1,7},{2,4},{3,1},{4,6},{5,3},{6,0},{7,5},{8,10},{9,15},{10,... | collective-permute-start | bytes 3145736 | tf_op jit(solution)/shard_map/ppermute | solution.py:472
  26.1 4.9 %collective-permute-done.1.refs_0_ = bf16[512,1024]{1,0:T(8,128)(2,1)S(1)} collective-permute-done((bf16[512,1024]{1,0:T(8,128)(2,1)S(1)}, bf16[512,1024]{1,0:T(8,128)(2,1)S(1)}, u32[]{:S(2)}, u32[]{:S(2)}) %collective-permute-start.1) | collective-permute-done | bytes 1048608 | tf_op jit(solution)/shard_map/ppermute | solution.py:472
  31.0 0.0 collective-permute-start.2
  31.1 2.5 %project.6 = (f32[512,512]{1,0:T(8,128)S(1)}, f32[512,256]{1,0:T(8,128)S(1)}, f32[512,128]{1,0:T(8,128)S(1)}) custom-call(bf16[512,1024]{1,0:T(8,128)(2,1)S(1)} %collective-permute-done.1.refs_0_, bf16[8192,512]{1,0:T(8,128)(2,1)} %refs_1_.7, bf16[8192,256]{1,0:T(8,128)(2,1)} %refs_2_.7, f32[512,512]{1,0:T(8,128)S(1)} %get-tuple-element.30.refs_3_, ...), custom_call_target="tpu_custom_call" | custom-call | flops 20000000000 | bytes 1 | tf_op jit(solution)/shard_map/project/pallas_call | solution.py:226
  33.6 0.1 collective-permute-done.2.refs_0_
  33.7 3.3 %project.7 = (f32[512,512]{1,0:T(8,128)S(1)}, f32[512,256]{1,0:T(8,128)S(1)}, f32[512,128]{1,0:T(8,128)S(1)}, bf16[2,1024,512]{2,1,0:T(8,128)(2,1)S(1)}, bf16[2,1024,256]{2,1,0:T(8,128)(2,1)S(1)}) custom-call(bf16[512,1024]{1,0:T(8,128)(2,1)S(1)} %collective-permute-done.2.refs_0_, bf16[8192,512]{1,0:T(8,128)(2,1)} %refs_1_.7, bf16[8192,256]{1,0:T(8,128)(2,1)} %refs_2_.7, ...), custom_call_target="tpu_custom_call" | custom-call | bytes 1 | tf_op jit(solution)/shard_map/project/pallas_call | solution.py:226
  37.0 5.2 %collective-permute-done.5.refs_1_ = bf16[512,1024]{1,0:T(8,128)(2,1)S(1)} collective-permute-done((bf16[512,1024]{1,0:T(8,128)(2,1)S(1)}, bf16[512,1024]{1,0:T(8,128)(2,1)S(1)}, u32[]{:S(2)}, u32[]{:S(2)}) %collective-permute-start.5) | collective-permute-done | bytes 1048608 | tf_op jit(solution)/shard_map/ppermute | solution.py:472
  42.3 0.0 collective-permute-start.6
  42.3 1.0 %project_far.1 = (f32[512,512]{1,0:T(8,128)S(1)}, f32[512,256]{1,0:T(8,128)S(1)}, f32[512,128]{1,0:T(8,128)S(1)}) custom-call(bf16[512,1024]{1,0:T(8,128)(2,1)S(1)} %after.3.x_ref, bf16[2,1024,512]{2,1,0:T(8,128)(2,1)S(1)} %get-tuple-element.37.wq_ref, bf16[2,1024,256]{2,1,0:T(8,128)(2,1)S(1)} %get-tuple-element.38.wkv_ref, ...), custom_call_target="tpu_custom_call" | custom-call | bytes 1 | tf_op jit(solution)/shard_map/project_far/pallas_call | solution.py:259
  43.3 1.6 %collective-permute-done.6.x_ref = bf16[512,1024]{1,0:T(8,128)(2,1)S(1)} collective-permute-done((bf16[512,1024]{1,0:T(8,128)(2,1)S(1)}, bf16[512,1024]{1,0:T(8,128)(2,1)S(1)}, u32[]{:S(2)}, u32[]{:S(2)}) %collective-permute-start.6) | collective-permute-done | bytes 1048608 | tf_op jit(solution)/shard_map/ppermute | solution.py:476
  44.9 3.1 %project_late.1 = (bf16[4,512,128]{2,1,0:T(8,128)(2,1)}, bf16[512,128]{1,0:T(8,128)(2,1)}, bf16[512,256]{1,0:T(8,128)(2,1)}, bf16[32,128,128]{2,1,0:T(8,128)(2,1)}) custom-call(s32[24,128]{1,0:T(8,128)S(1)} %get-tuple-element.25.table_ref, bf16[512,1024]{1,0:T(8,128)(2,1)S(1)} %collective-permute-done.6.x_ref, f32[512,512]{1,0:T(8,128)S(1)} %get-tuple-element.41.q_in, ...), custom_call_target="tpu_custom_call" | custom-call | bytes 1 | tf_op jit(solution)/shard_map/project_late/pallas_call | solution.py:342
  48.0 0.0 all-to-all-done.refs_0_
  48.0 7.2 %all-to-all-start.1 = ((bf16[32,128,128]{2,1,0:T(8,128)(2,1)}), bf16[32,128,128]{2,1,0:T(8,128)(2,1)S(1)}, u32[]{:S(2)}, u32[]{:S(2)}) async-start(bf16[32,128,128]{2,1,0:T(8,128)(2,1)} %get-tuple-element.47), calls=%async_computation.1 | async-start | bytes 2097152 | tf_op jit(solution)/shard_map/all_to_all | solution.py:489
  55.2 9.8 %attend.1 = bf16[512,512]{1,0:T(8,128)(2,1)} custom-call(s32[24,128]{1,0:T(8,128)S(1)} %get-tuple-element.25.table_ref, bf16[64,128,128]{2,1,0:T(8,128)(2,1)} %all-to-all-done.refs_0_, bf16[4,512,128]{2,1,0:T(8,128)(2,1)} %get-tuple-element.44.refs_1_, bf16[512,128]{1,0:T(8,128)(2,1)} %get-tuple-element.45.refs_2_, bf16[512,256]{1,0:T(8,128)(2,1)} %get-tuple-element.46.refs_3_), custom_call_target="tpu_custom_call" | custom-call | flops 5368709120 | bytes 8388608 | tf_op jit(solution)/shard_map/attend/pallas_call | solution.py:413
  65.0 8.0 %all-to-all-done.1.received_ref = bf16[32,128,128]{2,1,0:T(8,128)(2,1)S(1)} async-done(((bf16[32,128,128]{2,1,0:T(8,128)(2,1)}), bf16[32,128,128]{2,1,0:T(8,128)(2,1)S(1)}, u32[]{:S(2)}, u32[]{:S(2)}) %all-to-all-start.1) | async-done | bytes 1048608 | tf_op jit(solution)/shard_map/all_to_all | solution.py:489
  73.0 1.8 %place_pages.1 = bf16[32,128,128]{2,1,0:T(8,128)(2,1)} custom-call(s32[24,128]{1,0:T(8,128)S(1)} %get-tuple-element.25.table_ref, bf16[32,128,128]{2,1,0:T(8,128)(2,1)S(1)} %all-to-all-done.1.received_ref), custom_call_target="tpu_custom_call" | custom-call | bytes 2097152 | tf_op jit(solution)/shard_map/place_pages/pallas_call | solution.py:453
  (4 shorter events, 0.0 us)
Async XLA Ops:
  0.6 14.3 %collective-permute-start = (bf16[512,1024]{1,0:T(8,128)(2,1)}, bf16[512,1024]{1,0:T(8,128)(2,1)S(1)}, u32[]{:S(2)}, u32[]{:S(2)}) collective-permute-start(bf16[512,1024]{1,0:T(8,128)(2,1)} %refs_1_.5), channel_id=1, source_target_pairs={{0,1},{1,0},{2,3},{3,2},{4,5},{5,4},{6,7},{7,6},{8,9},{9,8},{10,11... | collective-permute-start | bytes 3145736 | tf_op jit(solution)/shard_map/ppermute | solution.py:476
  0.7 17.2 %collective-permute-start.3 = (bf16[512,1024]{1,0:T(8,128)(2,1)}, bf16[512,1024]{1,0:T(8,128)(2,1)S(1)}, u32[]{:S(2)}, u32[]{:S(2)}) collective-permute-start(bf16[512,1024]{1,0:T(8,128)(2,1)} %refs_1_.5), channel_id=1, source_target_pairs={{0,2},{1,7},{2,4},{3,1},{4,6},{5,3},{6,0},{7,5},{8,10},{9,15},{10,... | collective-permute-start | bytes 3145736 | tf_op jit(solution)/shard_map/ppermute | solution.py:472
  6.6 41.4 %all-to-all-start = ((bf16[64,128,128]{2,1,0:T(8,128)(2,1)}), bf16[64,128,128]{2,1,0:T(8,128)(2,1)}, u32[]{:S(2)}, u32[]{:S(2)}) async-start(bf16[64,128,128]{2,1,0:T(8,128)(2,1)} %get-tuple-element.26), calls=%async_computation | async-start | bytes 4194304 | tf_op jit(solution)/shard_map/all_to_all | solution.py:489
  15.0 16.1 %collective-permute-start.1 = (bf16[512,1024]{1,0:T(8,128)(2,1)S(1)}, bf16[512,1024]{1,0:T(8,128)(2,1)S(1)}, u32[]{:S(2)}, u32[]{:S(2)}) collective-permute-start(bf16[512,1024]{1,0:T(8,128)(2,1)S(1)} %collective-permute-done.refs_0_), channel_id=1, source_target_pairs={{0,2},{1,7},{2,4},{3,1},{4,6},{5,3},{6,0},{7,5},{8,10},{9,15},{10,... | collective-permute-start | bytes 3145736 | tf_op jit(solution)/shard_map/ppermute | solution.py:472
  17.9 3.7 %collective-permute-start.4 = (bf16[512,1024]{1,0:T(8,128)(2,1)S(1)}, bf16[512,1024]{1,0:T(8,128)(2,1)S(1)}, u32[]{:S(2)}, u32[]{:S(2)}) collective-permute-start(bf16[512,1024]{1,0:T(8,128)(2,1)S(1)} %collective-permute-done.3.refs_1_), channel_id=1, source_target_pairs={{0,1},{1,0},{2,3},{3,2},{4,5},{5,4},{6,7},{7,6},{8,9},{9,8},{10,11... | collective-permute-start | bytes 3145736 | tf_op jit(solution)/shard_map/ppermute | solution.py:476
  25.2 17.0 %collective-permute-start.5 = (bf16[512,1024]{1,0:T(8,128)(2,1)S(1)}, bf16[512,1024]{1,0:T(8,128)(2,1)S(1)}, u32[]{:S(2)}, u32[]{:S(2)}) collective-permute-start(bf16[512,1024]{1,0:T(8,128)(2,1)S(1)} %after.2), channel_id=1, source_target_pairs={{0,2},{1,7},{2,4},{3,1},{4,6},{5,3},{6,0},{7,5},{8,10},{9,15},{10,... | collective-permute-start | bytes 3145736 | tf_op jit(solution)/shard_map/ppermute | solution.py:472
  31.0 2.7 %collective-permute-start.2 = (bf16[512,1024]{1,0:T(8,128)(2,1)S(1)}, bf16[512,1024]{1,0:T(8,128)(2,1)S(1)}, u32[]{:S(2)}, u32[]{:S(2)}) collective-permute-start(bf16[512,1024]{1,0:T(8,128)(2,1)S(1)} %collective-permute-done.1.refs_0_), channel_id=1, source_target_pairs={{0,1},{1,0},{2,3},{3,2},{4,5},{5,4},{6,7},{7,6},{8,9},{9,8},{10,11... | collective-permute-start | bytes 3145736 | tf_op jit(solution)/shard_map/ppermute | solution.py:476
  42.3 2.7 %collective-permute-start.6 = (bf16[512,1024]{1,0:T(8,128)(2,1)S(1)}, bf16[512,1024]{1,0:T(8,128)(2,1)S(1)}, u32[]{:S(2)}, u32[]{:S(2)}) collective-permute-start(bf16[512,1024]{1,0:T(8,128)(2,1)S(1)} %after.3.x_ref), channel_id=1, source_target_pairs={{0,1},{1,0},{2,3},{3,2},{4,5},{5,4},{6,7},{7,6},{8,9},{9,8},{10,11... | collective-permute-start | bytes 3145736 | tf_op jit(solution)/shard_map/ppermute | solution.py:476
  48.0 25.0 %all-to-all-start.1 = ((bf16[32,128,128]{2,1,0:T(8,128)(2,1)}), bf16[32,128,128]{2,1,0:T(8,128)(2,1)S(1)}, u32[]{:S(2)}, u32[]{:S(2)}) async-start(bf16[32,128,128]{2,1,0:T(8,128)(2,1)} %get-tuple-element.47), calls=%async_computation.1 | async-start | bytes 2097152 | tf_op jit(solution)/shard_map/all_to_all | solution.py:489

commit v13 on v11

--- a/solution.py
+++ b/solution.py
@@ -428,10 +428,13 @@
     )(table, *[hbm(x) for x in sources])
 
 
-def place_kernel(table_ref, received_ref, out_ref, buffer, index_ref, index_sem, sems):
-    indices = pltpu.make_async_copy(table_ref, index_ref, index_sem)
+def place_kernel(table_ref, source_ref, out_ref, received_ref, buffer, index_ref, in_sems, sems):
+    indices = pltpu.make_async_copy(table_ref, index_ref, in_sems.at[0])
+    arrival = pltpu.make_async_copy(source_ref, received_ref, in_sems.at[1])
     indices.start()
+    arrival.start()
     indices.wait()
+    arrival.wait()
     group = 4
     copies = []
     for i in range(SLOTS):
@@ -453,18 +456,19 @@
     return pl.pallas_call(
         place_kernel,
         out_shape=pltpu.HBM((SLOTS, 2 * PAGE, HD), BF16),
-        in_specs=[VMEM, VMEM],
+        in_specs=[VMEM, HBM],
         out_specs=HBM,
         scratch_shapes=[
+            pltpu.VMEM(received.shape, BF16),
             pltpu.VMEM((SLOTS, 2 * PAGE, HD), BF16),
             pltpu.SMEM((24, HD), jnp.int32),
-            pltpu.SemaphoreType.DMA,
+            pltpu.SemaphoreType.DMA((2,)),
             pltpu.SemaphoreType.DMA((SLOTS // 4,)),
         ],
         compiler_params=params(8),
         cost_estimate=cost(0, 2 * MIB),
         name="place_pages",
-    )(table, received)
+    )(table, hbm(received))
 
 
 def shift(values, steps):

time: 73.4 us -> 74.9 us (1.020)
  local copies, waits for them, and re-layouts: 0 us -> 0.98 us
    unnamed x0 -> x2, local copies, waits for them, and re-layouts: none -> 0.98 us
where the time goes in v13:
time: 74.9 us; the launch traced here: 74.6 us
  Pallas kernels  31.1 us (42%)
  waiting for transfers between devices  23.7 us (32%)
  starting transfers between devices  16.6 us (22%)
  other arithmetic  1.21 us (2%)
  local copies, waits for them, and re-layouts  0.98 us (1%)
  between operations  0.95 us (1%)
    all_to_all x2, waiting for transfers between devices, exchange(): lax.all_to_all(values, 'pool', split_axis=0, concat_axis=0, tiled=True)  11.5 us
    pallas_call x3, Pallas kernels, project(): pl.pallas_call(functools.partial(project_kernel, blocks, len(held), bool(...  11.1 us
    all_to_all x2, starting transfers between devices, exchange(): lax.all_to_all(values, 'pool', split_axis=0, concat_axis=0, tiled=True)  10.7 us
    ppermute x3, waiting for transfers between devices, shift(): return lax.ppermute(values, 'tp', pairs)  10.6 us
    pallas_call x1, Pallas kernels, attend(): pl.pallas_call(attend_kernel, out_shape=shape((ROWS, QW), BF16), in_specs...  9.81 us
    ppermute x3, starting transfers between devices, shift(): return lax.ppermute(values, 'tp', pairs)  5.75 us
    pallas_call x1, Pallas kernels, prelude(): pl.pallas_call(prelude_kernel, out_shape=[shape((24, HD), jnp.int32), plt...  3.8 us
    pallas_call x1, Pallas kernels, project_late(): pl.pallas_call(late_kernel, out_shape=[pltpu.HBM(x, BF16) for x in result...  3.07 us
  transfers between devices with their start and end apart: 9, of which 5 were waited for; matrix products, arithmetic and copies ran while one was open for 2% of the time, Pallas kernels for 39%

profile of v13, /device:TPU:0, one launch (start us, length us, event | category | flops | bytes accessed | tf_op | source)
XLA Modules:
  0.0 74.6 jit_solution(8437863950040456273)
XLA Ops:
  0.6 0.1 collective-permute-start
  0.7 2.1 %collective-permute-start.1 = (bf16[512,1024]{1,0:T(8,128)(2,1)}, bf16[512,1024]{1,0:T(8,128)(2,1)S(1)}, u32[]{:S(2)}, u32[]{:S(2)}) collective-permute-start(bf16[512,1024]{1,0:T(8,128)(2,1)} %refs_1_.3), channel_id=1, source_target_pairs={{0,2},{1,7},{2,4},{3,1},{4,6},{5,3},{6,0},{7,5},{8,10},{9,15},{10,... | collective-permute-start | bytes 3145736 | tf_op jit(solution)/shard_map/ppermute | solution.py:476
  2.8 3.8 %prelude.1 = (s32[24,128]{1,0:T(8,128)S(1)}, bf16[64,128,128]{2,1,0:T(8,128)(2,1)}) custom-call(s32[16,32]{1,0:T(8,128)} %refs_0_.1, s32[16,32]{1,0:T(8,128)} %refs_1_.2, s32[8,16]{1,0:T(8,128)} %bitcast.7, bf16[64,128,128]{2,1,0:T(8,128)(2,1)} %bitcast.5), custom_call_target="tpu_custom_call" | custom-call | bytes 1 | tf_op jit(solution)/shard_map/prelude/pallas_call | solution.py:120
  6.6 0.0 collective-permute-done.refs_1_
  6.6 2.0 %collective-permute-start.3 = (bf16[512,1024]{1,0:T(8,128)(2,1)S(1)}, bf16[512,1024]{1,0:T(8,128)(2,1)S(1)}, u32[]{:S(2)}, u32[]{:S(2)}) collective-permute-start(bf16[512,1024]{1,0:T(8,128)(2,1)S(1)} %after.3.refs_0_), channel_id=1, source_target_pairs={{0,2},{1,7},{2,4},{3,1},{4,6},{5,3},{6,0},{7,5},{8,10},{9,15},{10,... | collective-permute-start | bytes 3145736 | tf_op jit(solution)/shard_map/ppermute | solution.py:476
  8.6 7.1 %all-to-all-start = ((bf16[64,128,128]{2,1,0:T(8,128)(2,1)}), bf16[64,128,128]{2,1,0:T(8,128)(2,1)}, u32[]{:S(2)}, u32[]{:S(2)}) async-start(bf16[64,128,128]{2,1,0:T(8,128)(2,1)} %get-tuple-element.23), calls=%async_computation | async-start | bytes 4194304 | tf_op jit(solution)/shard_map/all_to_all | solution.py:493
  15.7 1.0 %fusion = (f32[512,64]{1,0:T(8,128)S(1)}, f32[512,64]{1,0:T(8,128)S(1)}, f32[512,64]{1,0:T(8,128)S(1)}) fusion(f32[64]{0:T(128)S(1)} %negate_power_fusion, f32[512]{0:T(512)S(1)} %add_convert_fusion), kind=kLoop, calls=%fused_computation.4 | loop fusion | flops 65536 | bytes 395520 | tf_op jit(solution)/shard_map/neg | solution.py:489
  16.7 0.2 pad_maximum_fusion
  16.9 3.7 %project.3 = (f32[512,512]{1,0:T(8,128)S(1)}, f32[512,256]{1,0:T(8,128)S(1)}, f32[512,128]{1,0:T(8,128)S(1)}) custom-call(bf16[512,1024]{1,0:T(8,128)(2,1)S(1)} %after.3.refs_0_, bf16[512,1024]{1,0:T(8,128)(2,1)} %refs_1_.3, bf16[8192,512]{1,0:T(8,128)(2,1)} %refs_2_.5, bf16[8192,256]{1,0:T(8,128)(2,1)} %refs_3_.5, ...), custom_call_target="tpu_custom_call" | custom-call | bytes 1 | tf_op jit(solution)/shard_map/project/pallas_call | solution.py:226
  20.6 0.0 collective-permute-done.1.refs_1_
  20.6 1.7 %collective-permute-start.5 = (bf16[512,1024]{1,0:T(8,128)(2,1)S(1)}, bf16[512,1024]{1,0:T(8,128)(2,1)S(1)}, u32[]{:S(2)}, u32[]{:S(2)}) collective-permute-start(bf16[512,1024]{1,0:T(8,128)(2,1)S(1)} %after.4.refs_0_), channel_id=1, source_target_pairs={{0,2},{1,7},{2,4},{3,1},{4,6},{5,3},{6,0},{7,5},{8,10},{9,15},{10,... | collective-permute-start | bytes 3145736 | tf_op jit(solution)/shard_map/ppermute | solution.py:476
  22.3 0.0 collective-permute-start.2
  22.3 6.8 %collective-permute-done.3.refs_1_ = bf16[512,1024]{1,0:T(8,128)(2,1)S(1)} collective-permute-done((bf16[512,1024]{1,0:T(8,128)(2,1)S(1)}, bf16[512,1024]{1,0:T(8,128)(2,1)S(1)}, u32[]{:S(2)}, u32[]{:S(2)}) %collective-permute-start.3) | collective-permute-done | bytes 1048608 | tf_op jit(solution)/shard_map/ppermute | solution.py:476
  29.1 0.0 collective-permute-start.4
  29.1 3.6 %project.4 = (f32[512,512]{1,0:T(8,128)S(1)}, f32[512,256]{1,0:T(8,128)S(1)}, f32[512,128]{1,0:T(8,128)S(1)}) custom-call(bf16[512,1024]{1,0:T(8,128)(2,1)S(1)} %after.4.refs_0_, bf16[512,1024]{1,0:T(8,128)(2,1)S(1)} %collective-permute-done.3.refs_1_, bf16[8192,512]{1,0:T(8,128)(2,1)} %refs_2_.5, bf16[8192,256]{1,0:T(8,128)(2,1)} %refs_3_.5, ...), custom_call_target="tpu_custom_call" | custom-call | flops 20000000000 | bytes 1 | tf_op jit(solution)/shard_map/project/pallas_call | solution.py:226
  32.7 0.0 collective-permute-done.2.refs_0_
  32.7 0.0 collective-permute-done.4.refs_1_
  32.8 3.9 %project.5 = (f32[512,512]{1,0:T(8,128)S(1)}, f32[512,256]{1,0:T(8,128)S(1)}, f32[512,128]{1,0:T(8,128)S(1)}, bf16[2,1024,512]{2,1,0:T(8,128)(2,1)S(1)}, bf16[2,1024,256]{2,1,0:T(8,128)(2,1)S(1)}) custom-call(bf16[512,1024]{1,0:T(8,128)(2,1)S(1)} %collective-permute-done.2.refs_0_, bf16[512,1024]{1,0:T(8,128)(2,1)S(1)} %collective-permute-done.4.refs_1_, ...), custom_call_target="tpu_custom_call" | custom-call | bytes 1 | tf_op jit(solution)/shard_map/project/pallas_call | solution.py:226
  36.6 3.8 %collective-permute-done.5.refs_1_ = bf16[512,1024]{1,0:T(8,128)(2,1)S(1)} collective-permute-done((bf16[512,1024]{1,0:T(8,128)(2,1)S(1)}, bf16[512,1024]{1,0:T(8,128)(2,1)S(1)}, u32[]{:S(2)}, u32[]{:S(2)}) %collective-permute-start.5) | collective-permute-done | bytes 1048608 | tf_op jit(solution)/shard_map/ppermute | solution.py:476
  40.4 0.0 collective-permute-start.6
  40.4 1.0 %project_far.1 = (f32[512,512]{1,0:T(8,128)S(1)}, f32[512,256]{1,0:T(8,128)S(1)}, f32[512,128]{1,0:T(8,128)S(1)}) custom-call(bf16[512,1024]{1,0:T(8,128)(2,1)S(1)} %after.5.x_ref, bf16[2,1024,512]{2,1,0:T(8,128)(2,1)S(1)} %get-tuple-element.31.wq_ref, bf16[2,1024,256]{2,1,0:T(8,128)(2,1)S(1)} %get-tuple-element.32.wkv_ref, ...), custom_call_target="tpu_custom_call" | custom-call | bytes 1 | tf_op jit(solution)/shard_map/project_far/pallas_call | solution.py:259
  41.4 1.6 %collective-permute-done.6.x_ref = bf16[512,1024]{1,0:T(8,128)(2,1)S(1)} collective-permute-done((bf16[512,1024]{1,0:T(8,128)(2,1)S(1)}, bf16[512,1024]{1,0:T(8,128)(2,1)S(1)}, u32[]{:S(2)}, u32[]{:S(2)}) %collective-permute-start.6) | collective-permute-done | bytes 1048608 | tf_op jit(solution)/shard_map/ppermute | solution.py:480
  43.0 3.1 %project_late.1 = (bf16[4,512,128]{2,1,0:T(8,128)(2,1)}, bf16[512,128]{1,0:T(8,128)(2,1)}, bf16[512,256]{1,0:T(8,128)(2,1)}, bf16[32,128,128]{2,1,0:T(8,128)(2,1)}) custom-call(s32[24,128]{1,0:T(8,128)S(1)} %get-tuple-element.22.refs_0_.table_ref, bf16[512,1024]{1,0:T(8,128)(2,1)S(1)} %collective-permute-done.6.x_ref, ...), custom_call_target="tpu_custom_call" | custom-call | bytes 1 | tf_op jit(solution)/shard_map/project_late/pallas_call | solution.py:342
  46.1 3.8 %all-to-all-done.refs_0_ = bf16[64,128,128]{2,1,0:T(8,128)(2,1)} async-done(((bf16[64,128,128]{2,1,0:T(8,128)(2,1)}), bf16[64,128,128]{2,1,0:T(8,128)(2,1)}, u32[]{:S(2)}, u32[]{:S(2)}) %all-to-all-start) | async-done | bytes 2097184 | tf_op jit(solution)/shard_map/all_to_all | solution.py:493
  49.9 3.7 %all-to-all-start.1 = ((bf16[32,128,128]{2,1,0:T(8,128)(2,1)}), bf16[32,128,128]{2,1,0:T(8,128)(2,1)S(1)}, u32[]{:S(2)}, u32[]{:S(2)}) async-start(bf16[32,128,128]{2,1,0:T(8,128)(2,1)} %get-tuple-element.41), calls=%async_computation.1 | async-start | bytes 2097152 | tf_op jit(solution)/shard_map/all_to_all | solution.py:493
  53.5 9.8 %attend.1 = bf16[512,512]{1,0:T(8,128)(2,1)} custom-call(s32[24,128]{1,0:T(8,128)S(1)} %get-tuple-element.22.refs_0_.table_ref, bf16[64,128,128]{2,1,0:T(8,128)(2,1)} %all-to-all-done.refs_0_, bf16[4,512,128]{2,1,0:T(8,128)(2,1)} %get-tuple-element.38.refs_1_, bf16[512,128]{1,0:T(8,128)(2,1)} %get-tuple-element.39.refs_2_, ...), custom_call_target="tpu_custom_call" | custom-call | flops 5368709120 | bytes 8388608 | tf_op jit(solution)/shard_map/attend/pallas_call | solution.py:413
  63.4 7.8 %all-to-all-done.1.source_ref = bf16[32,128,128]{2,1,0:T(8,128)(2,1)S(1)} async-done(((bf16[32,128,128]{2,1,0:T(8,128)(2,1)}), bf16[32,128,128]{2,1,0:T(8,128)(2,1)S(1)}, u32[]{:S(2)}, u32[]{:S(2)}) %all-to-all-start.1) | async-done | bytes 1048608 | tf_op jit(solution)/shard_map/all_to_all | solution.py:493
  71.1 0.0 copy-start
  71.1 1.0 %copy-done = bf16[32,128,128]{2,1,0:T(8,128)(2,1)} copy-done((bf16[32,128,128]{2,1,0:T(8,128)(2,1)}, bf16[32,128,128]{2,1,0:T(8,128)(2,1)S(1)}, u32[]{:S(2)}) %copy-start) | copy-done | bytes 1048600
  72.1 2.3 %place_pages.1 = bf16[32,128,128]{2,1,0:T(8,128)(2,1)} custom-call(s32[24,128]{1,0:T(8,128)S(1)} %get-tuple-element.22.refs_0_.table_ref, bf16[32,128,128]{2,1,0:T(8,128)(2,1)} %copy-done), custom_call_target="tpu_custom_call" | custom-call | bytes 2097152 | tf_op jit(solution)/shard_map/place_pages/pallas_call | solution.py:456
  (5 shorter events, 0.0 us)
Async XLA Ops:
  0.6 6.0 %collective-permute-start = (bf16[512,1024]{1,0:T(8,128)(2,1)}, bf16[512,1024]{1,0:T(8,128)(2,1)S(1)}, u32[]{:S(2)}, u32[]{:S(2)}) collective-permute-start(bf16[512,1024]{1,0:T(8,128)(2,1)} %refs_1_.3), channel_id=1, source_target_pairs={{0,1},{1,0},{2,3},{3,2},{4,5},{5,4},{6,7},{7,6},{8,9},{9,8},{10,11... | collective-permute-start | bytes 3145736 | tf_op jit(solution)/shard_map/ppermute | solution.py:480
  0.7 19.9 %collective-permute-start.1 = (bf16[512,1024]{1,0:T(8,128)(2,1)}, bf16[512,1024]{1,0:T(8,128)(2,1)S(1)}, u32[]{:S(2)}, u32[]{:S(2)}) collective-permute-start(bf16[512,1024]{1,0:T(8,128)(2,1)} %refs_1_.3), channel_id=1, source_target_pairs={{0,2},{1,7},{2,4},{3,1},{4,6},{5,3},{6,0},{7,5},{8,10},{9,15},{10,... | collective-permute-start | bytes 3145736 | tf_op jit(solution)/shard_map/ppermute | solution.py:476
  6.6 22.5 %collective-permute-start.3 = (bf16[512,1024]{1,0:T(8,128)(2,1)S(1)}, bf16[512,1024]{1,0:T(8,128)(2,1)S(1)}, u32[]{:S(2)}, u32[]{:S(2)}) collective-permute-start(bf16[512,1024]{1,0:T(8,128)(2,1)S(1)} %after.3.refs_0_), channel_id=1, source_target_pairs={{0,2},{1,7},{2,4},{3,1},{4,6},{5,3},{6,0},{7,5},{8,10},{9,15},{10,... | collective-permute-start | bytes 3145736 | tf_op jit(solution)/shard_map/ppermute | solution.py:476
  8.6 41.3 %all-to-all-start = ((bf16[64,128,128]{2,1,0:T(8,128)(2,1)}), bf16[64,128,128]{2,1,0:T(8,128)(2,1)}, u32[]{:S(2)}, u32[]{:S(2)}) async-start(bf16[64,128,128]{2,1,0:T(8,128)(2,1)} %get-tuple-element.23), calls=%async_computation | async-start | bytes 4194304 | tf_op jit(solution)/shard_map/all_to_all | solution.py:493
  20.6 19.7 %collective-permute-start.5 = (bf16[512,1024]{1,0:T(8,128)(2,1)S(1)}, bf16[512,1024]{1,0:T(8,128)(2,1)S(1)}, u32[]{:S(2)}, u32[]{:S(2)}) collective-permute-start(bf16[512,1024]{1,0:T(8,128)(2,1)S(1)} %after.4.refs_0_), channel_id=1, source_target_pairs={{0,2},{1,7},{2,4},{3,1},{4,6},{5,3},{6,0},{7,5},{8,10},{9,15},{10,... | collective-permute-start | bytes 3145736 | tf_op jit(solution)/shard_map/ppermute | solution.py:476
  22.3 10.4 %collective-permute-start.2 = (bf16[512,1024]{1,0:T(8,128)(2,1)S(1)}, bf16[512,1024]{1,0:T(8,128)(2,1)S(1)}, u32[]{:S(2)}, u32[]{:S(2)}) collective-permute-start(bf16[512,1024]{1,0:T(8,128)(2,1)S(1)} %after.4.refs_0_), channel_id=1, source_target_pairs={{0,1},{1,0},{2,3},{3,2},{4,5},{5,4},{6,7},{7,6},{8,9},{9,8},{10,11... | collective-permute-start | bytes 3145736 | tf_op jit(solution)/shard_map/ppermute | solution.py:480
  29.1 3.6 %collective-permute-start.4 = (bf16[512,1024]{1,0:T(8,128)(2,1)S(1)}, bf16[512,1024]{1,0:T(8,128)(2,1)S(1)}, u32[]{:S(2)}, u32[]{:S(2)}) collective-permute-start(bf16[512,1024]{1,0:T(8,128)(2,1)S(1)} %collective-permute-done.3.refs_1_), channel_id=1, source_target_pairs={{0,1},{1,0},{2,3},{3,2},{4,5},{5,4},{6,7},{7,6},{8,9},{9,8},{10,11... | collective-permute-start | bytes 3145736 | tf_op jit(solution)/shard_map/ppermute | solution.py:480
  40.4 2.7 %collective-permute-start.6 = (bf16[512,1024]{1,0:T(8,128)(2,1)S(1)}, bf16[512,1024]{1,0:T(8,128)(2,1)S(1)}, u32[]{:S(2)}, u32[]{:S(2)}) collective-permute-start(bf16[512,1024]{1,0:T(8,128)(2,1)S(1)} %after.5.x_ref), channel_id=1, source_target_pairs={{0,1},{1,0},{2,3},{3,2},{4,5},{5,4},{6,7},{7,6},{8,9},{9,8},{10,11... | collective-permute-start | bytes 3145736 | tf_op jit(solution)/shard_map/ppermute | solution.py:480
  49.9 21.3 %all-to-all-start.1 = ((bf16[32,128,128]{2,1,0:T(8,128)(2,1)}), bf16[32,128,128]{2,1,0:T(8,128)(2,1)S(1)}, u32[]{:S(2)}, u32[]{:S(2)}) async-start(bf16[32,128,128]{2,1,0:T(8,128)(2,1)} %get-tuple-element.41), calls=%async_computation.1 | async-start | bytes 2097152 | tf_op jit(solution)/shard_map/all_to_all | solution.py:493
  71.1 1.0 %copy-start = (bf16[32,128,128]{2,1,0:T(8,128)(2,1)}, bf16[32,128,128]{2,1,0:T(8,128)(2,1)S(1)}, u32[]{:S(2)}) copy-start(bf16[32,128,128]{2,1,0:T(8,128)(2,1)S(1)} %all-to-all-done.1.source_ref) | copy-start | bytes 3145732

commit v14 on v10

--- a/solution.py
+++ b/solution.py
@@ -321,10 +321,12 @@
             target = send_out.at[index_ref[page, PUSH]]
             copies.append(pltpu.make_async_copy(page_buf.at[page], target, page_sems.at[page]))
             copies[-1].start()
-    results = ((keys_buf, keys_out), (values_buf, values_out), (inv_buf, inv_out))
-    for i, (source, target) in enumerate(results):
-        copies.append(pltpu.make_async_copy(source, target, sems.at[2 + i]))
-        copies[-1].start()
+        span = pl.ds(r, TILE)
+        results = ((keys_buf, keys_out), (values_buf, values_out), (inv_buf, inv_out))
+        for i, (source, target) in enumerate(results):
+            sem = sems.at[2 + 3 * (r // TILE) + i]
+            copies.append(pltpu.make_async_copy(source.at[span, :], target.at[span, :], sem))
+            copies[-1].start()
     for copy in copies:
         copy.wait()
 
@@ -341,7 +343,7 @@
             *[pltpu.VMEM(*x) for x in kept],
             pltpu.VMEM((NEW_PAGES, 2 * PAGE, HD), BF16),
             pltpu.SMEM((24, HD), jnp.int32),
-            pltpu.SemaphoreType.DMA((5,)),
+            pltpu.SemaphoreType.DMA((2 + 3 * ROWS // TILE,)),
             pltpu.SemaphoreType.DMA((NEW_PAGES,)),
         ],
         compiler_params=params(16),
@@ -356,10 +358,12 @@
 
 def attend_kernel(table_ref, *refs):
     sources, wq_ref, pages_ref, out_ref, refs = refs[:7], refs[7], refs[8], refs[9], refs[10:]
-    targets, wq_buf, index_ref, page_buf, q_buf, keys, values, sems, page_sems = refs[:7], *refs[7:]
+    targets, wq_buf, index_ref, page_buf, q_buf, keys, values, sems = refs[:7], *refs[7:]
     q_sum, x, inv_norm, cosine, sine, own_keys, own_values = targets
     indices = pltpu.make_async_copy(table_ref, index_ref, sems.at[8])
     indices.start()
+    fetch = pltpu.make_async_copy(pages_ref, page_buf, sems.at[9])
+    fetch.start()
     copies = [pltpu.make_async_copy(a, b, sems.at[i]) for i, (a, b) in enumerate(zip(sources, targets))]
     rows = pl.ds(pl.multiple_of(block_index(FAR, True) * FEAT, FEAT), FEAT)
     copies.insert(0, pltpu.make_async_copy(wq_ref.at[rows, :], wq_buf, sems.at[7]))
@@ -371,17 +375,9 @@
     picker = (column == wanted).astype(BF16)
     values[:, HD:] = jnp.ones((PAGES * PAGE, HD), BF16)
     indices.wait()
-    fetches = [
-        pltpu.make_async_copy(
-            pages_ref.at[index_ref[TAKE, page]], page_buf.at[page], page_sems.at[page]
-        )
-        for page in range(PAGES)
-    ]
-    for fetch in fetches:
-        fetch.start()
+    fetch.wait()
     for page in range(PAGES):
-        fetches[page].wait()
-        both = jnp.dot(picker, page_buf[page], preferred_element_type=F32)
+        both = jnp.dot(picker, page_buf[index_ref[TAKE, page]], preferred_element_type=F32)
         rows = slice(page * PAGE, (page + 1) * PAGE)
         keys[rows, :] = both[:PAGE].astype(BF16)
         values[rows, :HD] = both[PAGE:].astype(BF16)
@@ -427,12 +423,11 @@
             *[pltpu.VMEM(x.shape, x.dtype) for x in sources],
             pltpu.VMEM((FEAT, QW), BF16),
             pltpu.SMEM((24, HD), jnp.int32),
-            pltpu.VMEM((PAGES, 2 * PAGE, HD), BF16),
+            pltpu.VMEM(pages.shape, BF16),
             pltpu.VMEM((HEADS, ROWS, HD), BF16),
             pltpu.VMEM((PAGES * PAGE, HD), BF16),
             pltpu.VMEM((PAGES * PAGE, 2 * HD), BF16),
-            pltpu.SemaphoreType.DMA((9,)),
-            pltpu.SemaphoreType.DMA((PAGES,)),
+            pltpu.SemaphoreType.DMA((10,)),
         ],
         compiler_params=params(40),
         cost_estimate=cost(2 * ROWS * 4 * 2560 * 512, 8 * MIB),

time: 73.4 us -> 73.4 us (level)
  Pallas kernels: 38.5 us -> 34 us
  waiting for transfers between devices: 15.7 us -> 20.2 us
    all_to_all x2, waiting for transfers between devices: 5.89 us -> 10.4 us  [exchange(): lax.all_to_all(values, 'pool', split_axis=0, concat_axis=0, tiled=True)]
    pallas_call x1, Pallas kernels: 15.7 us -> 11.2 us  [attend(): pl.pallas_call(attend_kernel, out_shape=shape((ROWS, QW), BF16), in_specs...]
  transfers between devices with their start and end apart: 9 -> 9, of which waited for: 5 -> 5; matrix products, arithmetic and copies ran while one was open for 2% -> 2% of each run, Pallas kernels for 50% -> 44%
where the time goes in v14:
time: 73.4 us; the launch traced here: 73.1 us
  Pallas kernels  34 us (46%)
  waiting for transfers between devices  20.2 us (28%)
  starting transfers between devices  16.8 us (23%)
  other arithmetic  1.21 us (2%)
  between operations  0.96 us (1%)
    pallas_call x3, Pallas kernels, project(): pl.pallas_call(functools.partial(project_kernel, blocks, len(held), bool(...  12.5 us
    pallas_call x1, Pallas kernels, attend(): pl.pallas_call(attend_kernel, out_shape=shape((ROWS, QW), BF16), in_specs...  11.2 us
    all_to_all x2, starting transfers between devices, exchange(): lax.all_to_all(values, 'pool', split_axis=0, concat_axis=0, tiled=True)  10.9 us
    all_to_all x2, waiting for transfers between devices, exchange(): lax.all_to_all(values, 'pool', split_axis=0, concat_axis=0, tiled=True)  10.4 us
    ppermute x3, waiting for transfers between devices, shift(): return lax.ppermute(values, 'tp', pairs)  9.17 us
    ppermute x3, starting transfers between devices, shift(): return lax.ppermute(values, 'tp', pairs)  5.75 us
    pallas_call x1, Pallas kernels, prelude(): pl.pallas_call(prelude_kernel, out_shape=[shape((24, HD), jnp.int32), plt...  3.82 us
    pallas_call x1, Pallas kernels, project_keyval(): pl.pallas_call(keyval_kernel, out_shape=[pltpu.HBM(*x) for x in (*kept, (...  2.62 us
  transfers between devices with their start and end apart: 9, of which 5 were waited for; matrix products, arithmetic and copies ran while one was open for 2% of the time, Pallas kernels for 44%

profile of v14, /device:TPU:0, one launch (start us, length us, event | category | flops | bytes accessed | tf_op | source)
XLA Modules:
  0.0 73.1 jit_solution(12811548701639224763)
XLA Ops:
  0.6 0.1 collective-permute-start
  0.7 2.1 %collective-permute-start.1 = (bf16[512,1024]{1,0:T(8,128)(2,1)}, bf16[512,1024]{1,0:T(8,128)(2,1)S(1)}, u32[]{:S(2)}, u32[]{:S(2)}) collective-permute-start(bf16[512,1024]{1,0:T(8,128)(2,1)} %refs_1_.3), channel_id=1, source_target_pairs={{0,2},{1,7},{2,4},{3,1},{4,6},{5,3},{6,0},{7,5},{8,10},{9,15},{10,... | collective-permute-start | bytes 3145736 | tf_op jit(solution)/shard_map/ppermute | solution.py:479
  2.8 3.8 %prelude.1 = (s32[24,128]{1,0:T(8,128)S(1)}, bf16[64,128,128]{2,1,0:T(8,128)(2,1)}) custom-call(s32[16,32]{1,0:T(8,128)} %refs_0_.1, s32[16,32]{1,0:T(8,128)} %refs_1_.2, s32[8,16]{1,0:T(8,128)} %bitcast.7, bf16[64,128,128]{2,1,0:T(8,128)(2,1)} %bitcast.5), custom_call_target="tpu_custom_call" | custom-call | bytes 1 | tf_op jit(solution)/shard_map/prelude/pallas_call | solution.py:120
  6.6 0.0 collective-permute-done.refs_1_
  6.6 2.0 %collective-permute-start.3 = (bf16[512,1024]{1,0:T(8,128)(2,1)S(1)}, bf16[512,1024]{1,0:T(8,128)(2,1)}, u32[]{:S(2)}, u32[]{:S(2)}) collective-permute-start(bf16[512,1024]{1,0:T(8,128)(2,1)S(1)} %after.3.refs_0_), channel_id=1, source_target_pairs={{0,2},{1,7},{2,4},{3,1},{4,6},{5,3},{6,0},{7,5},{8,10},{9,15},{10,... | collective-permute-start | bytes 3145736 | tf_op jit(solution)/shard_map/ppermute | solution.py:479
  8.6 7.1 %all-to-all-start = ((bf16[64,128,128]{2,1,0:T(8,128)(2,1)}), bf16[64,128,128]{2,1,0:T(8,128)(2,1)}, u32[]{:S(2)}, u32[]{:S(2)}) async-start(bf16[64,128,128]{2,1,0:T(8,128)(2,1)} %get-tuple-element.42), calls=%async_computation | async-start | bytes 4194304 | tf_op jit(solution)/shard_map/all_to_all | solution.py:496
  15.8 1.0 %fusion = (f32[512,64]{1,0:T(8,128)S(1)}, f32[512,64]{1,0:T(8,128)S(1)}, f32[512,64]{1,0:T(8,128)S(1)}) fusion(f32[64]{0:T(128)S(1)} %negate_power_fusion, f32[512]{0:T(512)S(1)} %add_convert_fusion), kind=kLoop, calls=%fused_computation.4 | loop fusion | flops 65536 | bytes 395520 | tf_op jit(solution)/shard_map/neg | solution.py:492
  16.8 0.2 pad_maximum_fusion
  17.0 0.0 copy-start
  17.0 0.0 copy-start.1
  17.0 3.9 %project.3 = (f32[512,512]{1,0:T(8,128)S(1)}, f32[512,256]{1,0:T(8,128)S(1)}, f32[512,128]{1,0:T(8,128)S(1)}) custom-call(bf16[512,1024]{1,0:T(8,128)(2,1)S(1)} %after.3.refs_0_, bf16[512,1024]{1,0:T(8,128)(2,1)} %refs_1_.3, bf16[8192,512]{1,0:T(8,128)(2,1)} %refs_7_.1, bf16[8192,256]{1,0:T(8,128)(2,1)} %refs_3_.5, ...), custom_call_target="tpu_custom_call" | custom-call | bytes 1 | tf_op jit(solution)/shard_map/project/pallas_call | solution.py:226
  20.8 0.0 collective-permute-done.1.refs_1_
  20.9 1.7 %collective-permute-start.5 = (bf16[512,1024]{1,0:T(8,128)(2,1)S(1)}, bf16[512,1024]{1,0:T(8,128)(2,1)S(1)}, u32[]{:S(2)}, u32[]{:S(2)}) collective-permute-start(bf16[512,1024]{1,0:T(8,128)(2,1)S(1)} %after.4.refs_0_), channel_id=1, source_target_pairs={{0,2},{1,7},{2,4},{3,1},{4,6},{5,3},{6,0},{7,5},{8,10},{9,15},{10,... | collective-permute-start | bytes 3145736 | tf_op jit(solution)/shard_map/ppermute | solution.py:479
  22.6 0.0 collective-permute-start.2
  22.6 6.7 %collective-permute-done.3.refs_1_ = bf16[512,1024]{1,0:T(8,128)(2,1)} collective-permute-done((bf16[512,1024]{1,0:T(8,128)(2,1)S(1)}, bf16[512,1024]{1,0:T(8,128)(2,1)}, u32[]{:S(2)}, u32[]{:S(2)}) %collective-permute-start.3) | collective-permute-done | bytes 1048608 | tf_op jit(solution)/shard_map/ppermute | solution.py:479
  29.2 0.0 collective-permute-start.4
  29.3 4.7 %project.4 = (f32[512,512]{1,0:T(8,128)S(1)}, f32[512,256]{1,0:T(8,128)S(1)}, f32[512,128]{1,0:T(8,128)S(1)}) custom-call(bf16[512,1024]{1,0:T(8,128)(2,1)S(1)} %after.4.refs_0_, bf16[512,1024]{1,0:T(8,128)(2,1)} %collective-permute-done.3.refs_1_, bf16[8192,512]{1,0:T(8,128)(2,1)} %refs_7_.1, bf16[8192,256]{1,0:T(8,128)(2,1)} %refs_3_.5, ...), custom_call_target="tpu_custom_call" | custom-call | flops 20000000000 | bytes 1 | tf_op jit(solution)/shard_map/project/pallas_call | solution.py:226
  34.0 0.0 collective-permute-done.2.refs_0_
  34.0 0.0 collective-permute-done.4.refs_1_
  34.0 3.9 %project.5 = (f32[512,512]{1,0:T(8,128)S(1)}, f32[512,256]{1,0:T(8,128)S(1)}, f32[512,128]{1,0:T(8,128)S(1)}, bf16[2,1024,512]{2,1,0:T(8,128)(2,1)S(1)}, bf16[2,1024,256]{2,1,0:T(8,128)(2,1)S(1)}) custom-call(bf16[512,1024]{1,0:T(8,128)(2,1)S(1)} %collective-permute-done.2.refs_0_, bf16[512,1024]{1,0:T(8,128)(2,1)S(1)} %collective-permute-done.4.refs_1_, ...), custom_call_target="tpu_custom_call" | custom-call | bytes 1 | tf_op jit(solution)/shard_map/project/pallas_call | solution.py:226
  37.9 2.5 %collective-permute-done.5.refs_1_ = bf16[512,1024]{1,0:T(8,128)(2,1)S(1)} collective-permute-done((bf16[512,1024]{1,0:T(8,128)(2,1)S(1)}, bf16[512,1024]{1,0:T(8,128)(2,1)S(1)}, u32[]{:S(2)}, u32[]{:S(2)}) %collective-permute-start.5) | collective-permute-done | bytes 1048608 | tf_op jit(solution)/shard_map/ppermute | solution.py:479
  40.4 0.0 collective-permute-start.6
  40.4 2.0 %project_far.1 = (f32[512,512]{1,0:T(8,128)}, f32[512,256]{1,0:T(8,128)S(1)}, f32[512,128]{1,0:T(8,128)S(1)}) custom-call(bf16[512,1024]{1,0:T(8,128)(2,1)S(1)} %after.5.x_ref, bf16[2,1024,512]{2,1,0:T(8,128)(2,1)S(1)} %get-tuple-element.31.wq_ref, bf16[2,1024,256]{2,1,0:T(8,128)(2,1)S(1)} %get-tuple-element.32.wkv_ref, ...), custom_call_target="tpu_custom_call" | custom-call | bytes 1 | tf_op jit(solution)/shard_map/project_far/pallas_call | solution.py:259
  42.4 0.6 collective-permute-done.6.x_ref
  43.0 0.0 copy-done
  43.0 0.0 copy-done.1
  43.0 2.6 %project_keyval.1 = (bf16[512,128]{1,0:T(8,128)(2,1)}, bf16[512,256]{1,0:T(8,128)(2,1)}, f32[512,128]{1,0:T(8,128)}, bf16[512,1024]{1,0:T(8,128)(2,1)}, bf16[32,128,128]{2,1,0:T(8,128)(2,1)}) custom-call(s32[24,128]{1,0:T(8,128)S(1)} %get-tuple-element.23.refs_0_.table_ref, bf16[512,1024]{1,0:T(8,128)(2,1)S(1)} %collective-permute-done.6.x_ref, ...), custom_call_target="tpu_custom_call" | custom-call | bytes 1 | tf_op jit(solution)/shard_map/project_keyval/pallas_call | solution.py:337
  45.7 4.2 %all-to-all-done.refs_8_ = bf16[64,128,128]{2,1,0:T(8,128)(2,1)} async-done(((bf16[64,128,128]{2,1,0:T(8,128)(2,1)}), bf16[64,128,128]{2,1,0:T(8,128)(2,1)}, u32[]{:S(2)}, u32[]{:S(2)}) %all-to-all-start) | async-done | bytes 2097184 | tf_op jit(solution)/shard_map/all_to_all | solution.py:496
  49.9 3.8 %all-to-all-start.1 = ((bf16[32,128,128]{2,1,0:T(8,128)(2,1)}), bf16[32,128,128]{2,1,0:T(8,128)(2,1)S(1)}, u32[]{:S(2)}, u32[]{:S(2)}) async-start(bf16[32,128,128]{2,1,0:T(8,128)(2,1)} %get-tuple-element.43), calls=%async_computation.1 | async-start | bytes 2097152 | tf_op jit(solution)/shard_map/all_to_all | solution.py:496
  53.7 11.2 %attend.1 = bf16[512,512]{1,0:T(8,128)(2,1)} custom-call(s32[24,128]{1,0:T(8,128)S(1)} %get-tuple-element.23.refs_0_.table_ref, f32[512,512]{1,0:T(8,128)} %get-tuple-element.35.refs_0_, bf16[512,1024]{1,0:T(8,128)(2,1)} %get-tuple-element.38.refs_1_, f32[512,128]{1,0:T(8,128)} %get-tuple-element.39.refs_2_, f32[512,128]{1,0:T(8,128)} %copy-done, ...), custom_call_target="tpu_custom_call" | custom-call | flops 5368709120 | bytes 8388608 | tf_op jit(solution)/shard_map/attend/pallas_call | solution.py:417
  65.0 6.2 %all-to-all-done.1.received_ref = bf16[32,128,128]{2,1,0:T(8,128)(2,1)S(1)} async-done(((bf16[32,128,128]{2,1,0:T(8,128)(2,1)}), bf16[32,128,128]{2,1,0:T(8,128)(2,1)S(1)}, u32[]{:S(2)}, u32[]{:S(2)}) %all-to-all-start.1) | async-done | bytes 1048608 | tf_op jit(solution)/shard_map/all_to_all | solution.py:496
  71.1 1.8 %place_pages.1 = bf16[32,128,128]{2,1,0:T(8,128)(2,1)} custom-call(s32[24,128]{1,0:T(8,128)S(1)} %get-tuple-element.23.refs_0_.table_ref, bf16[32,128,128]{2,1,0:T(8,128)(2,1)S(1)} %all-to-all-done.1.received_ref), custom_call_target="tpu_custom_call" | custom-call | bytes 2097152 | tf_op jit(solution)/shard_map/place_pages/pallas_call | solution.py:460
  (5 shorter events, 0.0 us)
Async XLA Ops:
  0.6 6.0 %collective-permute-start = (bf16[512,1024]{1,0:T(8,128)(2,1)}, bf16[512,1024]{1,0:T(8,128)(2,1)S(1)}, u32[]{:S(2)}, u32[]{:S(2)}) collective-permute-start(bf16[512,1024]{1,0:T(8,128)(2,1)} %refs_1_.3), channel_id=1, source_target_pairs={{0,1},{1,0},{2,3},{3,2},{4,5},{5,4},{6,7},{7,6},{8,9},{9,8},{10,11... | collective-permute-start | bytes 3145736 | tf_op jit(solution)/shard_map/ppermute | solution.py:483
  0.7 20.1 %collective-permute-start.1 = (bf16[512,1024]{1,0:T(8,128)(2,1)}, bf16[512,1024]{1,0:T(8,128)(2,1)S(1)}, u32[]{:S(2)}, u32[]{:S(2)}) collective-permute-start(bf16[512,1024]{1,0:T(8,128)(2,1)} %refs_1_.3), channel_id=1, source_target_pairs={{0,2},{1,7},{2,4},{3,1},{4,6},{5,3},{6,0},{7,5},{8,10},{9,15},{10,... | collective-permute-start | bytes 3145736 | tf_op jit(solution)/shard_map/ppermute | solution.py:479
  6.6 22.6 %collective-permute-start.3 = (bf16[512,1024]{1,0:T(8,128)(2,1)S(1)}, bf16[512,1024]{1,0:T(8,128)(2,1)}, u32[]{:S(2)}, u32[]{:S(2)}) collective-permute-start(bf16[512,1024]{1,0:T(8,128)(2,1)S(1)} %after.3.refs_0_), channel_id=1, source_target_pairs={{0,2},{1,7},{2,4},{3,1},{4,6},{5,3},{6,0},{7,5},{8,10},{9,15},{10,... | collective-permute-start | bytes 3145736 | tf_op jit(solution)/shard_map/ppermute | solution.py:479
  8.6 41.3 %all-to-all-start = ((bf16[64,128,128]{2,1,0:T(8,128)(2,1)}), bf16[64,128,128]{2,1,0:T(8,128)(2,1)}, u32[]{:S(2)}, u32[]{:S(2)}) async-start(bf16[64,128,128]{2,1,0:T(8,128)(2,1)} %get-tuple-element.42), calls=%async_computation | async-start | bytes 4194304 | tf_op jit(solution)/shard_map/all_to_all | solution.py:496
  17.0 26.1 %copy-start = (f32[512,128]{1,0:T(8,128)}, f32[512,128]{1,0:T(8,128)S(1)}, u32[]{:S(2)}) copy-start(f32[512,128]{1,0:T(8,128)S(1)} %get-tuple-element.49.refs_4_.cos_ref.refs_3_) | copy-start | bytes 786436
  17.0 26.1 %copy-start.1 = (f32[512,128]{1,0:T(8,128)}, f32[512,128]{1,0:T(8,128)S(1)}, u32[]{:S(2)}) copy-start(f32[512,128]{1,0:T(8,128)S(1)} %get-tuple-element.50.refs_5_.sin_ref.refs_4_) | copy-start | bytes 786436
  20.9 19.5 %collective-permute-start.5 = (bf16[512,1024]{1,0:T(8,128)(2,1)S(1)}, bf16[512,1024]{1,0:T(8,128)(2,1)S(1)}, u32[]{:S(2)}, u32[]{:S(2)}) collective-permute-start(bf16[512,1024]{1,0:T(8,128)(2,1)S(1)} %after.4.refs_0_), channel_id=1, source_target_pairs={{0,2},{1,7},{2,4},{3,1},{4,6},{5,3},{6,0},{7,5},{8,10},{9,15},{10,... | collective-permute-start | bytes 3145736 | tf_op jit(solution)/shard_map/ppermute | solution.py:479
  22.6 11.4 %collective-permute-start.2 = (bf16[512,1024]{1,0:T(8,128)(2,1)S(1)}, bf16[512,1024]{1,0:T(8,128)(2,1)S(1)}, u32[]{:S(2)}, u32[]{:S(2)}) collective-permute-start(bf16[512,1024]{1,0:T(8,128)(2,1)S(1)} %after.4.refs_0_), channel_id=1, source_target_pairs={{0,1},{1,0},{2,3},{3,2},{4,5},{5,4},{6,7},{7,6},{8,9},{9,8},{10,11... | collective-permute-start | bytes 3145736 | tf_op jit(solution)/shard_map/ppermute | solution.py:483
  29.2 4.8 %collective-permute-start.4 = (bf16[512,1024]{1,0:T(8,128)(2,1)}, bf16[512,1024]{1,0:T(8,128)(2,1)S(1)}, u32[]{:S(2)}, u32[]{:S(2)}) collective-permute-start(bf16[512,1024]{1,0:T(8,128)(2,1)} %collective-permute-done.3.refs_1_), channel_id=1, source_target_pairs={{0,1},{1,0},{2,3},{3,2},{4,5},{5,4},{6,7},{7,6},{8,9},{9,8},{10,11... | collective-permute-start | bytes 3145736 | tf_op jit(solution)/shard_map/ppermute | solution.py:483
  40.4 2.7 %collective-permute-start.6 = (bf16[512,1024]{1,0:T(8,128)(2,1)S(1)}, bf16[512,1024]{1,0:T(8,128)(2,1)S(1)}, u32[]{:S(2)}, u32[]{:S(2)}) collective-permute-start(bf16[512,1024]{1,0:T(8,128)(2,1)S(1)} %after.5.x_ref), channel_id=1, source_target_pairs={{0,1},{1,0},{2,3},{3,2},{4,5},{5,4},{6,7},{7,6},{8,9},{9,8},{10,11... | collective-permute-start | bytes 3145736 | tf_op jit(solution)/shard_map/ppermute | solution.py:483
  49.9 21.2 %all-to-all-start.1 = ((bf16[32,128,128]{2,1,0:T(8,128)(2,1)}), bf16[32,128,128]{2,1,0:T(8,128)(2,1)S(1)}, u32[]{:S(2)}, u32[]{:S(2)}) async-start(bf16[32,128,128]{2,1,0:T(8,128)(2,1)} %get-tuple-element.43), calls=%async_computation.1 | async-start | bytes 2097152 | tf_op jit(solution)/shard_map/all_to_all | solution.py:496
